TPU v7x, 32 devices: a whole 2x2x4 slice. The times are simulated.
32 devices in a mesh: pages: 8 (over y, x, core), emb: 4 (over z).
Axes of the slice: x: 2, y: 2, z: 4, core: 2. Of those that a mesh axis runs over, the one named last changes fastest.
Arguments:
- text_embed: bfloat16 [16384, 1024], P(('pages', 'emb')), may hold values from -6 to 6
- boxes: int32 [4, 16384], P(None, ('pages', 'emb')), may hold values from 0 to 1000, as said below
- layout_tables: float32 [4, 1024, 1024], P('emb'), may hold values from -3 to 3
- emb_gain: float32 [1024], replicated, may hold values from 0.5 to 1.5
- emb_bias: float32 [1024], replicated, may hold values from -1.5 to 1.5
- w_qkv: bfloat16 [1024, 3072], replicated, may hold values from -0.1875 to 0.1875
- b_query: float32 [1024], replicated, may hold values from -1.5 to 1.5
- b_value: float32 [1024], replicated, may hold values from -1.5 to 1.5
- w_out: bfloat16 [1024, 1024], replicated, may hold values from -2 to 2
- b_out: float32 [1024], replicated, may hold values from -1.5 to 1.5
- attn_gain: float32 [1024], replicated, may hold values from 0.5 to 1.5
- attn_bias: float32 [1024], replicated, may hold values from -1.5 to 1.5
- w_in: bfloat16 [1024, 4096], replicated, may hold values from -0.1875 to 0.1875
- b_in: float32 [4096], replicated, may hold values from -1.5 to 1.5
- w_back: bfloat16 [4096, 1024], replicated, may hold values from -0.09375 to 0.09375
- b_back: float32 [1024], replicated, may hold values from -1.5 to 1.5
- ffn_gain: float32 [1024], replicated, may hold values from 0.5 to 1.5
- ffn_bias: float32 [1024], replicated, may hold values from -1.5 to 1.5
- cotangent: bfloat16 [16384, 1024], P(('pages', 'emb')), may hold values from -6 to 6
Outputs:
- output: bfloat16 [16384, 1024], P(('pages', 'emb'))
- grad_text: float32 [16384, 1024], P(('pages', 'emb'))
- grad_tables: float32 [4, 1024, 1024], P('emb', 'pages')
- grad_emb_gain: float32 [1024], P('pages')
- grad_emb_bias: float32 [1024], P('pages')
- grad_qkv: float32 [1024, 3072], P('pages')
- grad_query_bias: float32 [1024], P('pages')
- grad_value_bias: float32 [1024], P('pages')
- grad_out: float32 [1024, 1024], P('pages')
- grad_out_bias: float32 [1024], P('pages')
- grad_attn_gain: float32 [1024], P('pages')
- grad_attn_bias: float32 [1024], P('pages')
- grad_in: float32 [1024, 4096], P('pages')
- grad_in_bias: float32 [4096], P('pages')
- grad_back: float32 [4096, 1024], P('pages')
- grad_back_bias: float32 [1024], P('pages')
- grad_ffn_gain: float32 [1024], P('pages')
- grad_ffn_bias: float32 [1024], P('pages')
- rms_grad: float32 [], replicated
Inputs may be any that keep to these rules, and one draw needn't show every extreme that they name: `boxes`: rows are left x, top y, right x, bottom y of each token's cell, with right >= left and bottom >= top.
All inputs are finite; a program needn't handle non-finite values.
Results may differ from a plain program's by a relative error of at most 0.014.
Values sent between devices are 32-bit elements; how exact they have to be, the bound alone decides.
No kernel may reach another device: no remote copies, remote signals or barrier semaphores. Data moves between devices by JAX's collectives and lax.ppermute only.
A program may use at most 256 MiB of HBM per device.

v0:
```python
import jax
import jax.numpy as jnp
from jax import lax
from jax.sharding import PartitionSpec as P

HEADS = 16
HEAD = 64
PAGE = 512


EPSILON = 1e-05
SQRT_HALF = 0.7071067811865476
INV_ROOT_TAU = 0.3989422804014327


def normalize(values):
    averaged = jnp.mean(values, -1, keepdims=True)
    centered = values - averaged
    inverse = lax.rsqrt(jnp.mean(centered * centered, -1, keepdims=True) + EPSILON)
    return (centered * inverse, inverse)


def norm_back(incoming, normed, inverse, gain):
    scaled = incoming * gain
    offset_mean = jnp.mean(scaled, -1, keepdims=True)
    along_mean = jnp.mean(scaled * normed, -1, keepdims=True)
    return (
        inverse * (scaled - offset_mean - normed * along_mean),
        jnp.sum(incoming * normed, 0),
        jnp.sum(incoming, 0),
    )


def gelu_slope(pre_act):
    return (
        0.5 * (1.0 + lax.erf(pre_act * SQRT_HALF))
        + pre_act * jnp.exp(-0.5 * pre_act * pre_act) * INV_ROOT_TAU
    )


def matmul(left, right):
    return jnp.dot(left, right, preferred_element_type=jnp.float32)


def outer_sum(left, right):
    return jnp.einsum("ti,tj->ij", left, right, preferred_element_type=jnp.float32)


def back_mul(left, right):
    return jnp.einsum("tj,ij->ti", left, right, preferred_element_type=jnp.float32)


def owner_indices(box_rows, table_owner):
    left_x = box_rows[0]
    top_y = box_rows[1]
    right_x = box_rows[2]
    bottom_y = box_rows[3]
    first_idx = jnp.where(
        table_owner == 0,
        left_x,
        jnp.where(
            table_owner == 1, top_y, jnp.where(table_owner == 2, right_x - left_x, bottom_y - top_y)
        ),
    )
    second_idx = jnp.where(table_owner == 0, right_x, bottom_y)
    return (first_idx, second_idx)


def look_rows(table, first_idx, second_idx, table_owner):
    single = jnp.take(table, first_idx, axis=0)
    return lax.cond(
        table_owner < 2, lambda: single + jnp.take(table, second_idx, axis=0), lambda: single
    )


def segment_rows(incoming, index_rows, entries):
    return jax.ops.segment_sum(incoming, index_rows, num_segments=entries)


def table_rows_grad(incoming, first_idx, second_idx, table_owner, entries):
    single = segment_rows(incoming, first_idx, entries)
    return lax.cond(
        table_owner < 2,
        lambda: single + segment_rows(incoming, second_idx, entries),
        lambda: single,
    )


def on_device(
    text_embed,
    boxes,
    layout_tables,
    emb_gain,
    emb_bias,
    w_qkv,
    b_query,
    b_value,
    w_out,
    b_out,
    attn_gain,
    attn_bias,
    w_in,
    b_in,
    w_back,
    b_back,
    ffn_gain,
    ffn_bias,
    cotangent,
):
    wide = jnp.float32
    narrow = jnp.bfloat16
    token_rows = text_embed.shape[0]
    model_width = text_embed.shape[1]
    entries = layout_tables.shape[1]
    page_count = token_rows // PAGE
    score_scale = HEAD ** (-0.5)
    table_owner = lax.axis_index("emb")
    group_boxes = lax.all_gather(boxes, "emb", axis=1, tiled=True)
    first_idx, second_idx = owner_indices(group_boxes, table_owner)
    layout = lax.psum_scatter(
        look_rows(layout_tables[0], first_idx, second_idx, table_owner),
        "emb",
        scatter_dimension=0,
        tiled=True,
    )
    normed_emb, inverse_emb = normalize(text_embed.astype(wide) + layout)
    hidden_emb = normed_emb * emb_gain + emb_bias
    emb_low = hidden_emb.astype(narrow)
    bias_qkv = jnp.concatenate([b_query, jnp.zeros_like(b_query), b_value])
    packed = (matmul(emb_low, w_qkv) + bias_qkv).astype(narrow)
    split_heads = packed.reshape(page_count, PAGE, 3, HEADS, HEAD)
    queries = split_heads[:, :, 0]
    key_rows = split_heads[:, :, 1]
    value_rows = split_heads[:, :, 2]
    scores = (
        jnp.einsum("bqhe,bkhe->bhqk", queries, key_rows, preferred_element_type=wide) * score_scale
    )
    maxima = jnp.max(scores, -1, keepdims=True)
    exponent = jnp.exp(scores - maxima)
    summed = jnp.sum(exponent, -1, keepdims=True)
    attn_probs = exponent / summed
    log_total = maxima + jnp.log(summed)
    context = jnp.einsum(
        "bhqk,bkhe->bqhe", attn_probs.astype(narrow), value_rows, preferred_element_type=wide
    )
    context_low = context.reshape(token_rows, model_width).astype(narrow)
    attended = matmul(context_low, w_out) + b_out
    normed_attn, inverse_attn = normalize(hidden_emb + attended)
    hidden_attn = normed_attn * attn_gain + attn_bias
    attn_low = hidden_attn.astype(narrow)
    pre_act = matmul(attn_low, w_in) + b_in
    expanded = jax.nn.gelu(pre_act, approximate=False).astype(narrow)
    returned = matmul(expanded, w_back) + b_back
    normed_ffn, inverse_ffn = normalize(hidden_attn + returned)
    output = (normed_ffn * ffn_gain + ffn_bias).astype(narrow)
    d_r2, g_ffn_gain, g_ffn_bias = norm_back(
        cotangent.astype(wide), normed_ffn, inverse_ffn, ffn_gain
    )
    d_returned = d_r2.astype(narrow)
    g_back = outer_sum(expanded, d_returned)
    g_back_bias = jnp.sum(d_returned.astype(wide), 0)
    d_pre = (back_mul(d_returned, w_back) * gelu_slope(pre_act)).astype(narrow)
    g_in = outer_sum(attn_low, d_pre)
    g_in_bias = jnp.sum(d_pre.astype(wide), 0)
    d_h1 = d_r2 + back_mul(d_pre, w_in)
    d_r1, g_attn_gain, g_attn_bias = norm_back(d_h1, normed_attn, inverse_attn, attn_gain)
    d_attended = d_r1.astype(narrow)
    g_out = outer_sum(context_low, d_attended)
    g_out_bias = jnp.sum(d_attended.astype(wide), 0)
    d_context = back_mul(d_attended, w_out).astype(narrow).reshape(page_count, PAGE, HEADS, HEAD)
    scores_again = (
        jnp.einsum("bqhe,bkhe->bhqk", queries, key_rows, preferred_element_type=wide) * score_scale
    )
    probs_again = jnp.exp(scores_again - log_total)
    d_values = jnp.einsum(
        "bhqk,bqhe->bkhe", probs_again.astype(narrow), d_context, preferred_element_type=wide
    )
    d_probs = jnp.einsum("bqhe,bkhe->bhqk", d_context, value_rows, preferred_element_type=wide)
    d_scores = (probs_again * (d_probs - jnp.sum(probs_again * d_probs, -1, keepdims=True))).astype(
        narrow
    )
    d_queries = (
        jnp.einsum("bhqk,bkhe->bqhe", d_scores, key_rows, preferred_element_type=wide) * score_scale
    )
    d_keys = (
        jnp.einsum("bhqk,bqhe->bkhe", d_scores, queries, preferred_element_type=wide) * score_scale
    )
    d_packed = (
        jnp.stack([d_queries, d_keys, d_values], 2)
        .reshape(token_rows, 3 * model_width)
        .astype(narrow)
    )
    g_qkv = outer_sum(emb_low, d_packed)
    g_query_bias = jnp.sum(d_packed[:, :model_width].astype(wide), 0)
    g_value_bias = jnp.sum(d_packed[:, 2 * model_width :].astype(wide), 0)
    d_h0 = d_r1 + back_mul(d_packed, w_qkv)
    d_embed, g_emb_gain, g_emb_bias = norm_back(d_h0, normed_emb, inverse_emb, emb_gain)
    square_sum = lax.psum(jnp.sum(d_embed * d_embed), ("pages", "emb"))
    entry_count = token_rows * model_width * lax.axis_size("pages") * lax.axis_size("emb")
    rms_grad = jnp.sqrt(square_sum / entry_count)
    table_grad = table_rows_grad(
        lax.all_gather(d_embed, "emb", axis=0, tiled=True),
        first_idx,
        second_idx,
        table_owner,
        entries,
    )
    shares = (
        lax.psum_scatter(g_qkv, "pages", scatter_dimension=0, tiled=True),
        lax.psum_scatter(g_out, "pages", scatter_dimension=0, tiled=True),
        lax.psum_scatter(g_in, "pages", scatter_dimension=0, tiled=True),
        lax.psum_scatter(g_back, "pages", scatter_dimension=0, tiled=True),
        lax.psum_scatter(g_emb_gain, "pages", scatter_dimension=0, tiled=True),
        lax.psum_scatter(g_emb_bias, "pages", scatter_dimension=0, tiled=True),
        lax.psum_scatter(g_query_bias, "pages", scatter_dimension=0, tiled=True),
        lax.psum_scatter(g_value_bias, "pages", scatter_dimension=0, tiled=True),
        lax.psum_scatter(g_out_bias, "pages", scatter_dimension=0, tiled=True),
        lax.psum_scatter(g_attn_gain, "pages", scatter_dimension=0, tiled=True),
        lax.psum_scatter(g_attn_bias, "pages", scatter_dimension=0, tiled=True),
        lax.psum_scatter(g_in_bias, "pages", scatter_dimension=0, tiled=True),
        lax.psum_scatter(g_back_bias, "pages", scatter_dimension=0, tiled=True),
        lax.psum_scatter(g_ffn_gain, "pages", scatter_dimension=0, tiled=True),
        lax.psum_scatter(g_ffn_bias, "pages", scatter_dimension=0, tiled=True),
        lax.psum_scatter(table_grad, "pages", scatter_dimension=0, tiled=True),
    )
    totals = lax.psum(
        (
            shares[0],
            shares[1],
            shares[2],
            shares[3],
            shares[4],
            shares[5],
            shares[6],
            shares[7],
            shares[8],
            shares[9],
            shares[10],
            shares[11],
            shares[12],
            shares[13],
            shares[14],
        ),
        "emb",
    )
    table_share = shares[15]
    return (
        output,
        d_embed,
        table_share[None],
        totals[4],
        totals[5],
        totals[0],
        totals[6],
        totals[7],
        totals[1],
        totals[8],
        totals[9],
        totals[10],
        totals[2],
        totals[11],
        totals[3],
        totals[12],
        totals[13],
        totals[14],
        rms_grad,
    )


def solution(mesh):
    return jax.shard_map(
        on_device,
        mesh=mesh,
        in_specs=(
            P(("pages", "emb"), None),
            P(None, ("pages", "emb")),
            P("emb", None, None),
            P(),
            P(),
            P(),
            P(),
            P(),
            P(),
            P(),
            P(),
            P(),
            P(),
            P(),
            P(),
            P(),
            P(),
            P(),
            P(("pages", "emb"), None),
        ),
        out_specs=(
            P(("pages", "emb"), None),
            P(("pages", "emb"), None),
            P("emb", "pages", None),
            P("pages"),
            P("pages"),
            P("pages", None),
            P("pages"),
            P("pages"),
            P("pages", None),
            P("pages"),
            P("pages"),
            P("pages"),
            P("pages", None),
            P("pages"),
            P("pages", None),
            P("pages"),
            P("pages"),
            P("pages"),
            P(),
        ),
        check_vma=False,
    )
```

profile of v0, /device:TPU:0, one launch (start us, length us, event | category | flops | bytes accessed | tf_op | source)
XLA Modules:
  0.0 1202.2 jit_solution(13714737835673490843)
XLA Ops:
  7.3 15.1 %all_gather.6 = s32[4,2048]{1,0:T(4,128)S(1)} all-gather(s32[4,512]{1,0:T(4,128)} %param.26), channel_id=1, replica_groups=mesh['pages'=8,'emb'=4] {'emb'}, dimensions={1}, use_global_device_ids=true | all-gather | bytes 40960 | tf_op jit(solution)/shard_map/all_gather | solution.py:118
  23.1 14.0 %gather_fusion.1 = f32[2048,1024]{1,0:T(8,128)} fusion(f32[1024,1024]{1,0:T(8,128)} %bitcast.84, s32[2048]{0:T(1024)S(1)} %broadcast_clamp_fusion), kind=kCustom, calls=%fused_computation.1.clone | custom fusion | bytes 16785408 | tf_op jit(solution)/shard_map/jit(_take)/gather | solution.py:70
  37.1 5.8 broadcast_select_fusion
  42.9 23.8 %conditional.2 = (f32[2048,1024]{1,0:T(8,128)}) conditional(s32[]{:T(128)} %convert_element_type.81, f32[2048,1024]{1,0:T(8,128)} %broadcast_select_fusion, (f32[1024,1024]{1,0:T(8,128)}, s32[2048]{0:T(1024)S(1)}, f32[2048,1024]{1,0:T(8,128)}) %tuple.74), branch_computations={%region_0.2_spmd, %region_1.3_spmd} | conditional | flops 4214784 | bytes 41979912 | solution.py:71
  42.9 14.0 %gather_fusion = f32[2048,1024]{1,0:T(8,128)} fusion(f32[1024,1024]{1,0:T(8,128)} %get-tuple-element.22, s32[2048]{0:T(1024)S(1)} %fusion), kind=kCustom, calls=%fused_computation.clone | custom fusion | bytes 16785408 | tf_op jit(solution)/shard_map/cond/branch_1_fun/jit(_take)/gather | solution.py:72
  56.9 9.8 select_add_fusion
  67.4 143.1 %reduce-scatter.7.cloned.1.call-done = f32[512,1024]{1,0:T(8,128)} async-done(((f32[2048,1024]{1,0:T(8,128)}), f32[512,1024]{1,0:T(8,128)}) %reduce-scatter.7.cloned.1.call-update) | async-done | bytes 2097168 | tf_op jit(solution)/shard_map/reduce_scatter | solution.py:120
  210.5 1.9 fusion.62
  213.7 7.8 add_convert_fusion
  221.6 4.7 copy.53
  226.2 9.7 multiply_reduce_fusion.1
  236.0 8.6 fusion.1
  244.6 8.1 fusion.35
  252.8 1.6 fusion.64
  254.8 27.5 %fusion.7 = (bf16[512,4096]{1,0:T(8,128)(2,1)S(1)}, f32[512,4096]{1,0:T(8,128)}) fusion(f32[4096]{0:T(1024)S(1)} %copy-done.29, bf16[1024,4096]{1,0:T(8,128)(2,1)} %param.37, f32[512,1024]{1,0:T(8,128)S(1)} %get-tuple-element.104, f32[1024]{0:T(1024)S(1)} %copy-done.34, f32[1024]{0:T(1024)S(1)} %copy-done.24, f32[512]{0:T(512)S(1)} %add_rsqrt_fusion.1, ...), kind=kOutput, calls=%fused_computation.21 | convolution fusion | flops 4436000768 | bytes 23097344 | tf_op jit(solution)/shard_map/dot_general | solution.py:42
  282.4 4.9 fusion.65
  287.7 1.5 fusion.30
  289.3 2.4 convert_reduce_fusion.2
  291.7 11.1 convert_reduce_fusion
  302.8 9.0 multiply_reduce_fusion.3
  313.9 2.3 convolution_convert_fusion
  316.2 1.6 copy.55
  317.8 11.6 multiply_reduce_fusion
  329.4 12.0 multiply_convert_fusion
  342.9 2.6 fusion.40
  345.5 7.9 fusion.41
  353.8 1.8 copy-done.4
  356.8 4.1 multiply_reduce_fusion.4
  360.9 2.5 multiply_reduce_fusion.2
  363.5 4.9 fusion.46
  369.1 11.3 fusion.58
  380.7 13.4 %fusion.54 = f32[1024,4096]{1,0:T(8,128)} fusion(bf16[512,4096]{1,0:T(8,128)(2,1)} %get-tuple-element.114, f32[512,1024]{1,0:T(8,128)} %copy-done.8, f32[1024]{0:T(1024)S(1)} %copy-done.34, f32[1024]{0:T(1024)S(1)} %copy-done.24, f32[512]{0:T(512)S(1)} %add_rsqrt_fusion.1, f32[512]{0:T(512)S(1)} %broadcast_multiply_fusion.7), kind=kOutput, calls=%fused_computation.135 | convolution fusion | flops 4297588736 | bytes 23080960 | tf_op jit(solution)/shard_map/ti,tj->ij/dot_general | solution.py:46
  394.2 13.3 %fusion.49 = f32[4096,1024]{1,0:T(8,128)} fusion(bf16[512,4096]{1,0:T(8,128)(2,1)} %copy-done.36, f32[512,1024]{1,0:T(8,128)} %copy-done.14), kind=kOutput, calls=%fused_computation.130 | convolution fusion | flops 4295491584 | bytes 23068672 | tf_op jit(solution)/shard_map/ti,tj->ij/dot_general | solution.py:46
  408.2 105.7 %all-gather.2.cloned.1.call-done = f32[2048,1024]{1,0:T(8,128)} async-done(((f32[512,1024]{1,0:T(8,128)}), f32[2048,1024]{1,0:T(8,128)}) %all-gather.2.cloned.1.call-update) | async-done | bytes 8388624 | tf_op jit(solution)/shard_map/all_gather | solution.py:202
  514.0 21.2 %scatter_custom_fusion.1 = f32[1024,1024]{1,0:T(8,128)} fusion(s32[2048]{0:T(1024)S(1)} %bitcast.104, f32[2048,1024]{1,0:T(8,128)} %all-gather.2.cloned.1.call-done, f32[]{:T(128)} %constant.19.clone.1), kind=kCustom, calls=%fused_computation.67 | custom fusion | flops 2097152 | bytes 4194816 | tf_op jit(solution)/shard_map/scatter-add | solution.py:77
  535.2 23.6 %conditional.3 = (f32[1024,1024]{1,0:T(8,128)}) conditional(s32[]{:T(128)} %convert_element_type.81, f32[1024,1024]{1,0:T(8,128)} %scatter_custom_fusion.1, (s32[2048]{0:T(1024)S(1)}, f32[1024,1024]{1,0:T(8,128)}, f32[2048,1024]{1,0:T(8,128)}) %tuple.75), branch_computations={%region_19.21_spmd, %region_20.23_spmd} | conditional | flops 2097152 | bytes 25174024 | solution.py:82
  535.2 23.6 %scatter_fusion = f32[1024,1024]{1,0:T(8,128)} fusion(f32[1024,1024]{1,0:T(8,128)} %get-tuple-element.24, s32[2048]{0:T(1024)S(1)} %get-tuple-element.25, f32[2048,1024]{1,0:T(8,128)} %get-tuple-element.26), kind=kCustom, calls=%fused_computation.2 | custom fusion | flops 2097152 | bytes 25174016 | tf_op jit(solution)/shard_map/cond/branch_1_fun/scatter-add | solution.py:77
  558.9 8.0 reduce-scatter.13.cloned.1.call-done
  566.9 96.2 %reduce-scatter.11.cloned.1.call-done = f32[128,3072]{1,0:T(8,128)} async-done(((f32[1024,3072]{1,0:T(8,128)}), f32[128,3072]{1,0:T(8,128)}) %reduce-scatter.11.cloned.1.call-update) | async-done | bytes 1572880 | tf_op jit(solution)/shard_map/reduce_scatter | solution.py:209
  663.1 119.8 %reduce-scatter.15.cloned.1.call-done = f32[128,4096]{1,0:T(8,128)} async-done(((f32[1024,4096]{1,0:T(8,128)}), f32[128,4096]{1,0:T(8,128)}) %reduce-scatter.15.cloned.1.call-update) | async-done | bytes 2097168 | tf_op jit(solution)/shard_map/reduce_scatter | solution.py:211
  782.9 119.8 %reduce-scatter.17.cloned.1.call-done = f32[512,1024]{1,0:T(8,128)} async-done(((f32[4096,1024]{1,0:T(8,128)}), f32[512,1024]{1,0:T(8,128)}) %reduce-scatter.17.cloned.1.call-update) | async-done | bytes 2097168 | tf_op jit(solution)/shard_map/reduce_scatter | solution.py:212
  904.6 39.8 %psum.127 = f32[]{:T(128)} all-reduce(f32[]{:T(128)} %get-tuple-element.86), channel_id=1, replica_groups=mesh['pages'=8,'emb'=4] {'pages','emb'}, use_global_device_ids=true, to_apply=%region_65.67 | all-reduce | flops 1 | bytes 8 | tf_op jit(solution)/shard_map/psum | solution.py:198
  944.4 1.9 convert_reduce_fusion.4
  946.4 24.1 %all-reduce.11 = (f32[1024]{0:T(1024)S(1)}, f32[1024]{0:T(1024)S(1)}, f32[1024]{0:T(1024)S(1)}, f32[1024]{0:T(1024)S(1)}, f32[1024]{0:T(1024)S(1)}, /*index=5*/f...) all-reduce(f32[1024]{0:T(1024)S(1)} %get-tuple-element.48, ...), channel_id=4, replica_groups=mesh['pages'=8,'emb'=4] {'pages'}, use_global_device_ids=true, to_apply=%region_24.26.clone | all-reduce | flops 14336 | bytes 114688
  972.0 12.0 %all-reduce.12 = (f32[128]{0:T(128)}, f32[128]{0:T(128)}, f32[128]{0:T(128)}, f32[128]{0:T(128)}, f32[128]{0:T(128)}, /*index=5*/f32[128]{0:T(128)}, f32[128]{0:...) all-reduce(f32[128]{0:T(128)S(1)} %dynamic-slice.1, ...), channel_id=1, replica_groups=mesh['pages'=8,'emb'=4] {'emb'}, use_global_device_ids=true, to_apply=%region_25.27 | all-reduce | flops 1792 | bytes 14336 | tf_op jit(solution)/shard_map/psum | solution.py:226
  984.1 202.3 %all-reduce.16.cloned.1.call-done = (f32[128,3072]{1,0:T(8,128)}, f32[128,1024]{1,0:T(8,128)}, f32[128,4096]{1,0:T(8,128)}, f32[512,1024]{1,0:T(8,128)}) async-done(((f32[128,3072]{1,0:T(8,128)}, f32[128,1024]{1,0:T(8,128)}, f32[128,4096]{1,0:T(8,128)}, f32[512,1024]{1,0:T(8,128)}), (f32[128,3072]{1,0:T(8,128)}, f32[128,1024]{1,0:T(8,128)}, f32[128,4096]{1,0:T(8,128)}, ...) | async-done | bytes 6291472 | tf_op jit(solution)/shard_map/psum | solution.py:226
  1186.3 2.9 copy.72
  1189.2 1.9 copy.73
  (141 shorter events, 14.5 us)
Async XLA Ops:
  7.2 245.5 %copy-start = (bf16[1024,1024]{1,0:T(8,128)(2,1)S(1)}, bf16[1024,1024]{1,0:T(8,128)(2,1)}, u32[]{:S(2)}) copy-start(bf16[1024,1024]{1,0:T(8,128)(2,1)} %param.33) | copy-start | bytes 6291460
  7.2 203.3 %reduce-scatter.7.cloned.1.call-start = ((), (), s32[]{:S(2)}) async-start(), calls=%async_computation.6 | async-start | bytes 10485760 | tf_op jit(solution)/shard_map/reduce_scatter | solution.py:120
  23.1 19.8 %copy-start.18 = (s32[2048]{0:T(1024)}, s32[2048]{0:T(1024)S(1)}, u32[]{:S(2)}) copy-start(s32[2048]{0:T(1024)S(1)} %broadcast_select_fusion.4) | copy-start | bytes 24580
  66.7 0.7 copy-start.25
  66.7 0.7 copy-start.26
  66.7 143.8 %copy-start.15 = (bf16[512,1024]{1,0:T(8,128)(2,1)S(1)}, bf16[512,1024]{1,0:T(8,128)(2,1)}, u32[]{:S(2)}) copy-start(bf16[512,1024]{1,0:T(8,128)(2,1)} %param.25) | copy-start | bytes 3145732
  66.7 147.0 %copy-start.28 = (f32[1024]{0:T(1024)S(1)}, f32[1024]{0:T(1024)}, u32[]{:S(2)}) copy-start(f32[1024]{0:T(1024)} %param.28) | copy-start | bytes 12292
  66.7 147.0 %copy-start.32 = (f32[1024]{0:T(1024)S(1)}, f32[1024]{0:T(1024)}, u32[]{:S(2)}) copy-start(f32[1024]{0:T(1024)} %param.29) | copy-start | bytes 12292
  66.8 447.2 %all-gather.2.cloned.1.call-start = ((), (), s32[]{:S(2)}) async-start(), calls=%async_computation.7 | async-start | bytes 10485760 | tf_op jit(solution)/shard_map/all_gather | solution.py:202
  212.4 1.3 copy-start.2
  244.6 8.2 copy-start.3
  244.6 8.2 copy-start.30
  252.7 1.7 copy-start.10
  252.7 2.0 copy-start.24
  252.8 2.0 copy-start.29
  252.8 2.0 copy-start.34
  252.8 29.6 %slice-start = ((s8[8388608]{0:T(1024)(128)(4,1)}), s8[4194304]{0:T(1024)(128)(4,1)S(1)}, s32[]{:S(2)}) async-start(s8[8388608]{0:T(1024)(128)(4,1)} %bitcast.105), calls=%async_computation.14 | async-start | bytes 8388608
  254.4 57.5 %copy-start.8 = (f32[512,1024]{1,0:T(8,128)}, f32[512,1024]{1,0:T(8,128)S(1)}, u32[]{:S(2)}) copy-start(f32[512,1024]{1,0:T(8,128)S(1)} %get-tuple-element.104) | copy-start | bytes 6291460
  254.8 27.6 %slice-start.1 = ((s8[8388608]{0:T(1024)(128)(4,1)}), s8[4194304]{0:T(1024)(128)(4,1)S(1)}, s32[]{:S(2)}) async-start(s8[8388608]{0:T(1024)(128)(4,1)} %bitcast.105), calls=%async_computation.15 | async-start | bytes 8388608
  254.8 27.6 %copy-start.31 = (f32[1024]{0:T(1024)S(1)}, f32[1024]{0:T(1024)}, u32[]{:S(2)}) copy-start(f32[1024]{0:T(1024)} %param.40) | copy-start | bytes 12292
  282.4 4.9 copy-start.36
  282.4 5.3 copy-start.9
  282.4 5.3 copy-start.22
  287.3 1.9 copy-start.27
  291.7 11.1 copy-start.14
  312.6 1.3 copy-start.6
  329.4 12.0 copy-start.1
  342.9 10.9 slice-start.2
  345.5 8.3 slice-start.3
  353.4 2.2 copy-start.4
  353.4 3.4 copy-start.7
  353.8 7.1 copy-start.5
  360.9 2.6 copy-start.11
  363.4 203.5 %reduce-scatter.13.cloned.1.call-start = ((), (), s32[]{:S(2)}) async-start(), calls=%async_computation.10 | async-start | bytes 4718592 | tf_op jit(solution)/shard_map/reduce_scatter | solution.py:210
  368.4 0.7 copy-start.33
  368.4 294.7 %reduce-scatter.11.cloned.1.call-start = ((), (), s32[]{:S(2)}) async-start(), calls=%async_computation.9 | async-start | bytes 14155776 | tf_op jit(solution)/shard_map/reduce_scatter | solution.py:209
  380.4 402.5 %reduce-scatter.15.cloned.1.call-start = ((), (), s32[]{:S(2)}) async-start(), calls=%async_computation.11 | async-start | bytes 18874368 | tf_op jit(solution)/shard_map/reduce_scatter | solution.py:211
  394.1 508.6 %reduce-scatter.17.cloned.1.call-start = ((), (), s32[]{:S(2)}) async-start(), calls=%async_computation.12 | async-start | bytes 18874368 | tf_op jit(solution)/shard_map/reduce_scatter | solution.py:212
  407.4 0.8 copy-start.17
  407.5 127.7 %copy-start.19 = (s32[2048]{0:T(1024)S(1)}, s32[2048]{0:T(1024)}, u32[]{:S(2)}) copy-start(s32[2048]{0:T(1024)} %copy-done.18) | copy-start | bytes 24580
  407.5 576.6 %reduce-scatter.9.cloned.1.call-start = ((), (), s32[]{:S(2)}) async-start(), calls=%async_computation.8 | async-start | bytes 4718592 | tf_op jit(solution)/shard_map/reduce_scatter | solution.py:224
  558.8 343.9 %copy-start.35 = (u32[32]{0:T(128)S(1)}, u32[32]{0:T(128)}, u32[]{:S(2)}) copy-start(u32[32]{0:T(128)} %constant.115) | copy-start | bytes 388
  558.8 627.5 %all-reduce.16.cloned.1.call-start = ((), (), s32[]{:S(2)}) async-start(), calls=%async_computation.13 | async-start | bytes 12582912 | tf_op jit(solution)/shard_map/psum | solution.py:226
  902.7 43.6 %copy-start.20 = (f32[1024]{0:T(1024)S(1)}, f32[1024]{0:T(1024)}, u32[]{:S(2)}) copy-start(f32[1024]{0:T(1024)} %get-tuple-element.50) | copy-start | bytes 12292
  902.7 43.7 %copy-start.21 = (f32[1024]{0:T(1024)S(1)}, f32[1024]{0:T(1024)}, u32[]{:S(2)}) copy-start(f32[1024]{0:T(1024)} %get-tuple-element.59) | copy-start | bytes 12292
  902.7 43.7 %copy-start.23 = (f32[1024]{0:T(1024)S(1)}, f32[1024]{0:T(1024)}, u32[]{:S(2)}) copy-start(f32[1024]{0:T(1024)} %get-tuple-element.88) | copy-start | bytes 12292
  1186.3 4.7 copy-start.13
  1186.3 6.1 copy-start.12
  (1 other events, 0.6 us)
Sparse Core Ops, SparseCore 0:
  66.8 143.6 reduce-scatter.6
  363.6 150.3 all-gather.1
  517.3 49.5 reduce-scatter.12
  570.7 92.3 reduce-scatter.10
  666.9 115.9 reduce-scatter.14
  786.7 115.9 reduce-scatter.16
  907.0 52.1 reduce-scatter.8
  961.8 224.4 all-reduce.15
where the time goes:
time: 1210 us; the launch traced here: 1200 us
  waiting for transfers between devices  795 us (66%)
  matrix products  153 us (13%)
  other arithmetic  93.4 us (8%)
  blocking collectives  91.1 us (8%)
  local copies, waits for them, and re-layouts  50.5 us (4%)
  between operations  18.4 us (2%)
    psum x1, waiting for transfers between devices, on_device(): lax.psum((shares[0], shares[1], shares[2], shares[3], shares[4], shares[5...  202 us
    reduce_scatter x1, waiting for transfers between devices, on_device(): lax.psum_scatter(look_rows(layout_tables[0], first_idx, second_idx, table...  143 us
    reduce_scatter x1, waiting for transfers between devices, on_device(): lax.psum_scatter(g_back, 'pages', scatter_dimension=0, tiled=True)  120 us
    reduce_scatter x1, waiting for transfers between devices, on_device(): lax.psum_scatter(g_in, 'pages', scatter_dimension=0, tiled=True)  120 us
    all_gather x1, waiting for transfers between devices, on_device(): lax.all_gather(d_embed, 'emb', axis=0, tiled=True)  106 us
    reduce_scatter x1, waiting for transfers between devices, on_device(): lax.psum_scatter(g_qkv, 'pages', scatter_dimension=0, tiled=True)  96.2 us
    scatter-add x2, other arithmetic, segment_rows(): return jax.ops.segment_sum(incoming, index_rows, num_segments=entries)  44.8 us
    dot_general x4, matrix products, outer_sum(): jnp.einsum('ti,tj->ij', left, right, preferred_element_type=jnp.float32)  42.9 us
  transfers between devices with their start and end apart: 8, of which 7 were waited for; matrix products, arithmetic and copies ran while one was open for 8% of the time, Pallas kernels for 0%

commit v1 on v0

--- a/solution.py
+++ b/solution.py
@@ -1,3 +1,5 @@
+import itertools
+
 import jax
 import jax.numpy as jnp
 from jax import lax
@@ -84,6 +86,58 @@
         lambda: single + segment_rows(incoming, second_idx, entries),
         lambda: single,
     )
+
+
+def relative(array, masks, me, lanes, first, last):
+    blocks = []
+    for flips in itertools.product((0, 1), repeat=len(masks)):
+        offset = sum(mask for mask, flip in zip(masks, flips) if flip)
+        start = jnp.bitwise_xor(me, offset) * lanes + first
+        blocks.append(lax.dynamic_slice_in_dim(array, start, last - first, 1))
+    return jnp.concatenate(blocks, 1)
+
+
+def swap(array, mask):
+    return lax.ppermute(
+        array, "pages", [(one, one ^ mask) for one in range(lax.axis_size("pages"))]
+    )
+
+
+def halve(kept, masks):
+    arrived = None
+    for mask in masks:
+        half = kept.shape[0] // 2
+        sent = kept[half:] if arrived is None else kept[half:] + arrived[half:]
+        kept = kept[:half] if arrived is None else kept[:half] + arrived[:half]
+        arrived = swap(sent, mask)
+    return kept if arrived is None else kept + arrived
+
+
+def weight_share(left, right, masks):
+    if len(masks) < 2:
+        return halve(outer_sum(left, right), masks)
+    half = left.shape[1] // 2
+    quarter = half // 2
+    from_core = swap(outer_sum(left[:, half:], right), masks[0])
+    sent = outer_sum(left[:, quarter:half], right) + from_core[quarter:]
+    arrived = swap(sent, masks[1])
+    kept = outer_sum(left[:, :quarter], right) + from_core[:quarter]
+    for mask in masks[2:]:
+        half = kept.shape[0] // 2
+        sent = kept[half:] + arrived[half:]
+        kept = kept[:half] + arrived[:half]
+        arrived = swap(sent, mask)
+    return kept + arrived
+
+
+def emb_total(share):
+    if lax.axis_size("emb") != 4:
+        return lax.psum(share, "emb")
+    plane = lax.axis_index("emb")
+    middle = jnp.logical_or(plane == 1, plane == 2)
+    share = share + lax.ppermute(share, "emb", [(0, 1), (3, 2)])
+    share = share + lax.ppermute(share, "emb", [(1, 2), (2, 1)])
+    return jnp.where(middle, share, lax.ppermute(share, "emb", [(1, 0), (2, 3)]))
 
 
 def on_device(
@@ -115,6 +169,13 @@
     page_count = token_rows // PAGE
     score_scale = HEAD ** (-0.5)
     table_owner = lax.axis_index("emb")
+    me = lax.axis_index("pages")
+    devices = lax.axis_size("pages")
+    outer_masks = [1 << bit for bit in range(1, devices.bit_length() - 1)]
+    turn = len(outer_masks) // 2
+    masks_one = [1] + outer_masks
+    masks_two = [1] + outer_masks[turn:] + outer_masks[:turn]
+    lanes = model_width // devices
     group_boxes = lax.all_gather(boxes, "emb", axis=1, tiled=True)
     first_idx, second_idx = owner_indices(group_boxes, table_owner)
     layout = lax.psum_scatter(
@@ -157,15 +218,37 @@
         cotangent.astype(wide), normed_ffn, inverse_ffn, ffn_gain
     )
     d_returned = d_r2.astype(narrow)
-    g_back = outer_sum(expanded, d_returned)
+    wide_lanes = expanded.shape[1] // devices
+    back_one = relative(expanded, masks_one, me, wide_lanes, 0, wide_lanes // 2)
+    back_two = relative(expanded, masks_two, me, wide_lanes, wide_lanes // 2, wide_lanes)
+    g_back = emb_total(
+        jnp.concatenate(
+            [
+                weight_share(back_one, d_returned, masks_one),
+                weight_share(back_two, d_returned, masks_two),
+            ],
+            0,
+        )
+    )
     g_back_bias = jnp.sum(d_returned.astype(wide), 0)
     d_pre = (back_mul(d_returned, w_back) * gelu_slope(pre_act)).astype(narrow)
-    g_in = outer_sum(attn_low, d_pre)
+    g_in = emb_total(
+        jnp.concatenate(
+            [
+                weight_share(
+                    relative(attn_low, masks_one, me, lanes, 0, lanes), d_pre[:, :2 * model_width], masks_one
+                ),
+                weight_share(
+                    relative(attn_low, masks_two, me, lanes, 0, lanes), d_pre[:, 2 * model_width:], masks_two
+                ),
+            ],
+            1,
+        )
+    )
     g_in_bias = jnp.sum(d_pre.astype(wide), 0)
     d_h1 = d_r2 + back_mul(d_pre, w_in)
     d_r1, g_attn_gain, g_attn_bias = norm_back(d_h1, normed_attn, inverse_attn, attn_gain)
     d_attended = d_r1.astype(narrow)
-    g_out = outer_sum(context_low, d_attended)
     g_out_bias = jnp.sum(d_attended.astype(wide), 0)
     d_context = back_mul(d_attended, w_out).astype(narrow).reshape(page_count, PAGE, HEADS, HEAD)
     scores_again = (
@@ -190,14 +273,55 @@
         .reshape(token_rows, 3 * model_width)
         .astype(narrow)
     )
-    g_qkv = outer_sum(emb_low, d_packed)
+    out_share = weight_share(
+        relative(context_low, masks_one, me, lanes, 0, lanes), d_attended, masks_one
+    )
+    qkv_one = weight_share(
+        relative(emb_low, masks_one, me, lanes, 0, lanes), d_packed[:, :model_width], masks_one
+    )
+    qkv_two = weight_share(
+        relative(emb_low, masks_two, me, lanes, 0, lanes), d_packed[:, model_width:], masks_two
+    )
+    both = emb_total(jnp.concatenate([out_share, qkv_one, qkv_two], 1))
+    g_out = both[:, :model_width]
+    g_qkv = both[:, model_width:]
     g_query_bias = jnp.sum(d_packed[:, :model_width].astype(wide), 0)
     g_value_bias = jnp.sum(d_packed[:, 2 * model_width :].astype(wide), 0)
     d_h0 = d_r1 + back_mul(d_packed, w_qkv)
     d_embed, g_emb_gain, g_emb_bias = norm_back(d_h0, normed_emb, inverse_emb, emb_gain)
-    square_sum = lax.psum(jnp.sum(d_embed * d_embed), ("pages", "emb"))
+    vectors = [
+        g_query_bias,
+        g_value_bias,
+        g_out_bias,
+        g_attn_gain,
+        g_attn_bias,
+        g_in_bias,
+        g_back_bias,
+        g_ffn_gain,
+        g_ffn_bias,
+        g_emb_gain,
+        g_emb_bias,
+        jnp.full((devices,), jnp.sum(d_embed * d_embed)),
+    ]
+    stacked = jnp.concatenate([vector.reshape(devices, -1) for vector in vectors], 1)
+    in_order = [
+        lax.dynamic_slice_in_dim(
+            stacked,
+            jnp.bitwise_xor(me, sum(mask for mask, flip in zip(masks_one, flips) if flip)),
+            1,
+            0,
+        )
+        for flips in itertools.product((0, 1), repeat=len(masks_one))
+    ]
+    vector_share = emb_total(halve(jnp.concatenate(in_order, 0), masks_one))[0]
+    totals = []
+    first = 0
+    for vector in vectors:
+        length = vector.shape[0] // devices
+        totals.append(vector_share[first : first + length])
+        first += length
     entry_count = token_rows * model_width * lax.axis_size("pages") * lax.axis_size("emb")
-    rms_grad = jnp.sqrt(square_sum / entry_count)
+    rms_grad = jnp.sqrt(totals[11][0] / entry_count)
     table_grad = table_rows_grad(
         lax.all_gather(d_embed, "emb", axis=0, tiled=True),
         first_idx,
@@ -205,64 +329,26 @@
         table_owner,
         entries,
     )
-    shares = (
-        lax.psum_scatter(g_qkv, "pages", scatter_dimension=0, tiled=True),
-        lax.psum_scatter(g_out, "pages", scatter_dimension=0, tiled=True),
-        lax.psum_scatter(g_in, "pages", scatter_dimension=0, tiled=True),
-        lax.psum_scatter(g_back, "pages", scatter_dimension=0, tiled=True),
-        lax.psum_scatter(g_emb_gain, "pages", scatter_dimension=0, tiled=True),
-        lax.psum_scatter(g_emb_bias, "pages", scatter_dimension=0, tiled=True),
-        lax.psum_scatter(g_query_bias, "pages", scatter_dimension=0, tiled=True),
-        lax.psum_scatter(g_value_bias, "pages", scatter_dimension=0, tiled=True),
-        lax.psum_scatter(g_out_bias, "pages", scatter_dimension=0, tiled=True),
-        lax.psum_scatter(g_attn_gain, "pages", scatter_dimension=0, tiled=True),
-        lax.psum_scatter(g_attn_bias, "pages", scatter_dimension=0, tiled=True),
-        lax.psum_scatter(g_in_bias, "pages", scatter_dimension=0, tiled=True),
-        lax.psum_scatter(g_back_bias, "pages", scatter_dimension=0, tiled=True),
-        lax.psum_scatter(g_ffn_gain, "pages", scatter_dimension=0, tiled=True),
-        lax.psum_scatter(g_ffn_bias, "pages", scatter_dimension=0, tiled=True),
-        lax.psum_scatter(table_grad, "pages", scatter_dimension=0, tiled=True),
-    )
-    totals = lax.psum(
-        (
-            shares[0],
-            shares[1],
-            shares[2],
-            shares[3],
-            shares[4],
-            shares[5],
-            shares[6],
-            shares[7],
-            shares[8],
-            shares[9],
-            shares[10],
-            shares[11],
-            shares[12],
-            shares[13],
-            shares[14],
-        ),
-        "emb",
-    )
-    table_share = shares[15]
+    table_share = lax.psum_scatter(table_grad, "pages", scatter_dimension=0, tiled=True)
     return (
         output,
         d_embed,
         table_share[None],
+        totals[9],
+        totals[10],
+        g_qkv,
+        totals[0],
+        totals[1],
+        g_out,
+        totals[2],
+        totals[3],
         totals[4],
+        g_in,
         totals[5],
-        totals[0],
+        g_back,
         totals[6],
         totals[7],
-        totals[1],
         totals[8],
-        totals[9],
-        totals[10],
-        totals[2],
-        totals[11],
-        totals[3],
-        totals[12],
-        totals[13],
-        totals[14],
         rms_grad,
     )
 

time: 1210 us -> 927 us (0.77)
  waiting for transfers between devices: 795 us -> 474 us
  blocking collectives: 91.1 us -> 15.1 us
  starting transfers between devices: 1.05 us -> 75.9 us
  other arithmetic: 93.4 us -> 125 us
    reduce_scatter x4 -> x0, waiting for transfers between devices: 344 us -> none  [the longest x1 120 us: on_device(): lax.psum_scatter(g_back, 'pages', scatter_dimension=0, tiled=True)]
    ppermute x0 -> x36, waiting for transfers between devices: none -> 331 us  [the longest x24 192 us: swap(): lax.ppermute(array, 'pages', [(one, one ^ mask) for one in range(lax.axis...]
    psum x1 -> x0, waiting for transfers between devices: 202 us -> none  [on_device(): lax.psum((shares[0], shares[1], shares[2], shares[3], shares[4], shares[5...]
    all_gather x1, waiting for transfers between devices: 106 us -> 0.02 us  [on_device(): lax.all_gather(d_embed, 'emb', axis=0, tiled=True)]
    ppermute x0 -> x36, starting transfers between devices: none -> 74.9 us  [the longest x4 42.2 us: emb_total(): share = share + lax.ppermute(share, 'emb', [(0, 1), (3, 2)])]
    psum x2 -> x0, blocking collectives: 51.9 us -> none  [the longest x1 39.8 us: on_device(): square_sum = lax.psum(jnp.sum(d_embed * d_embed), ('pages', 'emb'))]
    unnamed x1 -> x0, blocking collectives: 24.1 us -> none
    add x0 -> x25, other arithmetic: none -> 19.8 us  [the longest x4 9.57 us: emb_total(): share = share + lax.ppermute(share, 'emb', [(1, 2), (2, 1)])]
  transfers between devices with their start and end apart: 8 -> 39, of which waited for: 7 -> 17; matrix products, arithmetic and copies ran while one was open for 8% -> 16% of each run, Pallas kernels for 0% -> 0%
where the time goes in v1:
time: 927 us; the launch traced here: 923 us
  waiting for transfers between devices  474 us (51%)
  matrix products  157 us (17%)
  other arithmetic  125 us (13%)
  starting transfers between devices  75.9 us (8%)
  local copies, waits for them, and re-layouts  58.7 us (6%)
  between operations  17.5 us (2%)
  blocking collectives  15.1 us (2%)
    ppermute x24, waiting for transfers between devices, swap(): lax.ppermute(array, 'pages', [(one, one ^ mask) for one in range(lax.axis...  192 us
    reduce_scatter x1, waiting for transfers between devices, on_device(): lax.psum_scatter(look_rows(layout_tables[0], first_idx, second_idx, table...  143 us
    ppermute x4, waiting for transfers between devices, emb_total(): lax.ppermute(share, 'emb', [(1, 0), (2, 3)])  74.6 us
    ppermute x4, waiting for transfers between devices, emb_total(): share = share + lax.ppermute(share, 'emb', [(0, 1), (3, 2)])  64.3 us
    scatter-add x2, other arithmetic, segment_rows(): return jax.ops.segment_sum(incoming, index_rows, num_segments=entries)  44.4 us
    dot_general x21, matrix products, outer_sum(): jnp.einsum('ti,tj->ij', left, right, preferred_element_type=jnp.float32)  44.1 us
    ppermute x4, starting transfers between devices, emb_total(): share = share + lax.ppermute(share, 'emb', [(0, 1), (3, 2)])  42.2 us
    dot_general x4, matrix products, matmul(): return jnp.dot(left, right, preferred_element_type=jnp.float32)  39.7 us
  transfers between devices with their start and end apart: 39, of which 17 were waited for; matrix products, arithmetic and copies ran while one was open for 16% of the time, Pallas kernels for 0%

profile of v1, /device:TPU:0, one launch (start us, length us, event | category | flops | bytes accessed | tf_op | source)
XLA Modules:
  0.0 922.9 jit_solution(10424157087134305955)
XLA Ops:
  7.3 15.1 %all_gather.6 = s32[4,2048]{1,0:T(4,128)S(1)} all-gather(s32[4,512]{1,0:T(4,128)} %param.26), channel_id=1, replica_groups=mesh['pages'=8,'emb'=4] {'emb'}, dimensions={1}, use_global_device_ids=true | all-gather | bytes 40960 | tf_op jit(solution)/shard_map/all_gather | solution.py:179
  23.1 13.9 %gather_fusion.1 = f32[2048,1024]{1,0:T(8,128)} fusion(f32[1024,1024]{1,0:T(8,128)} %bitcast.134, s32[2048]{0:T(1024)S(1)} %broadcast_clamp_fusion), kind=kCustom, calls=%fused_computation.1.clone | custom fusion | bytes 16785408 | tf_op jit(solution)/shard_map/jit(_take)/gather | solution.py:72
  37.0 5.9 broadcast_select_fusion
  42.8 23.7 %conditional.2 = (f32[2048,1024]{1,0:T(8,128)}) conditional(s32[]{:T(128)} %convert_element_type.81, f32[2048,1024]{1,0:T(8,128)} %broadcast_select_fusion, (f32[1024,1024]{1,0:T(8,128)}, s32[2048]{0:T(1024)S(1)}, f32[2048,1024]{1,0:T(8,128)}) %tuple.116), branch_computations={%region_0.2_spmd, %region_1.3_spmd} | conditional | flops 4214784 | bytes 41979912 | solution.py:73
  42.8 13.9 %gather_fusion = f32[2048,1024]{1,0:T(8,128)} fusion(f32[1024,1024]{1,0:T(8,128)} %get-tuple-element.22, s32[2048]{0:T(1024)S(1)} %fusion), kind=kCustom, calls=%fused_computation.clone | custom fusion | bytes 16785408 | tf_op jit(solution)/shard_map/cond/branch_1_fun/jit(_take)/gather | solution.py:74
  56.7 9.9 %select_add_fusion = f32[2048,1024]{1,0:T(8,128)} fusion(f32[2048,1024]{1,0:T(8,128)} %get-tuple-element.17, f32[2048,1024]{1,0:T(8,128)} %gather_fusion, pred[2048]{0:T(1024)(128)(4,1)S(1)} %compare_and_fusion), kind=kLoop, calls=%fused_computation.4 | loop fusion | flops 4194304 | bytes 25167872 | tf_op jit(solution)/shard_map/cond/branch_1_fun/add | solution.py:74
  67.4 143.1 %reduce-scatter.3.cloned.1.call-done = f32[512,1024]{1,0:T(8,128)} async-done(((f32[2048,1024]{1,0:T(8,128)}), f32[512,1024]{1,0:T(8,128)}) %reduce-scatter.3.cloned.1.call-update) | async-done | bytes 2097168 | tf_op jit(solution)/shard_map/reduce_scatter | solution.py:181
  215.0 7.5 add_convert_fusion
  222.5 4.7 copy.47
  227.2 9.7 %multiply_reduce_fusion.1 = (f32[16,512]{1,0:T(8,128)S(1)}, f32[16,512,512]{1,2,0:T(8,128)}) fusion(bf16[1,512,3,16,64]{1,4,3,2,0:T(8,128)(2,1)} %bitcast.144), kind=kOutput, calls=%fused_computation.14 | convolution fusion | flops 545251328 | bytes 18907136 | tf_op jit(solution)/shard_map/bqhe,bkhe->bhqk/dot_general | solution.py:197
  236.9 8.6 fusion.1
  245.5 8.1 fusion.65
  256.6 25.7 %fusion.7 = (bf16[512,4096]{1,0:T(8,128)(2,1)S(1)}, f32[512,4096]{1,0:T(8,128)}) fusion(f32[4096]{0:T(1024)S(1)} %copy-done.81, bf16[512,1024]{1,0:T(8,128)(2,1)S(1)} %fusion.34, bf16[1024,4096]{1,0:T(8,128)(2,1)} %param.37), kind=kOutput, calls=%fused_computation.21 | convolution fusion | flops 4433379328 | bytes 22036480 | tf_op jit(solution)/shard_map/dot_general | solution.py:44
  282.4 4.8 fusion.205
  292.5 11.5 %convert_reduce_fusion = (f32[4096]{0:T(1024)}, bf16[512,4096]{1,0:T(8,128)(2,1)S(1)}) fusion(f32[512,4096]{1,0:T(8,128)} %get-tuple-element.141, f32[4096]{0:T(1024)S(1)} %copy-done.81, bf16[512,1024]{1,0:T(8,128)(2,1)S(1)} %get-tuple-element.63, bf16[4096,1024]{1,0:T(8,128)(2,1)} %param.39), kind=kOutput, calls=%fused_computation.28 | convolution fusion | flops 4322226176 | bytes 22052864 | tf_op jit(solution)/shard_map/tj,ij->ti/dot_general | solution.py:52
  304.0 11.1 %multiply_reduce_fusion.4 = (f32[1024]{0:T(1024)S(1)}, f32[512]{0:T(512)S(1)}, f32[512]{0:T(512)S(1)}, f32[1024]{0:T(1024)}, f32[512,1024]{1,0:T(8,128)S(1)}) fusion(f32[512,1024]{1,0:T(8,128)S(1)} %get-tuple-element.139, f32[512]{0:T(512)S(1)} %add_rsqrt_fusion.1, f32[512]{0:T(512)S(1)} %broadcast_multiply_fusion.7, f32[1024]{0:T(1024)S(1)} %copy-done.67, ...), kind=kOutput, calls=%fused_computation.76 | convolution fusion | flops 4304401408 | bytes 19955712 | tf_op jit(solution)/shard_map/tj,ij->ti/dot_general | solution.py:52
  321.8 12.0 %multiply_reduce_fusion = (f32[16,512]{1,0:T(8,128)S(1)}, f32[16,512,512]{1,2,0:T(8,128)}) fusion(f32[16,512,512]{1,2,0:T(8,128)} %get-tuple-element.137, f32[16,512]{1,0:T(8,128)S(1)} %log_add_fusion, bf16[512,16,64]{0,2,1:T(8,128)(2,1)S(1)} %bitcast.149, bf16[1,512,3,16,64]{1,4,3,2,0:T(8,128)(2,1)} %bitcast.146), kind=kOutput, calls=%fused_computation.9 | convolution fusion | flops 553639936 | bytes 35717120 | tf_op jit(solution)/shard_map/bqhe,bkhe->bhqk/dot_general | solution.py:261
  333.9 12.0 %multiply_convert_fusion = bf16[16,512,512]{1,2,0:T(8,128)(2,1)S(1)} fusion(f32[16,512,512]{1,2,0:T(8,128)} %get-tuple-element.146, f32[16,512,512]{1,2,0:T(8,128)} %get-tuple-element.137, f32[16,512]{1,0:T(8,128)S(1)} %get-tuple-element.145, f32[16,512]{1,0:T(8,128)S(1)} %log_add_fusion), kind=kLoop, calls=%fused_computation.8 | loop fusion | flops 20971520 | bytes 42008576 | tf_op jit(solution)/shard_map/convert_element_type | solution.py:262
  349.9 7.8 fusion.71
  365.5 3.3 fusion.79
  369.3 3.2 fusion.87
  373.5 3.2 fusion.47
  380.4 6.9 multiply_reduce_fusion.3
  388.3 15.5 %collective-permute-done.7 = f32[256,1024]{1,0:T(8,128)S(1)} collective-permute-done((f32[256,1024]{1,0:T(8,128)S(1)}, f32[256,1024]{1,0:T(8,128)S(1)}, u32[]{:S(2)}, u32[]{:S(2)}) %collective-permute-start.7) | collective-permute-done | bytes 1048608 | tf_op jit(solution)/shard_map/ppermute | solution.py:101
  405.4 19.9 %collective-permute-done.10 = f32[256,1024]{1,0:T(8,128)S(1)} collective-permute-done((f32[256,1024]{1,0:T(8,128)S(1)}, f32[256,1024]{1,0:T(8,128)S(1)}, u32[]{:S(2)}, u32[]{:S(2)}) %collective-permute-start.10) | collective-permute-done | bytes 1048608 | tf_op jit(solution)/shard_map/ppermute | solution.py:101
  427.0 3.2 fusion.37
  430.4 3.4 fusion.57
  433.7 4.8 collective-permute-done.11
  481.0 20.6 %collective-permute-done.28 = f32[512,1024]{1,0:T(8,128)S(1)} collective-permute-done((f32[512,1024]{1,0:T(8,128)S(1)}, f32[512,1024]{1,0:T(8,128)S(1)}, u32[]{:S(2)}, u32[]{:S(2)}) %collective-permute-start.28) | collective-permute-done | bytes 2097184 | tf_op jit(solution)/shard_map/ppermute | solution.py:101
  506.6 39.8 %collective-permute-done.19 = f32[256,2048]{1,0:T(8,128)S(1)} collective-permute-done((f32[256,2048]{1,0:T(8,128)S(1)}, f32[256,2048]{1,0:T(8,128)S(1)}, u32[]{:S(2)}, u32[]{:S(2)}) %collective-permute-start.19) | collective-permute-done | bytes 2097184 | tf_op jit(solution)/shard_map/ppermute | solution.py:101
  548.2 47.5 %collective-permute-done.13 = f32[256,2048]{1,0:T(8,128)S(1)} collective-permute-done((f32[256,2048]{1,0:T(8,128)S(1)}, f32[256,2048]{1,0:T(8,128)S(1)}, u32[]{:S(2)}, u32[]{:S(2)}) %collective-permute-start.13) | collective-permute-done | bytes 2097184 | tf_op jit(solution)/shard_map/ppermute | solution.py:101
  598.1 20.0 %collective-permute-done.29 = f32[256,1024]{1,0:T(8,128)S(1)} collective-permute-done((f32[256,1024]{1,0:T(8,128)S(1)}, f32[256,1024]{1,0:T(8,128)S(1)}, u32[]{:S(2)}, u32[]{:S(2)}) %collective-permute-start.29) | collective-permute-done | bytes 1048608 | tf_op jit(solution)/shard_map/ppermute | solution.py:101
  618.9 3.2 collective-permute-start.33
  622.6 3.0 collective-permute-start.15
  625.6 14.3 %collective-permute-done.20 = f32[128,2048]{1,0:T(8,128)S(1)} collective-permute-done((f32[128,2048]{1,0:T(8,128)S(1)}, f32[128,2048]{1,0:T(8,128)S(1)}, u32[]{:S(2)}, u32[]{:S(2)}) %collective-permute-start.20) | collective-permute-done | bytes 1048608 | tf_op jit(solution)/shard_map/ppermute | solution.py:101
  643.8 4.5 collective-permute-start.24
  650.0 63.0 %collective-permute-done.15 = f32[128,4096]{1,0:T(8,128)S(1)} collective-permute-done((f32[128,4096]{1,0:T(8,128)S(1)}, f32[128,4096]{1,0:T(8,128)S(1)}, u32[]{:S(2)}, u32[]{:S(2)}) %collective-permute-start.15) | collective-permute-done | bytes 2097184 | tf_op jit(solution)/shard_map/ppermute | solution.py:138
  721.2 21.3 %scatter_custom_fusion.1 = f32[1024,1024]{1,0:T(8,128)} fusion(s32[2048]{0:T(1024)} %bitcast.159, f32[2048,1024]{1,0:T(8,128)} %all-gather.2.cloned.1.call-done, f32[]{:T(128)} %constant.32.clone.1), kind=kCustom, calls=%fused_computation.80 | custom fusion | flops 2097152 | bytes 4194816 | tf_op jit(solution)/shard_map/scatter-add | solution.py:79
  742.4 23.2 %conditional.3 = (f32[1024,1024]{1,0:T(8,128)}) conditional(s32[]{:T(128)} %convert_element_type.81, f32[1024,1024]{1,0:T(8,128)} %scatter_custom_fusion.1, (s32[2048]{0:T(1024)S(1)}, f32[1024,1024]{1,0:T(8,128)}, f32[2048,1024]{1,0:T(8,128)}) %tuple.117), branch_computations={%region_19.21_spmd, %region_20.23_spmd} | conditional | flops 2097152 | bytes 25174024 | solution.py:84
  742.4 23.2 %scatter_fusion = f32[1024,1024]{1,0:T(8,128)} fusion(f32[1024,1024]{1,0:T(8,128)} %get-tuple-element.24, s32[2048]{0:T(1024)S(1)} %get-tuple-element.25, f32[2048,1024]{1,0:T(8,128)} %get-tuple-element.26), kind=kCustom, calls=%fused_computation.2 | custom fusion | flops 2097152 | bytes 25174016 | tf_op jit(solution)/shard_map/cond/branch_1_fun/scatter-add | solution.py:79
  765.6 3.2 fusion.198
  773.9 3.0 add.504
  779.9 3.5 collective-permute-done.1
  784.9 4.1 add.552
  790.3 31.6 %collective-permute-start.3 = (f32[1,1793]{1,0:T(1,128)S(1)}, f32[1,1793]{1,0:T(1,128)S(1)}, u32[]{:S(2)}, u32[]{:S(2)}) collective-permute-start(f32[1,1793]{1,0:T(1,128)S(1)} %fusion.173), channel_id=1, source_target_pairs={{0,1},{3,2},{4,5},{7,6},{8,9},{11,10},{12,13},{15,14},{16,17},{19,... | collective-permute-start | bytes 21524 | tf_op jit(solution)/shard_map/ppermute | solution.py:138
  829.0 45.5 %collective-permute-done.5 = f32[1,1793]{1,0:T(1,128)S(1)} collective-permute-done((f32[1,1793]{1,0:T(1,128)S(1)}, f32[1,1793]{1,0:T(1,128)S(1)}, u32[]{:S(2)}, u32[]{:S(2)}) %collective-permute-start.5) | collective-permute-done | bytes 7204 | tf_op jit(solution)/shard_map/ppermute | solution.py:140
  880.7 3.6 broadcast_select_fusion.1
  884.4 29.2 %collective-permute-done.26 = f32[128,4096]{1,0:T(8,128)S(1)} collective-permute-done((f32[128,4096]{1,0:T(8,128)S(1)}, f32[128,4096]{1,0:T(8,128)S(1)}, u32[]{:S(2)}, u32[]{:S(2)}) %collective-permute-start.26) | collective-permute-done | bytes 2097184 | tf_op jit(solution)/shard_map/ppermute | solution.py:140
  (343 shorter events, 133.0 us)
Async XLA Ops:
  7.2 246.5 %copy-start = (bf16[1024,1024]{1,0:T(8,128)(2,1)S(1)}, bf16[1024,1024]{1,0:T(8,128)(2,1)}, u32[]{:S(2)}) copy-start(bf16[1024,1024]{1,0:T(8,128)(2,1)} %param.33) | copy-start | bytes 6291460
  7.2 203.2 %reduce-scatter.3.cloned.1.call-start = ((), (), s32[]{:S(2)}) async-start(), calls=%async_computation.2 | async-start | bytes 10485760 | tf_op jit(solution)/shard_map/reduce_scatter | solution.py:181
  66.6 143.8 %copy-start.34 = (bf16[512,1024]{1,0:T(8,128)(2,1)S(1)}, bf16[512,1024]{1,0:T(8,128)(2,1)}, u32[]{:S(2)}) copy-start(bf16[512,1024]{1,0:T(8,128)(2,1)} %param.25) | copy-start | bytes 3145732
  66.6 654.5 %all-gather.2.cloned.1.call-start = ((), (), s32[]{:S(2)}) async-start(), calls=%async_computation.3 | async-start | bytes 10485760 | tf_op jit(solution)/shard_map/all_gather | solution.py:326
  212.3 41.3 %copy-start.63 = (f32[512]{0:T(512)}, f32[512]{0:T(512)S(1)}, u32[]{:S(2)}) copy-start(f32[512]{0:T(512)S(1)} %broadcast_multiply_fusion.8) | copy-start | bytes 6148
  213.6 40.0 %copy-start.65 = (f32[512]{0:T(512)}, f32[512]{0:T(512)S(1)}, u32[]{:S(2)}) copy-start(f32[512]{0:T(512)S(1)} %add_rsqrt_fusion.2) | copy-start | bytes 6148
  359.3 28.5 %copy-start.28 = (bf16[512,128]{1,0:T(8,128)(2,1)}, bf16[512,128]{1,0:T(8,128)(2,1)S(1)}, u32[]{:S(2)}) copy-start(bf16[512,128]{1,0:T(8,128)(2,1)S(1)} %get-tuple-element.111) | copy-start | bytes 393220
  360.0 17.2 %collective-permute-start.6 = (f32[512,1024]{1,0:T(8,128)S(1)}, f32[512,1024]{1,0:T(8,128)S(1)}, u32[]{:S(2)}, u32[]{:S(2)}) collective-permute-start(f32[512,1024]{1,0:T(8,128)S(1)} %fusion.113), channel_id=1, source_target_pairs={{0,4},{4,0},{8,12},{12,8},{16,20},{20,16},{24,28},{28,24},{1,5},{5... | collective-permute-start | bytes 6291464 | tf_op jit(solution)/shard_map/ppermute | solution.py:101
  360.5 69.8 %copy-start.2 = (bf16[1,512,3,16,64]{1,4,3,2,0:T(8,128)(2,1)}, bf16[1,512,3,16,64]{1,4,3,2,0:T(8,128)(2,1)S(1)}, u32[]{:S(2)}) copy-start(bf16[1,512,3,16,64]{1,4,3,2,0:T(8,128)(2,1)S(1)} %pad_maximum_fusion) | copy-start | bytes 9437188
  361.3 17.9 %collective-permute-start.9 = (f32[512,1024]{1,0:T(8,128)S(1)}, f32[512,1024]{1,0:T(8,128)S(1)}, u32[]{:S(2)}, u32[]{:S(2)}) collective-permute-start(f32[512,1024]{1,0:T(8,128)S(1)} %fusion.99), channel_id=1, source_target_pairs={{0,4},{4,0},{8,12},{12,8},{16,20},{20,16},{24,28},{28,24},{1,5},{5... | collective-permute-start | bytes 6291464 | tf_op jit(solution)/shard_map/ppermute | solution.py:101
  368.8 81.5 %collective-permute-start.27 = (f32[1024,1024]{1,0:T(8,128)}, f32[1024,1024]{1,0:T(8,128)}, u32[]{:S(2)}, u32[]{:S(2)}) collective-permute-start(f32[1024,1024]{1,0:T(8,128)} %fusion.79), channel_id=1, source_target_pairs={{0,4},{4,0},{8,12},{12,8},{16,20},{20,16},{24,28},{28,24},{1,5},{5... | collective-permute-start | bytes 12582920 | tf_op jit(solution)/shard_map/ppermute | solution.py:101
  372.5 82.1 %collective-permute-start.30 = (f32[1024,1024]{1,0:T(8,128)}, f32[1024,1024]{1,0:T(8,128)}, u32[]{:S(2)}, u32[]{:S(2)}) collective-permute-start(f32[1024,1024]{1,0:T(8,128)} %fusion.87), channel_id=1, source_target_pairs={{0,4},{4,0},{8,12},{12,8},{16,20},{20,16},{24,28},{28,24},{1,5},{5... | collective-permute-start | bytes 12582920 | tf_op jit(solution)/shard_map/ppermute | solution.py:101
  376.7 82.1 %collective-permute-start.18 = (f32[512,2048]{1,0:T(8,128)}, f32[512,2048]{1,0:T(8,128)}, u32[]{:S(2)}, u32[]{:S(2)}) collective-permute-start(f32[512,2048]{1,0:T(8,128)} %fusion.47), channel_id=1, source_target_pairs={{0,4},{4,0},{8,12},{12,8},{16,20},{20,16},{24,28},{28,24},{1,5},{5... | collective-permute-start | bytes 12582920 | tf_op jit(solution)/shard_map/ppermute | solution.py:101
  377.7 26.1 %collective-permute-start.7 = (f32[256,1024]{1,0:T(8,128)S(1)}, f32[256,1024]{1,0:T(8,128)S(1)}, u32[]{:S(2)}, u32[]{:S(2)}) collective-permute-start(f32[256,1024]{1,0:T(8,128)S(1)} %slice_add_fusion.22), channel_id=1, source_target_pairs={{0,8},{4,12},{8,0},{12,4},{16,24},{20,28},{24,16},{28,20},{1,9},{5... | collective-permute-start | bytes 3145736 | tf_op jit(solution)/shard_map/ppermute | solution.py:101
  379.7 45.6 %collective-permute-start.10 = (f32[256,1024]{1,0:T(8,128)S(1)}, f32[256,1024]{1,0:T(8,128)S(1)}, u32[]{:S(2)}, u32[]{:S(2)}) collective-permute-start(f32[256,1024]{1,0:T(8,128)S(1)} %slice_add_fusion.20), channel_id=1, source_target_pairs={{0,8},{4,12},{8,0},{12,4},{16,24},{20,28},{24,16},{28,20},{1,9},{5... | collective-permute-start | bytes 3145736 | tf_op jit(solution)/shard_map/ppermute | solution.py:101
  388.3 41.9 %copy-start.21 = (f32[256,1024]{1,0:T(8,128)}, f32[256,1024]{1,0:T(8,128)S(1)}, u32[]{:S(2)}) copy-start(f32[256,1024]{1,0:T(8,128)S(1)} %slice_add_fusion.21) | copy-start | bytes 3145732
  403.9 26.3 %collective-permute-start.8 = (f32[128,1024]{1,0:T(8,128)S(1)}, f32[128,1024]{1,0:T(8,128)S(1)}, u32[]{:S(2)}, u32[]{:S(2)}) collective-permute-start(f32[128,1024]{1,0:T(8,128)S(1)} %slice_add_fusion.26), channel_id=1, source_target_pairs={{0,16},{4,20},{8,24},{12,28},{16,0},{20,4},{24,8},{28,12},{1,17},{... | collective-permute-start | bytes 1572872 | tf_op jit(solution)/shard_map/ppermute | solution.py:101
  425.4 13.1 %collective-permute-start.11 = (f32[128,1024]{1,0:T(8,128)S(1)}, f32[128,1024]{1,0:T(8,128)S(1)}, u32[]{:S(2)}, u32[]{:S(2)}) collective-permute-start(f32[128,1024]{1,0:T(8,128)S(1)} %slice_add_fusion.24), channel_id=1, source_target_pairs={{0,16},{4,20},{8,24},{12,28},{16,0},{20,4},{24,8},{28,12},{1,17},{... | collective-permute-start | bytes 1572872 | tf_op jit(solution)/shard_map/ppermute | solution.py:101
  430.2 31.6 %collective-permute-start.21 = (f32[512,2048]{1,0:T(8,128)}, f32[512,2048]{1,0:T(8,128)}, u32[]{:S(2)}, u32[]{:S(2)}) collective-permute-start(f32[512,2048]{1,0:T(8,128)} %fusion.37), channel_id=1, source_target_pairs={{0,4},{4,0},{8,12},{12,8},{16,20},{20,16},{24,28},{28,24},{1,5},{5... | collective-permute-start | bytes 12582920 | tf_op jit(solution)/shard_map/ppermute | solution.py:101
  438.5 26.5 %collective-permute-start.12 = (f32[512,2048]{1,0:T(8,128)}, f32[512,2048]{1,0:T(8,128)}, u32[]{:S(2)}, u32[]{:S(2)}) collective-permute-start(f32[512,2048]{1,0:T(8,128)} %fusion.57), channel_id=1, source_target_pairs={{0,4},{4,0},{8,12},{12,8},{16,20},{20,16},{24,28},{28,24},{1,5},{5... | collective-permute-start | bytes 12582920 | tf_op jit(solution)/shard_map/ppermute | solution.py:101
  441.1 474.0 %reduce-scatter.5.cloned.1.call-start = ((), (), s32[]{:S(2)}) async-start(), calls=%async_computation.4 | async-start | bytes 4718592 | tf_op jit(solution)/shard_map/reduce_scatter | solution.py:332
  453.0 48.5 %collective-permute-start.28 = (f32[512,1024]{1,0:T(8,128)S(1)}, f32[512,1024]{1,0:T(8,128)S(1)}, u32[]{:S(2)}, u32[]{:S(2)}) collective-permute-start(f32[512,1024]{1,0:T(8,128)S(1)} %slice_add_fusion.2), channel_id=1, source_target_pairs={{0,8},{4,12},{8,0},{12,4},{16,24},{20,28},{24,16},{28,20},{1,9},{5... | collective-permute-start | bytes 6291464 | tf_op jit(solution)/shard_map/ppermute | solution.py:101
  457.3 48.5 %collective-permute-start.31 = (f32[512,1024]{1,0:T(8,128)S(1)}, f32[512,1024]{1,0:T(8,128)S(1)}, u32[]{:S(2)}, u32[]{:S(2)}) collective-permute-start(f32[512,1024]{1,0:T(8,128)S(1)} %slice_add_fusion), channel_id=1, source_target_pairs={{0,16},{4,20},{8,24},{12,28},{16,0},{20,4},{24,8},{28,12},{1,17},{... | collective-permute-start | bytes 6291464 | tf_op jit(solution)/shard_map/ppermute | solution.py:101
  461.2 85.3 %collective-permute-start.19 = (f32[256,2048]{1,0:T(8,128)S(1)}, f32[256,2048]{1,0:T(8,128)S(1)}, u32[]{:S(2)}, u32[]{:S(2)}) collective-permute-start(f32[256,2048]{1,0:T(8,128)S(1)} %slice_add_fusion.6), channel_id=1, source_target_pairs={{0,8},{4,12},{8,0},{12,4},{16,24},{20,28},{24,16},{28,20},{1,9},{5... | collective-permute-start | bytes 6291464 | tf_op jit(solution)/shard_map/ppermute | solution.py:101
  464.4 132.1 %collective-permute-start.22 = (f32[256,2048]{1,0:T(8,128)S(1)}, f32[256,2048]{1,0:T(8,128)S(1)}, u32[]{:S(2)}, u32[]{:S(2)}) collective-permute-start(f32[256,2048]{1,0:T(8,128)S(1)} %slice_add_fusion.4), channel_id=1, source_target_pairs={{0,16},{4,20},{8,24},{12,28},{16,0},{20,4},{24,8},{28,12},{1,17},{... | collective-permute-start | bytes 6291464 | tf_op jit(solution)/shard_map/ppermute | solution.py:101
  467.4 128.3 %collective-permute-start.13 = (f32[256,2048]{1,0:T(8,128)S(1)}, f32[256,2048]{1,0:T(8,128)S(1)}, u32[]{:S(2)}, u32[]{:S(2)}) collective-permute-start(f32[256,2048]{1,0:T(8,128)S(1)} %slice_add_fusion.8), channel_id=1, source_target_pairs={{0,16},{4,20},{8,24},{12,28},{16,0},{20,4},{24,8},{28,12},{1,17},{... | collective-permute-start | bytes 6291464 | tf_op jit(solution)/shard_map/ppermute | solution.py:101
  501.7 116.4 %collective-permute-start.29 = (f32[256,1024]{1,0:T(8,128)S(1)}, f32[256,1024]{1,0:T(8,128)S(1)}, u32[]{:S(2)}, u32[]{:S(2)}) collective-permute-start(f32[256,1024]{1,0:T(8,128)S(1)} %slice_add_fusion.12), channel_id=1, source_target_pairs={{0,16},{4,20},{8,24},{12,28},{16,0},{20,4},{24,8},{28,12},{1,17},{... | collective-permute-start | bytes 3145736 | tf_op jit(solution)/shard_map/ppermute | solution.py:101
  506.0 112.5 %collective-permute-start.32 = (f32[256,1024]{1,0:T(8,128)S(1)}, f32[256,1024]{1,0:T(8,128)S(1)}, u32[]{:S(2)}, u32[]{:S(2)}) collective-permute-start(f32[256,1024]{1,0:T(8,128)S(1)} %slice_add_fusion.10), channel_id=1, source_target_pairs={{0,8},{4,12},{8,0},{12,4},{16,24},{20,28},{24,16},{28,20},{1,9},{5... | collective-permute-start | bytes 3145736 | tf_op jit(solution)/shard_map/ppermute | solution.py:101
  546.6 93.3 %collective-permute-start.20 = (f32[128,2048]{1,0:T(8,128)S(1)}, f32[128,2048]{1,0:T(8,128)S(1)}, u32[]{:S(2)}, u32[]{:S(2)}) collective-permute-start(f32[128,2048]{1,0:T(8,128)S(1)} %slice_add_fusion.16), channel_id=1, source_target_pairs={{0,16},{4,20},{8,24},{12,28},{16,0},{20,4},{24,8},{28,12},{1,17},{... | collective-permute-start | bytes 3145736 | tf_op jit(solution)/shard_map/ppermute | solution.py:101
  595.8 26.4 %collective-permute-start.14 = (f32[128,2048]{1,0:T(8,128)S(1)}, f32[128,2048]{1,0:T(8,128)S(1)}, u32[]{:S(2)}, u32[]{:S(2)}) collective-permute-start(f32[128,2048]{1,0:T(8,128)S(1)} %slice_add_fusion.18), channel_id=1, source_target_pairs={{0,8},{4,12},{8,0},{12,4},{16,24},{20,28},{24,16},{28,20},{1,9},{5... | collective-permute-start | bytes 3145736 | tf_op jit(solution)/shard_map/ppermute | solution.py:101
  596.6 45.5 %collective-permute-start.23 = (f32[128,2048]{1,0:T(8,128)S(1)}, f32[128,2048]{1,0:T(8,128)S(1)}, u32[]{:S(2)}, u32[]{:S(2)}) collective-permute-start(f32[128,2048]{1,0:T(8,128)S(1)} %slice_add_fusion.14), channel_id=1, source_target_pairs={{0,8},{4,12},{8,0},{12,4},{16,24},{20,28},{24,16},{28,20},{1,9},{5... | collective-permute-start | bytes 3145736 | tf_op jit(solution)/shard_map/ppermute | solution.py:101
  618.9 98.2 %collective-permute-start.33 = (f32[512,1024]{1,0:T(8,128)S(1)}, f32[512,1024]{1,0:T(8,128)S(1)}, u32[]{:S(2)}, u32[]{:S(2)}) collective-permute-start(f32[512,1024]{1,0:T(8,128)S(1)} %pad_maximum_fusion.3), channel_id=1, source_target_pairs={{0,1},{3,2},{4,5},{7,6},{8,9},{11,10},{12,13},{15,14},{16,17},{19,... | collective-permute-start | bytes 6291464 | tf_op jit(solution)/shard_map/ppermute | solution.py:138
  622.6 90.5 %collective-permute-start.15 = (f32[128,4096]{1,0:T(8,128)S(1)}, f32[128,4096]{1,0:T(8,128)S(1)}, u32[]{:S(2)}, u32[]{:S(2)}) collective-permute-start(f32[128,4096]{1,0:T(8,128)S(1)} %pad_maximum_fusion.1), channel_id=1, source_target_pairs={{0,1},{3,2},{4,5},{7,6},{8,9},{11,10},{12,13},{15,14},{16,17},{19,... | collective-permute-start | bytes 6291464 | tf_op jit(solution)/shard_map/ppermute | solution.py:138
  643.8 121.8 %collective-permute-start.24 = (f32[128,4096]{1,0:T(8,128)}, f32[128,4096]{1,0:T(8,128)}, u32[]{:S(2)}, u32[]{:S(2)}) collective-permute-start(f32[128,4096]{1,0:T(8,128)} %pad_maximum_fusion.2), channel_id=1, source_target_pairs={{0,1},{3,2},{4,5},{7,6},{8,9},{11,10},{12,13},{15,14},{16,17},{19,... | collective-permute-start | bytes 6291464 | tf_op jit(solution)/shard_map/ppermute | solution.py:138
  650.0 66.5 %copy-start.77 = (f32[1024]{0:T(1024)S(1)}, f32[1024]{0:T(1024)}, u32[]{:S(2)}) copy-start(f32[1024]{0:T(1024)} %get-tuple-element.46) | copy-start | bytes 12292
  714.6 59.2 %collective-permute-start.16 = (f32[128,4096]{1,0:T(8,128)}, f32[128,4096]{1,0:T(8,128)}, u32[]{:S(2)}, u32[]{:S(2)}) collective-permute-start(f32[128,4096]{1,0:T(8,128)} %fusion.199), channel_id=1, source_target_pairs={{1,2},{2,1},{5,6},{6,5},{9,10},{10,9},{13,14},{14,13},{17,18},{18,... | collective-permute-start | bytes 6291464 | tf_op jit(solution)/shard_map/ppermute | solution.py:139
  719.0 65.9 %collective-permute-start.34 = (f32[512,1024]{1,0:T(8,128)}, f32[512,1024]{1,0:T(8,128)}, u32[]{:S(2)}, u32[]{:S(2)}) collective-permute-start(f32[512,1024]{1,0:T(8,128)} %fusion.197), channel_id=1, source_target_pairs={{1,2},{2,1},{5,6},{6,5},{9,10},{10,9},{13,14},{14,13},{17,18},{18,... | collective-permute-start | bytes 6291464 | tf_op jit(solution)/shard_map/ppermute | solution.py:139
  768.8 56.4 %collective-permute-start.25 = (f32[128,4096]{1,0:T(8,128)}, f32[128,4096]{1,0:T(8,128)}, u32[]{:S(2)}, u32[]{:S(2)}) collective-permute-start(f32[128,4096]{1,0:T(8,128)} %fusion.198), channel_id=1, source_target_pairs={{1,2},{2,1},{5,6},{6,5},{9,10},{10,9},{13,14},{14,13},{17,18},{18,... | collective-permute-start | bytes 6291464 | tf_op jit(solution)/shard_map/ppermute | solution.py:139
  776.9 99.9 %collective-permute-start.17 = (f32[128,4096]{1,0:T(8,128)S(1)}, f32[128,4096]{1,0:T(8,128)}, u32[]{:S(2)}, u32[]{:S(2)}) collective-permute-start(f32[128,4096]{1,0:T(8,128)S(1)} %add.504), channel_id=1, source_target_pairs={{1,0},{2,3},{5,4},{6,7},{9,8},{10,11},{13,12},{14,15},{17,16},{18,... | collective-permute-start | bytes 6291464 | tf_op jit(solution)/shard_map/ppermute | solution.py:140
  778.2 1.3 collective-permute-start
  779.5 3.8 collective-permute-start.1
  783.3 6.9 collective-permute-start.2
  789.0 91.8 %collective-permute-start.35 = (f32[512,1024]{1,0:T(8,128)}, f32[512,1024]{1,0:T(8,128)}, u32[]{:S(2)}, u32[]{:S(2)}) collective-permute-start(f32[512,1024]{1,0:T(8,128)} %add.552), channel_id=1, source_target_pairs={{1,0},{2,3},{5,4},{6,7},{9,8},{10,11},{13,12},{14,15},{17,16},{18,... | collective-permute-start | bytes 6291464 | tf_op jit(solution)/shard_map/ppermute | solution.py:140
  790.3 32.9 %collective-permute-start.3 = (f32[1,1793]{1,0:T(1,128)S(1)}, f32[1,1793]{1,0:T(1,128)S(1)}, u32[]{:S(2)}, u32[]{:S(2)}) collective-permute-start(f32[1,1793]{1,0:T(1,128)S(1)} %fusion.173), channel_id=1, source_target_pairs={{0,1},{3,2},{4,5},{7,6},{8,9},{11,10},{12,13},{15,14},{16,17},{19,... | collective-permute-start | bytes 21524 | tf_op jit(solution)/shard_map/ppermute | solution.py:138
  823.2 0.7 collective-permute-start.4
  823.9 50.6 %collective-permute-start.5 = (f32[1,1793]{1,0:T(1,128)S(1)}, f32[1,1793]{1,0:T(1,128)S(1)}, u32[]{:S(2)}, u32[]{:S(2)}) collective-permute-start(f32[1,1793]{1,0:T(1,128)S(1)} %add.479), channel_id=1, source_target_pairs={{1,0},{2,3},{5,4},{6,7},{9,8},{10,11},{13,12},{14,15},{17,16},{18,... | collective-permute-start | bytes 21524 | tf_op jit(solution)/shard_map/ppermute | solution.py:140
  827.7 85.8 %collective-permute-start.26 = (f32[128,4096]{1,0:T(8,128)S(1)}, f32[128,4096]{1,0:T(8,128)S(1)}, u32[]{:S(2)}, u32[]{:S(2)}) collective-permute-start(f32[128,4096]{1,0:T(8,128)S(1)} %add.516), channel_id=1, source_target_pairs={{1,0},{2,3},{5,4},{6,7},{9,8},{10,11},{13,12},{14,15},{17,16},{18,... | collective-permute-start | bytes 6291464 | tf_op jit(solution)/shard_map/ppermute | solution.py:140
  880.7 34.3 %copy-start.1 = (bf16[1024,1024]{1,0:T(8,128)(2,1)S(1)}, bf16[1024,1024]{1,0:T(8,128)(2,1)}, u32[]{:S(2)}) copy-start(bf16[1024,1024]{1,0:T(8,128)(2,1)} %param.33) | copy-start | bytes 6291460
  (77 other events, 482.5 us)
Sparse Core Ops, SparseCore 0:
  66.7 143.6 reduce-scatter.2
  441.2 150.4 all-gather.1
  765.7 52.8 reduce-scatter.4

commit v2 on v1

v2 whole, which is shorter than its diff:
```python
import itertools

import jax
import jax.numpy as jnp
from jax import lax
from jax.experimental import pallas as pl
from jax.experimental.pallas import tpu as pltpu
from jax.sharding import PartitionSpec as P

HEADS = 16
HEAD = 64
PAGE = 512


EPSILON = 1e-05
SQRT_HALF = 0.7071067811865476
INV_ROOT_TAU = 0.3989422804014327


def normalize(values):
    averaged = jnp.mean(values, -1, keepdims=True)
    centered = values - averaged
    inverse = lax.rsqrt(jnp.mean(centered * centered, -1, keepdims=True) + EPSILON)
    return (centered * inverse, inverse)


def norm_back(incoming, normed, inverse, gain):
    scaled = incoming * gain
    offset_mean = jnp.mean(scaled, -1, keepdims=True)
    along_mean = jnp.mean(scaled * normed, -1, keepdims=True)
    return (
        inverse * (scaled - offset_mean - normed * along_mean),
        jnp.sum(incoming * normed, 0),
        jnp.sum(incoming, 0),
    )


def gelu_slope(pre_act):
    return (
        0.5 * (1.0 + lax.erf(pre_act * SQRT_HALF))
        + pre_act * jnp.exp(-0.5 * pre_act * pre_act) * INV_ROOT_TAU
    )


def matmul(left, right):
    return jnp.dot(left, right, preferred_element_type=jnp.float32)


def outer_sum(left, right):
    return jnp.einsum("ti,tj->ij", left, right, preferred_element_type=jnp.float32)


def back_mul(left, right):
    return jnp.einsum("tj,ij->ti", left, right, preferred_element_type=jnp.float32)


def table_indices(box_rows, table):
    left_x, top_y, right_x, bottom_y = box_rows[0], box_rows[1], box_rows[2], box_rows[3]
    first = jnp.where(
        table == 0,
        left_x,
        jnp.where(table == 1, top_y, jnp.where(table == 2, right_x - left_x, bottom_y - top_y)),
    )
    second = jnp.where(table == 0, right_x, jnp.where(table == 1, bottom_y, -1))
    return first, second


def two_halves(values):
    high = values.astype(jnp.bfloat16)
    return high, (values - high.astype(jnp.float32)).astype(jnp.bfloat16)


def hits(entry, indices):
    return jnp.where(entry == indices, 1.0, 0.0)


def lookup_kernel(idx_ref, table_ref, total_ref, out_ref, halves):
    width = table_ref.shape[1]

    @pl.when(pl.program_id(0) == 0)
    def _():
        halves[:, :width], halves[:, width:] = two_halves(table_ref[...])

    entry = lax.broadcasted_iota(jnp.int32, (idx_ref.shape[0], table_ref.shape[0]), 1)
    counts = hits(entry, idx_ref[:, 0:1]) + hits(entry, idx_ref[:, 1:2])
    rows = jnp.dot(
        counts.astype(jnp.bfloat16), halves[...], preferred_element_type=jnp.float32
    )
    out_ref[...] = total_ref[...] + rows[:, :width] + rows[:, width:]


def add_rows(indices, table, total):
    tokens = total.shape[0]
    entries, width = table.shape
    block = PAGE
    return pl.pallas_call(
        lookup_kernel,
        grid=(tokens // block,),
        in_specs=[
            pl.BlockSpec((block, 2), lambda step: (step, 0)),
            pl.BlockSpec((entries, width), lambda step: (0, 0)),
            pl.BlockSpec((block, width), lambda step: (step, 0)),
        ],
        out_specs=pl.BlockSpec((block, width), lambda step: (step, 0)),
        out_shape=jax.ShapeDtypeStruct((tokens, width), jnp.float32),
        scratch_shapes=[pltpu.VMEM((entries, 2 * width), jnp.bfloat16)],
        input_output_aliases={2: 0},
        compiler_params=pltpu.CompilerParams(vmem_limit_bytes=32 * 2**20),
        cost_estimate=pl.CostEstimate(
            flops=4 * tokens * entries * width, bytes_accessed=12 * tokens * width, transcendentals=0
        ),
    )(indices, table, total)


def spread_kernel(idx_ref, rows_ref, out_ref):
    width = rows_ref.shape[1]
    entry = lax.broadcasted_iota(jnp.int32, (out_ref.shape[0], rows_ref.shape[0]), 0)
    counts = hits(entry, idx_ref[0:1, :]) + hits(entry, idx_ref[1:2, :])
    both = jnp.dot(
        counts.astype(jnp.bfloat16),
        jnp.concatenate(two_halves(rows_ref[...]), 1),
        preferred_element_type=jnp.float32,
    )
    share = both[:, :width] + both[:, width:]

    @pl.when(pl.program_id(0) == 0)
    def _():
        out_ref[...] = share

    @pl.when(pl.program_id(0) > 0)
    def _():
        out_ref[...] += share


def spread_rows(indices, rows, entries):
    tokens, width = rows.shape
    block = 2 * PAGE
    return pl.pallas_call(
        spread_kernel,
        grid=(tokens // block,),
        in_specs=[
            pl.BlockSpec((2, block), lambda step: (0, step)),
            pl.BlockSpec((block, width), lambda step: (step, 0)),
        ],
        out_specs=pl.BlockSpec((entries, width), lambda step: (0, 0)),
        out_shape=jax.ShapeDtypeStruct((entries, width), jnp.float32),
        compiler_params=pltpu.CompilerParams(vmem_limit_bytes=32 * 2**20),
        cost_estimate=pl.CostEstimate(
            flops=4 * tokens * entries * width, bytes_accessed=8 * tokens * width, transcendentals=0
        ),
    )(indices, rows)


def flips_of(masks):
    return [
        sum(mask for mask, flip in zip(masks, flips) if flip)
        for flips in itertools.product((0, 1), repeat=len(masks))
    ]


def relative(array, offsets, me, size, axis, first=0, last=None):
    last = size if last is None else last
    blocks = [
        lax.dynamic_slice_in_dim(
            array, jnp.bitwise_xor(me, offset) * size + first, last - first, axis
        )
        for offset in offsets
    ]
    return jnp.concatenate(blocks, axis)


def swap(array, mask):
    return lax.ppermute(
        array, "pages", [(one, one ^ mask) for one in range(lax.axis_size("pages"))]
    )


def fold(kept, arrived):
    half = kept.shape[0] // 2
    return kept[:half] + arrived[:half], kept[half:] + arrived[half:]


def halve(kept, masks):
    for mask in masks:
        half = kept.shape[0] // 2
        kept = kept[:half] + swap(kept[half:], mask)
    return kept


def in_order(*values):
    return lax.optimization_barrier(values)


class Share:
    def __init__(self, left, right, masks):
        self.left, self.right, self.masks = left, right, masks
        self.half = left.shape[1] // 2

    def send(self):
        return outer_sum(self.left[:, self.half :], self.right)

    def to_core(self, sent):
        self.arrived = swap(sent, self.masks[0])

    def next(self):
        quarter = self.half // 2
        sent = (
            outer_sum(self.left[:, quarter : self.half], self.right) + self.arrived[quarter:]
        )
        self.kept = outer_sum(self.left[:, :quarter], self.right) + self.arrived[:quarter]
        return sent

    def to_second(self, sent):
        self.arrived = swap(sent, self.masks[1])

    def third(self):
        for mask in self.masks[2:-1]:
            self.kept, sent = fold(self.kept, self.arrived)
            self.arrived = swap(sent, mask)
        self.kept, sent = fold(self.kept, self.arrived)
        return sent

    def to_last(self, sent):
        self.arrived = swap(sent, self.masks[-1])

    def result(self):
        return self.kept + self.arrived


def emb_total(share):
    if lax.axis_size("emb") != 4:
        return lax.psum(share, "emb")
    plane = lax.axis_index("emb")
    middle = jnp.logical_or(plane == 1, plane == 2)
    share = share + lax.ppermute(share, "emb", [(0, 1), (3, 2)])
    share = share + lax.ppermute(share, "emb", [(1, 2), (2, 1)])
    return jnp.where(middle, share, lax.ppermute(share, "emb", [(1, 0), (2, 3)]))


def on_device(
    text_embed,
    boxes,
    layout_tables,
    emb_gain,
    emb_bias,
    w_qkv,
    b_query,
    b_value,
    w_out,
    b_out,
    attn_gain,
    attn_bias,
    w_in,
    b_in,
    w_back,
    b_back,
    ffn_gain,
    ffn_bias,
    cotangent,
):
    wide = jnp.float32
    narrow = jnp.bfloat16
    token_rows = text_embed.shape[0]
    model_width = text_embed.shape[1]
    entries = layout_tables.shape[1]
    page_count = token_rows // PAGE
    score_scale = HEAD ** (-0.5)
    me = lax.axis_index("pages")
    plane = lax.axis_index("emb")
    devices = lax.axis_size("pages")
    planes = lax.axis_size("emb")
    outer_masks = [1 << bit for bit in range(1, devices.bit_length() - 1)]
    turn = len(outer_masks) // 2
    masks_one = [1] + outer_masks
    masks_two = [1] + outer_masks[turn:] + outer_masks[:turn]
    flips_one = flips_of(masks_one)
    flips_two = flips_of(masks_two)
    lanes = model_width // devices
    group = min(devices, 8)
    inner = me % group
    columns = model_width // group

    def around(array, offset):
        return lax.ppermute(
            array, "emb", [((one + offset) % planes, one) for one in range(planes)]
        )

    def exchange(blocks):
        return [blocks[0]] + [swap(blocks[offset], offset) for offset in range(1, group)]

    def in_columns(blocks):
        return relative(
            jnp.concatenate(blocks, 1), range(group), inner, blocks[0].shape[1], 1
        )

    own_columns = lax.dynamic_slice_in_dim(layout_tables[0], inner * columns, columns, 1)
    table_columns = [own_columns] + [around(own_columns, offset) for offset in range(1, planes)]
    group_boxes = lax.all_gather(
        boxes,
        "pages",
        axis=1,
        tiled=True,
        axis_index_groups=[
            list(range(first, first + group)) for first in range(0, devices, group)
        ],
    )
    group_boxes = relative(group_boxes, range(group), inner, token_rows, 1)
    table_uses = [
        jnp.stack(table_indices(group_boxes, (plane + offset) % planes))
        for offset in range(planes)
    ]
    looked_up = jnp.zeros((group * token_rows, columns), wide)
    for offset in [0, 1, planes - 1] + list(range(2, planes - 1)):
        looked_up = add_rows(table_uses[offset].T, table_columns[offset], looked_up)
    layout = in_columns(
        exchange(
            [looked_up[one * token_rows : (one + 1) * token_rows] for one in range(group)]
        )
    )
    normed_emb, inverse_emb = normalize(text_embed.astype(wide) + layout)
    hidden_emb = normed_emb * emb_gain + emb_bias
    emb_low = hidden_emb.astype(narrow)
    bias_qkv = jnp.concatenate([b_query, jnp.zeros_like(b_query), b_value])
    packed = (matmul(emb_low, w_qkv) + bias_qkv).astype(narrow)
    split_heads = packed.reshape(page_count, PAGE, 3, HEADS, HEAD)
    queries = split_heads[:, :, 0]
    key_rows = split_heads[:, :, 1]
    value_rows = split_heads[:, :, 2]
    scores = (
        jnp.einsum("bqhe,bkhe->bhqk", queries, key_rows, preferred_element_type=wide) * score_scale
    )
    maxima = jnp.max(scores, -1, keepdims=True)
    exponent = jnp.exp(scores - maxima)
    summed = jnp.sum(exponent, -1, keepdims=True)
    attn_probs = exponent / summed
    log_total = maxima + jnp.log(summed)
    context = jnp.einsum(
        "bhqk,bkhe->bqhe", attn_probs.astype(narrow), value_rows, preferred_element_type=wide
    )
    context_low = context.reshape(token_rows, model_width).astype(narrow)
    attended = matmul(context_low, w_out) + b_out
    normed_attn, inverse_attn = normalize(hidden_emb + attended)
    hidden_attn = normed_attn * attn_gain + attn_bias
    attn_low = hidden_attn.astype(narrow)
    pre_act = matmul(attn_low, w_in) + b_in
    expanded = jax.nn.gelu(pre_act, approximate=False).astype(narrow)
    returned = matmul(expanded, w_back) + b_back
    normed_ffn, inverse_ffn = normalize(hidden_attn + returned)
    output = (normed_ffn * ffn_gain + ffn_bias).astype(narrow)
    d_r2, g_ffn_gain, g_ffn_bias = norm_back(
        cotangent.astype(wide), normed_ffn, inverse_ffn, ffn_gain
    )
    d_returned = d_r2.astype(narrow)
    wide_lanes = expanded.shape[1] // devices
    half_lanes = wide_lanes // 2
    back_one = Share(
        relative(expanded, flips_one, me, wide_lanes, 1, 0, half_lanes), d_returned, masks_one
    )
    back_two = Share(
        relative(expanded, flips_two, me, wide_lanes, 1, half_lanes, wide_lanes),
        d_returned,
        masks_two,
    )
    sent_one, sent_two = back_one.send(), back_two.send()
    sent_one, sent_two, d_returned = in_order(sent_one, sent_two, d_returned)
    back_one.to_core(sent_one)
    back_two.to_core(sent_two)
    g_back_bias = jnp.sum(d_returned.astype(wide), 0)
    d_pre = (back_mul(d_returned, w_back) * gelu_slope(pre_act)).astype(narrow)
    attn_one = relative(attn_low, flips_one, me, lanes, 1)
    attn_two = relative(attn_low, flips_two, me, lanes, 1)
    in_one = Share(attn_one, d_pre[:, : 2 * model_width], masks_one)
    in_two = Share(attn_two, d_pre[:, 2 * model_width :], masks_two)
    sent_one, sent_two = in_one.send(), in_two.send()
    sent_one, sent_two, back_one.arrived, back_two.arrived = in_order(
        sent_one, sent_two, back_one.arrived, back_two.arrived
    )
    in_one.to_core(sent_one)
    in_two.to_core(sent_two)
    sent_one, sent_two = back_one.next(), back_two.next()
    sent_one, sent_two, in_one.arrived, in_two.arrived = in_order(
        sent_one, sent_two, in_one.arrived, in_two.arrived
    )
    back_one.to_second(sent_one)
    back_two.to_second(sent_two)
    sent_one, sent_two = in_one.next(), in_two.next()
    sent_one, sent_two, d_pre = in_order(sent_one, sent_two, d_pre)
    in_one.to_second(sent_one)
    in_two.to_second(sent_two)
    g_in_bias = jnp.sum(d_pre.astype(wide), 0)
    d_h1 = d_r2 + back_mul(d_pre, w_in)
    d_r1, g_attn_gain, g_attn_bias = norm_back(d_h1, normed_attn, inverse_attn, attn_gain)
    d_attended = d_r1.astype(narrow)
    g_out_bias = jnp.sum(d_attended.astype(wide), 0)
    out_one = Share(
        relative(context_low, flips_one, me, lanes, 1),
        d_attended[:, : model_width // 2],
        masks_one,
    )
    out_two = Share(
        relative(context_low, flips_two, me, lanes, 1),
        d_attended[:, model_width // 2 :],
        masks_two,
    )
    sent_one, sent_two = out_one.send(), out_two.send()
    sent_one, sent_two, d_attended = in_order(sent_one, sent_two, d_attended)
    out_one.to_core(sent_one)
    out_two.to_core(sent_two)
    d_context = back_mul(d_attended, w_out).astype(narrow).reshape(page_count, PAGE, HEADS, HEAD)
    d_probs = jnp.einsum("bqhe,bkhe->bhqk", d_context, value_rows, preferred_element_type=wide)
    sent_one, sent_two = back_one.third(), back_two.third()
    sent_one, sent_two, out_one.arrived, out_two.arrived, d_probs = in_order(
        sent_one, sent_two, out_one.arrived, out_two.arrived, d_probs
    )
    back_one.to_last(sent_one)
    back_two.to_last(sent_two)
    sent_one, sent_two = out_one.next(), out_two.next()
    sent_one, sent_two, d_probs = in_order(sent_one, sent_two, d_probs)
    out_one.to_second(sent_one)
    out_two.to_second(sent_two)
    scores_again = (
        jnp.einsum("bqhe,bkhe->bhqk", queries, key_rows, preferred_element_type=wide) * score_scale
    )
    probs_again = jnp.exp(scores_again - log_total)
    d_values = jnp.einsum(
        "bhqk,bqhe->bkhe", probs_again.astype(narrow), d_context, preferred_element_type=wide
    )
    d_scores = (probs_again * (d_probs - jnp.sum(probs_again * d_probs, -1, keepdims=True))).astype(
        narrow
    )
    d_queries = (
        jnp.einsum("bhqk,bkhe->bqhe", d_scores, key_rows, preferred_element_type=wide) * score_scale
    )
    d_keys = (
        jnp.einsum("bhqk,bqhe->bkhe", d_scores, queries, preferred_element_type=wide) * score_scale
    )
    d_packed = (
        jnp.stack([d_queries, d_keys, d_values], 2)
        .reshape(token_rows, 3 * model_width)
        .astype(narrow)
    )
    emb_one = relative(emb_low, flips_one, me, lanes, 1)
    emb_two = relative(emb_low, flips_two, me, lanes, 1)
    qkv_one = Share(emb_one, d_packed[:, : 3 * model_width // 2], masks_one)
    qkv_two = Share(emb_two, d_packed[:, 3 * model_width // 2 :], masks_two)
    sent_one, sent_two = qkv_one.send(), qkv_two.send()
    sent_one, sent_two, in_one.arrived, in_two.arrived, d_packed = in_order(
        sent_one, sent_two, in_one.arrived, in_two.arrived, d_packed
    )
    qkv_one.to_core(sent_one)
    qkv_two.to_core(sent_two)
    sent_one, sent_two = in_one.third(), in_two.third()
    back_share = jnp.concatenate([back_one.result(), back_two.result()], 0)
    sent_one, sent_two, d_packed, back_share = in_order(sent_one, sent_two, d_packed, back_share)
    in_one.to_last(sent_one)
    in_two.to_last(sent_two)
    g_back = emb_total(back_share)
    g_query_bias = jnp.sum(d_packed[:, :model_width].astype(wide), 0)
    g_value_bias = jnp.sum(d_packed[:, 2 * model_width :].astype(wide), 0)
    d_h0 = d_r1 + back_mul(d_packed, w_qkv)
    d_embed, g_emb_gain, g_emb_bias = norm_back(d_h0, normed_emb, inverse_emb, emb_gain)
    embed_blocks = [
        relative(d_embed, [offset], inner, columns, 1) for offset in range(group)
    ]
    embed_columns = jnp.concatenate(exchange(embed_blocks), 0)
    embed_columns, qkv_one.arrived, qkv_two.arrived = in_order(
        embed_columns, qkv_one.arrived, qkv_two.arrived
    )
    sent_one, sent_two = qkv_one.next(), qkv_two.next()
    qkv_one.to_second(sent_one)
    qkv_two.to_second(sent_two)
    table_total = None
    for offset in list(range(2, planes - 1)) + [1, planes - 1, 0]:
        part = spread_rows(table_uses[offset], embed_columns, entries)
        part = around(part, (planes - offset) % planes) if offset else part
        table_total = part if table_total is None else table_total + part
    row_masks = [mask for mask in masks_one if mask >= group]
    table_total = halve(
        relative(
            table_total,
            flips_of([mask // group for mask in row_masks]),
            me // group,
            entries * group // devices,
            0,
        ),
        row_masks,
    )
    table_share = in_columns(
        exchange(
            [
                relative(table_total, [offset], inner, entries // devices, 0)
                for offset in range(group)
            ]
        )
    )
    out_one.to_last(out_one.third())
    out_two.to_last(out_two.third())
    g_in = emb_total(jnp.concatenate([in_one.result(), in_two.result()], 1))
    g_out = emb_total(jnp.concatenate([out_one.result(), out_two.result()], 1))
    qkv_one.to_last(qkv_one.third())
    qkv_two.to_last(qkv_two.third())
    g_qkv = emb_total(jnp.concatenate([qkv_one.result(), qkv_two.result()], 1))
    vectors = [
        g_query_bias,
        g_value_bias,
        g_out_bias,
        g_attn_gain,
        g_attn_bias,
        g_in_bias,
        g_back_bias,
        g_ffn_gain,
        g_ffn_bias,
        g_emb_gain,
        g_emb_bias,
        jnp.full((devices,), jnp.sum(d_embed * d_embed)),
    ]
    stacked = jnp.concatenate([vector.reshape(devices, -1) for vector in vectors], 1)
    vector_share = emb_total(halve(relative(stacked, flips_one, me, 1, 0), masks_one))[0]
    totals = []
    first = 0
    for vector in vectors:
        length = vector.shape[0] // devices
        totals.append(vector_share[first : first + length])
        first += length
    entry_count = token_rows * model_width * devices * planes
    rms_grad = jnp.sqrt(totals[11][0] / entry_count)
    return (
        output,
        d_embed,
        table_share[None],
        totals[9],
        totals[10],
        g_qkv,
        totals[0],
        totals[1],
        g_out,
        totals[2],
        totals[3],
        totals[4],
        g_in,
        totals[5],
        g_back,
        totals[6],
        totals[7],
        totals[8],
        rms_grad,
    )


def solution(mesh):
    return jax.shard_map(
        on_device,
        mesh=mesh,
        in_specs=(
            P(("pages", "emb"), None),
            P(None, ("pages", "emb")),
            P("emb", None, None),
            P(),
            P(),
            P(),
            P(),
            P(),
            P(),
            P(),
            P(),
            P(),
            P(),
            P(),
            P(),
            P(),
            P(),
            P(),
            P(("pages", "emb"), None),
        ),
        out_specs=(
            P(("pages", "emb"), None),
            P(("pages", "emb"), None),
            P("emb", "pages", None),
            P("pages"),
            P("pages"),
            P("pages", None),
            P("pages"),
            P("pages"),
            P("pages", None),
            P("pages"),
            P("pages"),
            P("pages"),
            P("pages", None),
            P("pages"),
            P("pages", None),
            P("pages"),
            P("pages"),
            P("pages"),
            P(),
        ),
        check_vma=False,
    )
```

time: 927 us -> 846 us (0.913)
  waiting for transfers between devices: 474 us -> 378 us
  other arithmetic: 125 us -> 70 us
  Pallas kernels: 0 us -> 43.3 us
  matrix products: 157 us -> 186 us
  starting transfers between devices: 75.9 us -> 89.1 us
  between operations: 17.5 us -> 5.65 us
    reduce_scatter x2 -> x0, waiting for transfers between devices: 143 us -> none  [the longest x1 143 us: on_device(): lax.psum_scatter(look_rows(layout_tables[0], first_idx, second_idx, table...]
    ppermute x4 -> x5, waiting for transfers between devices: 74.6 us -> 127 us  [emb_total(): lax.ppermute(share, 'emb', [(1, 0), (2, 3)])]
    ppermute x24 -> x48, waiting for transfers between devices: 192 us -> 139 us  [swap(): lax.ppermute(array, 'pages', [(one, one ^ mask) for one in range(lax.axis...]
    scatter-add x2 -> x0, other arithmetic: 44.4 us -> none  [segment_rows(): return jax.ops.segment_sum(incoming, index_rows, num_segments=entries)]
    pallas_call x0 -> x8, Pallas kernels: none -> 43.3 us  [the longest x4 25.1 us: add_rows(): pl.pallas_call(lookup_kernel, grid=(tokens // block,), in_specs=[pl.Block...]
    ppermute x0 -> x6, waiting for transfers between devices: none -> 39.6 us  [around(): lax.ppermute(array, 'emb', [((one + offset) % planes, one) for one in ran...]
    gather x2 -> x0, local copies, waits for them, and re-layouts: 27.7 us -> none  [the longest x1 13.9 us: look_rows(): single = jnp.take(table, first_idx, axis=0)]
    ppermute x24 -> x48, starting transfers between devices: 20.8 us -> 46.9 us  [swap(): lax.ppermute(array, 'pages', [(one, one ^ mask) for one in range(lax.axis...]
  transfers between devices with their start and end apart: 39 -> 69, of which waited for: 17 -> 31; matrix products, arithmetic and copies ran while one was open for 16% -> 20% of each run, Pallas kernels for 0% -> 4%
where the time goes in v2:
time: 846 us; the launch traced here: 836 us
  waiting for transfers between devices  378 us (45%)
  matrix products  186 us (22%)
  starting transfers between devices  89.1 us (11%)
  other arithmetic  70 us (8%)
  local copies, waits for them, and re-layouts  54.7 us (6%)
  Pallas kernels  43.3 us (5%)
  blocking collectives  9.37 us (1%)
    ppermute x48, waiting for transfers between devices, swap(): lax.ppermute(array, 'pages', [(one, one ^ mask) for one in range(lax.axis...  139 us
    ppermute x5, waiting for transfers between devices, emb_total(): lax.ppermute(share, 'emb', [(1, 0), (2, 3)])  127 us
    ppermute x5, waiting for transfers between devices, emb_total(): share = share + lax.ppermute(share, 'emb', [(0, 1), (3, 2)])  72 us
    dot_general x24, matrix products, outer_sum(): jnp.einsum('ti,tj->ij', left, right, preferred_element_type=jnp.float32)  68.5 us
    dot_general x4, matrix products, matmul(): return jnp.dot(left, right, preferred_element_type=jnp.float32)  47.9 us
    ppermute x48, starting transfers between devices, swap(): lax.ppermute(array, 'pages', [(one, one ^ mask) for one in range(lax.axis...  46.9 us
    ppermute x6, waiting for transfers between devices, around(): lax.ppermute(array, 'emb', [((one + offset) % planes, one) for one in ran...  39.6 us
    dot_general x4, matrix products, back_mul(): jnp.einsum('tj,ij->ti', left, right, preferred_element_type=jnp.float32)  28.9 us
  transfers between devices with their start and end apart: 69, of which 31 were waited for; matrix products, arithmetic and copies ran while one was open for 20% of the time, Pallas kernels for 4%

profile of v2, /device:TPU:0, one launch (start us, length us, event | category | flops | bytes accessed | tf_op | source)
XLA Modules:
  0.0 836.5 jit_solution(15074527814134113578)
XLA Ops:
  1.9 5.1 collective-permute-start.2
  8.0 9.4 %all_gather.3 = s32[4,4096]{1,0:T(4,128)S(1)} all-gather(s32[4,512]{1,0:T(4,128)} %param.20), channel_id=1, replica_groups={{0,4,8,12,16,20,24,28},{1,5,9,13,17,21,25,29},{2,6,10,14,18,22,26,30},{..., dimensions={1}, use_global_device_ids=true | all-gather | bytes 73728 | tf_op jit(solution)/shard_map/all_gather | solution.py:298
  27.4 5.6 shard_map.330.total_ref
  33.0 6.9 shard_map.331.total_ref
  40.0 6.9 shard_map.332.total_ref
  46.9 4.9 collective-permute-done.table_ref
  51.8 5.6 shard_map.333
  75.1 12.7 %collective-permute-done.7 = f32[512,128]{1,0:T(8,128)S(1)} collective-permute-done((f32[512,128]{1,0:T(8,128)S(1)}, f32[512,128]{1,0:T(8,128)S(1)}, u32[]{:S(2)}, u32[]{:S(2)}) %collective-permute-start.7) | collective-permute-done | bytes 262176 | tf_op jit(solution)/shard_map/ppermute | solution.py:173
  97.2 7.5 add_convert_fusion
  104.8 4.9 copy.60
  109.7 9.8 %multiply_reduce_fusion = (f32[16,512]{1,0:T(8,128)S(1)}, f32[16,512,512]{1,2,0:T(8,128)}) fusion(bf16[1,512,3,16,64]{1,4,3,2,0:T(8,128)(2,1)} %bitcast.144), kind=kOutput, calls=%fused_computation.8 | convolution fusion | flops 545251328 | bytes 18907136 | tf_op jit(solution)/shard_map/bqhe,bkhe->bhqk/dot_general | solution.py:330
  119.4 8.6 %fusion.2 = f32[16,512]{1,0:T(8,128)S(1)} fusion(f32[16,512,512]{1,2,0:T(8,128)} %get-tuple-element.217, f32[16,512]{1,0:T(8,128)S(1)} %get-tuple-element.216), kind=kLoop, calls=%fused_computation.7 | loop fusion | flops 12574720 | bytes 16842752 | tf_op jit(solution)/shard_map/reduce_sum | solution.py:334
  128.1 8.1 fusion.55
  139.9 34.0 %fusion.8 = (bf16[512,4096]{1,0:T(8,128)(2,1)S(1)}, f32[512,4096]{1,0:T(8,128)}) fusion(f32[4096]{0:T(1024)S(1)} %copy-done.102, bf16[512,1024]{1,0:T(8,128)(2,1)S(1)} %fusion.34, bf16[1024,4096]{1,0:T(8,128)(2,1)} %param.31), kind=kOutput, calls=%fused_computation.16 | convolution fusion | flops 4433379328 | bytes 22036480 | tf_op jit(solution)/shard_map/dot_general | solution.py:46
  173.9 4.8 fusion.220
  194.9 10.6 %fusion.14 = bf16[512,4096]{1,0:T(8,128)(2,1)S(1)} fusion(f32[512,4096]{1,0:T(8,128)} %get-tuple-element.221, bf16[512,1024]{1,0:T(8,128)(2,1)S(1)} %get-tuple-element.56, bf16[4096,1024]{1,0:T(8,128)(2,1)} %param.33, f32[4096]{0:T(1024)S(1)} %copy-done.102), kind=kOutput, calls=%fused_computation.22 | convolution fusion | flops 4318035968 | bytes 22036480 | tf_op jit(solution)/shard_map/tj,ij->ti/dot_general | solution.py:54
  240.2 9.7 %multiply_reduce_fusion.3 = (f32[1024]{0:T(1024)}, f32[512]{0:T(512)S(1)}, f32[512]{0:T(512)S(1)}, f32[1024]{0:T(1024)}, f32[512,1024]{1,0:T(8,128)S(1)}) fusion(f32[512,1024]{1,0:T(8,128)S(1)} %copy-done.16, f32[512]{0:T(512)S(1)} %add_rsqrt_fusion.1, f32[512]{0:T(512)S(1)} %broadcast_multiply_fusion.7, f32[1024]{0:T(1024)S(1)} %copy-done.81, ...), kind=kOutput, calls=%fused_computation.60 | convolution fusion | flops 4304401408 | bytes 19955712 | tf_op jit(solution)/shard_map/tj,ij->ti/dot_general | solution.py:54
  263.8 4.5 slice_add_fusion.3
  269.6 8.4 %fusion.61 = bf16[1,512,1,16,64]{1,4,3,2,0:T(8,128)(2,1)} fusion(bf16[512,16,64]{0,2,1:T(8,128)(2,1)S(1)} %bitcast.149, f32[16,512,512]{1,2,0:T(8,128)} %get-tuple-element.217, f32[16,512]{1,0:T(8,128)S(1)} %copy-done.62), kind=kOutput, calls=%fused_computation.118 | convolution fusion | flops 549978112 | bytes 18907136 | tf_op jit(solution)/shard_map/bhqk,bqhe->bkhe/dot_general | solution.py:425
  278.0 9.3 %convolution_bitcast_fusion = f32[1,16,512,512]{2,3,1,0:T(8,128)} fusion(bf16[512,16,64]{0,2,1:T(8,128)(2,1)S(1)} %bitcast.150, bf16[1,512,3,16,64]{1,4,3,2,0:T(8,128)(2,1)} %bitcast.146), kind=kOutput, calls=%fused_computation.12 | convolution fusion | flops 536870912 | bytes 18874368 | tf_op jit(solution)/shard_map/bqhe,bkhe->bhqk/dot_general | solution.py:410
  293.1 16.5 %collective-permute-done.14 = f32[512,1024]{1,0:T(8,128)} collective-permute-done((f32[512,1024]{1,0:T(8,128)}, f32[512,1024]{1,0:T(8,128)}, u32[]{:S(2)}, u32[]{:S(2)}) %collective-permute-start.14) | collective-permute-done | bytes 2097184 | tf_op jit(solution)/shard_map/ppermute | solution.py:173
  320.4 12.2 %fusion = f32[16,512]{1,0:T(8,128)S(1)} fusion(f32[1,16,512,512]{2,3,1,0:T(8,128)} %convolution_bitcast_fusion, f32[16,512,512]{1,2,0:T(8,128)} %get-tuple-element.217, f32[16,512]{1,0:T(8,128)S(1)} %copy-done.63), kind=kLoop, calls=%fused_computation.2 | loop fusion | flops 16769024 | bytes 33619968 | tf_op jit(solution)/shard_map/reduce_sum | solution.py:428
  334.7 8.1 fusion.15
  364.8 14.2 %collective-permute-done.20 = f32[256,1024]{1,0:T(8,128)} collective-permute-done((f32[256,1024]{1,0:T(8,128)}, f32[256,1024]{1,0:T(8,128)}, u32[]{:S(2)}, u32[]{:S(2)}) %collective-permute-start.20) | collective-permute-done | bytes 1048608 | tf_op jit(solution)/shard_map/ppermute | solution.py:173
  380.9 6.8 collective-permute-done.21
  392.5 6.3 multiply_reduce_fusion.2
  409.6 8.2 collective-permute-done.56
  423.3 6.2 collective-permute-start.44
  449.8 4.9 collective-permute-done.24
  456.2 17.0 %collective-permute-done.25 = f32[512,128]{1,0:T(8,128)S(1)} collective-permute-done((f32[512,128]{1,0:T(8,128)S(1)}, f32[512,128]{1,0:T(8,128)S(1)}, u32[]{:S(2)}, u32[]{:S(2)}) %collective-permute-start.25) | collective-permute-done | bytes 262176 | tf_op jit(solution)/shard_map/ppermute | solution.py:173
  477.4 9.7 %collective-permute-done.28 = f32[512,128]{1,0:T(8,128)S(1)} collective-permute-done((f32[512,128]{1,0:T(8,128)S(1)}, f32[512,128]{1,0:T(8,128)S(1)}, u32[]{:S(2)}, u32[]{:S(2)}) %collective-permute-start.28) | collective-permute-done | bytes 262176 | tf_op jit(solution)/shard_map/ppermute | solution.py:173
  499.8 4.7 collective-permute-start.63
  508.1 38.6 %collective-permute-done.66 = f32[512,1024]{1,0:T(8,128)S(1)} collective-permute-done((f32[512,1024]{1,0:T(8,128)S(1)}, f32[512,1024]{1,0:T(8,128)S(1)}, u32[]{:S(2)}, u32[]{:S(2)}) %collective-permute-start.66) | collective-permute-done | bytes 2097184 | tf_op jit(solution)/shard_map/ppermute | solution.py:235
  547.8 4.6 shard_map.334
  558.0 33.4 %collective-permute-done.63 = f32[128,4096]{1,0:T(8,128)S(1)} collective-permute-done((f32[128,4096]{1,0:T(8,128)S(1)}, f32[128,4096]{1,0:T(8,128)S(1)}, u32[]{:S(2)}, u32[]{:S(2)}) %collective-permute-start.63) | collective-permute-done | bytes 2097184 | tf_op jit(solution)/shard_map/ppermute | solution.py:235
  595.2 15.5 %collective-permute-done.48 = f32[128,1536]{1,0:T(8,128)S(1)} collective-permute-done((f32[128,1536]{1,0:T(8,128)S(1)}, f32[128,1536]{1,0:T(8,128)S(1)}, u32[]{:S(2)}, u32[]{:S(2)}) %collective-permute-start.48) | collective-permute-done | bytes 786464 | tf_op jit(solution)/shard_map/ppermute | solution.py:173
  611.7 5.9 collective-permute-start.51
  617.6 4.6 shard_map.336
  622.2 4.6 shard_map.335
  626.8 6.0 collective-permute-done.31
  638.1 4.6 shard_map.337
  642.7 24.1 %collective-permute-done.32 = f32[1024,128]{1,0:T(8,128)S(1)} collective-permute-done((f32[1024,128]{1,0:T(8,128)S(1)}, f32[1024,128]{1,0:T(8,128)S(1)}, u32[]{:S(2)}, u32[]{:S(2)}) %collective-permute-start.32) | collective-permute-done | bytes 524320 | tf_op jit(solution)/shard_map/ppermute | solution.py:284
  668.0 4.5 collective-permute-done.33
  677.0 35.4 %collective-permute-done.60 = f32[128,1024]{1,0:T(8,128)S(1)} collective-permute-done((f32[128,1024]{1,0:T(8,128)S(1)}, f32[128,1024]{1,0:T(8,128)S(1)}, u32[]{:S(2)}, u32[]{:S(2)}) %collective-permute-start.60) | collective-permute-done | bytes 524320 | tf_op jit(solution)/shard_map/ppermute | solution.py:237
  713.4 4.7 collective-permute-done.35
  738.3 19.0 %collective-permute-done.68 = f32[512,1024]{1,0:T(8,128)S(1)} collective-permute-done((f32[512,1024]{1,0:T(8,128)S(1)}, f32[512,1024]{1,0:T(8,128)S(1)}, u32[]{:S(2)}, u32[]{:S(2)}) %collective-permute-start.68) | collective-permute-done | bytes 2097184 | tf_op jit(solution)/shard_map/ppermute | solution.py:237
  759.1 43.2 %collective-permute-done.65 = f32[128,4096]{1,0:T(8,128)S(1)} collective-permute-done((f32[128,4096]{1,0:T(8,128)S(1)}, f32[128,4096]{1,0:T(8,128)S(1)}, u32[]{:S(2)}, u32[]{:S(2)}) %collective-permute-start.65) | collective-permute-done | bytes 2097184 | tf_op jit(solution)/shard_map/ppermute | solution.py:237
  803.8 29.8 %collective-permute-done.53 = f32[128,3072]{1,0:T(8,128)S(1)} collective-permute-done((f32[128,3072]{1,0:T(8,128)S(1)}, f32[128,3072]{1,0:T(8,128)S(1)}, u32[]{:S(2)}, u32[]{:S(2)}) %collective-permute-start.53) | collective-permute-done | bytes 1572896 | tf_op jit(solution)/shard_map/ppermute | solution.py:237
  (517 shorter events, 260.3 us)
Async XLA Ops:
  1.9 31.1 %collective-permute-start.2 = (f32[1024,128]{1,0:T(8,128)S(1)}, f32[1024,128]{1,0:T(8,128)}, u32[]{:S(2)}, u32[]{:S(2)}) collective-permute-start(f32[1024,128]{1,0:T(8,128)S(1)} %dynamic-slice_bitcast_fusion.table_ref), channel_id=1, source_target_pairs={{1,0},{2,1},{3,2},{0,3},{5,4},{6,5},{7,6},{4,7},{9,8},{10,9},{11,1... | collective-permute-start | bytes 1572872 | tf_op jit(solution)/shard_map/ppermute | solution.py:284
  7.0 32.9 %collective-permute-start.1 = (f32[1024,128]{1,0:T(8,128)S(1)}, f32[1024,128]{1,0:T(8,128)}, u32[]{:S(2)}, u32[]{:S(2)}) collective-permute-start(f32[1024,128]{1,0:T(8,128)S(1)} %dynamic-slice_bitcast_fusion.table_ref), channel_id=1, source_target_pairs={{3,0},{0,1},{1,2},{2,3},{7,4},{4,5},{5,6},{6,7},{11,8},{8,9},{9,10... | collective-permute-start | bytes 1572872 | tf_op jit(solution)/shard_map/ppermute | solution.py:284
  7.0 44.8 %collective-permute-start = (f32[1024,128]{1,0:T(8,128)S(1)}, f32[1024,128]{1,0:T(8,128)S(1)}, u32[]{:S(2)}, u32[]{:S(2)}) collective-permute-start(f32[1024,128]{1,0:T(8,128)S(1)} %dynamic-slice_bitcast_fusion.table_ref), channel_id=1, source_target_pairs={{2,0},{3,1},{0,2},{1,3},{6,4},{7,5},{4,6},{5,7},{10,8},{11,9},{8,1... | collective-permute-start | bytes 1572872 | tf_op jit(solution)/shard_map/ppermute | solution.py:284
  60.4 28.7 %collective-permute-start.9 = (f32[512,128]{1,0:T(8,128)S(1)}, f32[512,128]{1,0:T(8,128)S(1)}, u32[]{:S(2)}, u32[]{:S(2)}) collective-permute-start(f32[512,128]{1,0:T(8,128)S(1)} %get-tuple-element.143), channel_id=1, source_target_pairs={{0,28},{4,24},{8,20},{12,16},{16,12},{20,8},{24,4},{28,0},{1,29},{... | collective-permute-start | bytes 786440 | tf_op jit(solution)/shard_map/ppermute | solution.py:173
  62.8 25.6 %collective-permute-start.8 = (f32[512,128]{1,0:T(8,128)S(1)}, f32[512,128]{1,0:T(8,128)S(1)}, u32[]{:S(2)}, u32[]{:S(2)}) collective-permute-start(f32[512,128]{1,0:T(8,128)S(1)} %get-tuple-element.144), channel_id=1, source_target_pairs={{0,24},{4,28},{8,16},{12,20},{16,8},{20,12},{24,0},{28,4},{1,25},{... | collective-permute-start | bytes 786440 | tf_op jit(solution)/shard_map/ppermute | solution.py:173
  67.8 19.9 %collective-permute-start.7 = (f32[512,128]{1,0:T(8,128)S(1)}, f32[512,128]{1,0:T(8,128)S(1)}, u32[]{:S(2)}, u32[]{:S(2)}) collective-permute-start(f32[512,128]{1,0:T(8,128)S(1)} %get-tuple-element.145), channel_id=1, source_target_pairs={{0,20},{4,16},{8,28},{12,24},{16,4},{20,0},{24,12},{28,8},{1,21},{... | collective-permute-start | bytes 786440 | tf_op jit(solution)/shard_map/ppermute | solution.py:173
  192.2 20.0 %collective-permute-start.10 = (f32[1024,1024]{1,0:T(8,128)}, f32[1024,1024]{1,0:T(8,128)}, u32[]{:S(2)}, u32[]{:S(2)}) collective-permute-start(f32[1024,1024]{1,0:T(8,128)} %fusion.88), channel_id=1, source_target_pairs={{0,4},{4,0},{8,12},{12,8},{16,20},{20,16},{24,28},{28,24},{1,5},{5... | collective-permute-start | bytes 12582920 | tf_op jit(solution)/shard_map/ppermute | solution.py:173
  192.6 19.6 %collective-permute-start.11 = (f32[1024,1024]{1,0:T(8,128)}, f32[1024,1024]{1,0:T(8,128)}, u32[]{:S(2)}, u32[]{:S(2)}) collective-permute-start(f32[1024,1024]{1,0:T(8,128)} %fusion.96), channel_id=1, source_target_pairs={{0,4},{4,0},{8,12},{12,8},{16,20},{20,16},{24,28},{28,24},{1,5},{5... | collective-permute-start | bytes 12582920 | tf_op jit(solution)/shard_map/ppermute | solution.py:173
  212.2 20.3 %collective-permute-start.12 = (f32[512,2048]{1,0:T(8,128)}, f32[512,2048]{1,0:T(8,128)}, u32[]{:S(2)}, u32[]{:S(2)}) collective-permute-start(f32[512,2048]{1,0:T(8,128)} %fusion.47), channel_id=1, source_target_pairs={{0,4},{4,0},{8,12},{12,8},{16,20},{20,16},{24,28},{28,24},{1,5},{5... | collective-permute-start | bytes 12582920 | tf_op jit(solution)/shard_map/ppermute | solution.py:173
  212.7 19.8 %collective-permute-start.13 = (f32[512,2048]{1,0:T(8,128)}, f32[512,2048]{1,0:T(8,128)}, u32[]{:S(2)}, u32[]{:S(2)}) collective-permute-start(f32[512,2048]{1,0:T(8,128)} %fusion.39), channel_id=1, source_target_pairs={{0,4},{4,0},{8,12},{12,8},{16,20},{20,16},{24,28},{28,24},{1,5},{5... | collective-permute-start | bytes 12582920 | tf_op jit(solution)/shard_map/ppermute | solution.py:173
  260.3 55.6 %collective-permute-start.16 = (f32[512,512]{1,0:T(8,128)}, f32[512,512]{1,0:T(8,128)}, u32[]{:S(2)}, u32[]{:S(2)}) collective-permute-start(f32[512,512]{1,0:T(8,128)} %fusion.109), channel_id=1, source_target_pairs={{0,4},{4,0},{8,12},{12,8},{16,20},{20,16},{24,28},{28,24},{1,5},{5... | collective-permute-start | bytes 3145736 | tf_op jit(solution)/shard_map/ppermute | solution.py:173
  260.7 55.2 %collective-permute-start.17 = (f32[512,512]{1,0:T(8,128)}, f32[512,512]{1,0:T(8,128)}, u32[]{:S(2)}, u32[]{:S(2)}) collective-permute-start(f32[512,512]{1,0:T(8,128)} %fusion.110), channel_id=1, source_target_pairs={{0,4},{4,0},{8,12},{12,8},{16,20},{20,16},{24,28},{28,24},{1,5},{5... | collective-permute-start | bytes 3145736 | tf_op jit(solution)/shard_map/ppermute | solution.py:173
  260.8 48.8 %collective-permute-start.14 = (f32[512,1024]{1,0:T(8,128)}, f32[512,1024]{1,0:T(8,128)}, u32[]{:S(2)}, u32[]{:S(2)}) collective-permute-start(f32[512,1024]{1,0:T(8,128)} %slice_add_fusion.7), channel_id=1, source_target_pairs={{0,8},{4,12},{8,0},{12,4},{16,24},{20,28},{24,16},{28,20},{1,9},{5... | collective-permute-start | bytes 6291464 | tf_op jit(solution)/shard_map/ppermute | solution.py:173
  262.3 51.2 %collective-permute-start.15 = (f32[512,1024]{1,0:T(8,128)}, f32[512,1024]{1,0:T(8,128)}, u32[]{:S(2)}, u32[]{:S(2)}) collective-permute-start(f32[512,1024]{1,0:T(8,128)} %slice_add_fusion.6), channel_id=1, source_target_pairs={{0,16},{4,20},{8,24},{12,28},{16,0},{20,4},{24,8},{28,12},{1,17},{... | collective-permute-start | bytes 6291464 | tf_op jit(solution)/shard_map/ppermute | solution.py:173
  288.0 69.3 %collective-permute-start.18 = (f32[256,2048]{1,0:T(8,128)}, f32[256,2048]{1,0:T(8,128)}, u32[]{:S(2)}, u32[]{:S(2)}) collective-permute-start(f32[256,2048]{1,0:T(8,128)} %slice_add_fusion.5), channel_id=1, source_target_pairs={{0,8},{4,12},{8,0},{12,4},{16,24},{20,28},{24,16},{28,20},{1,9},{5... | collective-permute-start | bytes 6291464 | tf_op jit(solution)/shard_map/ppermute | solution.py:173
  309.6 48.9 %collective-permute-start.19 = (f32[256,2048]{1,0:T(8,128)}, f32[256,2048]{1,0:T(8,128)}, u32[]{:S(2)}, u32[]{:S(2)}) collective-permute-start(f32[256,2048]{1,0:T(8,128)} %slice_add_fusion.4), channel_id=1, source_target_pairs={{0,16},{4,20},{8,24},{12,28},{16,0},{20,4},{24,8},{28,12},{1,17},{... | collective-permute-start | bytes 6291464 | tf_op jit(solution)/shard_map/ppermute | solution.py:173
  342.8 64.0 %collective-permute-start.54 = (f32[256,512]{1,0:T(8,128)}, f32[256,512]{1,0:T(8,128)S(1)}, u32[]{:S(2)}, u32[]{:S(2)}) collective-permute-start(f32[256,512]{1,0:T(8,128)} %slice_add_fusion.27), channel_id=1, source_target_pairs={{0,8},{4,12},{8,0},{12,4},{16,24},{20,28},{24,16},{28,20},{1,9},{5... | collective-permute-start | bytes 1572872 | tf_op jit(solution)/shard_map/ppermute | solution.py:173
  344.3 34.8 %collective-permute-start.20 = (f32[256,1024]{1,0:T(8,128)}, f32[256,1024]{1,0:T(8,128)}, u32[]{:S(2)}, u32[]{:S(2)}) collective-permute-start(f32[256,1024]{1,0:T(8,128)} %slice_add_fusion.18), channel_id=1, source_target_pairs={{0,16},{4,20},{8,24},{12,28},{16,0},{20,4},{24,8},{28,12},{1,17},{... | collective-permute-start | bytes 3145736 | tf_op jit(solution)/shard_map/ppermute | solution.py:173
  344.8 42.9 %collective-permute-start.21 = (f32[256,1024]{1,0:T(8,128)}, f32[256,1024]{1,0:T(8,128)S(1)}, u32[]{:S(2)}, u32[]{:S(2)}) collective-permute-start(f32[256,1024]{1,0:T(8,128)} %slice_add_fusion.17), channel_id=1, source_target_pairs={{0,8},{4,12},{8,0},{12,4},{16,24},{20,28},{24,16},{28,20},{1,9},{5... | collective-permute-start | bytes 3145736 | tf_op jit(solution)/shard_map/ppermute | solution.py:173
  404.7 91.0 %collective-permute-start.29 = (f32[512,1536]{1,0:T(8,128)}, f32[512,1536]{1,0:T(8,128)}, u32[]{:S(2)}, u32[]{:S(2)}) collective-permute-start(f32[512,1536]{1,0:T(8,128)} %fusion.78), channel_id=1, source_target_pairs={{0,4},{4,0},{8,12},{12,8},{16,20},{20,16},{24,28},{28,24},{1,5},{5... | collective-permute-start | bytes 9437192 | tf_op jit(solution)/shard_map/ppermute | solution.py:173
  404.9 90.8 %collective-permute-start.30 = (f32[512,1536]{1,0:T(8,128)}, f32[512,1536]{1,0:T(8,128)}, u32[]{:S(2)}, u32[]{:S(2)}) collective-permute-start(f32[512,1536]{1,0:T(8,128)} %fusion.68), channel_id=1, source_target_pairs={{0,4},{4,0},{8,12},{12,8},{16,20},{20,16},{24,28},{28,24},{1,5},{5... | collective-permute-start | bytes 9437192 | tf_op jit(solution)/shard_map/ppermute | solution.py:173
  406.9 23.9 %collective-permute-start.55 = (f32[128,512]{1,0:T(8,128)S(1)}, f32[128,512]{1,0:T(8,128)S(1)}, u32[]{:S(2)}, u32[]{:S(2)}) collective-permute-start(f32[128,512]{1,0:T(8,128)S(1)} %slice_add_fusion.30), channel_id=1, source_target_pairs={{0,16},{4,20},{8,24},{12,28},{16,0},{20,4},{24,8},{28,12},{1,17},{... | collective-permute-start | bytes 786440 | tf_op jit(solution)/shard_map/ppermute | solution.py:173
  417.9 15.4 %collective-permute-start.57 = (f32[128,512]{1,0:T(8,128)S(1)}, f32[128,512]{1,0:T(8,128)S(1)}, u32[]{:S(2)}, u32[]{:S(2)}) collective-permute-start(f32[128,512]{1,0:T(8,128)S(1)} %slice_add_fusion.28), channel_id=1, source_target_pairs={{0,8},{4,12},{8,0},{12,4},{16,24},{20,28},{24,16},{28,20},{1,9},{5... | collective-permute-start | bytes 786440 | tf_op jit(solution)/shard_map/ppermute | solution.py:173
  440.4 49.2 %collective-permute-start.61 = (f32[128,2048]{1,0:T(8,128)}, f32[128,2048]{1,0:T(8,128)S(1)}, u32[]{:S(2)}, u32[]{:S(2)}) collective-permute-start(f32[128,2048]{1,0:T(8,128)} %slice_add_fusion.19), channel_id=1, source_target_pairs={{0,16},{4,20},{8,24},{12,28},{16,0},{20,4},{24,8},{28,12},{1,17},{... | collective-permute-start | bytes 3145736 | tf_op jit(solution)/shard_map/ppermute | solution.py:173
  448.2 25.0 %collective-permute-start.25 = (f32[512,128]{1,0:T(8,128)S(1)}, f32[512,128]{1,0:T(8,128)S(1)}, u32[]{:S(2)}, u32[]{:S(2)}) collective-permute-start(f32[512,128]{1,0:T(8,128)S(1)} %copy-done.66), channel_id=1, source_target_pairs={{0,16},{4,20},{8,24},{12,28},{16,0},{20,4},{24,8},{28,12},{1,17},{... | collective-permute-start | bytes 786440 | tf_op jit(solution)/shard_map/ppermute | solution.py:173
  454.7 37.9 %collective-permute-start.62 = (f32[128,2048]{1,0:T(8,128)}, f32[128,2048]{1,0:T(8,128)S(1)}, u32[]{:S(2)}, u32[]{:S(2)}) collective-permute-start(f32[128,2048]{1,0:T(8,128)} %slice_add_fusion.16), channel_id=1, source_target_pairs={{0,8},{4,12},{8,0},{12,4},{16,24},{20,28},{24,16},{28,20},{1,9},{5... | collective-permute-start | bytes 3145736 | tf_op jit(solution)/shard_map/ppermute | solution.py:173
  487.2 19.4 %collective-permute-start.58 = (f32[128,1024]{1,0:T(8,128)S(1)}, f32[128,1024]{1,0:T(8,128)S(1)}, u32[]{:S(2)}, u32[]{:S(2)}) collective-permute-start(f32[128,1024]{1,0:T(8,128)S(1)} %pad_maximum_fusion.22), channel_id=1, source_target_pairs={{0,1},{3,2},{4,5},{7,6},{8,9},{11,10},{12,13},{15,14},{16,17},{19,... | collective-permute-start | bytes 1572872 | tf_op jit(solution)/shard_map/ppermute | solution.py:235
  489.6 57.1 %collective-permute-start.66 = (f32[512,1024]{1,0:T(8,128)S(1)}, f32[512,1024]{1,0:T(8,128)S(1)}, u32[]{:S(2)}, u32[]{:S(2)}) collective-permute-start(f32[512,1024]{1,0:T(8,128)S(1)} %copy-done.24), channel_id=1, source_target_pairs={{0,1},{3,2},{4,5},{7,6},{8,9},{11,10},{12,13},{15,14},{16,17},{19,... | collective-permute-start | bytes 6291464 | tf_op jit(solution)/shard_map/ppermute | solution.py:235
  492.7 119.1 %collective-permute-start.46 = (f32[1,1793]{1,0:T(1,128)S(1)}, f32[1,1793]{1,0:T(1,128)S(1)}, u32[]{:S(2)}, u32[]{:S(2)}) collective-permute-start(f32[1,1793]{1,0:T(1,128)S(1)} %add.667), channel_id=1, source_target_pairs={{1,0},{2,3},{5,4},{6,7},{9,8},{10,11},{13,12},{14,15},{17,16},{18,... | collective-permute-start | bytes 21524 | tf_op jit(solution)/shard_map/ppermute | solution.py:237
  497.8 58.7 %collective-permute-start.49 = (f32[256,1536]{1,0:T(8,128)S(1)}, f32[256,1536]{1,0:T(8,128)S(1)}, u32[]{:S(2)}, u32[]{:S(2)}) collective-permute-start(f32[256,1536]{1,0:T(8,128)S(1)} %slice_add_fusion.8), channel_id=1, source_target_pairs={{0,16},{4,20},{8,24},{12,28},{16,0},{20,4},{24,8},{28,12},{1,17},{... | collective-permute-start | bytes 4718600 | tf_op jit(solution)/shard_map/ppermute | solution.py:173
  499.8 91.5 %collective-permute-start.63 = (f32[128,4096]{1,0:T(8,128)S(1)}, f32[128,4096]{1,0:T(8,128)S(1)}, u32[]{:S(2)}, u32[]{:S(2)}) collective-permute-start(f32[128,4096]{1,0:T(8,128)S(1)} %pad_maximum_fusion.2), channel_id=1, source_target_pairs={{0,1},{3,2},{4,5},{7,6},{8,9},{11,10},{12,13},{15,14},{16,17},{19,... | collective-permute-start | bytes 6291464 | tf_op jit(solution)/shard_map/ppermute | solution.py:235
  506.6 50.8 %collective-permute-start.47 = (f32[256,1536]{1,0:T(8,128)S(1)}, f32[256,1536]{1,0:T(8,128)S(1)}, u32[]{:S(2)}, u32[]{:S(2)}) collective-permute-start(f32[256,1536]{1,0:T(8,128)S(1)} %slice_add_fusion.10), channel_id=1, source_target_pairs={{0,8},{4,12},{8,0},{12,4},{16,24},{20,28},{24,16},{28,20},{1,9},{5... | collective-permute-start | bytes 4718600 | tf_op jit(solution)/shard_map/ppermute | solution.py:173
  546.7 80.1 %collective-permute-start.59 = (f32[128,1024]{1,0:T(8,128)S(1)}, f32[128,1024]{1,0:T(8,128)S(1)}, u32[]{:S(2)}, u32[]{:S(2)}) collective-permute-start(f32[128,1024]{1,0:T(8,128)S(1)} %fusion.213), channel_id=1, source_target_pairs={{1,2},{2,1},{5,6},{6,5},{9,10},{10,9},{13,14},{14,13},{17,18},{18,... | collective-permute-start | bytes 1572872 | tf_op jit(solution)/shard_map/ppermute | solution.py:236
  556.5 116.3 %collective-permute-start.67 = (f32[512,1024]{1,0:T(8,128)S(1)}, f32[512,1024]{1,0:T(8,128)S(1)}, u32[]{:S(2)}, u32[]{:S(2)}) collective-permute-start(f32[512,1024]{1,0:T(8,128)S(1)} %add.696), channel_id=1, source_target_pairs={{1,2},{2,1},{5,6},{6,5},{9,10},{10,9},{13,14},{14,13},{17,18},{18,... | collective-permute-start | bytes 6291464 | tf_op jit(solution)/shard_map/ppermute | solution.py:236
  557.4 35.8 %collective-permute-start.50 = (f32[128,1536]{1,0:T(8,128)S(1)}, f32[128,1536]{1,0:T(8,128)S(1)}, u32[]{:S(2)}, u32[]{:S(2)}) collective-permute-start(f32[128,1536]{1,0:T(8,128)S(1)} %slice_add_fusion.20), channel_id=1, source_target_pairs={{0,8},{4,12},{8,0},{12,4},{16,24},{20,28},{24,16},{28,20},{1,9},{5... | collective-permute-start | bytes 2359304 | tf_op jit(solution)/shard_map/ppermute | solution.py:173
  591.4 19.3 %collective-permute-start.48 = (f32[128,1536]{1,0:T(8,128)S(1)}, f32[128,1536]{1,0:T(8,128)S(1)}, u32[]{:S(2)}, u32[]{:S(2)}) collective-permute-start(f32[128,1536]{1,0:T(8,128)S(1)} %slice_add_fusion.22), channel_id=1, source_target_pairs={{0,16},{4,20},{8,24},{12,28},{16,0},{20,4},{24,8},{28,12},{1,17},{... | collective-permute-start | bytes 2359304 | tf_op jit(solution)/shard_map/ppermute | solution.py:173
  593.2 39.6 %collective-permute-start.31 = (f32[1024,128]{1,0:T(8,128)S(1)}, f32[1024,128]{1,0:T(8,128)S(1)}, u32[]{:S(2)}, u32[]{:S(2)}) collective-permute-start(f32[1024,128]{1,0:T(8,128)S(1)} %shard_map.334), channel_id=1, source_target_pairs={{2,0},{3,1},{0,2},{1,3},{6,4},{7,5},{4,6},{5,7},{10,8},{11,9},{8,1... | collective-permute-start | bytes 1572872 | tf_op jit(solution)/shard_map/ppermute | solution.py:284
  610.6 63.8 %collective-permute-start.64 = (f32[128,4096]{1,0:T(8,128)S(1)}, f32[128,4096]{1,0:T(8,128)S(1)}, u32[]{:S(2)}, u32[]{:S(2)}) collective-permute-start(f32[128,4096]{1,0:T(8,128)S(1)} %fusion.215), channel_id=1, source_target_pairs={{1,2},{2,1},{5,6},{6,5},{9,10},{10,9},{13,14},{14,13},{17,18},{18,... | collective-permute-start | bytes 6291464 | tf_op jit(solution)/shard_map/ppermute | solution.py:236
  611.7 64.3 %collective-permute-start.51 = (f32[128,3072]{1,0:T(8,128)S(1)}, f32[128,3072]{1,0:T(8,128)S(1)}, u32[]{:S(2)}, u32[]{:S(2)}) collective-permute-start(f32[128,3072]{1,0:T(8,128)S(1)} %pad_maximum_fusion.3), channel_id=1, source_target_pairs={{0,1},{3,2},{4,5},{7,6},{8,9},{11,10},{12,13},{15,14},{16,17},{19,... | collective-permute-start | bytes 4718600 | tf_op jit(solution)/shard_map/ppermute | solution.py:235
  626.7 40.0 %collective-permute-start.32 = (f32[1024,128]{1,0:T(8,128)S(1)}, f32[1024,128]{1,0:T(8,128)S(1)}, u32[]{:S(2)}, u32[]{:S(2)}) collective-permute-start(f32[1024,128]{1,0:T(8,128)S(1)} %shard_map.335), channel_id=1, source_target_pairs={{3,0},{0,1},{1,2},{2,3},{7,4},{4,5},{5,6},{6,7},{11,8},{8,9},{9,10... | collective-permute-start | bytes 1572872 | tf_op jit(solution)/shard_map/ppermute | solution.py:284
  632.8 39.7 %collective-permute-start.33 = (f32[1024,128]{1,0:T(8,128)S(1)}, f32[1024,128]{1,0:T(8,128)S(1)}, u32[]{:S(2)}, u32[]{:S(2)}) collective-permute-start(f32[1024,128]{1,0:T(8,128)S(1)} %shard_map.336), channel_id=1, source_target_pairs={{1,0},{2,1},{3,2},{0,3},{5,4},{6,5},{7,6},{4,7},{9,8},{10,9},{11,1... | collective-permute-start | bytes 1572872 | tf_op jit(solution)/shard_map/ppermute | solution.py:284
  666.7 45.7 %collective-permute-start.60 = (f32[128,1024]{1,0:T(8,128)S(1)}, f32[128,1024]{1,0:T(8,128)S(1)}, u32[]{:S(2)}, u32[]{:S(2)}) collective-permute-start(f32[128,1024]{1,0:T(8,128)S(1)} %add.689), channel_id=1, source_target_pairs={{1,0},{2,3},{5,4},{6,7},{9,8},{10,11},{13,12},{14,15},{17,16},{18,... | collective-permute-start | bytes 1572872 | tf_op jit(solution)/shard_map/ppermute | solution.py:237
  672.7 40.6 %collective-permute-start.34 = (f32[128,128]{1,0:T(8,128)S(1)}, f32[128,128]{1,0:T(8,128)S(1)}, u32[]{:S(2)}, u32[]{:S(2)}) collective-permute-start(f32[128,128]{1,0:T(8,128)S(1)} %get-tuple-element.181), channel_id=1, source_target_pairs={{0,4},{4,0},{8,12},{12,8},{16,20},{20,16},{24,28},{28,24},{1,5},{5... | collective-permute-start | bytes 196616 | tf_op jit(solution)/shard_map/ppermute | solution.py:173
  673.2 84.2 %collective-permute-start.68 = (f32[512,1024]{1,0:T(8,128)S(1)}, f32[512,1024]{1,0:T(8,128)S(1)}, u32[]{:S(2)}, u32[]{:S(2)}) collective-permute-start(f32[512,1024]{1,0:T(8,128)S(1)} %add.697), channel_id=1, source_target_pairs={{1,0},{2,3},{5,4},{6,7},{9,8},{10,11},{13,12},{14,15},{17,16},{18,... | collective-permute-start | bytes 6291464 | tf_op jit(solution)/shard_map/ppermute | solution.py:237
  674.7 127.5 %collective-permute-start.65 = (f32[128,4096]{1,0:T(8,128)S(1)}, f32[128,4096]{1,0:T(8,128)S(1)}, u32[]{:S(2)}, u32[]{:S(2)}) collective-permute-start(f32[128,4096]{1,0:T(8,128)S(1)} %add.695), channel_id=1, source_target_pairs={{1,0},{2,3},{5,4},{6,7},{9,8},{10,11},{13,12},{14,15},{17,16},{18,... | collective-permute-start | bytes 6291464 | tf_op jit(solution)/shard_map/ppermute | solution.py:237
  676.2 60.5 %collective-permute-start.52 = (f32[128,3072]{1,0:T(8,128)S(1)}, f32[128,3072]{1,0:T(8,128)S(1)}, u32[]{:S(2)}, u32[]{:S(2)}) collective-permute-start(f32[128,3072]{1,0:T(8,128)S(1)} %fusion.214), channel_id=1, source_target_pairs={{1,2},{2,1},{5,6},{6,5},{9,10},{10,9},{13,14},{14,13},{17,18},{18,... | collective-permute-start | bytes 4718600 | tf_op jit(solution)/shard_map/ppermute | solution.py:236
  713.3 23.3 %collective-permute-start.40 = (f32[128,128]{1,0:T(8,128)S(1)}, f32[128,128]{1,0:T(8,128)S(1)}, u32[]{:S(2)}, u32[]{:S(2)}) collective-permute-start(f32[128,128]{1,0:T(8,128)S(1)} %get-tuple-element.175), channel_id=1, source_target_pairs={{0,28},{4,24},{8,20},{12,16},{16,12},{20,8},{24,4},{28,0},{1,29},{... | collective-permute-start | bytes 196616 | tf_op jit(solution)/shard_map/ppermute | solution.py:173
  737.0 96.6 %collective-permute-start.53 = (f32[128,3072]{1,0:T(8,128)S(1)}, f32[128,3072]{1,0:T(8,128)S(1)}, u32[]{:S(2)}, u32[]{:S(2)}) collective-permute-start(f32[128,3072]{1,0:T(8,128)S(1)} %add.679), channel_id=1, source_target_pairs={{1,0},{2,3},{5,4},{6,7},{9,8},{10,11},{13,12},{14,15},{17,16},{18,... | collective-permute-start | bytes 4718600 | tf_op jit(solution)/shard_map/ppermute | solution.py:237
  (132 other events, 1310.6 us)

commit v3 on v2

v3 whole, which is shorter than its diff:
```python
import itertools

import jax
import jax.numpy as jnp
from jax import lax
from jax.experimental import pallas as pl
from jax.experimental.pallas import tpu as pltpu
from jax.sharding import PartitionSpec as P

HEADS = 16
HEAD = 64
PAGE = 512
PAIR = 2 * HEAD

EPSILON = 1e-05
SQRT_HALF = 0.7071067811865476
INV_ROOT_TAU = 0.3989422804014327

wide = jnp.float32
narrow = jnp.bfloat16
LITTLE = pl.CostEstimate(flops=1024, bytes_accessed=1024, transcendentals=0)
ROOM = pltpu.CompilerParams(vmem_limit_bytes=48 * 2**20)


def shape(dims, dtype=wide):
    return jax.ShapeDtypeStruct(dims, dtype)


def whole(*dims):
    return pl.BlockSpec(dims, lambda *_: (0,) * len(dims))


def normalize(values):
    averaged = jnp.mean(values, -1, keepdims=True)
    centered = values - averaged
    inverse = lax.rsqrt(jnp.mean(centered * centered, -1, keepdims=True) + EPSILON)
    return centered * inverse, inverse


def norm_back(incoming, normed, inverse, gain):
    scaled = incoming * gain
    offset_mean = jnp.mean(scaled, -1, keepdims=True)
    along_mean = jnp.mean(scaled * normed, -1, keepdims=True)
    return inverse * (scaled - offset_mean - normed * along_mean)


def down(values):
    return jnp.sum(values, 0, keepdims=True)


def mul(left, right):
    return jnp.dot(left, right, preferred_element_type=wide)


def mul_rows(left, right):
    return lax.dot_general(left, right, (((1,), (1,)), ((), ())), preferred_element_type=wide)


def mul_down(left, right):
    return lax.dot_general(left, right, (((0,), (0,)), ((), ())), preferred_element_type=wide)


def table_indices(box_rows, table):
    left_x, top_y, right_x, bottom_y = box_rows[0], box_rows[1], box_rows[2], box_rows[3]
    first = jnp.where(
        table == 0,
        left_x,
        jnp.where(table == 1, top_y, jnp.where(table == 2, right_x - left_x, bottom_y - top_y)),
    )
    second = jnp.where(table == 0, right_x, jnp.where(table == 1, bottom_y, -1))
    return first, second


def two_halves(values):
    high = values.astype(narrow)
    return high, (values - high.astype(wide)).astype(narrow)


def hits(entry, indices):
    return jnp.where(entry == indices, 1.0, 0.0)


def lookup_kernel(idx_ref, table_ref, total_ref, out_ref, halves):
    width = table_ref.shape[1]

    @pl.when(pl.program_id(0) == 0)
    def _():
        halves[:, :width], halves[:, width:] = two_halves(table_ref[...])

    entry = lax.broadcasted_iota(jnp.int32, (idx_ref.shape[0], table_ref.shape[0]), 1)
    counts = hits(entry, idx_ref[:, 0:1]) + hits(entry, idx_ref[:, 1:2])
    rows = mul(counts.astype(narrow), halves[...])
    out_ref[...] = total_ref[...] + rows[:, :width] + rows[:, width:]


def add_rows(indices, table, total):
    tokens = total.shape[0]
    entries, width = table.shape
    return pl.pallas_call(
        lookup_kernel,
        grid=(tokens // PAGE,),
        in_specs=[
            pl.BlockSpec((PAGE, 2), lambda step: (step, 0)),
            whole(entries, width),
            pl.BlockSpec((PAGE, width), lambda step: (step, 0)),
        ],
        out_specs=pl.BlockSpec((PAGE, width), lambda step: (step, 0)),
        out_shape=shape((tokens, width)),
        scratch_shapes=[pltpu.VMEM((entries, 2 * width), narrow)],
        input_output_aliases={2: 0},
        compiler_params=ROOM,
        cost_estimate=LITTLE,
        name="look_up",
    )(indices, table, total)


def spread_kernel(idx_ref, rows_ref, out_ref):
    width = rows_ref.shape[1]
    entry = lax.broadcasted_iota(jnp.int32, (out_ref.shape[0], rows_ref.shape[0]), 0)
    counts = hits(entry, idx_ref[0:1, :]) + hits(entry, idx_ref[1:2, :])
    both = mul(counts.astype(narrow), jnp.concatenate(two_halves(rows_ref[...]), 1))
    share = both[:, :width] + both[:, width:]

    @pl.when(pl.program_id(0) == 0)
    def _():
        out_ref[...] = share

    @pl.when(pl.program_id(0) > 0)
    def _():
        out_ref[...] += share


def spread_rows(indices, rows, entries):
    tokens, width = rows.shape
    block = 2 * PAGE
    return pl.pallas_call(
        spread_kernel,
        grid=(tokens // block,),
        in_specs=[
            pl.BlockSpec((2, block), lambda step: (0, step)),
            pl.BlockSpec((block, width), lambda step: (step, 0)),
        ],
        out_specs=whole(entries, width),
        out_shape=shape((entries, width)),
        compiler_params=ROOM,
        cost_estimate=LITTLE,
        name="spread",
    )(indices, rows)


def project_kernel(
    inner_ref, *refs
):
    group = len(refs) - 9
    parts = refs[:group]
    text, gain, bias, weight, weight_bias, packed, normed, inverse, low = refs[group:]
    width = parts[0].shape[1]

    @pl.when(pl.program_id(0) == 0)
    def _():
        for offset in range(group):
            place = pl.multiple_of(jnp.bitwise_xor(inner_ref[0], offset) * width, width)
            normed[:, pl.ds(place, width)] = parts[offset][...]
        normed[...], inverse[...] = normalize(normed[...] + text[...].astype(wide))
        low[...] = (normed[...] * gain[...] + bias[...]).astype(narrow)

    packed[...] = (mul(low[...], weight[...]) + weight_bias[...]).astype(narrow)


def embed_and_project(inner, parts, text, gain, bias, weight, weight_bias):
    tokens, width = text.shape
    block = width // 2
    steps = weight.shape[1] // block
    return pl.pallas_call(
        project_kernel,
        grid_spec=pltpu.PrefetchScalarGridSpec(
            num_scalar_prefetch=1,
            grid=(steps,),
            in_specs=[whole(*part.shape) for part in parts]
            + [
                whole(tokens, width),
                whole(1, width),
                whole(1, width),
                pl.BlockSpec((width, block), lambda step, *_: (0, step)),
                pl.BlockSpec((1, block), lambda step, *_: (0, step)),
            ],
            out_specs=[
                pl.BlockSpec((tokens, block), lambda step, *_: (0, step)),
                whole(tokens, width),
                whole(tokens, 1),
                whole(tokens, width),
            ],
        ),
        out_shape=[
            shape((tokens, weight.shape[1]), narrow),
            shape((tokens, width)),
            shape((tokens, 1)),
            shape((tokens, width), narrow),
        ],
        compiler_params=ROOM,
        cost_estimate=LITTLE,
        name="embed_and_project",
    )(inner, *parts, text, gain, bias, weight, weight_bias)


def one_head(rows, head):
    lane = lax.broadcasted_iota(jnp.int32, rows.shape, 1)
    return jnp.where((lane < HEAD) == (head == 0), rows, jnp.zeros_like(rows))


def head_probs(queries, keys, head):
    scores = mul_rows(one_head(queries, head), keys) * HEAD ** (-0.5)
    exponent = jnp.exp(scores - jnp.max(scores, -1, keepdims=True))
    return exponent * (1.0 / jnp.sum(exponent, -1, keepdims=True))


def attend_kernel(
    queries, keys, values, weight, weight_bias, normed_emb, emb_gain, emb_bias, gain, bias,
    context, normed, inverse, low, total,
):
    pair = pl.program_id(0)
    summed = None
    for head in range(2):
        probs = head_probs(queries[...], keys[...], head).astype(narrow)
        part = mul(probs, one_head(values[...], head))
        summed = part if summed is None else summed + part
    context[...] = summed.astype(narrow)
    share = mul(context[...], weight[...])

    @pl.when(pair == 0)
    def _():
        total[...] = share

    @pl.when(pair > 0)
    def _():
        total[...] += share

    @pl.when(pair == pl.num_programs(0) - 1)
    def _():
        hidden = normed_emb[...] * emb_gain[...] + emb_bias[...]
        normed[...], inverse[...] = normalize(hidden + (total[...] + weight_bias[...]))
        low[...] = (normed[...] * gain[...] + bias[...]).astype(narrow)


def attend(packed, weight, weight_bias, normed_emb, emb_gain, emb_bias, gain, bias):
    tokens, width = normed_emb.shape
    pairs = width // PAIR
    vector = whole(1, width)
    return pl.pallas_call(
        attend_kernel,
        grid=(pairs,),
        in_specs=[
            pl.BlockSpec((tokens, PAIR), lambda pair: (0, pair)),
            pl.BlockSpec((tokens, PAIR), lambda pair: (0, pairs + pair)),
            pl.BlockSpec((tokens, PAIR), lambda pair: (0, 2 * pairs + pair)),
            pl.BlockSpec((PAIR, width), lambda pair: (pair, 0)),
            vector,
            whole(tokens, width),
            vector,
            vector,
            vector,
            vector,
        ],
        out_specs=[
            pl.BlockSpec((tokens, PAIR), lambda pair: (0, pair)),
            whole(tokens, width),
            whole(tokens, 1),
            whole(tokens, width),
        ],
        out_shape=[
            shape((tokens, width), narrow),
            shape((tokens, width)),
            shape((tokens, 1)),
            shape((tokens, width), narrow),
        ],
        scratch_shapes=[pltpu.VMEM((tokens, width), wide)],
        compiler_params=ROOM,
        cost_estimate=LITTLE,
        name="attend",
    )(packed, packed, packed, weight, weight_bias, normed_emb, emb_gain, emb_bias, gain, bias)


def feed_kernel(
    low, w_in, b_in, w_back, b_back, normed_attn, attn_gain, attn_bias, gain, bias, cotangent,
    pre_act, expanded, output, d_r2, d_returned, g_gain, g_bias, g_back_bias, total,
):
    step = pl.program_id(0)
    pre = mul(low[...], w_in[...]) + b_in[...]
    pre_act[...] = pre
    expanded[...] = (pre * (0.5 * (1.0 + lax.erf(pre * SQRT_HALF)))).astype(narrow)
    share = mul(expanded[...], w_back[...])

    @pl.when(step == 0)
    def _():
        total[...] = share

    @pl.when(step > 0)
    def _():
        total[...] += share

    @pl.when(step == pl.num_programs(0) - 1)
    def _():
        hidden = normed_attn[...] * attn_gain[...] + attn_bias[...]
        normed, inverse = normalize(hidden + (total[...] + b_back[...]))
        output[...] = (normed * gain[...] + bias[...]).astype(narrow)
        incoming = cotangent[...].astype(wide)
        d_r2[...] = norm_back(incoming, normed, inverse, gain[...])
        g_gain[...] = down(incoming * normed)
        g_bias[...] = down(incoming)
        rounded = d_r2[...].astype(narrow)
        d_returned[...] = rounded
        g_back_bias[...] = down(rounded.astype(wide))


def feed(low, w_in, b_in, w_back, b_back, normed, attn_gain, attn_bias, gain, bias, cotangent):
    tokens, width = low.shape
    expand = w_in.shape[1]
    block = width // 2
    vector = whole(1, width)
    rows = whole(tokens, width)
    part = pl.BlockSpec((tokens, block), lambda step: (0, step))
    return pl.pallas_call(
        feed_kernel,
        grid=(expand // block,),
        in_specs=[
            rows,
            pl.BlockSpec((width, block), lambda step: (0, step)),
            pl.BlockSpec((1, block), lambda step: (0, step)),
            pl.BlockSpec((block, width), lambda step: (step, 0)),
            vector,
            rows,
            vector,
            vector,
            vector,
            vector,
            rows,
        ],
        out_specs=[part, part, rows, rows, rows, vector, vector, vector],
        out_shape=[
            shape((tokens, expand)),
            shape((tokens, expand), narrow),
            shape((tokens, width), narrow),
            shape((tokens, width)),
            shape((tokens, width), narrow),
            shape((1, width)),
            shape((1, width)),
            shape((1, width)),
        ],
        scratch_shapes=[pltpu.VMEM((tokens, width), wide)],
        compiler_params=ROOM,
        cost_estimate=LITTLE,
        name="feed",
    )(low, w_in, b_in, w_back, b_back, normed, attn_gain, attn_bias, gain, bias, cotangent)


def gelu_slope(pre_act):
    return (
        0.5 * (1.0 + lax.erf(pre_act * SQRT_HALF))
        + pre_act * jnp.exp(-0.5 * pre_act * pre_act) * INV_ROOT_TAU
    )


def feed_back_kernel(
    d_returned, w_back, pre_act, w_in, d_r2, normed, inverse, gain,
    d_pre, g_in_bias, d_r1, d_attended, g_gain, g_bias, g_out_bias, total,
):
    step = pl.program_id(0)
    rounded = (mul_rows(d_returned[...], w_back[...]) * gelu_slope(pre_act[...])).astype(narrow)
    d_pre[...] = rounded
    g_in_bias[...] = down(rounded.astype(wide))
    share = mul_rows(rounded, w_in[...])

    @pl.when(step == 0)
    def _():
        total[...] = share

    @pl.when(step > 0)
    def _():
        total[...] += share

    @pl.when(step == pl.num_programs(0) - 1)
    def _():
        incoming = d_r2[...] + total[...]
        d_r1[...] = norm_back(incoming, normed[...], inverse[...], gain[...])
        g_gain[...] = down(incoming * normed[...])
        g_bias[...] = down(incoming)
        d_attended[...] = d_r1[...].astype(narrow)
        g_out_bias[...] = down(d_attended[...].astype(wide))


def feed_back(d_returned, w_back, pre_act, w_in, d_r2, normed, inverse, gain):
    tokens, width = d_returned.shape
    expand = pre_act.shape[1]
    block = width // 2
    vector = whole(1, width)
    rows = whole(tokens, width)
    part = pl.BlockSpec((tokens, block), lambda step: (0, step))
    return pl.pallas_call(
        feed_back_kernel,
        grid=(expand // block,),
        in_specs=[
            rows,
            pl.BlockSpec((block, width), lambda step: (step, 0)),
            part,
            pl.BlockSpec((width, block), lambda step: (0, step)),
            rows,
            rows,
            whole(tokens, 1),
            vector,
        ],
        out_specs=[
            part,
            pl.BlockSpec((1, block), lambda step: (0, step)),
            rows,
            rows,
            vector,
            vector,
            vector,
        ],
        out_shape=[
            shape((tokens, expand), narrow),
            shape((1, expand)),
            shape((tokens, width)),
            shape((tokens, width), narrow),
            shape((1, width)),
            shape((1, width)),
            shape((1, width)),
        ],
        scratch_shapes=[pltpu.VMEM((tokens, width), wide)],
        compiler_params=ROOM,
        cost_estimate=LITTLE,
        name="feed_back",
    )(d_returned, w_back, pre_act, w_in, d_r2, normed, inverse, gain)


def attend_back_kernel(
    queries, keys, values, d_attended, weight, d_packed, g_query_bias, g_value_bias
):
    d_context = mul_rows(d_attended[...], weight[...]).astype(narrow)
    d_queries, d_keys, d_values = 0.0, 0.0, 0.0
    for head in range(2):
        probs = head_probs(queries[...], keys[...], head)
        own_context = one_head(d_context, head)
        d_values += mul_down(probs.astype(narrow), own_context)
        d_probs = mul_rows(own_context, values[...])
        along = jnp.sum(probs * d_probs, -1, keepdims=True)
        d_scores = (probs * (d_probs - along)).astype(narrow)
        d_queries += mul(d_scores, one_head(keys[...], head))
        d_keys += mul_down(d_scores, one_head(queries[...], head))
    d_queries = (d_queries * HEAD ** (-0.5)).astype(narrow)
    d_values = d_values.astype(narrow)
    d_packed[0] = d_queries
    d_packed[1] = (d_keys * HEAD ** (-0.5)).astype(narrow)
    d_packed[2] = d_values
    g_query_bias[...] = down(d_queries.astype(wide))
    g_value_bias[...] = down(d_values.astype(wide))


def attend_back(packed, d_attended, weight):
    tokens, width = d_attended.shape
    pairs = width // PAIR
    return pl.pallas_call(
        attend_back_kernel,
        grid=(pairs,),
        in_specs=[
            pl.BlockSpec((tokens, PAIR), lambda pair: (0, pair)),
            pl.BlockSpec((tokens, PAIR), lambda pair: (0, pairs + pair)),
            pl.BlockSpec((tokens, PAIR), lambda pair: (0, 2 * pairs + pair)),
            whole(tokens, width),
            pl.BlockSpec((PAIR, width), lambda pair: (pair, 0)),
        ],
        out_specs=[
            pl.BlockSpec((3, tokens, PAIR), lambda pair: (0, 0, pair)),
            pl.BlockSpec((1, PAIR), lambda pair: (0, pair)),
            pl.BlockSpec((1, PAIR), lambda pair: (0, pair)),
        ],
        out_shape=[shape((3, tokens, width), narrow), shape((1, width)), shape((1, width))],
        compiler_params=ROOM,
        cost_estimate=LITTLE,
        name="attend_back",
    )(packed, packed, packed, d_attended, weight)


def embed_back_kernel(inner_ref, d_packed, weight, d_r1, normed, inverse, gain, *refs):
    d_embed, g_gain, g_bias, squares = refs[:4]
    blocks, total = refs[4:-1], refs[-1]
    step = pl.program_id(0)
    share = mul_rows(d_packed[0], weight[...])

    @pl.when(step == 0)
    def _():
        total[...] = d_r1[...] + share

    @pl.when(step > 0)
    def _():
        total[...] += share

    @pl.when(step == pl.num_programs(0) - 1)
    def _():
        incoming = total[...]
        d_embed[...] = norm_back(incoming, normed[...], inverse[...], gain[...])
        g_gain[...] = down(incoming * normed[...])
        g_bias[...] = down(incoming)
        squares[...] = down(d_embed[...] * d_embed[...])
        columns = blocks[0].shape[1]
        for offset in range(len(blocks)):
            place = pl.multiple_of(jnp.bitwise_xor(inner_ref[0], offset) * columns, columns)
            blocks[offset][...] = d_embed[:, pl.ds(place, columns)]


def embed_back(inner, group, d_packed, weight, d_r1, normed, inverse, gain):
    tokens, width = d_r1.shape
    block = width // 2
    vector = whole(1, width)
    rows = whole(tokens, width)
    columns = width // group
    return pl.pallas_call(
        embed_back_kernel,
        grid_spec=pltpu.PrefetchScalarGridSpec(
            num_scalar_prefetch=1,
            grid=(3 * width // block,),
            in_specs=[
                pl.BlockSpec((1, tokens, block), lambda step, *_: (step // 2, 0, step % 2)),
                pl.BlockSpec((width, block), lambda step, *_: (0, step)),
                rows,
                rows,
                whole(tokens, 1),
                vector,
            ],
            out_specs=[rows, vector, vector, vector] + [whole(tokens, columns)] * group,
            scratch_shapes=[pltpu.VMEM((tokens, width), wide)],
        ),
        out_shape=[shape((tokens, width)), shape((1, width)), shape((1, width)), shape((1, width))]
        + [shape((tokens, columns))] * group,
        compiler_params=ROOM,
        cost_estimate=LITTLE,
        name="embed_back",
    )(inner, d_packed, weight, d_r1, normed, inverse, gain)


def outer_first_kernel(table_ref, *refs):
    half = len(refs) // 3
    for left, right, out in zip(refs[:half], refs[half : 2 * half], refs[2 * half :]):
        out[...] = mul(left[...], right[...].reshape(right.shape[-2:]))


def outer_next_kernel(table_ref, *refs):
    streams = len(refs) // 7
    for one in range(streams):
        right = refs[one][...]
        right = right.reshape(right.shape[-2:])
        for part in range(2):
            place = streams + 2 * one + part
            left, arrived, out = refs[place], refs[place + 2 * streams], refs[place + 4 * streams]
            out[...] = mul(left[...], right) + arrived[...]


class Shares:
    def __init__(self, me, streams):
        self.me, self.streams = me, streams
        self.devices = lax.axis_size("pages")
        self.tables = [
            jnp.bitwise_xor(me, jnp.array(flips_of(stream["masks"]), jnp.int32))
            * stream["units"]
            + stream["unit"]
            for stream in streams
        ]

    def right_spec(self, stream, splits):
        right, columns = stream["right"], stream["columns"] // splits
        first = stream["first"] * splits
        if right.ndim == 3:
            per = right.shape[2] // columns
            return pl.BlockSpec(
                (1, right.shape[1], columns),
                lambda row, col, *_: ((first + col) // per, 0, (first + col) % per),
            )
        return pl.BlockSpec((right.shape[0], columns), lambda row, col, *_: (0, first + col))

    def left_spec(self, stream, index, start):
        count = len(self.tables[0])
        return pl.BlockSpec(
            (stream["rows"], stream["left"].shape[1]),
            lambda row, col, table: (table[index * count + start + row], 0),
        )

    def first(self, splits=1):
        half = self.devices // 2
        streams = self.streams
        return pl.pallas_call(
            outer_first_kernel,
            grid_spec=pltpu.PrefetchScalarGridSpec(
                num_scalar_prefetch=1,
                grid=(half, splits),
                in_specs=[self.left_spec(one, i, half) for i, one in enumerate(streams)]
                + [self.right_spec(one, splits) for one in streams],
                out_specs=[
                    pl.BlockSpec(
                        (one["rows"], one["columns"] // splits), lambda row, col, *_: (row, col)
                    )
                    for one in streams
                ],
            ),
            out_shape=[shape((half * one["rows"], one["columns"])) for one in streams],
            compiler_params=ROOM,
            cost_estimate=LITTLE,
            name="outer_first",
        )(
            jnp.concatenate(self.tables),
            *[one["left"] for one in streams],
            *[one["right"] for one in streams],
        )

    def to_core(self, sent):
        self.arrived = [swap(one, 1) for one in sent]

    def next(self, splits=1):
        quarter = self.devices // 4
        streams = self.streams

        def block(one, start):
            return pl.BlockSpec(
                (one["rows"], one["columns"] // splits),
                lambda row, col, *_: (start + row, col),
            )

        results = pl.pallas_call(
            outer_next_kernel,
            grid_spec=pltpu.PrefetchScalarGridSpec(
                num_scalar_prefetch=1,
                grid=(quarter, splits),
                in_specs=[self.right_spec(one, splits) for one in streams]
                + [
                    self.left_spec(one, i, start)
                    for i, one in enumerate(streams)
                    for start in (0, quarter)
                ]
                + [block(one, start) for one in streams for start in (0, quarter)],
                out_specs=[block(one, 0) for one in streams for _ in range(2)],
            ),
            out_shape=[
                shape((quarter * one["rows"], one["columns"])) for one in streams for _ in range(2)
            ],
            compiler_params=ROOM,
            cost_estimate=LITTLE,
            name="outer_next",
        )(
            jnp.concatenate(self.tables),
            *[one["right"] for one in streams],
            *[one["left"] for one in streams for _ in range(2)],
            *[arrived for arrived in self.arrived for _ in range(2)],
        )
        self.kept = results[0::2]
        return results[1::2]

    def to_second(self, sent):
        self.arrived = [swap(one, s["masks"][1]) for one, s in zip(sent, self.streams)]

    def third(self):
        for step in range(2, len(self.streams[0]["masks"])):
            folded = [fold(kept, arrived) for kept, arrived in zip(self.kept, self.arrived)]
            self.kept = [one[0] for one in folded]
            sent = [one[1] for one in folded]
            if step == len(self.streams[0]["masks"]) - 1:
                return sent
            self.arrived = [swap(one, s["masks"][step]) for one, s in zip(sent, self.streams)]

    def to_last(self, sent):
        self.arrived = [swap(one, s["masks"][-1]) for one, s in zip(sent, self.streams)]

    def result(self):
        return [kept + arrived for kept, arrived in zip(self.kept, self.arrived)]


def flips_of(masks):
    return [
        sum(mask for mask, flip in zip(masks, flips) if flip)
        for flips in itertools.product((0, 1), repeat=len(masks))
    ]


def relative(array, offsets, me, size, axis):
    blocks = [
        lax.dynamic_slice_in_dim(array, jnp.bitwise_xor(me, offset) * size, size, axis)
        for offset in offsets
    ]
    return jnp.concatenate(blocks, axis)


def swap(array, mask):
    return lax.ppermute(
        array, "pages", [(one, one ^ mask) for one in range(lax.axis_size("pages"))]
    )


def fold(kept, arrived):
    half = kept.shape[0] // 2
    return kept[:half] + arrived[:half], kept[half:] + arrived[half:]


def halve(kept, masks):
    for mask in masks:
        half = kept.shape[0] // 2
        kept = kept[:half] + swap(kept[half:], mask)
    return kept


def in_order(*values):
    return lax.optimization_barrier(values)


def emb_total(share):
    if lax.axis_size("emb") != 4:
        return lax.psum(share, "emb")
    plane = lax.axis_index("emb")
    middle = jnp.logical_or(plane == 1, plane == 2)
    share = share + lax.ppermute(share, "emb", [(0, 1), (3, 2)])
    share = share + lax.ppermute(share, "emb", [(1, 2), (2, 1)])
    return jnp.where(middle, share, lax.ppermute(share, "emb", [(1, 0), (2, 3)]))


def on_device(
    text_embed,
    boxes,
    layout_tables,
    emb_gain,
    emb_bias,
    w_qkv,
    b_query,
    b_value,
    w_out,
    b_out,
    attn_gain,
    attn_bias,
    w_in,
    b_in,
    w_back,
    b_back,
    ffn_gain,
    ffn_bias,
    cotangent,
):
    token_rows = text_embed.shape[0]
    model_width = text_embed.shape[1]
    entries = layout_tables.shape[1]
    me = lax.axis_index("pages")
    plane = lax.axis_index("emb")
    devices = lax.axis_size("pages")
    planes = lax.axis_size("emb")
    outer_masks = [1 << bit for bit in range(1, devices.bit_length() - 1)]
    turn = len(outer_masks) // 2
    masks_one = [1] + outer_masks
    masks_two = [1] + outer_masks[turn:] + outer_masks[:turn]
    lanes = model_width // devices
    group = min(devices, 8)
    inner = me % group
    inner_list = inner.reshape(1).astype(jnp.int32)
    columns = model_width // group

    def row(vector):
        return vector.reshape(1, -1)

    def around(array, offset):
        return lax.ppermute(
            array, "emb", [((one + offset) % planes, one) for one in range(planes)]
        )

    def exchange(blocks):
        return [blocks[0]] + [swap(blocks[offset], offset) for offset in range(1, group)]

    own_columns = lax.dynamic_slice_in_dim(layout_tables[0], inner * columns, columns, 1)
    table_columns = [own_columns] + [around(own_columns, offset) for offset in range(1, planes)]
    group_boxes = lax.all_gather(
        boxes,
        "pages",
        axis=1,
        tiled=True,
        axis_index_groups=[
            list(range(first, first + group)) for first in range(0, devices, group)
        ],
    )
    group_boxes = relative(group_boxes, range(group), inner, token_rows, 1)
    table_uses = [
        jnp.stack(table_indices(group_boxes, (plane + offset) % planes))
        for offset in range(planes)
    ]
    looked_up = jnp.zeros((group * token_rows, columns), wide)
    for offset in [0, 1, planes - 1] + list(range(2, planes - 1)):
        looked_up = add_rows(table_uses[offset].T, table_columns[offset], looked_up)
    parts = exchange(
        [looked_up[one * token_rows : (one + 1) * token_rows] for one in range(group)]
    )

    bias_qkv = jnp.concatenate([b_query, jnp.zeros_like(b_query), b_value])
    packed, normed_emb, inverse_emb, emb_low = embed_and_project(
        inner_list, parts, text_embed, row(emb_gain), row(emb_bias), w_qkv, row(bias_qkv)
    )
    context_low, normed_attn, inverse_attn, attn_low = attend(
        packed,
        w_out,
        row(b_out),
        normed_emb,
        row(emb_gain),
        row(emb_bias),
        row(attn_gain),
        row(attn_bias),
    )
    pre_act, expanded, output, d_r2, d_returned, g_ffn_gain, g_ffn_bias, g_back_bias = feed(
        attn_low,
        w_in,
        row(b_in),
        w_back,
        row(b_back),
        normed_attn,
        row(attn_gain),
        row(attn_bias),
        row(ffn_gain),
        row(ffn_bias),
        cotangent,
    )

    def stream(left, right, masks, first=0, parts=1, units=1, unit=0):
        total = right.shape[-1] * (right.shape[0] if right.ndim == 3 else 1)
        return dict(
            left=left,
            rows=left.shape[0] // devices // units,
            units=units,
            unit=unit,
            right=right,
            columns=total // parts,
            first=first,
            masks=masks,
        )

    expanded_t = expanded.T
    back = Shares(
        me,
        [
            stream(expanded_t, d_returned, masks_one, units=2, unit=0),
            stream(expanded_t, d_returned, masks_two, units=2, unit=1),
        ],
    )
    sent = back.first()
    *sent, d_returned = in_order(*sent, d_returned)
    back.to_core(sent)
    d_pre, g_in_bias, d_r1, d_attended, g_attn_gain, g_attn_bias, g_out_bias = feed_back(
        d_returned, w_back, pre_act, w_in, d_r2, normed_attn, inverse_attn, row(attn_gain)
    )
    *back.arrived, d_pre = in_order(*back.arrived, d_pre)
    sent = back.next()
    *sent, d_pre = in_order(*sent, d_pre)
    back.to_second(sent)

    attn_t = attn_low.T
    inward = Shares(
        me,
        [
            stream(attn_t, d_pre, masks_one, 0, 2),
            stream(attn_t, d_pre, masks_two, 1, 2),
        ],
    )
    sent = inward.first()
    *sent, d_attended = in_order(*sent, d_attended)
    inward.to_core(sent)
    outward = Shares(
        me,
        [
            stream(context_low.T, d_attended, masks_one, 0, 2),
            stream(context_low.T, d_attended, masks_two, 1, 2),
        ],
    )
    sent = outward.first()
    *sent, d_attended = in_order(*sent, d_attended)
    outward.to_core(sent)
    *inward.arrived, d_attended = in_order(*inward.arrived, d_attended)
    sent = inward.next()
    *sent, d_attended = in_order(*sent, d_attended)
    inward.to_second(sent)

    d_packed, g_query_bias, g_value_bias = attend_back(packed, d_attended, w_out)

    *back.arrived, d_packed = in_order(*back.arrived, d_packed)
    sent = back.third()
    *sent, d_packed = in_order(*sent, d_packed)
    back.to_last(sent)
    *outward.arrived, d_packed = in_order(*outward.arrived, d_packed)
    sent = outward.next()
    *sent, d_packed = in_order(*sent, d_packed)
    outward.to_second(sent)

    emb_t = emb_low.T
    inmost = Shares(
        me,
        [
            stream(emb_t, d_packed, masks_one, 0, 2),
            stream(emb_t, d_packed, masks_two, 1, 2),
        ],
    )
    sent = inmost.first(3)
    *sent, d_packed = in_order(*sent, d_packed)
    inmost.to_core(sent)
    d_embed, g_emb_gain, g_emb_bias, squares, *embed_blocks = embed_back(
        inner_list, group, d_packed, w_qkv, d_r1, normed_emb, inverse_emb, row(emb_gain)
    )
    embed_columns = jnp.concatenate(exchange(embed_blocks), 0)

    *inward.arrived, embed_columns = in_order(*inward.arrived, embed_columns)
    sent = inward.third()
    *sent, embed_columns = in_order(*sent, embed_columns)
    inward.to_last(sent)
    *inmost.arrived, embed_columns = in_order(*inmost.arrived, embed_columns)
    sent = inmost.next(3)
    *sent, embed_columns = in_order(*sent, embed_columns)
    inmost.to_second(sent)
    back_share = jnp.concatenate(back.result(), 0)
    g_back = emb_total(back_share)

    table_total = None
    for offset in list(range(2, planes - 1)) + [1, planes - 1, 0]:
        part = spread_rows(table_uses[offset], embed_columns, entries)
        part = around(part, (planes - offset) % planes) if offset else part
        table_total = part if table_total is None else table_total + part
    row_masks = [mask for mask in masks_one if mask >= group]
    if row_masks:
        table_total = halve(
            relative(
                table_total,
                flips_of([mask // group for mask in row_masks]),
                me // group,
                entries * group // devices,
                0,
            ),
            row_masks,
        )
    table_parts = exchange(
        [relative(table_total, [offset], inner, entries // devices, 0) for offset in range(group)]
    )
    table_share = relative(jnp.concatenate(table_parts, 1), range(group), inner, columns, 1)

    outward.to_last(outward.third())
    g_in = emb_total(jnp.concatenate(inward.result(), 1))
    g_out = emb_total(jnp.concatenate(outward.result(), 1))
    inmost.to_last(inmost.third())
    g_qkv = emb_total(jnp.concatenate(inmost.result(), 1))

    vectors = [
        g_query_bias,
        g_value_bias,
        g_out_bias,
        g_attn_gain,
        g_attn_bias,
        g_in_bias,
        g_back_bias,
        g_ffn_gain,
        g_ffn_bias,
        g_emb_gain,
        g_emb_bias,
        jnp.full((devices,), jnp.sum(squares)),
    ]
    stacked = jnp.concatenate([vector.reshape(devices, -1) for vector in vectors], 1)
    vector_share = emb_total(
        halve(relative(stacked, flips_of(masks_one), me, 1, 0), masks_one)
    )[0]
    totals = []
    first = 0
    for vector in vectors:
        length = vector.size // devices
        totals.append(vector_share[first : first + length])
        first += length
    entry_count = token_rows * model_width * devices * planes
    rms_grad = jnp.sqrt(totals[11][0] / entry_count)
    return (
        output,
        d_embed,
        table_share[None],
        totals[9],
        totals[10],
        g_qkv,
        totals[0],
        totals[1],
        g_out,
        totals[2],
        totals[3],
        totals[4],
        g_in,
        totals[5],
        g_back,
        totals[6],
        totals[7],
        totals[8],
        rms_grad,
    )


def solution(mesh):
    return jax.shard_map(
        on_device,
        mesh=mesh,
        in_specs=(
            P(("pages", "emb"), None),
            P(None, ("pages", "emb")),
            P("emb", None, None),
            P(),
            P(),
            P(),
            P(),
            P(),
            P(),
            P(),
            P(),
            P(),
            P(),
            P(),
            P(),
            P(),
            P(),
            P(),
            P(("pages", "emb"), None),
        ),
        out_specs=(
            P(("pages", "emb"), None),
            P(("pages", "emb"), None),
            P("emb", "pages", None),
            P("pages"),
            P("pages"),
            P("pages", None),
            P("pages"),
            P("pages"),
            P("pages", None),
            P("pages"),
            P("pages"),
            P("pages"),
            P("pages", None),
            P("pages"),
            P("pages", None),
            P("pages"),
            P("pages"),
            P("pages"),
            P(),
        ),
        check_vma=False,
    )
```

time: 846 us -> 785 us (0.928)
  matrix products: 186 us -> 0 us
  Pallas kernels: 43.3 us -> 207 us
  other arithmetic: 70 us -> 40.3 us
    dot_general x38 -> x0, matrix products: 186 us -> none  [the longest x24 68.5 us: outer_sum(): jnp.einsum('ti,tj->ij', left, right, preferred_element_type=jnp.float32)]
    pallas_call x4 -> x18, Pallas kernels: 25.1 us -> 189 us  [the longest x4 28.6 us: first(): pl.pallas_call(outer_first_kernel, grid_spec=pltpu.PrefetchScalarGridSpec...]
    ppermute x5, waiting for transfers between devices: 72 us -> 23.3 us  [emb_total(): share = share + lax.ppermute(share, 'emb', [(0, 1), (3, 2)])]
    ppermute x48, waiting for transfers between devices: 139 us -> 181 us  [swap(): lax.ppermute(array, 'pages', [(one, one ^ mask) for one in range(lax.axis...]
    ppermute x6, waiting for transfers between devices: 39.6 us -> 72.5 us  [around(): lax.ppermute(array, 'emb', [((one + offset) % planes, one) for one in ran...]
    reduce_sum x12 -> x1, other arithmetic: 30.2 us -> 0.61 us  [on_device(): jnp.sum(squares)]
    ppermute x5, waiting for transfers between devices: 127 us -> 104 us  [emb_total(): lax.ppermute(share, 'emb', [(1, 0), (2, 3)])]
    pallas_call x0 -> x5, local copies, waits for them, and re-layouts: none -> 11.8 us  [the longest x1 6.49 us: feed(): pl.pallas_call(feed_kernel, grid=(expand // block,), in_specs=[rows, pl.B...]
  transfers between devices with their start and end apart: 69 -> 69, of which waited for: 31 -> 30; matrix products, arithmetic and copies ran while one was open for 20% -> 7% of each run, Pallas kernels for 4% -> 13%
where the time goes in v3:
time: 785 us; the launch traced here: 774 us
  waiting for transfers between devices  380 us (48%)
  Pallas kernels  207 us (26%)
  starting transfers between devices  83.6 us (11%)
  local copies, waits for them, and re-layouts  49 us (6%)
  other arithmetic  40.3 us (5%)
  blocking collectives  9.37 us (1%)
    ppermute x48, waiting for transfers between devices, swap(): lax.ppermute(array, 'pages', [(one, one ^ mask) for one in range(lax.axis...  181 us
    ppermute x5, waiting for transfers between devices, emb_total(): lax.ppermute(share, 'emb', [(1, 0), (2, 3)])  104 us
    ppermute x6, waiting for transfers between devices, around(): lax.ppermute(array, 'emb', [((one + offset) % planes, one) for one in ran...  72.5 us
    ppermute x48, starting transfers between devices, swap(): lax.ppermute(array, 'pages', [(one, one ^ mask) for one in range(lax.axis...  35.9 us
    pallas_call x4, Pallas kernels, first(): pl.pallas_call(outer_first_kernel, grid_spec=pltpu.PrefetchScalarGridSpec...  28.6 us
    pallas_call x4, Pallas kernels, next(): pl.pallas_call(outer_next_kernel, grid_spec=pltpu.PrefetchScalarGridSpec(...  27.6 us
    pallas_call x4, Pallas kernels, add_rows(): pl.pallas_call(lookup_kernel, grid=(tokens // PAGE,), in_specs=[pl.BlockS...  25 us
    unnamed x194, local copies, waits for them, and re-layouts  24.1 us
  transfers between devices with their start and end apart: 69, of which 30 were waited for; matrix products, arithmetic and copies ran while one was open for 7% of the time, Pallas kernels for 13%

profile of v3, /device:TPU:0, one launch (start us, length us, event | category | flops | bytes accessed | tf_op | source)
XLA Modules:
  0.0 773.7 jit_solution(11084796171984626036)
XLA Ops:
  1.8 5.1 collective-permute-start.2
  7.9 9.4 %all_gather.3 = s32[4,4096]{1,0:T(4,128)S(1)} all-gather(s32[4,512]{1,0:T(4,128)} %param.28), channel_id=1, replica_groups={{0,4,8,12,16,20,24,28},{1,5,9,13,17,21,25,29},{2,6,10,14,18,22,26,30},{..., dimensions={1}, use_global_device_ids=true | all-gather | bytes 73728 | tf_op jit(solution)/shard_map/all_gather | solution.py:773
  21.2 5.6 look_up.4.total_ref
  34.5 6.9 look_up.5.total_ref
  41.4 6.9 look_up.6.total_ref
  48.3 3.4 collective-permute-done.table_ref
  51.6 5.6 look_up.7
  68.2 3.3 collective-permute-done.5.refs_3_
  71.5 12.8 %collective-permute-done.7.refs_5_ = f32[512,128]{1,0:T(8,128)S(1)} collective-permute-done((f32[512,128]{1,0:T(8,128)S(1)}, f32[512,128]{1,0:T(8,128)S(1)}, u32[]{:S(2)}, u32[]{:S(2)}) %collective-permute-start.7) | collective-permute-done | bytes 262176 | tf_op jit(solution)/shard_map/ppermute | solution.py:691
  84.4 9.6 %embed_and_project.1 = (bf16[512,3072]{1,0:T(8,128)(2,1)}, f32[512,1024]{1,0:T(8,128)}, f32[512,1]{1,0:T(8,128)S(1)}, bf16[512,1024]{1,0:T(8,128)(2,1)S(1)}) custom-call(s32[1]{0:T(128)} %bitcast.inner_ref, f32[512,128]{1,0:T(8,128)S(1)} %get-tuple-element.249.refs_0_, f32[512,128]{1,0:T(8,128)S(1)} %collective-permute-done.3.refs_1_, ...), custom_call_target="tpu_custom_call" | custom-call | flops 1024 | bytes 1024 | tf_op jit(solution)/shard_map/embed_and_project/pallas_call | solution.py:174
  95.1 20.2 %attend.1 = (bf16[512,1024]{1,0:T(8,128)(2,1)S(1)}, f32[512,1024]{1,0:T(8,128)S(1)}, f32[512,1]{1,0:T(8,128)S(1)}, bf16[512,1024]{1,0:T(8,128)(2,1)S(1)}) custom-call(bf16[512,3072]{1,0:T(8,128)(2,1)} %get-tuple-element.129.queries.keys.values, bf16[512,3072]{1,0:T(8,128)(2,1)} %get-tuple-element.129.queries.keys.values, ...), custom_call_target="tpu_custom_call" | custom-call | flops 1024 | bytes 1024 | tf_op jit(solution)/shard_map/attend/pallas_call | solution.py:249
  117.7 20.7 %feed.1 = (f32[512,4096]{1,0:T(8,128)}, bf16[512,4096]{1,0:T(8,128)(2,1)}, bf16[512,1024]{1,0:T(8,128)(2,1)}, f32[512,1024]{1,0:T(8,128)S(1)}, bf16[512,1024]{1,...) custom-call(bf16[512,1024]{1,0:T(8,128)(2,1)S(1)} %get-tuple-element.131.low, ...), custom_call_target="tpu_custom_call" | custom-call | flops 1024 | bytes 1024 | tf_op jit(solution)/shard_map/feed/pallas_call | solution.py:322
  139.7 6.5 copy.56
  146.2 6.5 outer_first.4
  153.3 20.9 %feed_back.1 = (bf16[512,4096]{1,0:T(8,128)(2,1)}, f32[1,4096]{1,0:T(1,128)S(1)}, f32[512,1024]{1,0:T(8,128)S(1)}, bf16[512,1024]{1,0:T(8,128)(2,1)S(1)}, f32[1,...) custom-call(bf16[512,1024]{1,0:T(8,128)(2,1)S(1)} %get-tuple-element.141.refs_2_.refs_3_.d_returned.refs_0_.refs_1_, ...), custom_call_target="tpu_custom_call" | custom-call | flops 1024 | bytes 1024 | tf_op jit(solution)/shard_map/feed_back/pallas_call | solution.py:398
  180.4 7.1 outer_next.4
  188.9 7.1 outer_first.5
  210.0 8.5 %outer_next.5 = (f32[256,2048]{1,0:T(8,128)S(1)}, f32[256,2048]{1,0:T(8,128)S(1)}, f32[256,2048]{1,0:T(8,128)}, f32[256,2048]{1,0:T(8,128)}) custom-call(s32[16]{0:T(128)S(1)} %pad_add_fusion.4.table_ref, bf16[512,4096]{1,0:T(8,128)(2,1)} %get-tuple-element.151.refs_2_.refs_3_.refs_0_.refs_1_, ...), custom_call_target="tpu_custom_call" | custom-call | flops 1024 | bytes 1024 | tf_op jit(solution)/shard_map/outer_next/pallas_call | solution.py:627
  218.5 23.9 %attend_back.1 = (bf16[3,512,1024]{2,1,0:T(8,128)(2,1)}, f32[1,1024]{1,0:T(1,128)S(1)}, f32[1,1024]{1,0:T(1,128)S(1)}) custom-call(bf16[512,3072]{1,0:T(8,128)(2,1)} %get-tuple-element.129.queries.keys.values, bf16[512,3072]{1,0:T(8,128)(2,1)} %get-tuple-element.129.queries.keys.values, bf16[512,3072]{1,0:T(8,128)(2,1)} %get-tuple-element.129.queries.keys.values, ...), custom_call_target="tpu_custom_call" | custom-call | flops 1024 | bytes 1024 | tf_op jit(solution)/shard_map/attend_back/pallas_call | solution.py:462
  256.5 12.0 %outer_first.7 = (f32[512,1536]{1,0:T(8,128)S(1)}, f32[512,1536]{1,0:T(8,128)}) custom-call(s32[16]{0:T(128)S(1)} %pad_add_fusion.4.table_ref, bf16[1024,512]{1,0:T(8,128)(2,1)S(1)} %bitcast.58, bf16[1024,512]{1,0:T(8,128)(2,1)S(1)} %bitcast.59, bf16[3,512,1024]{2,1,0:T(8,128)(2,1)} %get-tuple-element.187.refs_2_.refs_3_.d_packed.refs_0_.refs_1_, ...), custom_call_target="tpu_custom_call" | custom-call | flops 1024 | bytes 1024 | tf_op jit(solution)/shard_map/outer_first/pallas_call | solution.py:590
  270.2 12.0 %embed_back.1 = (f32[512,1024]{1,0:T(8,128)}, f32[1,1024]{1,0:T(1,128)S(1)}, f32[1,1024]{1,0:T(1,128)S(1)}, f32[1,1024]{1,0:T(1,128)S(1)}, f32[512,128]{1,0:T(8,...) custom-call(s32[1]{0:T(128)} %bitcast.inner_ref, ...), custom_call_target="tpu_custom_call" | custom-call | flops 1024 | bytes 1024 | tf_op jit(solution)/shard_map/embed_back/pallas_call | solution.py:517
  295.3 7.9 %collective-permute-start.42 = (f32[1,1793]{1,0:T(1,128)S(1)}, f32[1,1793]{1,0:T(1,128)S(1)}, u32[]{:S(2)}, u32[]{:S(2)}) collective-permute-start(f32[1,1793]{1,0:T(1,128)S(1)} %slice_add_fusion.13), channel_id=1, source_target_pairs={{0,1},{3,2},{4,5},{7,6},{8,9},{11,10},{12,13},{15,14},{16,17},{19,... | collective-permute-start | bytes 21524 | tf_op jit(solution)/shard_map/ppermute | solution.py:717
  309.3 46.6 %collective-permute-done.24 = f32[512,128]{1,0:T(8,128)S(1)} collective-permute-done((f32[512,128]{1,0:T(8,128)}, f32[512,128]{1,0:T(8,128)S(1)}, u32[]{:S(2)}, u32[]{:S(2)}) %collective-permute-start.24) | collective-permute-done | bytes 262176 | tf_op jit(solution)/shard_map/ppermute | solution.py:691
  359.4 6.4 collective-permute-done.26
  369.8 6.2 collective-permute-done.27
  375.9 5.0 collective-permute-done.28
  381.1 7.1 collective-permute-done.54
  388.8 7.0 collective-permute-done.53
  396.4 6.0 collective-permute-done.55
  409.6 15.9 %collective-permute-done.64 = f32[256,1024]{1,0:T(8,128)S(1)} collective-permute-done((f32[256,1024]{1,0:T(8,128)S(1)}, f32[256,1024]{1,0:T(8,128)S(1)}, u32[]{:S(2)}, u32[]{:S(2)}) %collective-permute-start.64) | collective-permute-done | bytes 1048608 | tf_op jit(solution)/shard_map/ppermute | solution.py:691
  434.1 4.7 collective-permute-start.66
  442.0 8.7 %outer_next.7 = (f32[256,1536]{1,0:T(8,128)S(1)}, f32[256,1536]{1,0:T(8,128)S(1)}, f32[256,1536]{1,0:T(8,128)S(1)}, f32[256,1536]{1,0:T(8,128)}) custom-call(s32[16]{0:T(128)S(1)} %pad_add_fusion.4.table_ref, bf16[3,512,1024]{2,1,0:T(8,128)(2,1)} %get-tuple-element.187.refs_2_.refs_3_.d_packed.refs_0_.refs_1_, ...), custom_call_target="tpu_custom_call" | custom-call | flops 1024 | bytes 1024 | tf_op jit(solution)/shard_map/outer_next/pallas_call | solution.py:627
  450.7 4.5 spread.5
  461.2 25.2 %collective-permute-done.45 = f32[256,1536]{1,0:T(8,128)S(1)} collective-permute-done((f32[256,1536]{1,0:T(8,128)S(1)}, f32[256,1536]{1,0:T(8,128)S(1)}, u32[]{:S(2)}, u32[]{:S(2)}) %collective-permute-start.45) | collective-permute-done | bytes 1572896 | tf_op jit(solution)/shard_map/ppermute | solution.py:691
  488.8 3.7 collective-permute-done.47
  497.0 9.4 %collective-permute-done.46 = f32[128,1536]{1,0:T(8,128)S(1)} collective-permute-done((f32[128,1536]{1,0:T(8,128)S(1)}, f32[128,1536]{1,0:T(8,128)S(1)}, u32[]{:S(2)}, u32[]{:S(2)}) %collective-permute-start.46) | collective-permute-done | bytes 786464 | tf_op jit(solution)/shard_map/ppermute | solution.py:691
  512.1 22.6 %collective-permute-done.61 = f32[128,4096]{1,0:T(8,128)S(1)} collective-permute-done((f32[128,4096]{1,0:T(8,128)S(1)}, f32[128,4096]{1,0:T(8,128)S(1)}, u32[]{:S(2)}, u32[]{:S(2)}) %collective-permute-start.61) | collective-permute-done | bytes 2097184 | tf_op jit(solution)/shard_map/ppermute | solution.py:717
  534.7 5.5 collective-permute-start.49
  544.4 4.5 spread.4
  549.0 4.6 spread.6
  559.9 4.6 spread.7
  564.5 69.1 %collective-permute-done.29 = f32[1024,128]{1,0:T(8,128)S(1)} collective-permute-done((f32[1024,128]{1,0:T(8,128)S(1)}, f32[1024,128]{1,0:T(8,128)S(1)}, u32[]{:S(2)}, u32[]{:S(2)}) %collective-permute-start.29) | collective-permute-done | bytes 524320 | tf_op jit(solution)/shard_map/ppermute | solution.py:764
  649.3 4.4 collective-permute-done.33
  654.6 4.0 collective-permute-done.35
  659.0 5.0 collective-permute-done.37
  665.7 27.2 %collective-permute-done.68 = f32[512,1024]{1,0:T(8,128)S(1)} collective-permute-done((f32[512,1024]{1,0:T(8,128)S(1)}, f32[512,1024]{1,0:T(8,128)S(1)}, u32[]{:S(2)}, u32[]{:S(2)}) %collective-permute-start.68) | collective-permute-done | bytes 2097184 | tf_op jit(solution)/shard_map/ppermute | solution.py:719
  694.6 43.2 %collective-permute-done.63 = f32[128,4096]{1,0:T(8,128)S(1)} collective-permute-done((f32[128,4096]{1,0:T(8,128)S(1)}, f32[128,4096]{1,0:T(8,128)S(1)}, u32[]{:S(2)}, u32[]{:S(2)}) %collective-permute-start.63) | collective-permute-done | bytes 2097184 | tf_op jit(solution)/shard_map/ppermute | solution.py:719
  739.4 31.7 %collective-permute-done.51 = f32[128,3072]{1,0:T(8,128)S(1)} collective-permute-done((f32[128,3072]{1,0:T(8,128)S(1)}, f32[128,3072]{1,0:T(8,128)S(1)}, u32[]{:S(2)}, u32[]{:S(2)}) %collective-permute-start.51) | collective-permute-done | bytes 1572896 | tf_op jit(solution)/shard_map/ppermute | solution.py:719
  (384 shorter events, 164.7 us)
Async XLA Ops:
  1.8 31.1 %collective-permute-start.2 = (f32[1024,128]{1,0:T(8,128)S(1)}, f32[1024,128]{1,0:T(8,128)}, u32[]{:S(2)}, u32[]{:S(2)}) collective-permute-start(f32[1024,128]{1,0:T(8,128)S(1)} %dynamic-slice_bitcast_fusion.table_ref), channel_id=1, source_target_pairs={{1,0},{2,1},{3,2},{0,3},{5,4},{6,5},{7,6},{4,7},{9,8},{10,9},{11,1... | collective-permute-start | bytes 1572872 | tf_op jit(solution)/shard_map/ppermute | solution.py:764
  6.9 34.5 %collective-permute-start.1 = (f32[1024,128]{1,0:T(8,128)S(1)}, f32[1024,128]{1,0:T(8,128)}, u32[]{:S(2)}, u32[]{:S(2)}) collective-permute-start(f32[1024,128]{1,0:T(8,128)S(1)} %dynamic-slice_bitcast_fusion.table_ref), channel_id=1, source_target_pairs={{3,0},{0,1},{1,2},{2,3},{7,4},{4,5},{5,6},{6,7},{11,8},{8,9},{9,10... | collective-permute-start | bytes 1572872 | tf_op jit(solution)/shard_map/ppermute | solution.py:764
  6.9 44.8 %collective-permute-start = (f32[1024,128]{1,0:T(8,128)S(1)}, f32[1024,128]{1,0:T(8,128)S(1)}, u32[]{:S(2)}, u32[]{:S(2)}) collective-permute-start(f32[1024,128]{1,0:T(8,128)S(1)} %dynamic-slice_bitcast_fusion.table_ref), channel_id=1, source_target_pairs={{2,0},{3,1},{0,2},{1,3},{6,4},{7,5},{4,6},{5,7},{10,8},{11,9},{8,1... | collective-permute-start | bytes 1572872 | tf_op jit(solution)/shard_map/ppermute | solution.py:764
  61.0 23.3 %collective-permute-start.7 = (f32[512,128]{1,0:T(8,128)S(1)}, f32[512,128]{1,0:T(8,128)S(1)}, u32[]{:S(2)}, u32[]{:S(2)}) collective-permute-start(f32[512,128]{1,0:T(8,128)S(1)} %get-tuple-element.244), channel_id=1, source_target_pairs={{0,20},{4,16},{8,28},{12,24},{16,4},{20,0},{24,12},{28,8},{1,21},{... | collective-permute-start | bytes 786440 | tf_op jit(solution)/shard_map/ppermute | solution.py:691
  61.2 23.1 %collective-permute-start.8 = (f32[512,128]{1,0:T(8,128)S(1)}, f32[512,128]{1,0:T(8,128)S(1)}, u32[]{:S(2)}, u32[]{:S(2)}) collective-permute-start(f32[512,128]{1,0:T(8,128)S(1)} %get-tuple-element.243), channel_id=1, source_target_pairs={{0,24},{4,28},{8,16},{12,20},{16,8},{20,12},{24,0},{28,4},{1,25},{... | collective-permute-start | bytes 786440 | tf_op jit(solution)/shard_map/ppermute | solution.py:691
  66.8 17.5 %collective-permute-start.9 = (f32[512,128]{1,0:T(8,128)S(1)}, f32[512,128]{1,0:T(8,128)S(1)}, u32[]{:S(2)}, u32[]{:S(2)}) collective-permute-start(f32[512,128]{1,0:T(8,128)S(1)} %get-tuple-element.242), channel_id=1, source_target_pairs={{0,28},{4,24},{8,20},{12,16},{16,12},{20,8},{24,4},{28,0},{1,29},{... | collective-permute-start | bytes 786440 | tf_op jit(solution)/shard_map/ppermute | solution.py:691
  152.7 27.0 %collective-permute-start.10 = (f32[1024,1024]{1,0:T(8,128)}, f32[1024,1024]{1,0:T(8,128)}, u32[]{:S(2)}, u32[]{:S(2)}) collective-permute-start(f32[1024,1024]{1,0:T(8,128)} %get-tuple-element.139), channel_id=1, source_target_pairs={{0,4},{4,0},{8,12},{12,8},{16,20},{20,16},{24,28},{28,24},{1,5},{5... | collective-permute-start | bytes 12582920 | tf_op jit(solution)/shard_map/ppermute | solution.py:691
  153.1 26.7 %collective-permute-start.11 = (f32[1024,1024]{1,0:T(8,128)}, f32[1024,1024]{1,0:T(8,128)}, u32[]{:S(2)}, u32[]{:S(2)}) collective-permute-start(f32[1024,1024]{1,0:T(8,128)} %get-tuple-element.140), channel_id=1, source_target_pairs={{0,4},{4,0},{8,12},{12,8},{16,20},{20,16},{24,28},{28,24},{1,5},{5... | collective-permute-start | bytes 12582920 | tf_op jit(solution)/shard_map/ppermute | solution.py:691
  196.4 13.6 %collective-permute-start.17 = (f32[512,2048]{1,0:T(8,128)}, f32[512,2048]{1,0:T(8,128)}, u32[]{:S(2)}, u32[]{:S(2)}) collective-permute-start(f32[512,2048]{1,0:T(8,128)} %get-tuple-element.165), channel_id=1, source_target_pairs={{0,4},{4,0},{8,12},{12,8},{16,20},{20,16},{24,28},{28,24},{1,5},{5... | collective-permute-start | bytes 12582920 | tf_op jit(solution)/shard_map/ppermute | solution.py:691
  196.5 48.2 %collective-permute-start.14 = (f32[512,1024]{1,0:T(8,128)}, f32[512,1024]{1,0:T(8,128)}, u32[]{:S(2)}, u32[]{:S(2)}) collective-permute-start(f32[512,1024]{1,0:T(8,128)} %get-tuple-element.162), channel_id=1, source_target_pairs={{0,8},{4,12},{8,0},{12,4},{16,24},{20,28},{24,16},{28,20},{1,9},{5... | collective-permute-start | bytes 6291464 | tf_op jit(solution)/shard_map/ppermute | solution.py:691
  198.1 47.9 %collective-permute-start.15 = (f32[512,1024]{1,0:T(8,128)}, f32[512,1024]{1,0:T(8,128)}, u32[]{:S(2)}, u32[]{:S(2)}) collective-permute-start(f32[512,1024]{1,0:T(8,128)} %get-tuple-element.163), channel_id=1, source_target_pairs={{0,16},{4,20},{8,24},{12,28},{16,0},{20,4},{24,8},{28,12},{1,17},{... | collective-permute-start | bytes 6291464 | tf_op jit(solution)/shard_map/ppermute | solution.py:691
  204.1 46.6 %collective-permute-start.12 = (f32[512,512]{1,0:T(8,128)}, f32[512,512]{1,0:T(8,128)}, u32[]{:S(2)}, u32[]{:S(2)}) collective-permute-start(f32[512,512]{1,0:T(8,128)} %get-tuple-element.159), channel_id=1, source_target_pairs={{0,4},{4,0},{8,12},{12,8},{16,20},{20,16},{24,28},{28,24},{1,5},{5... | collective-permute-start | bytes 3145736 | tf_op jit(solution)/shard_map/ppermute | solution.py:691
  204.1 46.6 %collective-permute-start.13 = (f32[512,512]{1,0:T(8,128)}, f32[512,512]{1,0:T(8,128)}, u32[]{:S(2)}, u32[]{:S(2)}) collective-permute-start(f32[512,512]{1,0:T(8,128)} %get-tuple-element.160), channel_id=1, source_target_pairs={{0,4},{4,0},{8,12},{12,8},{16,20},{20,16},{24,28},{28,24},{1,5},{5... | collective-permute-start | bytes 3145736 | tf_op jit(solution)/shard_map/ppermute | solution.py:691
  293.2 13.7 %collective-permute-start.22 = (f32[512,128]{1,0:T(8,128)S(1)}, f32[512,128]{1,0:T(8,128)S(1)}, u32[]{:S(2)}, u32[]{:S(2)}) collective-permute-start(f32[512,128]{1,0:T(8,128)S(1)} %get-tuple-element.197), channel_id=1, source_target_pairs={{0,4},{4,0},{8,12},{12,8},{16,20},{20,16},{24,28},{28,24},{1,5},{5... | collective-permute-start | bytes 786440 | tf_op jit(solution)/shard_map/ppermute | solution.py:691
  293.2 14.3 %collective-permute-start.23 = (f32[512,128]{1,0:T(8,128)S(1)}, f32[512,128]{1,0:T(8,128)S(1)}, u32[]{:S(2)}, u32[]{:S(2)}) collective-permute-start(f32[512,128]{1,0:T(8,128)S(1)} %get-tuple-element.198), channel_id=1, source_target_pairs={{0,8},{4,12},{8,0},{12,4},{16,24},{20,28},{24,16},{28,20},{1,9},{5... | collective-permute-start | bytes 786440 | tf_op jit(solution)/shard_map/ppermute | solution.py:691
  303.3 99.3 %collective-permute-start.20 = (f32[256,2048]{1,0:T(8,128)}, f32[256,2048]{1,0:T(8,128)S(1)}, u32[]{:S(2)}, u32[]{:S(2)}) collective-permute-start(f32[256,2048]{1,0:T(8,128)} %copy-done.48), channel_id=1, source_target_pairs={{0,8},{4,12},{8,0},{12,4},{16,24},{20,28},{24,16},{28,20},{1,9},{5... | collective-permute-start | bytes 6291464 | tf_op jit(solution)/shard_map/ppermute | solution.py:691
  305.3 99.1 %collective-permute-start.21 = (f32[256,2048]{1,0:T(8,128)}, f32[256,2048]{1,0:T(8,128)S(1)}, u32[]{:S(2)}, u32[]{:S(2)}) collective-permute-start(f32[256,2048]{1,0:T(8,128)} %get-tuple-element.195), channel_id=1, source_target_pairs={{0,16},{4,20},{8,24},{12,28},{16,0},{20,4},{24,8},{28,12},{1,17},{... | collective-permute-start | bytes 6291464 | tf_op jit(solution)/shard_map/ppermute | solution.py:691
  306.9 49.0 %collective-permute-start.24 = (f32[512,128]{1,0:T(8,128)}, f32[512,128]{1,0:T(8,128)S(1)}, u32[]{:S(2)}, u32[]{:S(2)}) collective-permute-start(f32[512,128]{1,0:T(8,128)} %get-tuple-element.199), channel_id=1, source_target_pairs={{0,12},{4,8},{8,4},{12,0},{16,28},{20,24},{24,20},{28,16},{1,13},{... | collective-permute-start | bytes 786440 | tf_op jit(solution)/shard_map/ppermute | solution.py:691
  306.9 51.8 %collective-permute-start.25 = (f32[512,128]{1,0:T(8,128)}, f32[512,128]{1,0:T(8,128)S(1)}, u32[]{:S(2)}, u32[]{:S(2)}) collective-permute-start(f32[512,128]{1,0:T(8,128)} %get-tuple-element.200), channel_id=1, source_target_pairs={{0,16},{4,20},{8,24},{12,28},{16,0},{20,4},{24,8},{28,12},{1,17},{... | collective-permute-start | bytes 786440 | tf_op jit(solution)/shard_map/ppermute | solution.py:691
  307.5 58.8 %collective-permute-start.52 = (f32[256,512]{1,0:T(8,128)}, f32[256,512]{1,0:T(8,128)S(1)}, u32[]{:S(2)}, u32[]{:S(2)}) collective-permute-start(f32[256,512]{1,0:T(8,128)} %get-tuple-element.232), channel_id=1, source_target_pairs={{0,8},{4,12},{8,0},{12,4},{16,24},{20,28},{24,16},{28,20},{1,9},{5... | collective-permute-start | bytes 1572872 | tf_op jit(solution)/shard_map/ppermute | solution.py:691
  358.7 29.5 %collective-permute-start.54 = (f32[256,512]{1,0:T(8,128)}, f32[256,512]{1,0:T(8,128)S(1)}, u32[]{:S(2)}, u32[]{:S(2)}) collective-permute-start(f32[256,512]{1,0:T(8,128)} %copy-done.49), channel_id=1, source_target_pairs={{0,16},{4,20},{8,24},{12,28},{16,0},{20,4},{24,8},{28,12},{1,17},{... | collective-permute-start | bytes 1572872 | tf_op jit(solution)/shard_map/ppermute | solution.py:691
  366.3 14.6 %collective-permute-start.28 = (f32[512,128]{1,0:T(8,128)S(1)}, f32[512,128]{1,0:T(8,128)S(1)}, u32[]{:S(2)}, u32[]{:S(2)}) collective-permute-start(f32[512,128]{1,0:T(8,128)S(1)} %copy-done.51), channel_id=1, source_target_pairs={{0,28},{4,24},{8,20},{12,16},{16,12},{20,8},{24,4},{28,0},{1,29},{... | collective-permute-start | bytes 786440 | tf_op jit(solution)/shard_map/ppermute | solution.py:691
  375.9 58.2 %collective-permute-start.18 = (f32[512,1536]{1,0:T(8,128)S(1)}, f32[512,1536]{1,0:T(8,128)S(1)}, u32[]{:S(2)}, u32[]{:S(2)}) collective-permute-start(f32[512,1536]{1,0:T(8,128)S(1)} %copy-done.47), channel_id=1, source_target_pairs={{0,4},{4,0},{8,12},{12,8},{16,20},{20,16},{24,28},{28,24},{1,5},{5... | collective-permute-start | bytes 9437192 | tf_op jit(solution)/shard_map/ppermute | solution.py:691
  381.0 57.8 %collective-permute-start.19 = (f32[512,1536]{1,0:T(8,128)}, f32[512,1536]{1,0:T(8,128)S(1)}, u32[]{:S(2)}, u32[]{:S(2)}) collective-permute-start(f32[512,1536]{1,0:T(8,128)} %get-tuple-element.192), channel_id=1, source_target_pairs={{0,4},{4,0},{8,12},{12,8},{16,20},{20,16},{24,28},{28,24},{1,5},{5... | collective-permute-start | bytes 9437192 | tf_op jit(solution)/shard_map/ppermute | solution.py:691
  402.4 23.1 %collective-permute-start.64 = (f32[256,1024]{1,0:T(8,128)S(1)}, f32[256,1024]{1,0:T(8,128)S(1)}, u32[]{:S(2)}, u32[]{:S(2)}) collective-permute-start(f32[256,1024]{1,0:T(8,128)S(1)} %copy-done.69), channel_id=1, source_target_pairs={{0,16},{4,20},{8,24},{12,28},{16,0},{20,4},{24,8},{28,12},{1,17},{... | collective-permute-start | bytes 3145736 | tf_op jit(solution)/shard_map/ppermute | solution.py:691
  402.6 24.5 %collective-permute-start.65 = (f32[256,1024]{1,0:T(8,128)S(1)}, f32[256,1024]{1,0:T(8,128)S(1)}, u32[]{:S(2)}, u32[]{:S(2)}) collective-permute-start(f32[256,1024]{1,0:T(8,128)S(1)} %copy-done.68), channel_id=1, source_target_pairs={{0,8},{4,12},{8,0},{12,4},{16,24},{20,28},{24,16},{28,20},{1,9},{5... | collective-permute-start | bytes 3145736 | tf_op jit(solution)/shard_map/ppermute | solution.py:691
  404.4 27.6 %collective-permute-start.56 = (f32[128,1024]{1,0:T(8,128)S(1)}, f32[128,1024]{1,0:T(8,128)S(1)}, u32[]{:S(2)}, u32[]{:S(2)}) collective-permute-start(f32[128,1024]{1,0:T(8,128)S(1)} %pad_maximum_fusion.3), channel_id=1, source_target_pairs={{0,1},{3,2},{4,5},{7,6},{8,9},{11,10},{12,13},{15,14},{16,17},{19,... | collective-permute-start | bytes 1572872 | tf_op jit(solution)/shard_map/ppermute | solution.py:717
  425.5 29.8 %collective-permute-start.59 = (f32[128,2048]{1,0:T(8,128)}, f32[128,2048]{1,0:T(8,128)}, u32[]{:S(2)}, u32[]{:S(2)}) collective-permute-start(f32[128,2048]{1,0:T(8,128)} %slice_add_fusion.1), channel_id=1, source_target_pairs={{0,16},{4,20},{8,24},{12,28},{16,0},{20,4},{24,8},{28,12},{1,17},{... | collective-permute-start | bytes 3145736 | tf_op jit(solution)/shard_map/ppermute | solution.py:691
  427.1 30.6 %collective-permute-start.60 = (f32[128,2048]{1,0:T(8,128)}, f32[128,2048]{1,0:T(8,128)}, u32[]{:S(2)}, u32[]{:S(2)}) collective-permute-start(f32[128,2048]{1,0:T(8,128)} %slice_add_fusion), channel_id=1, source_target_pairs={{0,8},{4,12},{8,0},{12,4},{16,24},{20,28},{24,16},{28,20},{1,9},{5... | collective-permute-start | bytes 3145736 | tf_op jit(solution)/shard_map/ppermute | solution.py:691
  432.0 109.8 %collective-permute-start.44 = (f32[1,1793]{1,0:T(1,128)S(1)}, f32[1,1793]{1,0:T(1,128)S(1)}, u32[]{:S(2)}, u32[]{:S(2)}) collective-permute-start(f32[1,1793]{1,0:T(1,128)S(1)} %add.273), channel_id=1, source_target_pairs={{1,0},{2,3},{5,4},{6,7},{9,8},{10,11},{13,12},{14,15},{17,16},{18,... | collective-permute-start | bytes 21524 | tf_op jit(solution)/shard_map/ppermute | solution.py:719
  434.1 60.3 %collective-permute-start.66 = (f32[512,1024]{1,0:T(8,128)}, f32[512,1024]{1,0:T(8,128)S(1)}, u32[]{:S(2)}, u32[]{:S(2)}) collective-permute-start(f32[512,1024]{1,0:T(8,128)} %pad_maximum_fusion.1), channel_id=1, source_target_pairs={{0,1},{3,2},{4,5},{7,6},{8,9},{11,10},{12,13},{15,14},{16,17},{19,... | collective-permute-start | bytes 6291464 | tf_op jit(solution)/shard_map/ppermute | solution.py:717
  440.5 113.0 %collective-permute-start.57 = (f32[128,1024]{1,0:T(8,128)}, f32[128,1024]{1,0:T(8,128)}, u32[]{:S(2)}, u32[]{:S(2)}) collective-permute-start(f32[128,1024]{1,0:T(8,128)} %fusion.8), channel_id=1, source_target_pairs={{1,2},{2,1},{5,6},{6,5},{9,10},{10,9},{13,14},{14,13},{17,18},{18,... | collective-permute-start | bytes 1572872 | tf_op jit(solution)/shard_map/ppermute | solution.py:718
  455.3 31.0 %collective-permute-start.45 = (f32[256,1536]{1,0:T(8,128)S(1)}, f32[256,1536]{1,0:T(8,128)S(1)}, u32[]{:S(2)}, u32[]{:S(2)}) collective-permute-start(f32[256,1536]{1,0:T(8,128)S(1)} %get-tuple-element.228), channel_id=1, source_target_pairs={{0,8},{4,12},{8,0},{12,4},{16,24},{20,28},{24,16},{28,20},{1,9},{5... | collective-permute-start | bytes 4718600 | tf_op jit(solution)/shard_map/ppermute | solution.py:691
  457.7 34.8 %collective-permute-start.47 = (f32[256,1536]{1,0:T(8,128)}, f32[256,1536]{1,0:T(8,128)S(1)}, u32[]{:S(2)}, u32[]{:S(2)}) collective-permute-start(f32[256,1536]{1,0:T(8,128)} %get-tuple-element.230), channel_id=1, source_target_pairs={{0,16},{4,20},{8,24},{12,28},{16,0},{20,4},{24,8},{28,12},{1,17},{... | collective-permute-start | bytes 4718600 | tf_op jit(solution)/shard_map/ppermute | solution.py:691
  486.3 48.3 %collective-permute-start.61 = (f32[128,4096]{1,0:T(8,128)S(1)}, f32[128,4096]{1,0:T(8,128)S(1)}, u32[]{:S(2)}, u32[]{:S(2)}) collective-permute-start(f32[128,4096]{1,0:T(8,128)S(1)} %pad_maximum_fusion), channel_id=1, source_target_pairs={{0,1},{3,2},{4,5},{7,6},{8,9},{11,10},{12,13},{15,14},{16,17},{19,... | collective-permute-start | bytes 6291464 | tf_op jit(solution)/shard_map/ppermute | solution.py:717
  492.6 13.8 %collective-permute-start.46 = (f32[128,1536]{1,0:T(8,128)S(1)}, f32[128,1536]{1,0:T(8,128)S(1)}, u32[]{:S(2)}, u32[]{:S(2)}) collective-permute-start(f32[128,1536]{1,0:T(8,128)S(1)} %slice_add_fusion.6), channel_id=1, source_target_pairs={{0,16},{4,20},{8,24},{12,28},{16,0},{20,4},{24,8},{28,12},{1,17},{... | collective-permute-start | bytes 2359304 | tf_op jit(solution)/shard_map/ppermute | solution.py:691
  494.4 14.1 %collective-permute-start.48 = (f32[128,1536]{1,0:T(8,128)S(1)}, f32[128,1536]{1,0:T(8,128)S(1)}, u32[]{:S(2)}, u32[]{:S(2)}) collective-permute-start(f32[128,1536]{1,0:T(8,128)S(1)} %slice_add_fusion.4), channel_id=1, source_target_pairs={{0,8},{4,12},{8,0},{12,4},{16,24},{20,28},{24,16},{28,20},{1,9},{5... | collective-permute-start | bytes 2359304 | tf_op jit(solution)/shard_map/ppermute | solution.py:691
  506.4 129.8 %collective-permute-start.67 = (f32[512,1024]{1,0:T(8,128)}, f32[512,1024]{1,0:T(8,128)}, u32[]{:S(2)}, u32[]{:S(2)}) collective-permute-start(f32[512,1024]{1,0:T(8,128)} %fusion.10), channel_id=1, source_target_pairs={{1,2},{2,1},{5,6},{6,5},{9,10},{10,9},{13,14},{14,13},{17,18},{18,... | collective-permute-start | bytes 6291464 | tf_op jit(solution)/shard_map/ppermute | solution.py:718
  508.6 45.1 %collective-permute-start.30 = (f32[1024,128]{1,0:T(8,128)S(1)}, f32[1024,128]{1,0:T(8,128)}, u32[]{:S(2)}, u32[]{:S(2)}) collective-permute-start(f32[1024,128]{1,0:T(8,128)S(1)} %spread.5), channel_id=1, source_target_pairs={{3,0},{0,1},{1,2},{2,3},{7,4},{4,5},{5,6},{6,7},{11,8},{8,9},{9,10... | collective-permute-start | bytes 1572872 | tf_op jit(solution)/shard_map/ppermute | solution.py:764
  534.7 105.5 %collective-permute-start.49 = (f32[128,3072]{1,0:T(8,128)}, f32[128,3072]{1,0:T(8,128)}, u32[]{:S(2)}, u32[]{:S(2)}) collective-permute-start(f32[128,3072]{1,0:T(8,128)} %pad_maximum_fusion.2), channel_id=1, source_target_pairs={{0,1},{3,2},{4,5},{7,6},{8,9},{11,10},{12,13},{15,14},{16,17},{19,... | collective-permute-start | bytes 4718600 | tf_op jit(solution)/shard_map/ppermute | solution.py:717
  542.4 100.2 %collective-permute-start.62 = (f32[128,4096]{1,0:T(8,128)}, f32[128,4096]{1,0:T(8,128)}, u32[]{:S(2)}, u32[]{:S(2)}) collective-permute-start(f32[128,4096]{1,0:T(8,128)} %fusion.11), channel_id=1, source_target_pairs={{1,2},{2,1},{5,6},{6,5},{9,10},{10,9},{13,14},{14,13},{17,18},{18,... | collective-permute-start | bytes 6291464 | tf_op jit(solution)/shard_map/ppermute | solution.py:718
  553.5 80.0 %collective-permute-start.29 = (f32[1024,128]{1,0:T(8,128)S(1)}, f32[1024,128]{1,0:T(8,128)S(1)}, u32[]{:S(2)}, u32[]{:S(2)}) collective-permute-start(f32[1024,128]{1,0:T(8,128)S(1)} %spread.4), channel_id=1, source_target_pairs={{2,0},{3,1},{0,2},{1,3},{6,4},{7,5},{4,6},{5,7},{10,8},{11,9},{8,1... | collective-permute-start | bytes 1572872 | tf_op jit(solution)/shard_map/ppermute | solution.py:764
  553.6 81.2 %collective-permute-start.31 = (f32[1024,128]{1,0:T(8,128)S(1)}, f32[1024,128]{1,0:T(8,128)S(1)}, u32[]{:S(2)}, u32[]{:S(2)}) collective-permute-start(f32[1024,128]{1,0:T(8,128)S(1)} %spread.6), channel_id=1, source_target_pairs={{1,0},{2,1},{3,2},{0,3},{5,4},{6,5},{7,6},{4,7},{9,8},{10,9},{11,1... | collective-permute-start | bytes 1572872 | tf_op jit(solution)/shard_map/ppermute | solution.py:764
  633.6 14.4 %collective-permute-start.58 = (f32[128,1024]{1,0:T(8,128)S(1)}, f32[128,1024]{1,0:T(8,128)S(1)}, u32[]{:S(2)}, u32[]{:S(2)}) collective-permute-start(f32[128,1024]{1,0:T(8,128)S(1)} %add.289), channel_id=1, source_target_pairs={{1,0},{2,3},{5,4},{6,7},{9,8},{10,11},{13,12},{14,15},{17,16},{18,... | collective-permute-start | bytes 1572872 | tf_op jit(solution)/shard_map/ppermute | solution.py:719
  638.9 54.0 %collective-permute-start.68 = (f32[512,1024]{1,0:T(8,128)S(1)}, f32[512,1024]{1,0:T(8,128)S(1)}, u32[]{:S(2)}, u32[]{:S(2)}) collective-permute-start(f32[512,1024]{1,0:T(8,128)S(1)} %add.301), channel_id=1, source_target_pairs={{1,0},{2,3},{5,4},{6,7},{9,8},{10,11},{13,12},{14,15},{17,16},{18,... | collective-permute-start | bytes 6291464 | tf_op jit(solution)/shard_map/ppermute | solution.py:719
  641.8 22.3 %collective-permute-start.50 = (f32[128,3072]{1,0:T(8,128)S(1)}, f32[128,3072]{1,0:T(8,128)S(1)}, u32[]{:S(2)}, u32[]{:S(2)}) collective-permute-start(f32[128,3072]{1,0:T(8,128)S(1)} %fusion.9), channel_id=1, source_target_pairs={{1,2},{2,1},{5,6},{6,5},{9,10},{10,9},{13,14},{14,13},{17,18},{18,... | collective-permute-start | bytes 4718600 | tf_op jit(solution)/shard_map/ppermute | solution.py:718
  645.1 92.7 %collective-permute-start.63 = (f32[128,4096]{1,0:T(8,128)S(1)}, f32[128,4096]{1,0:T(8,128)S(1)}, u32[]{:S(2)}, u32[]{:S(2)}) collective-permute-start(f32[128,4096]{1,0:T(8,128)S(1)} %add.295), channel_id=1, source_target_pairs={{1,0},{2,3},{5,4},{6,7},{9,8},{10,11},{13,12},{14,15},{17,16},{18,... | collective-permute-start | bytes 6291464 | tf_op jit(solution)/shard_map/ppermute | solution.py:719
  664.4 106.7 %collective-permute-start.51 = (f32[128,3072]{1,0:T(8,128)S(1)}, f32[128,3072]{1,0:T(8,128)S(1)}, u32[]{:S(2)}, u32[]{:S(2)}) collective-permute-start(f32[128,3072]{1,0:T(8,128)S(1)} %add.281), channel_id=1, source_target_pairs={{1,0},{2,3},{5,4},{6,7},{9,8},{10,11},{13,12},{14,15},{17,16},{18,... | collective-permute-start | bytes 4718600 | tf_op jit(solution)/shard_map/ppermute | solution.py:719
  (99 other events, 1354.2 us)

commit v4 on v3

--- a/solution.py
+++ b/solution.py
@@ -1,3 +1,4 @@
+import functools
 import itertools
 
 import jax
@@ -18,6 +19,49 @@
 
 wide = jnp.float32
 narrow = jnp.bfloat16
+ATTEND_PARTS = 4
+ORDER = (
+    "first back",
+    "feed all",
+    "first in",
+    "attend all",
+    "first q1",
+    "first q2",
+    "next in",
+    "embed all",
+    "next q1",
+    "fold in",
+    "finish back",
+    "spread 0",
+    "spread 1",
+    "spread 2",
+    "spread 3",
+    "fold q1",
+    "exchange back",
+    "finish in",
+    "next q2",
+    "tables 0",
+    "return back",
+    "finish q1",
+    "exchange in",
+    "fold q2",
+    "vector 0",
+    "tables 1",
+    "end back",
+    "return in",
+    "exchange q1",
+    "finish q2",
+    "vector 1",
+    "return q1",
+    "exchange q2",
+    "vector 2",
+    "end in",
+    "return q2",
+    "vector 3",
+    "end q1",
+    "end q2",
+    "vector 4",
+)
 LITTLE = pl.CostEstimate(flops=1024, bytes_accessed=1024, transcendentals=0)
 ROOM = pltpu.CompilerParams(vmem_limit_bytes=48 * 2**20)
 
@@ -149,48 +193,41 @@
 
 
 def project_kernel(
-    inner_ref, *refs
+    parts, text, gain, bias, weight, weight_bias, packed, normed, inverse, low
 ):
-    group = len(refs) - 9
-    parts = refs[:group]
-    text, gain, bias, weight, weight_bias, packed, normed, inverse, low = refs[group:]
-    width = parts[0].shape[1]
+    group, _, width = parts.shape
 
     @pl.when(pl.program_id(0) == 0)
     def _():
-        for offset in range(group):
-            place = pl.multiple_of(jnp.bitwise_xor(inner_ref[0], offset) * width, width)
-            normed[:, pl.ds(place, width)] = parts[offset][...]
+        for one in range(group):
+            normed[:, one * width : (one + 1) * width] = parts[one]
         normed[...], inverse[...] = normalize(normed[...] + text[...].astype(wide))
         low[...] = (normed[...] * gain[...] + bias[...]).astype(narrow)
 
     packed[...] = (mul(low[...], weight[...]) + weight_bias[...]).astype(narrow)
 
 
-def embed_and_project(inner, parts, text, gain, bias, weight, weight_bias):
+def embed_and_project(parts, text, gain, bias, weight, weight_bias):
     tokens, width = text.shape
     block = width // 2
     steps = weight.shape[1] // block
     return pl.pallas_call(
         project_kernel,
-        grid_spec=pltpu.PrefetchScalarGridSpec(
-            num_scalar_prefetch=1,
-            grid=(steps,),
-            in_specs=[whole(*part.shape) for part in parts]
-            + [
-                whole(tokens, width),
-                whole(1, width),
-                whole(1, width),
-                pl.BlockSpec((width, block), lambda step, *_: (0, step)),
-                pl.BlockSpec((1, block), lambda step, *_: (0, step)),
-            ],
-            out_specs=[
-                pl.BlockSpec((tokens, block), lambda step, *_: (0, step)),
-                whole(tokens, width),
-                whole(tokens, 1),
-                whole(tokens, width),
-            ],
-        ),
+        grid=(steps,),
+        in_specs=[
+            whole(*parts.shape),
+            whole(tokens, width),
+            whole(1, width),
+            whole(1, width),
+            pl.BlockSpec((width, block), lambda step: (0, step)),
+            pl.BlockSpec((1, block), lambda step: (0, step)),
+        ],
+        out_specs=[
+            pl.BlockSpec((tokens, block), lambda step: (0, step)),
+            whole(tokens, width),
+            whole(tokens, 1),
+            whole(tokens, width),
+        ],
         out_shape=[
             shape((tokens, weight.shape[1]), narrow),
             shape((tokens, width)),
@@ -200,7 +237,7 @@
         compiler_params=ROOM,
         cost_estimate=LITTLE,
         name="embed_and_project",
-    )(inner, *parts, text, gain, bias, weight, weight_bias)
+    )(parts, text, gain, bias, weight, weight_bias)
 
 
 def one_head(rows, head):
@@ -481,9 +518,9 @@
     )(packed, packed, packed, d_attended, weight)
 
 
-def embed_back_kernel(inner_ref, d_packed, weight, d_r1, normed, inverse, gain, *refs):
-    d_embed, g_gain, g_bias, squares = refs[:4]
-    blocks, total = refs[4:-1], refs[-1]
+def embed_back_kernel(
+    d_packed, weight, d_r1, normed, inverse, gain, d_embed, g_gain, g_bias, squares, blocks, total
+):
     step = pl.program_id(0)
     share = mul_rows(d_packed[0], weight[...])
 
@@ -502,13 +539,12 @@
         g_gain[...] = down(incoming * normed[...])
         g_bias[...] = down(incoming)
         squares[...] = down(d_embed[...] * d_embed[...])
-        columns = blocks[0].shape[1]
-        for offset in range(len(blocks)):
-            place = pl.multiple_of(jnp.bitwise_xor(inner_ref[0], offset) * columns, columns)
-            blocks[offset][...] = d_embed[:, pl.ds(place, columns)]
-
-
-def embed_back(inner, group, d_packed, weight, d_r1, normed, inverse, gain):
+        columns = blocks.shape[2]
+        for one in range(blocks.shape[0]):
+            blocks[one] = d_embed[:, one * columns : (one + 1) * columns]
+
+
+def embed_back(group, d_packed, weight, d_r1, normed, inverse, gain):
     tokens, width = d_r1.shape
     block = width // 2
     vector = whole(1, width)
@@ -516,160 +552,178 @@
     columns = width // group
     return pl.pallas_call(
         embed_back_kernel,
-        grid_spec=pltpu.PrefetchScalarGridSpec(
-            num_scalar_prefetch=1,
-            grid=(3 * width // block,),
-            in_specs=[
-                pl.BlockSpec((1, tokens, block), lambda step, *_: (step // 2, 0, step % 2)),
-                pl.BlockSpec((width, block), lambda step, *_: (0, step)),
-                rows,
-                rows,
-                whole(tokens, 1),
-                vector,
-            ],
-            out_specs=[rows, vector, vector, vector] + [whole(tokens, columns)] * group,
-            scratch_shapes=[pltpu.VMEM((tokens, width), wide)],
-        ),
-        out_shape=[shape((tokens, width)), shape((1, width)), shape((1, width)), shape((1, width))]
-        + [shape((tokens, columns))] * group,
+        grid=(3 * width // block,),
+        in_specs=[
+            pl.BlockSpec((1, tokens, block), lambda step: (step // 2, 0, step % 2)),
+            pl.BlockSpec((width, block), lambda step: (0, step)),
+            rows,
+            rows,
+            whole(tokens, 1),
+            vector,
+        ],
+        out_specs=[rows, vector, vector, vector, whole(group, tokens, columns)],
+        scratch_shapes=[pltpu.VMEM((tokens, width), wide)],
+        out_shape=[
+            shape((tokens, width)),
+            shape((1, width)),
+            shape((1, width)),
+            shape((1, width)),
+            shape((group, tokens, columns)),
+        ],
         compiler_params=ROOM,
         cost_estimate=LITTLE,
         name="embed_back",
-    )(inner, d_packed, weight, d_r1, normed, inverse, gain)
-
-
-def outer_first_kernel(table_ref, *refs):
-    half = len(refs) // 3
-    for left, right, out in zip(refs[:half], refs[half : 2 * half], refs[2 * half :]):
-        out[...] = mul(left[...], right[...].reshape(right.shape[-2:]))
-
-
-def outer_next_kernel(table_ref, *refs):
-    streams = len(refs) // 7
-    for one in range(streams):
-        right = refs[one][...]
-        right = right.reshape(right.shape[-2:])
-        for part in range(2):
-            place = streams + 2 * one + part
-            left, arrived, out = refs[place], refs[place + 2 * streams], refs[place + 4 * streams]
-            out[...] = mul(left[...], right) + arrived[...]
-
-
-class Shares:
-    def __init__(self, me, streams):
-        self.me, self.streams = me, streams
+    )(d_packed, weight, d_r1, normed, inverse, gain)
+
+
+def outer_kernel(left, right, out):
+    out[...] = mul_down(left[...], right[...].reshape(right.shape[-2:]))
+
+
+def outer(left, right):
+    tokens, rows = left.shape
+    width = right.shape[1]
+    block = min(rows, 512)
+    return pl.pallas_call(
+        outer_kernel,
+        grid=(rows // block,),
+        in_specs=[pl.BlockSpec((tokens, block), lambda row: (0, row)), whole(tokens, width)],
+        out_specs=pl.BlockSpec((block, width), lambda row: (row, 0)),
+        out_shape=shape((rows, width)),
+        compiler_params=ROOM,
+        cost_estimate=LITTLE,
+        name="outer",
+    )(left, right)
+
+
+def flat(ref):
+    return ref[...].reshape(ref.shape[-2:])
+
+
+def first_kernel(plan, table, *refs):
+    count = len(plan)
+    lefts, rights, out = refs[:count], refs[count : 2 * count], refs[-1]
+    for one in range(count):
+        out[one] = mul(lefts[one][...], flat(rights[one]))
+
+
+def next_kernel(plan, table, *refs):
+    count = len(plan)
+    keeps, sends, rights = refs[:count], refs[count : 2 * count], refs[2 * count : 3 * count]
+    arrived_keep, arrived_send, kept, sent_one, sent_two = refs[3 * count :]
+    for one in range(count):
+        right = flat(rights[one])
+        kept[one] = mul(keeps[one][...], right) + arrived_keep[one]
+        sent = sent_one if one < count // 2 else sent_two
+        sent[one % (count // 2)] = mul(sends[one][...], right) + arrived_send[one]
+
+
+class Halving:
+    def __init__(self, me, masks_one, masks_two, streams, width):
+        self.masks = (masks_one, masks_two)
+        self.streams = streams
         self.devices = lax.axis_size("pages")
-        self.tables = [
-            jnp.bitwise_xor(me, jnp.array(flips_of(stream["masks"]), jnp.int32))
-            * stream["units"]
-            + stream["unit"]
-            for stream in streams
-        ]
-
-    def right_spec(self, stream, splits):
-        right, columns = stream["right"], stream["columns"] // splits
-        first = stream["first"] * splits
+        self.width = width
+        self.rows = streams[0][0].shape[0] // self.devices
+        self.table = jnp.concatenate(
+            [
+                jnp.bitwise_xor(me, jnp.array(flips_of(masks), jnp.int32))
+                for masks in self.masks
+            ]
+        )
+
+    def left(self, one, start):
+        place = (one >= len(self.streams) // 2) * self.devices + start
+        return pl.BlockSpec(
+            (self.rows, self.streams[one][0].shape[1]),
+            lambda row, table: (table[place + row], 0),
+        )
+
+    def right(self, one):
+        _, right, part, column = self.streams[one]
         if right.ndim == 3:
-            per = right.shape[2] // columns
-            return pl.BlockSpec(
-                (1, right.shape[1], columns),
-                lambda row, col, *_: ((first + col) // per, 0, (first + col) % per),
-            )
-        return pl.BlockSpec((right.shape[0], columns), lambda row, col, *_: (0, first + col))
-
-    def left_spec(self, stream, index, start):
-        count = len(self.tables[0])
-        return pl.BlockSpec(
-            (stream["rows"], stream["left"].shape[1]),
-            lambda row, col, table: (table[index * count + start + row], 0),
-        )
-
-    def first(self, splits=1):
+            return pl.BlockSpec((1, right.shape[1], self.width), lambda *_: (part, 0, column))
+        return pl.BlockSpec((right.shape[0], self.width), lambda *_: (0, column))
+
+    def block(self, count, start):
+        return pl.BlockSpec((count, self.rows, self.width), lambda row, *_: (0, start + row, 0))
+
+    def first(self, table):
         half = self.devices // 2
-        streams = self.streams
+        count = len(self.streams)
         return pl.pallas_call(
-            outer_first_kernel,
+            functools.partial(first_kernel, self.streams),
             grid_spec=pltpu.PrefetchScalarGridSpec(
                 num_scalar_prefetch=1,
-                grid=(half, splits),
-                in_specs=[self.left_spec(one, i, half) for i, one in enumerate(streams)]
-                + [self.right_spec(one, splits) for one in streams],
+                grid=(half,),
+                in_specs=[self.left(one, half) for one in range(count)]
+                + [self.right(one) for one in range(count)],
+                out_specs=self.block(count, 0),
+            ),
+            out_shape=shape((count, half * self.rows, self.width)),
+            compiler_params=ROOM,
+            cost_estimate=LITTLE,
+            name="halving_first",
+        )(table, *[one[0] for one in self.streams], *[one[1] for one in self.streams])
+
+    def next(self, table, arrived):
+        quarter = self.devices // 4
+        count = len(self.streams)
+        lefts = [one[0] for one in self.streams]
+        return pl.pallas_call(
+            functools.partial(next_kernel, self.streams),
+            grid_spec=pltpu.PrefetchScalarGridSpec(
+                num_scalar_prefetch=1,
+                grid=(quarter,),
+                in_specs=[self.left(one, 0) for one in range(count)]
+                + [self.left(one, quarter) for one in range(count)]
+                + [self.right(one) for one in range(count)]
+                + [self.block(count, 0), self.block(count, quarter)],
                 out_specs=[
-                    pl.BlockSpec(
-                        (one["rows"], one["columns"] // splits), lambda row, col, *_: (row, col)
-                    )
-                    for one in streams
+                    self.block(count, 0),
+                    self.block(count // 2, 0),
+                    self.block(count // 2, 0),
                 ],
             ),
-            out_shape=[shape((half * one["rows"], one["columns"])) for one in streams],
-            compiler_params=ROOM,
-            cost_estimate=LITTLE,
-            name="outer_first",
-        )(
-            jnp.concatenate(self.tables),
-            *[one["left"] for one in streams],
-            *[one["right"] for one in streams],
-        )
-
-    def to_core(self, sent):
-        self.arrived = [swap(one, 1) for one in sent]
-
-    def next(self, splits=1):
-        quarter = self.devices // 4
-        streams = self.streams
-
-        def block(one, start):
-            return pl.BlockSpec(
-                (one["rows"], one["columns"] // splits),
-                lambda row, col, *_: (start + row, col),
-            )
-
-        results = pl.pallas_call(
-            outer_next_kernel,
-            grid_spec=pltpu.PrefetchScalarGridSpec(
-                num_scalar_prefetch=1,
-                grid=(quarter, splits),
-                in_specs=[self.right_spec(one, splits) for one in streams]
-                + [
-                    self.left_spec(one, i, start)
-                    for i, one in enumerate(streams)
-                    for start in (0, quarter)
-                ]
-                + [block(one, start) for one in streams for start in (0, quarter)],
-                out_specs=[block(one, 0) for one in streams for _ in range(2)],
-            ),
             out_shape=[
-                shape((quarter * one["rows"], one["columns"])) for one in streams for _ in range(2)
+                shape((part, quarter * self.rows, self.width))
+                for part in (count, count // 2, count // 2)
             ],
             compiler_params=ROOM,
             cost_estimate=LITTLE,
-            name="outer_next",
-        )(
-            jnp.concatenate(self.tables),
-            *[one["right"] for one in streams],
-            *[one["left"] for one in streams for _ in range(2)],
-            *[arrived for arrived in self.arrived for _ in range(2)],
-        )
-        self.kept = results[0::2]
-        return results[1::2]
-
-    def to_second(self, sent):
-        self.arrived = [swap(one, s["masks"][1]) for one, s in zip(sent, self.streams)]
-
-    def third(self):
-        for step in range(2, len(self.streams[0]["masks"])):
-            folded = [fold(kept, arrived) for kept, arrived in zip(self.kept, self.arrived)]
-            self.kept = [one[0] for one in folded]
-            sent = [one[1] for one in folded]
-            if step == len(self.streams[0]["masks"]) - 1:
-                return sent
-            self.arrived = [swap(one, s["masks"][step]) for one, s in zip(sent, self.streams)]
-
-    def to_last(self, sent):
-        self.arrived = [swap(one, s["masks"][-1]) for one, s in zip(sent, self.streams)]
-
-    def result(self):
-        return [kept + arrived for kept, arrived in zip(self.kept, self.arrived)]
+            name="halving_next",
+        )(table, *lefts, *lefts, *[one[1] for one in self.streams], arrived, arrived)
+
+    def start(self, token):
+        self.from_core = swap(token.after(self.first(token(self.table))), 1)
+
+    def second(self, token):
+        self.kept, *sent = token.after(*self.next(self.table, token(self.from_core)))
+        self.arrived = [swap(one, masks[1]) for one, masks in zip(sent, self.masks)]
+
+    def third(self, token):
+        for at in range(2, len(self.masks[0])):
+            arrived = jnp.concatenate(token(*self.arrived), 0)
+            middle = self.kept.shape[1] // 2
+            half = len(self.streams) // 2
+            sent = self.kept[:, middle:] + arrived[:, middle:]
+            sent = token.after(sent[:half], sent[half:])
+            self.kept = self.kept[:, :middle] + arrived[:, :middle]
+            self.arrived = [swap(one, masks[at]) for one, masks in zip(sent, self.masks)]
+
+    def shares(self, token):
+        return self.kept + jnp.concatenate(token(*self.arrived), 0)
+
+
+class Token:
+    def __init__(self, mark):
+        self.mark = mark
+
+    def __call__(self, *values):
+        *values, self.mark = lax.optimization_barrier((*values, self.mark))
+        return values[0] if len(values) == 1 else values
+
+    after = __call__
 
 
 def flips_of(masks):
@@ -751,11 +805,10 @@
     turn = len(outer_masks) // 2
     masks_one = [1] + outer_masks
     masks_two = [1] + outer_masks[turn:] + outer_masks[:turn]
-    lanes = model_width // devices
     group = min(devices, 8)
     inner = me % group
-    inner_list = inner.reshape(1).astype(jnp.int32)
     columns = model_width // group
+    groups = [list(range(first, first + group)) for first in range(0, devices, group)]
 
     def row(vector):
         return vector.reshape(1, -1)
@@ -766,34 +819,20 @@
         )
 
     def exchange(blocks):
-        return [blocks[0]] + [swap(blocks[offset], offset) for offset in range(1, group)]
+        return lax.all_to_all(blocks, "pages", 0, 0, tiled=True, axis_index_groups=groups)
 
     own_columns = lax.dynamic_slice_in_dim(layout_tables[0], inner * columns, columns, 1)
     table_columns = [own_columns] + [around(own_columns, offset) for offset in range(1, planes)]
-    group_boxes = lax.all_gather(
-        boxes,
-        "pages",
-        axis=1,
-        tiled=True,
-        axis_index_groups=[
-            list(range(first, first + group)) for first in range(0, devices, group)
-        ],
-    )
-    group_boxes = relative(group_boxes, range(group), inner, token_rows, 1)
-    table_uses = [
-        jnp.stack(table_indices(group_boxes, (plane + offset) % planes))
-        for offset in range(planes)
-    ]
+    group_boxes = lax.all_gather(boxes, "pages", axis=1, tiled=True, axis_index_groups=groups)
     looked_up = jnp.zeros((group * token_rows, columns), wide)
     for offset in [0, 1, planes - 1] + list(range(2, planes - 1)):
-        looked_up = add_rows(table_uses[offset].T, table_columns[offset], looked_up)
-    parts = exchange(
-        [looked_up[one * token_rows : (one + 1) * token_rows] for one in range(group)]
-    )
+        uses = jnp.stack(table_indices(group_boxes, (plane + offset) % planes))
+        looked_up = add_rows(uses.T, table_columns[offset], looked_up)
+    parts = exchange(looked_up.reshape(group, token_rows, columns))
 
     bias_qkv = jnp.concatenate([b_query, jnp.zeros_like(b_query), b_value])
     packed, normed_emb, inverse_emb, emb_low = embed_and_project(
-        inner_list, parts, text_embed, row(emb_gain), row(emb_bias), w_qkv, row(bias_qkv)
+        parts, text_embed, row(emb_gain), row(emb_bias), w_qkv, row(bias_qkv)
     )
     context_low, normed_attn, inverse_attn, attn_low = attend(
         packed,
@@ -819,148 +858,157 @@
         cotangent,
     )
 
-    def stream(left, right, masks, first=0, parts=1, units=1, unit=0):
-        total = right.shape[-1] * (right.shape[0] if right.ndim == 3 else 1)
-        return dict(
-            left=left,
-            rows=left.shape[0] // devices // units,
-            units=units,
-            unit=unit,
-            right=right,
-            columns=total // parts,
-            first=first,
-            masks=masks,
-        )
-
-    expanded_t = expanded.T
-    back = Shares(
-        me,
-        [
-            stream(expanded_t, d_returned, masks_one, units=2, unit=0),
-            stream(expanded_t, d_returned, masks_two, units=2, unit=1),
-        ],
-    )
-    sent = back.first()
-    *sent, d_returned = in_order(*sent, d_returned)
-    back.to_core(sent)
-    d_pre, g_in_bias, d_r1, d_attended, g_attn_gain, g_attn_bias, g_out_bias = feed_back(
-        d_returned, w_back, pre_act, w_in, d_r2, normed_attn, inverse_attn, row(attn_gain)
-    )
-    *back.arrived, d_pre = in_order(*back.arrived, d_pre)
-    sent = back.next()
-    *sent, d_pre = in_order(*sent, d_pre)
-    back.to_second(sent)
-
-    attn_t = attn_low.T
-    inward = Shares(
-        me,
-        [
-            stream(attn_t, d_pre, masks_one, 0, 2),
-            stream(attn_t, d_pre, masks_two, 1, 2),
-        ],
-    )
-    sent = inward.first()
-    *sent, d_attended = in_order(*sent, d_attended)
-    inward.to_core(sent)
-    outward = Shares(
-        me,
-        [
-            stream(context_low.T, d_attended, masks_one, 0, 2),
-            stream(context_low.T, d_attended, masks_two, 1, 2),
-        ],
-    )
-    sent = outward.first()
-    *sent, d_attended = in_order(*sent, d_attended)
-    outward.to_core(sent)
-    *inward.arrived, d_attended = in_order(*inward.arrived, d_attended)
-    sent = inward.next()
-    *sent, d_attended = in_order(*sent, d_attended)
-    inward.to_second(sent)
-
-    d_packed, g_query_bias, g_value_bias = attend_back(packed, d_attended, w_out)
-
-    *back.arrived, d_packed = in_order(*back.arrived, d_packed)
-    sent = back.third()
-    *sent, d_packed = in_order(*sent, d_packed)
-    back.to_last(sent)
-    *outward.arrived, d_packed = in_order(*outward.arrived, d_packed)
-    sent = outward.next()
-    *sent, d_packed = in_order(*sent, d_packed)
-    outward.to_second(sent)
-
-    emb_t = emb_low.T
-    inmost = Shares(
-        me,
-        [
-            stream(emb_t, d_packed, masks_one, 0, 2),
-            stream(emb_t, d_packed, masks_two, 1, 2),
-        ],
-    )
-    sent = inmost.first(3)
-    *sent, d_packed = in_order(*sent, d_packed)
-    inmost.to_core(sent)
-    d_embed, g_emb_gain, g_emb_bias, squares, *embed_blocks = embed_back(
-        inner_list, group, d_packed, w_qkv, d_r1, normed_emb, inverse_emb, row(emb_gain)
-    )
-    embed_columns = jnp.concatenate(exchange(embed_blocks), 0)
-
-    *inward.arrived, embed_columns = in_order(*inward.arrived, embed_columns)
-    sent = inward.third()
-    *sent, embed_columns = in_order(*sent, embed_columns)
-    inward.to_last(sent)
-    *inmost.arrived, embed_columns = in_order(*inmost.arrived, embed_columns)
-    sent = inmost.next(3)
-    *sent, embed_columns = in_order(*sent, embed_columns)
-    inmost.to_second(sent)
-    back_share = jnp.concatenate(back.result(), 0)
-    g_back = emb_total(back_share)
-
-    table_total = None
-    for offset in list(range(2, planes - 1)) + [1, planes - 1, 0]:
-        part = spread_rows(table_uses[offset], embed_columns, entries)
-        part = around(part, (planes - offset) % planes) if offset else part
-        table_total = part if table_total is None else table_total + part
-    row_masks = [mask for mask in masks_one if mask >= group]
-    if row_masks:
-        table_total = halve(
-            relative(
-                table_total,
-                flips_of([mask // group for mask in row_masks]),
-                me // group,
-                entries * group // devices,
-                0,
-            ),
-            row_masks,
-        )
-    table_parts = exchange(
-        [relative(table_total, [offset], inner, entries // devices, 0) for offset in range(group)]
-    )
-    table_share = relative(jnp.concatenate(table_parts, 1), range(group), inner, columns, 1)
-
-    outward.to_last(outward.third())
-    g_in = emb_total(jnp.concatenate(inward.result(), 1))
-    g_out = emb_total(jnp.concatenate(outward.result(), 1))
-    inmost.to_last(inmost.third())
-    g_qkv = emb_total(jnp.concatenate(inmost.result(), 1))
-
-    vectors = [
-        g_query_bias,
-        g_value_bias,
-        g_out_bias,
-        g_attn_gain,
-        g_attn_bias,
-        g_in_bias,
-        g_back_bias,
-        g_ffn_gain,
-        g_ffn_bias,
-        g_emb_gain,
-        g_emb_bias,
-        jnp.full((devices,), jnp.sum(squares)),
-    ]
-    stacked = jnp.concatenate([vector.reshape(devices, -1) for vector in vectors], 1)
-    vector_share = emb_total(
-        halve(relative(stacked, flips_of(masks_one), me, 1, 0), masks_one)
-    )[0]
+    token = Token(output)
+    flight = {}
+
+    def gather_pages(product):
+        return lax.psum_scatter(product, "pages", scatter_dimension=0, tiled=True)
+
+    def inward(share):
+        return lax.ppermute(share, "emb", [(0, 1), (3, 2)])
+
+    def across(share):
+        return lax.ppermute(share, "emb", [(1, 2), (2, 1)])
+
+    def outward(share):
+        return lax.ppermute(share, "emb", [(1, 0), (2, 3)])
+
+    def settled(share, arrived):
+        return jnp.where(jnp.logical_or(plane == 1, plane == 2), share, arrived)
+
+    shares, halvings = {}, {}
+    for step in ORDER:
+        kind, name = step.split()
+        if step == "first back":
+            flight[name] = gather_pages(token.after(outer(expanded, token(d_returned))))
+        elif step == "feed all":
+            d_pre, g_in_bias, d_r1, d_attended, g_attn_gain, g_attn_bias, g_out_bias = feed_back(
+                d_returned,
+                w_back,
+                pre_act,
+                w_in,
+                d_r2,
+                normed_attn,
+                inverse_attn,
+                token(row(attn_gain)),
+            )
+            d_pre, d_attended = token.after(d_pre, d_attended)
+            attn_rows = attn_low.T
+            halvings["in"] = Halving(
+                me,
+                masks_one,
+                masks_two,
+                [(attn_rows, d_pre, 0, one) for one in range(4)],
+                model_width,
+            )
+        elif step == "attend all":
+            d_packed, g_query_bias, g_value_bias = attend_back(packed, token(d_attended), w_out)
+            d_packed = token.after(d_packed)
+            emb_rows = emb_low.T
+            context_rows = context_low.T
+            quarter = model_width // 4
+            for name, width, column in (("q1", 3 * quarter, 0), ("q2", quarter, 3)):
+                halvings[name] = Halving(
+                    me,
+                    masks_one,
+                    masks_two,
+                    [(emb_rows, d_packed, one, column) for one in range(3)]
+                    + [(context_rows, d_attended, 0, column)],
+                    width,
+                )
+        elif kind == "first":
+            halvings[name].start(token)
+        elif kind == "next":
+            halvings[name].second(token)
+        elif kind == "fold":
+            halvings[name].third(token)
+        elif kind == "finish":
+            shares[name] = halvings[name].shares(token) if name in halvings else flight[name]
+            shares[name] = token.after(shares[name])
+            flight[name] = inward(shares[name])
+        elif kind == "exchange":
+            shares[name] = token.after(shares[name] + token(flight[name]))
+            flight[name] = across(shares[name])
+        elif kind == "return":
+            shares[name] = token.after(shares[name] + token(flight[name]))
+            flight[name] = outward(shares[name])
+        elif kind == "end":
+            shares[name] = token.after(settled(shares[name], token(flight[name])))
+        elif kind == "embed":
+            d_embed, g_emb_gain, g_emb_bias, squares, embed_blocks = embed_back(
+                group,
+                d_packed,
+                w_qkv,
+                d_r1,
+                normed_emb,
+                inverse_emb,
+                token(row(emb_gain)),
+            )
+            squares, embed_blocks = token.after(squares, embed_blocks)
+            flight["h"] = exchange(embed_blocks)
+        elif kind == "spread":
+            if name == "0":
+                embed_columns = token(flight["h"]).reshape(group * token_rows, columns)
+            uses = jnp.stack(table_indices(group_boxes, int(name)))
+            flight["t" + name] = token.after(spread_rows(token(uses), embed_columns, entries))
+            if int(name) == planes - 1:
+                table_shares = jnp.concatenate([flight["t" + str(one)] for one in range(planes)], 0)
+                flight["t"] = lax.all_to_all(table_shares, "emb", 0, 0, tiled=True)
+        elif step == "tables 0":
+            owned = token(flight["t"]).reshape(planes, entries, columns)
+            table_total = token.after(functools.reduce(jnp.add, list(owned)))
+            row_masks = [mask for mask in masks_one if mask >= group]
+            if row_masks:
+                table_total = halve(
+                    relative(
+                        table_total,
+                        flips_of([mask // group for mask in row_masks]),
+                        me // group,
+                        entries * group // devices,
+                        0,
+                    ),
+                    row_masks,
+                )
+            flight["u"] = exchange(table_total.reshape(group, entries // devices, columns))
+        elif step == "tables 1":
+            table_share = jnp.concatenate(list(token(flight["u"])), 1)
+            table_share = token.after(table_share)
+        elif step == "vector 0":
+            vectors = [
+                g_query_bias,
+                g_value_bias,
+                g_out_bias,
+                g_attn_gain,
+                g_attn_bias,
+                g_in_bias,
+                g_back_bias,
+                g_ffn_gain,
+                g_ffn_bias,
+                g_emb_gain,
+                g_emb_bias,
+                jnp.full((devices,), jnp.sum(squares)),
+            ]
+            stacked = jnp.concatenate([vector.reshape(devices, -1) for vector in vectors], 1)
+            stacked = token.after(token(stacked))
+            flight["v1"] = lax.all_to_all(stacked, "pages", 0, 0, tiled=True)
+        elif step == "vector 1":
+            vector_share = token.after(jnp.sum(token(flight["v1"]), 0, keepdims=True))
+            flight["v2"] = lax.ppermute(vector_share, "emb", [(0, 1), (3, 2)])
+        elif step == "vector 2":
+            vector_share = token.after(vector_share + token(flight["v2"]))
+            flight["v3"] = lax.ppermute(vector_share, "emb", [(1, 2), (2, 1)])
+        elif step == "vector 3":
+            vector_share = token.after(vector_share + token(flight["v3"]))
+            flight["v4"] = lax.ppermute(vector_share, "emb", [(1, 0), (2, 3)])
+        elif step == "vector 4":
+            middle = jnp.logical_or(plane == 1, plane == 2)
+            vector_share = jnp.where(middle, vector_share, token(flight["v4"]))[0]
+    g_back = shares["back"]
+    g_in = jnp.concatenate(list(shares["in"]), 1)
+    g_four = jnp.concatenate([shares["q1"], shares["q2"]], 2)
+    g_qkv = jnp.concatenate(list(g_four[:3]), 1)
+    g_out = g_four[3]
+
     totals = []
     first = 0
     for vector in vectors:
@@ -970,7 +1018,7 @@
     entry_count = token_rows * model_width * devices * planes
     rms_grad = jnp.sqrt(totals[11][0] / entry_count)
     return (
-        output,
+        token.mark,
         d_embed,
         table_share[None],
         totals[9],

time: 785 us -> 657 us (0.84)
  waiting for transfers between devices: 380 us -> 176 us
  starting transfers between devices: 83.6 us -> 125 us
  local copies, waits for them, and re-layouts: 49 us -> 70 us
  between operations: 4.1 us -> 17 us
    ppermute x48 -> x15, waiting for transfers between devices: 181 us -> 63.5 us  [swap(): lax.ppermute(array, 'pages', [(one, one ^ mask) for one in range(lax.axis...]
    ppermute x6 -> x3, waiting for transfers between devices: 72.5 us -> 0.01 us  [around(): lax.ppermute(array, 'emb', [((one + offset) % planes, one) for one in ran...]
    ppermute x15, starting transfers between devices: 36.8 us -> 84.9 us  [the longest x4 51.8 us: inward(): return lax.ppermute(share, 'emb', [(0, 1), (3, 2)])]
    ppermute x15, waiting for transfers between devices: 127 us -> 82.1 us  [the longest x4 58.6 us: outward(): return lax.ppermute(share, 'emb', [(1, 0), (2, 3)])]
    all_to_all x0 -> x4, waiting for transfers between devices: none -> 30.8 us  [the longest x3 30.8 us: exchange(): lax.all_to_all(blocks, 'pages', 0, 0, tiled=True, axis_index_groups=groups)]
    ppermute x48 -> x15, starting transfers between devices: 35.9 us -> 14.1 us  [swap(): lax.ppermute(array, 'pages', [(one, one ^ mask) for one in range(lax.axis...]
    unnamed x194 -> x137, local copies, waits for them, and re-layouts: 24.1 us -> 44.9 us
    all_to_all x0 -> x4, starting transfers between devices: none -> 19.6 us  [the longest x3 11.9 us: exchange(): lax.all_to_all(blocks, 'pages', 0, 0, tiled=True, axis_index_groups=groups)]
  transfers between devices with their start and end apart: 69 -> 38, of which waited for: 30 -> 16; matrix products, arithmetic and copies ran while one was open for 7% -> 11% of each run, Pallas kernels for 13% -> 21%
where the time goes in v4:
time: 657 us; the launch traced here: 649 us
  Pallas kernels  206 us (31%)
  waiting for transfers between devices  176 us (27%)
  starting transfers between devices  125 us (19%)
  local copies, waits for them, and re-layouts  70 us (11%)
  other arithmetic  37.4 us (6%)
  between operations  17 us (3%)
  blocking collectives  16.9 us (3%)
    ppermute x15, waiting for transfers between devices, swap(): lax.ppermute(array, 'pages', [(one, one ^ mask) for one in range(lax.axis...  63.5 us
    ppermute x4, waiting for transfers between devices, outward(): return lax.ppermute(share, 'emb', [(1, 0), (2, 3)])  58.6 us
    ppermute x4, starting transfers between devices, inward(): return lax.ppermute(share, 'emb', [(0, 1), (3, 2)])  51.8 us
    unnamed x137, local copies, waits for them, and re-layouts  44.9 us
    pallas_call x4, Pallas kernels, add_rows(): pl.pallas_call(lookup_kernel, grid=(tokens // PAGE,), in_specs=[pl.BlockS...  34.1 us
    all_to_all x3, waiting for transfers between devices, exchange(): lax.all_to_all(blocks, 'pages', 0, 0, tiled=True, axis_index_groups=groups)  30.8 us
    pallas_call x1, Pallas kernels, attend_back(): pl.pallas_call(attend_back_kernel, grid=(pairs,), in_specs=[pl.BlockSpec(...  23.3 us
    pallas_call x1, Pallas kernels, feed_back(): pl.pallas_call(feed_back_kernel, grid=(expand // block,), in_specs=[rows,...  22.4 us
  transfers between devices with their start and end apart: 38, of which 16 were waited for; matrix products, arithmetic and copies ran while one was open for 11% of the time, Pallas kernels for 21%

profile of v4, /device:TPU:0, one launch (start us, length us, event | category | flops | bytes accessed | tf_op | source)
XLA Modules:
  0.0 648.9 jit_solution(4358853730381303417)
XLA Ops:
  8.3 5.1 collective-permute-start.2
  14.4 9.4 %all_gather.3 = s32[4,4096]{1,0:T(4,128)S(1)} all-gather(s32[4,512]{1,0:T(4,128)} %param.26), channel_id=1, replica_groups={{0,4,8,12,16,20,24,28},{1,5,9,13,17,21,25,29},{2,6,10,14,18,22,26,30},{..., dimensions={1}, use_global_device_ids=true | all-gather | bytes 73728 | tf_op jit(solution)/shard_map/all_gather | solution.py:826
  26.8 8.4 %look_up.4.total_ref = f32[4096,128]{1,0:T(8,128)} custom-call(s32[4096,2]{1,0:T(8,128)S(1)} %copy.55.idx_ref, f32[1024,128]{1,0:T(8,128)S(1)} %dynamic-slice_bitcast_fusion.table_ref, f32[4096,128]{1,0:T(8,128)} %broadcast_in_dim.26.total_ref), custom_call_target="tpu_custom_call", output_to_operand_aliasing={{}: (2, {})} | custom-call | flops 1024 | bytes 1024 | tf_op jit(solution)/shard_map/look_up/pallas_call | solution.py:143
  41.7 8.6 %look_up.5.total_ref = f32[4096,128]{1,0:T(8,128)} custom-call(s32[4096,2]{1,0:T(8,128)S(1)} %copy-done.12, f32[1024,128]{1,0:T(8,128)} %collective-permute-done.2.table_ref, f32[4096,128]{1,0:T(8,128)} %look_up.4.total_ref), custom_call_target="tpu_custom_call", output_to_operand_aliasing={{}: (2, {})} | custom-call | flops 1024 | bytes 1024 | tf_op jit(solution)/shard_map/look_up/pallas_call | solution.py:143
  50.3 8.6 %look_up.6.total_ref = f32[4096,128]{1,0:T(8,128)} custom-call(s32[4096,2]{1,0:T(8,128)S(1)} %copy-done.11, f32[1024,128]{1,0:T(8,128)} %collective-permute-done.1.table_ref, f32[4096,128]{1,0:T(8,128)} %look_up.5.total_ref), custom_call_target="tpu_custom_call", output_to_operand_aliasing={{}: (2, {})} | custom-call | flops 1024 | bytes 1024 | tf_op jit(solution)/shard_map/look_up/pallas_call | solution.py:143
  58.9 8.4 %look_up.7 = f32[4096,128]{1,0:T(8,128)} custom-call(s32[4096,2]{1,0:T(8,128)S(1)} %copy.58.idx_ref, f32[1024,128]{1,0:T(8,128)S(1)} %collective-permute-done.table_ref, f32[4096,128]{1,0:T(8,128)} %look_up.6.total_ref), custom_call_target="tpu_custom_call", output_to_operand_aliasing={{}: (2, {})} | custom-call | flops 1024 | bytes 1024 | tf_op jit(solution)/shard_map/look_up/pallas_call | solution.py:143
  67.4 3.7 all-to-all-start
  71.4 26.3 %all-to-all-done.parts = f32[8,512,128]{2,1,0:T(8,128)S(1)} async-done(((f32[8,512,128]{2,1,0:T(8,128)}), f32[8,512,128]{2,1,0:T(8,128)S(1)}, u32[]{:S(2)}, u32[]{:S(2)}) %all-to-all-start) | async-done | bytes 2097184 | tf_op jit(solution)/shard_map/all_to_all | solution.py:822
  99.1 9.5 %embed_and_project.1 = (bf16[512,3072]{1,0:T(8,128)(2,1)}, f32[512,1024]{1,0:T(8,128)S(1)}, f32[512,1]{1,0:T(8,128)S(1)}, bf16[512,1024]{1,0:T(8,128)(2,1)S(1)}) custom-call(f32[8,512,128]{2,1,0:T(8,128)} %copy-done.39, bf16[512,1024]{1,0:T(8,128)(2,1)S(1)} %copy-done.18, f32[1,1024]{1,0:T(1,128)S(1)} %bitcast.137, f32[1,1024]{1,0:T(1,128)S(1)} %bitcast.143, ...), custom_call_target="tpu_custom_call" | custom-call | flops 1024 | bytes 1024 | tf_op jit(solution)/shard_map/embed_and_project/pallas_call | solution.py:214
  111.6 20.3 %attend.1 = (bf16[512,1024]{1,0:T(8,128)(2,1)S(1)}, f32[512,1024]{1,0:T(8,128)S(1)}, f32[512,1]{1,0:T(8,128)S(1)}, bf16[512,1024]{1,0:T(8,128)(2,1)S(1)}) custom-call(bf16[512,3072]{1,0:T(8,128)(2,1)} %get-tuple-element.232.queries.keys.values, bf16[512,3072]{1,0:T(8,128)(2,1)} %get-tuple-element.232.queries.keys.values, ...), custom_call_target="tpu_custom_call" | custom-call | flops 1024 | bytes 1024 | tf_op jit(solution)/shard_map/attend/pallas_call | solution.py:286
  134.2 20.4 %feed.1 = (f32[512,4096]{1,0:T(8,128)}, bf16[512,4096]{1,0:T(8,128)(2,1)}, bf16[512,1024]{1,0:T(8,128)(2,1)}, f32[512,1024]{1,0:T(8,128)S(1)}, bf16[512,1024]{1,...) custom-call(bf16[512,1024]{1,0:T(8,128)(2,1)S(1)} %get-tuple-element.234.low, ...), custom_call_target="tpu_custom_call" | custom-call | flops 1024 | bytes 1024 | tf_op jit(solution)/shard_map/feed/pallas_call | solution.py:359
  158.1 9.4 %outer.1 = f32[4096,1024]{1,0:T(8,128)} custom-call(bf16[512,4096]{1,0:T(8,128)(2,1)S(1)} %copy-done.13, bf16[512,1024]{1,0:T(8,128)(2,1)S(1)} %get-tuple-element.242.right.d_returned), custom_call_target="tpu_custom_call" | custom-call | flops 1024 | bytes 1024 | tf_op jit(solution)/shard_map/outer/pallas_call | solution.py:587
  168.3 22.4 %feed_back.1 = (bf16[512,4096]{1,0:T(8,128)(2,1)}, f32[1,4096]{1,0:T(1,128)S(1)}, f32[512,1024]{1,0:T(8,128)S(1)}, bf16[512,1024]{1,0:T(8,128)(2,1)S(1)}, f32[1,...) custom-call(bf16[512,1024]{1,0:T(8,128)(2,1)S(1)} %get-tuple-element.242.right.d_returned, ...), custom_call_target="tpu_custom_call" | custom-call | flops 1024 | bytes 1024 | tf_op jit(solution)/shard_map/feed_back/pallas_call | solution.py:435
  192.5 3.0 copy-done
  195.5 6.1 halving_first.3
  201.7 23.3 %attend_back.1 = (bf16[3,512,1024]{2,1,0:T(8,128)(2,1)}, f32[1,1024]{1,0:T(1,128)S(1)}, f32[1,1024]{1,0:T(1,128)S(1)}) custom-call(bf16[512,3072]{1,0:T(8,128)(2,1)} %get-tuple-element.232.queries.keys.values, bf16[512,3072]{1,0:T(8,128)(2,1)} %get-tuple-element.232.queries.keys.values, bf16[512,3072]{1,0:T(8,128)(2,1)} %get-tuple-element.232.queries.keys.values, ...), custom_call_target="tpu_custom_call" | custom-call | flops 1024 | bytes 1024 | tf_op jit(solution)/shard_map/attend_back/pallas_call | solution.py:499
  229.7 6.3 halving_first.4
  236.7 4.3 halving_first.5
  241.0 9.3 %halving_next.3 = (f32[4,256,1024]{2,1,0:T(8,128)}, f32[2,256,1024]{2,1,0:T(8,128)}, f32[2,256,1024]{2,1,0:T(8,128)}) custom-call(s32[16]{0:T(128)S(1)} %pad_add_fusion.2.table, bf16[1024,512]{1,0:T(8,128)(2,1)S(1)} %bitcast.118, bf16[1024,512]{1,0:T(8,128)(2,1)S(1)} %bitcast.119, bf16[1024,512]{1,0:T(8,128)(2,1)S(1)} %bitcast.120, ...), custom_call_target="tpu_custom_call" | custom-call | flops 1024 | bytes 1024 | tf_op jit(solution)/shard_map/halving_next/pallas_call | solution.py:673
  251.1 11.7 %embed_back.1 = (f32[512,1024]{1,0:T(8,128)}, f32[1,1024]{1,0:T(1,128)S(1)}, f32[1,1024]{1,0:T(1,128)S(1)}, f32[1,1024]{1,0:T(1,128)S(1)}, f32[8,512,128]{2,1,0:T(8,128)S(1)}) custom-call(bf16[3,512,1024]{2,1,0:T(8,128)(2,1)} %get-tuple-element.267.refs_4_.refs_5_.refs_6_.d_packed.refs_8_.refs_9_.refs_10_, bf16[1024,3072]{1,0:T(8,128)(2,1)} %weight.7, ...), custom_call_target="tpu_custom_call" | custom-call | flops 1024 | bytes 1024 | tf_op jit(solution)/shard_map/embed_back/pallas_call | solution.py:553
  264.1 4.0 all-to-all-start.1
  270.5 6.8 %halving_next.4 = (f32[4,256,768]{2,1,0:T(8,128)}, f32[2,256,768]{2,1,0:T(8,128)}, f32[2,256,768]{2,1,0:T(8,128)}) custom-call(s32[16]{0:T(128)S(1)} %pad_add_fusion.2.table, bf16[1024,512]{1,0:T(8,128)(2,1)S(1)} %bitcast.102, bf16[1024,512]{1,0:T(8,128)(2,1)S(1)} %bitcast.103, bf16[1024,512]{1,0:T(8,128)(2,1)S(1)} %bitcast.104, ...), custom_call_target="tpu_custom_call" | custom-call | flops 1024 | bytes 1024 | tf_op jit(solution)/shard_map/halving_next/pallas_call | solution.py:673
  280.8 42.5 %collective-permute-done.5 = f32[2,256,1024]{2,1,0:T(8,128)} collective-permute-done((f32[2,256,1024]{2,1,0:T(8,128)}, f32[2,256,1024]{2,1,0:T(8,128)}, u32[]{:S(2)}, u32[]{:S(2)}) %collective-permute-start.5) | collective-permute-done | bytes 2097184 | tf_op jit(solution)/shard_map/ppermute | solution.py:745
  331.3 10.8 %collective-permute-start.10 = (f32[512,1024]{1,0:T(8,128)}, f32[512,1024]{1,0:T(8,128)}, u32[]{:S(2)}, u32[]{:S(2)}) collective-permute-start(f32[512,1024]{1,0:T(8,128)} %reduce-scatter.2.cloned.1.call-done), channel_id=1, source_target_pairs={{0,1},{3,2},{4,5},{7,6},{8,9},{11,10},{12,13},{15,14},{16,17},{19,... | collective-permute-start | bytes 6291464 | tf_op jit(solution)/shard_map/ppermute | solution.py:868
  342.2 4.5 all-to-all-done.1
  346.7 4.9 spread.4
  351.6 4.6 spread.5
  356.2 4.6 spread.6
  360.7 4.6 spread.7
  366.7 7.8 %all-to-all-start.2 = ((f32[4,1024,128]{2,1,0:T(8,128)}), f32[4,1024,128]{2,1,0:T(8,128)}, u32[]{:S(2)}, u32[]{:S(2)}) async-start(f32[4,1024,128]{2,1,0:T(8,128)} %bitcast.30), calls=%async_computation.3 | async-start | bytes 4194304 | tf_op jit(solution)/shard_map/all_to_all | solution.py:956
  376.0 3.2 collective-permute-done.11
  387.1 4.3 add.112
  393.6 7.9 %collective-permute-done.8 = f32[2,128,1024]{2,1,0:T(8,128)S(1)} collective-permute-done((f32[2,128,1024]{2,1,0:T(8,128)}, f32[2,128,1024]{2,1,0:T(8,128)S(1)}, u32[]{:S(2)}, u32[]{:S(2)}) %collective-permute-start.8) | collective-permute-done | bytes 1048608 | tf_op jit(solution)/shard_map/ppermute | solution.py:745
  406.4 9.5 %collective-permute-start.15 = (f32[4,128,1024]{2,1,0:T(8,128)}, f32[4,128,1024]{2,1,0:T(8,128)}, u32[]{:S(2)}, u32[]{:S(2)}) collective-permute-start(f32[4,128,1024]{2,1,0:T(8,128)} %fusion), channel_id=1, source_target_pairs={{0,1},{3,2},{4,5},{7,6},{8,9},{11,10},{12,13},{15,14},{16,17},{19,... | collective-permute-start | bytes 6291464 | tf_op jit(solution)/shard_map/ppermute | solution.py:868
  419.6 3.8 halving_next.5
  430.6 4.1 all-to-all-start.4
  438.8 2.8 fusion.1
  441.7 21.3 %collective-permute-done.15 = f32[4,128,1024]{2,1,0:T(8,128)} collective-permute-done((f32[4,128,1024]{2,1,0:T(8,128)}, f32[4,128,1024]{2,1,0:T(8,128)}, u32[]{:S(2)}, u32[]{:S(2)}) %collective-permute-start.15) | collective-permute-done | bytes 2097184 | tf_op jit(solution)/shard_map/ppermute | solution.py:868
  463.0 4.1 add.120
  472.5 20.6 %collective-permute-start.21 = (f32[4,128,768]{2,1,0:T(8,128)}, f32[4,128,768]{2,1,0:T(8,128)S(1)}, u32[]{:S(2)}, u32[]{:S(2)}) collective-permute-start(f32[4,128,768]{2,1,0:T(8,128)} %fusion.1), channel_id=1, source_target_pairs={{0,1},{3,2},{4,5},{7,6},{8,9},{11,10},{12,13},{15,14},{16,17},{19,... | collective-permute-start | bytes 4718600 | tf_op jit(solution)/shard_map/ppermute | solution.py:868
  505.6 27.6 %collective-permute-done.23 = f32[512,1024]{1,0:T(8,128)} collective-permute-done((f32[512,1024]{1,0:T(8,128)S(1)}, f32[512,1024]{1,0:T(8,128)}, u32[]{:S(2)}, u32[]{:S(2)}) %collective-permute-start.23) | collective-permute-done | bytes 2097184 | tf_op jit(solution)/shard_map/ppermute | solution.py:874
  533.2 3.3 broadcast_select_fusion.1
  544.9 5.0 collective-permute-done.19
  551.9 11.0 %collective-permute-start.25 = (f32[4,128,256]{2,1,0:T(8,128)}, f32[4,128,256]{2,1,0:T(8,128)S(1)}, u32[]{:S(2)}, u32[]{:S(2)}) collective-permute-start(f32[4,128,256]{2,1,0:T(8,128)} %fusion.2), channel_id=1, source_target_pairs={{0,1},{3,2},{4,5},{7,6},{8,9},{11,10},{12,13},{15,14},{16,17},{19,... | collective-permute-start | bytes 1572872 | tf_op jit(solution)/shard_map/ppermute | solution.py:868
  563.0 7.5 %all_to_all.39 = f32[8,1,1793]{2,1,0:T(1,128)S(1)} all-to-all(f32[8,1,1793]{2,1,0:T(1,128)S(1)} %all_to_all.30), channel_id=1, replica_groups=mesh['pages'=8,'emb'=4] {'pages'}, dimensions={0} | all-to-all | bytes 114752 | tf_op jit(solution)/shard_map/all_to_all | solution.py:993
  575.8 20.2 %collective-permute-start.24 = (f32[1,1793]{1,0:T(1,128)S(1)}, f32[1,1793]{1,0:T(1,128)S(1)}, u32[]{:S(2)}, u32[]{:S(2)}) collective-permute-start(f32[1,1793]{1,0:T(1,128)S(1)} %broadcast_in_dim.28), channel_id=1, source_target_pairs={{0,1},{3,2},{4,5},{7,6},{8,9},{11,10},{12,13},{15,14},{16,17},{19,... | collective-permute-start | bytes 21524 | tf_op jit(solution)/shard_map/ppermute | solution.py:996
  604.4 20.6 %collective-permute-done.32 = f32[4,128,768]{2,1,0:T(8,128)S(1)} collective-permute-done((f32[4,128,768]{2,1,0:T(8,128)S(1)}, f32[4,128,768]{2,1,0:T(8,128)S(1)}, u32[]{:S(2)}, u32[]{:S(2)}) %collective-permute-start.32) | collective-permute-done | bytes 1572896 | tf_op jit(solution)/shard_map/ppermute | solution.py:874
  625.2 10.5 %collective-permute-done.31 = f32[4,128,256]{2,1,0:T(8,128)S(1)} collective-permute-done((f32[4,128,256]{2,1,0:T(8,128)S(1)}, f32[4,128,256]{2,1,0:T(8,128)S(1)}, u32[]{:S(2)}, u32[]{:S(2)}) %collective-permute-start.31) | collective-permute-done | bytes 524320 | tf_op jit(solution)/shard_map/ppermute | solution.py:874
  (258 shorter events, 125.2 us)
Async XLA Ops:
  8.3 31.6 %collective-permute-start.2 = (f32[1024,128]{1,0:T(8,128)S(1)}, f32[1024,128]{1,0:T(8,128)}, u32[]{:S(2)}, u32[]{:S(2)}) collective-permute-start(f32[1024,128]{1,0:T(8,128)S(1)} %dynamic-slice_bitcast_fusion.table_ref), channel_id=1, source_target_pairs={{1,0},{2,1},{3,2},{0,3},{5,4},{6,5},{7,6},{4,7},{9,8},{10,9},{11,1... | collective-permute-start | bytes 1572872 | tf_op jit(solution)/shard_map/ppermute | solution.py:817
  13.4 36.9 %collective-permute-start.1 = (f32[1024,128]{1,0:T(8,128)S(1)}, f32[1024,128]{1,0:T(8,128)}, u32[]{:S(2)}, u32[]{:S(2)}) collective-permute-start(f32[1024,128]{1,0:T(8,128)S(1)} %dynamic-slice_bitcast_fusion.table_ref), channel_id=1, source_target_pairs={{3,0},{0,1},{1,2},{2,3},{7,4},{4,5},{5,6},{6,7},{11,8},{8,9},{9,10... | collective-permute-start | bytes 1572872 | tf_op jit(solution)/shard_map/ppermute | solution.py:817
  13.4 45.5 %collective-permute-start = (f32[1024,128]{1,0:T(8,128)S(1)}, f32[1024,128]{1,0:T(8,128)S(1)}, u32[]{:S(2)}, u32[]{:S(2)}) collective-permute-start(f32[1024,128]{1,0:T(8,128)S(1)} %dynamic-slice_bitcast_fusion.table_ref), channel_id=1, source_target_pairs={{2,0},{3,1},{0,2},{1,3},{6,4},{7,5},{4,6},{5,7},{10,8},{11,9},{8,1... | collective-permute-start | bytes 1572872 | tf_op jit(solution)/shard_map/ppermute | solution.py:817
  67.3 31.7 %copy-start.18 = (bf16[512,1024]{1,0:T(8,128)(2,1)S(1)}, bf16[512,1024]{1,0:T(8,128)(2,1)}, u32[]{:S(2)}) copy-start(bf16[512,1024]{1,0:T(8,128)(2,1)} %text.1) | copy-start | bytes 3145732
  67.3 31.7 %copy-start.26 = (f32[1024]{0:T(1024)S(1)}, f32[1024]{0:T(1024)}, u32[]{:S(2)}) copy-start(f32[1024]{0:T(1024)} %param.28) | copy-start | bytes 12292
  67.4 31.7 %copy-start.28 = (f32[1024]{0:T(1024)S(1)}, f32[1024]{0:T(1024)}, u32[]{:S(2)}) copy-start(f32[1024]{0:T(1024)} %param.29) | copy-start | bytes 12292
  67.4 30.3 %all-to-all-start = ((f32[8,512,128]{2,1,0:T(8,128)}), f32[8,512,128]{2,1,0:T(8,128)S(1)}, u32[]{:S(2)}, u32[]{:S(2)}) async-start(f32[8,512,128]{2,1,0:T(8,128)} %bitcast.5), calls=%async_computation | async-start | bytes 4194304 | tf_op jit(solution)/shard_map/all_to_all | solution.py:822
  71.1 260.2 %reduce-scatter.2.cloned.1.call-start = ((), (), s32[]{:S(2)}) async-start(), calls=%async_computation.6 | async-start | bytes 18874368 | tf_op jit(solution)/shard_map/reduce_scatter | solution.py:865
  111.5 22.6 %copy-start.19 = (bf16[512,1024]{1,0:T(8,128)(2,1)S(1)}, bf16[512,1024]{1,0:T(8,128)(2,1)}, u32[]{:S(2)}) copy-start(bf16[512,1024]{1,0:T(8,128)(2,1)} %cotangent.1) | copy-start | bytes 3145732
  111.5 22.6 %copy-start.29 = (f32[4096]{0:T(1024)S(1)}, f32[4096]{0:T(1024)}, u32[]{:S(2)}) copy-start(f32[4096]{0:T(1024)} %param.38) | copy-start | bytes 49156
  111.5 22.6 %copy-start.32 = (f32[1024]{0:T(1024)S(1)}, f32[1024]{0:T(1024)}, u32[]{:S(2)}) copy-start(f32[1024]{0:T(1024)} %param.40) | copy-start | bytes 12292
  111.5 22.6 %copy-start.33 = (f32[1024]{0:T(1024)S(1)}, f32[1024]{0:T(1024)}, u32[]{:S(2)}) copy-start(f32[1024]{0:T(1024)} %param.41) | copy-start | bytes 12292
  201.7 39.3 %collective-permute-start.3 = (f32[4,512,1024]{2,1,0:T(8,128)}, f32[4,512,1024]{2,1,0:T(8,128)}, u32[]{:S(2)}, u32[]{:S(2)}) collective-permute-start(f32[4,512,1024]{2,1,0:T(8,128)} %halving_first.3), channel_id=1, source_target_pairs={{0,4},{4,0},{8,12},{12,8},{16,20},{20,16},{24,28},{28,24},{1,5},{5... | collective-permute-start | bytes 25165832 | tf_op jit(solution)/shard_map/ppermute | solution.py:745
  236.0 32.0 %collective-permute-start.7 = (f32[4,512,768]{2,1,0:T(8,128)}, f32[4,512,768]{2,1,0:T(8,128)}, u32[]{:S(2)}, u32[]{:S(2)}) collective-permute-start(f32[4,512,768]{2,1,0:T(8,128)} %halving_first.4), channel_id=1, source_target_pairs={{0,4},{4,0},{8,12},{12,8},{16,20},{20,16},{24,28},{28,24},{1,5},{5... | collective-permute-start | bytes 18874376 | tf_op jit(solution)/shard_map/ppermute | solution.py:745
  250.3 73.0 %collective-permute-start.5 = (f32[2,256,1024]{2,1,0:T(8,128)}, f32[2,256,1024]{2,1,0:T(8,128)}, u32[]{:S(2)}, u32[]{:S(2)}) collective-permute-start(f32[2,256,1024]{2,1,0:T(8,128)} %get-tuple-element.295), channel_id=1, source_target_pairs={{0,8},{4,12},{8,0},{12,4},{16,24},{20,28},{24,16},{28,20},{1,9},{5... | collective-permute-start | bytes 6291464 | tf_op jit(solution)/shard_map/ppermute | solution.py:745
  250.5 72.8 %collective-permute-start.6 = (f32[2,256,1024]{2,1,0:T(8,128)}, f32[2,256,1024]{2,1,0:T(8,128)}, u32[]{:S(2)}, u32[]{:S(2)}) collective-permute-start(f32[2,256,1024]{2,1,0:T(8,128)} %get-tuple-element.296), channel_id=1, source_target_pairs={{0,16},{4,20},{8,24},{12,28},{16,0},{20,4},{24,8},{28,12},{1,17},{... | collective-permute-start | bytes 6291464 | tf_op jit(solution)/shard_map/ppermute | solution.py:745
  264.1 82.6 %all-to-all-start.1 = ((f32[8,512,128]{2,1,0:T(8,128)}), f32[8,512,128]{2,1,0:T(8,128)S(1)}, u32[]{:S(2)}, u32[]{:S(2)}) async-start(f32[8,512,128]{2,1,0:T(8,128)} %copy-done.17), calls=%async_computation.2 | async-start | bytes 4194304 | tf_op jit(solution)/shard_map/all_to_all | solution.py:822
  277.3 101.9 %collective-permute-start.11 = (f32[2,256,768]{2,1,0:T(8,128)}, f32[2,256,768]{2,1,0:T(8,128)}, u32[]{:S(2)}, u32[]{:S(2)}) collective-permute-start(f32[2,256,768]{2,1,0:T(8,128)} %get-tuple-element.314), channel_id=1, source_target_pairs={{0,8},{4,12},{8,0},{12,4},{16,24},{20,28},{24,16},{28,20},{1,9},{5... | collective-permute-start | bytes 4718600 | tf_op jit(solution)/shard_map/ppermute | solution.py:745
  279.3 100.2 %collective-permute-start.12 = (f32[2,256,768]{2,1,0:T(8,128)}, f32[2,256,768]{2,1,0:T(8,128)}, u32[]{:S(2)}, u32[]{:S(2)}) collective-permute-start(f32[2,256,768]{2,1,0:T(8,128)} %get-tuple-element.315), channel_id=1, source_target_pairs={{0,16},{4,20},{8,24},{12,28},{16,0},{20,4},{24,8},{28,12},{1,17},{... | collective-permute-start | bytes 4718600 | tf_op jit(solution)/shard_map/ppermute | solution.py:745
  331.3 55.8 %collective-permute-start.10 = (f32[512,1024]{1,0:T(8,128)}, f32[512,1024]{1,0:T(8,128)}, u32[]{:S(2)}, u32[]{:S(2)}) collective-permute-start(f32[512,1024]{1,0:T(8,128)} %reduce-scatter.2.cloned.1.call-done), channel_id=1, source_target_pairs={{0,1},{3,2},{4,5},{7,6},{8,9},{11,10},{12,13},{15,14},{16,17},{19,... | collective-permute-start | bytes 6291464 | tf_op jit(solution)/shard_map/ppermute | solution.py:868
  366.7 59.8 %all-to-all-start.2 = ((f32[4,1024,128]{2,1,0:T(8,128)}), f32[4,1024,128]{2,1,0:T(8,128)}, u32[]{:S(2)}, u32[]{:S(2)}) async-start(f32[4,1024,128]{2,1,0:T(8,128)} %bitcast.30), calls=%async_computation.3 | async-start | bytes 4194304 | tf_op jit(solution)/shard_map/all_to_all | solution.py:956
  374.5 45.1 %collective-permute-start.4 = (f32[4,512,256]{2,1,0:T(8,128)}, f32[4,512,256]{2,1,0:T(8,128)}, u32[]{:S(2)}, u32[]{:S(2)}) collective-permute-start(f32[4,512,256]{2,1,0:T(8,128)} %halving_first.5), channel_id=1, source_target_pairs={{0,4},{4,0},{8,12},{12,8},{16,20},{20,16},{24,28},{28,24},{1,5},{5... | collective-permute-start | bytes 6291464 | tf_op jit(solution)/shard_map/ppermute | solution.py:745
  374.5 27.0 %collective-permute-start.8 = (f32[2,128,1024]{2,1,0:T(8,128)}, f32[2,128,1024]{2,1,0:T(8,128)S(1)}, u32[]{:S(2)}, u32[]{:S(2)}) collective-permute-start(f32[2,128,1024]{2,1,0:T(8,128)} %get-tuple-element.308), channel_id=1, source_target_pairs={{0,16},{4,20},{8,24},{12,28},{16,0},{20,4},{24,8},{28,12},{1,17},{... | collective-permute-start | bytes 3145736 | tf_op jit(solution)/shard_map/ppermute | solution.py:745
  379.2 25.1 %collective-permute-start.9 = (f32[2,128,1024]{2,1,0:T(8,128)}, f32[2,128,1024]{2,1,0:T(8,128)S(1)}, u32[]{:S(2)}, u32[]{:S(2)}) collective-permute-start(f32[2,128,1024]{2,1,0:T(8,128)} %get-tuple-element.309), channel_id=1, source_target_pairs={{0,8},{4,12},{8,0},{12,4},{16,24},{20,28},{24,16},{28,20},{1,9},{5... | collective-permute-start | bytes 3145736 | tf_op jit(solution)/shard_map/ppermute | solution.py:745
  391.4 28.2 %copy-start.3 = (bf16[512,1024]{0,1:T(8,128)(2,1)S(1)}, bf16[512,1024]{0,1:T(8,128)(2,1)}, u32[]{:S(2)}) copy-start(bf16[512,1024]{0,1:T(8,128)(2,1)} %copy-done.1) | copy-start | bytes 3145732
  391.4 28.2 %copy-start.7 = (bf16[512,1024]{1,0:T(8,128)(2,1)S(1)}, bf16[512,1024]{1,0:T(8,128)(2,1)}, u32[]{:S(2)}) copy-start(bf16[512,1024]{1,0:T(8,128)(2,1)} %copy-done.4) | copy-start | bytes 3145732
  391.4 35.2 %collective-permute-start.18 = (f32[512,1024]{1,0:T(8,128)}, f32[512,1024]{1,0:T(8,128)}, u32[]{:S(2)}, u32[]{:S(2)}) collective-permute-start(f32[512,1024]{1,0:T(8,128)} %add.112), channel_id=1, source_target_pairs={{1,2},{2,1},{5,6},{6,5},{9,10},{10,9},{13,14},{14,13},{17,18},{18,... | collective-permute-start | bytes 6291464 | tf_op jit(solution)/shard_map/ppermute | solution.py:871
  406.4 56.5 %collective-permute-start.15 = (f32[4,128,1024]{2,1,0:T(8,128)}, f32[4,128,1024]{2,1,0:T(8,128)}, u32[]{:S(2)}, u32[]{:S(2)}) collective-permute-start(f32[4,128,1024]{2,1,0:T(8,128)} %fusion), channel_id=1, source_target_pairs={{0,1},{3,2},{4,5},{7,6},{8,9},{11,10},{12,13},{15,14},{16,17},{19,... | collective-permute-start | bytes 6291464 | tf_op jit(solution)/shard_map/ppermute | solution.py:868
  417.2 20.9 %collective-permute-start.16 = (f32[2,128,768]{2,1,0:T(8,128)}, f32[2,128,768]{2,1,0:T(8,128)}, u32[]{:S(2)}, u32[]{:S(2)}) collective-permute-start(f32[2,128,768]{2,1,0:T(8,128)} %get-tuple-element.352), channel_id=1, source_target_pairs={{0,16},{4,20},{8,24},{12,28},{16,0},{20,4},{24,8},{28,12},{1,17},{... | collective-permute-start | bytes 2359304 | tf_op jit(solution)/shard_map/ppermute | solution.py:745
  417.7 20.8 %collective-permute-start.17 = (f32[2,128,768]{2,1,0:T(8,128)}, f32[2,128,768]{2,1,0:T(8,128)}, u32[]{:S(2)}, u32[]{:S(2)}) collective-permute-start(f32[2,128,768]{2,1,0:T(8,128)} %get-tuple-element.353), channel_id=1, source_target_pairs={{0,8},{4,12},{8,0},{12,4},{16,24},{20,28},{24,16},{28,20},{1,9},{5... | collective-permute-start | bytes 2359304 | tf_op jit(solution)/shard_map/ppermute | solution.py:745
  425.1 42.0 %collective-permute-start.13 = (f32[2,256,256]{2,1,0:T(8,128)}, f32[2,256,256]{2,1,0:T(8,128)}, u32[]{:S(2)}, u32[]{:S(2)}) collective-permute-start(f32[2,256,256]{2,1,0:T(8,128)} %get-tuple-element.349), channel_id=1, source_target_pairs={{0,8},{4,12},{8,0},{12,4},{16,24},{20,28},{24,16},{28,20},{1,9},{5... | collective-permute-start | bytes 1572872 | tf_op jit(solution)/shard_map/ppermute | solution.py:745
  426.6 40.5 %collective-permute-start.14 = (f32[2,256,256]{2,1,0:T(8,128)}, f32[2,256,256]{2,1,0:T(8,128)}, u32[]{:S(2)}, u32[]{:S(2)}) collective-permute-start(f32[2,256,256]{2,1,0:T(8,128)} %copy-done.35), channel_id=1, source_target_pairs={{0,16},{4,20},{8,24},{12,28},{16,0},{20,4},{24,8},{28,12},{1,17},{... | collective-permute-start | bytes 1572872 | tf_op jit(solution)/shard_map/ppermute | solution.py:745
  430.6 41.9 %all-to-all-start.4 = ((f32[8,128,128]{2,1,0:T(8,128)}), f32[8,128,128]{2,1,0:T(8,128)}, u32[]{:S(2)}, u32[]{:S(2)}) async-start(f32[8,128,128]{2,1,0:T(8,128)} %bitcast.32), calls=%async_computation.5 | async-start | bytes 1048576 | tf_op jit(solution)/shard_map/all_to_all | solution.py:822
  468.3 64.9 %collective-permute-start.23 = (f32[512,1024]{1,0:T(8,128)S(1)}, f32[512,1024]{1,0:T(8,128)}, u32[]{:S(2)}, u32[]{:S(2)}) collective-permute-start(f32[512,1024]{1,0:T(8,128)S(1)} %add.118), channel_id=1, source_target_pairs={{1,0},{2,3},{5,4},{6,7},{9,8},{10,11},{13,12},{14,15},{17,16},{18,... | collective-permute-start | bytes 6291464 | tf_op jit(solution)/shard_map/ppermute | solution.py:874
  472.5 65.9 %collective-permute-start.21 = (f32[4,128,768]{2,1,0:T(8,128)}, f32[4,128,768]{2,1,0:T(8,128)S(1)}, u32[]{:S(2)}, u32[]{:S(2)}) collective-permute-start(f32[4,128,768]{2,1,0:T(8,128)} %fusion.1), channel_id=1, source_target_pairs={{0,1},{3,2},{4,5},{7,6},{8,9},{11,10},{12,13},{15,14},{16,17},{19,... | collective-permute-start | bytes 4718600 | tf_op jit(solution)/shard_map/ppermute | solution.py:868
  493.1 43.5 %collective-permute-start.22 = (f32[4,128,1024]{2,1,0:T(8,128)}, f32[4,128,1024]{2,1,0:T(8,128)S(1)}, u32[]{:S(2)}, u32[]{:S(2)}) collective-permute-start(f32[4,128,1024]{2,1,0:T(8,128)} %add.120), channel_id=1, source_target_pairs={{1,2},{2,1},{5,6},{6,5},{9,10},{10,9},{13,14},{14,13},{17,18},{18,... | collective-permute-start | bytes 6291464 | tf_op jit(solution)/shard_map/ppermute | solution.py:871
  505.6 30.9 %copy-start.38 = (f32[4,128,1024]{2,1,0:T(8,128)S(1)}, f32[4,128,1024]{2,1,0:T(8,128)}, u32[]{:S(2)}) copy-start(f32[4,128,1024]{2,1,0:T(8,128)} %add.120) | copy-start | bytes 6291460
  536.9 61.0 %collective-permute-start.29 = (f32[4,128,1024]{2,1,0:T(8,128)S(1)}, f32[4,128,1024]{2,1,0:T(8,128)}, u32[]{:S(2)}, u32[]{:S(2)}) collective-permute-start(f32[4,128,1024]{2,1,0:T(8,128)S(1)} %add.123), channel_id=1, source_target_pairs={{1,0},{2,3},{5,4},{6,7},{9,8},{10,11},{13,12},{14,15},{17,16},{18,... | collective-permute-start | bytes 6291464 | tf_op jit(solution)/shard_map/ppermute | solution.py:874
  539.7 30.8 %collective-permute-start.26 = (f32[4,128,768]{2,1,0:T(8,128)}, f32[4,128,768]{2,1,0:T(8,128)}, u32[]{:S(2)}, u32[]{:S(2)}) collective-permute-start(f32[4,128,768]{2,1,0:T(8,128)} %add.124), channel_id=1, source_target_pairs={{1,2},{2,1},{5,6},{6,5},{9,10},{10,9},{13,14},{14,13},{17,18},{18,... | collective-permute-start | bytes 4718600 | tf_op jit(solution)/shard_map/ppermute | solution.py:871
  541.7 8.2 %collective-permute-start.19 = (f32[2,128,256]{2,1,0:T(8,128)S(1)}, f32[2,128,256]{2,1,0:T(8,128)S(1)}, u32[]{:S(2)}, u32[]{:S(2)}) collective-permute-start(f32[2,128,256]{2,1,0:T(8,128)S(1)} %copy-done.50), channel_id=1, source_target_pairs={{0,16},{4,20},{8,24},{12,28},{16,0},{20,4},{24,8},{28,12},{1,17},{... | collective-permute-start | bytes 786440 | tf_op jit(solution)/shard_map/ppermute | solution.py:745
  543.4 7.6 %collective-permute-start.20 = (f32[2,128,256]{2,1,0:T(8,128)S(1)}, f32[2,128,256]{2,1,0:T(8,128)S(1)}, u32[]{:S(2)}, u32[]{:S(2)}) collective-permute-start(f32[2,128,256]{2,1,0:T(8,128)S(1)} %get-tuple-element.379), channel_id=1, source_target_pairs={{0,8},{4,12},{8,0},{12,4},{16,24},{20,28},{24,16},{28,20},{1,9},{5... | collective-permute-start | bytes 786440 | tf_op jit(solution)/shard_map/ppermute | solution.py:745
  551.9 22.0 %collective-permute-start.25 = (f32[4,128,256]{2,1,0:T(8,128)}, f32[4,128,256]{2,1,0:T(8,128)S(1)}, u32[]{:S(2)}, u32[]{:S(2)}) collective-permute-start(f32[4,128,256]{2,1,0:T(8,128)} %fusion.2), channel_id=1, source_target_pairs={{0,1},{3,2},{4,5},{7,6},{8,9},{11,10},{12,13},{15,14},{16,17},{19,... | collective-permute-start | bytes 1572872 | tf_op jit(solution)/shard_map/ppermute | solution.py:868
  572.6 52.4 %collective-permute-start.32 = (f32[4,128,768]{2,1,0:T(8,128)S(1)}, f32[4,128,768]{2,1,0:T(8,128)S(1)}, u32[]{:S(2)}, u32[]{:S(2)}) collective-permute-start(f32[4,128,768]{2,1,0:T(8,128)S(1)} %add.126), channel_id=1, source_target_pairs={{1,0},{2,3},{5,4},{6,7},{9,8},{10,11},{13,12},{14,15},{17,16},{18,... | collective-permute-start | bytes 4718600 | tf_op jit(solution)/shard_map/ppermute | solution.py:874
  575.1 24.9 %collective-permute-start.28 = (f32[4,128,256]{2,1,0:T(8,128)S(1)}, f32[4,128,256]{2,1,0:T(8,128)S(1)}, u32[]{:S(2)}, u32[]{:S(2)}) collective-permute-start(f32[4,128,256]{2,1,0:T(8,128)S(1)} %add.127), channel_id=1, source_target_pairs={{1,2},{2,1},{5,6},{6,5},{9,10},{10,9},{13,14},{14,13},{17,18},{18,... | collective-permute-start | bytes 1572872 | tf_op jit(solution)/shard_map/ppermute | solution.py:871
  575.8 21.5 %collective-permute-start.24 = (f32[1,1793]{1,0:T(1,128)S(1)}, f32[1,1793]{1,0:T(1,128)S(1)}, u32[]{:S(2)}, u32[]{:S(2)}) collective-permute-start(f32[1,1793]{1,0:T(1,128)S(1)} %broadcast_in_dim.28), channel_id=1, source_target_pairs={{0,1},{3,2},{4,5},{7,6},{8,9},{11,10},{12,13},{15,14},{16,17},{19,... | collective-permute-start | bytes 21524 | tf_op jit(solution)/shard_map/ppermute | solution.py:996
  597.3 2.8 collective-permute-start.27
  600.1 35.7 %collective-permute-start.30 = (f32[1,1793]{1,0:T(1,128)S(1)}, f32[1,1793]{1,0:T(1,128)S(1)}, u32[]{:S(2)}, u32[]{:S(2)}) collective-permute-start(f32[1,1793]{1,0:T(1,128)S(1)} %add.130), channel_id=1, source_target_pairs={{1,0},{2,3},{5,4},{6,7},{9,8},{10,11},{13,12},{14,15},{17,16},{18,... | collective-permute-start | bytes 21524 | tf_op jit(solution)/shard_map/ppermute | solution.py:1002
  601.4 34.3 %collective-permute-start.31 = (f32[4,128,256]{2,1,0:T(8,128)S(1)}, f32[4,128,256]{2,1,0:T(8,128)S(1)}, u32[]{:S(2)}, u32[]{:S(2)}) collective-permute-start(f32[4,128,256]{2,1,0:T(8,128)S(1)} %add.129), channel_id=1, source_target_pairs={{1,0},{2,3},{5,4},{6,7},{9,8},{10,11},{13,12},{14,15},{17,16},{18,... | collective-permute-start | bytes 1572872 | tf_op jit(solution)/shard_map/ppermute | solution.py:874
  (47 other events, 256.4 us)
Sparse Core Ops, SparseCore 0:
  167.7 147.2 reduce-scatter.1

commit v5 on v4

--- a/solution.py
+++ b/solution.py
@@ -20,50 +20,62 @@
 wide = jnp.float32
 narrow = jnp.bfloat16
 ATTEND_PARTS = 4
+SPREAD = (2, 1, 3, 0)
+SPLIT = {"back": ("backa", "backb"), "in": ("ina", "inb"), "q": ("qa", "qb")}
 ORDER = (
     "first back",
     "feed all",
     "first in",
     "attend all",
-    "first q1",
-    "first q2",
+    "embed all",
+    "first q",
+    "spread 0",
     "next in",
-    "embed all",
-    "next q1",
-    "fold in",
-    "finish back",
-    "spread 0",
     "spread 1",
     "spread 2",
     "spread 3",
-    "fold q1",
-    "exchange back",
+    "fold in",
+    "tables 0",
+    "next q",
+    "finish back",
+    "send backa",
     "finish in",
-    "next q2",
-    "tables 0",
-    "return back",
-    "finish q1",
-    "exchange in",
-    "fold q2",
+    "send backb",
+    "tables 1",
+    "exchange backa",
+    "send ina",
     "vector 0",
-    "tables 1",
-    "end back",
-    "return in",
-    "exchange q1",
-    "finish q2",
+    "exchange backb",
+    "return backa",
+    "fold q",
+    "end backa",
+    "send inb",
+    "return backb",
+    "exchange ina",
     "vector 1",
-    "return q1",
-    "exchange q2",
+    "finish q",
+    "send qa",
+    "send qb",
+    "end backb",
+    "return ina",
+    "exchange inb",
     "vector 2",
-    "end in",
-    "return q2",
+    "end ina",
+    "return inb",
+    "exchange qa",
     "vector 3",
-    "end q1",
-    "end q2",
+    "end inb",
+    "return qa",
+    "exchange qb",
     "vector 4",
+    "end qa",
+    "return qb",
+    "end qb",
 )
+PARTS = 1
 LITTLE = pl.CostEstimate(flops=1024, bytes_accessed=1024, transcendentals=0)
-ROOM = pltpu.CompilerParams(vmem_limit_bytes=48 * 2**20)
+ROOM = pltpu.CompilerParams(vmem_limit_bytes=32 * 2**20)
+MOST = pltpu.CompilerParams(vmem_limit_bytes=32 * 2**20)
 
 
 def shape(dims, dtype=wide):
@@ -124,38 +136,58 @@
     return jnp.where(entry == indices, 1.0, 0.0)
 
 
-def lookup_kernel(idx_ref, table_ref, total_ref, out_ref, halves):
-    width = table_ref.shape[1]
+def lookup_kernel(twice_ref, idx_ref, *refs):
+    tables, total_ref, out_ref, halves = refs[:-3], refs[-3], refs[-2], refs[-1]
+    entries, width = tables[0].shape
 
     @pl.when(pl.program_id(0) == 0)
     def _():
-        halves[:, :width], halves[:, width:] = two_halves(table_ref[...])
-
-    entry = lax.broadcasted_iota(jnp.int32, (idx_ref.shape[0], table_ref.shape[0]), 1)
-    counts = hits(entry, idx_ref[:, 0:1]) + hits(entry, idx_ref[:, 1:2])
-    rows = mul(counts.astype(narrow), halves[...])
-    out_ref[...] = total_ref[...] + rows[:, :width] + rows[:, width:]
-
-
-def add_rows(indices, table, total):
+        for one, table in enumerate(tables):
+            halves[one, :, :width], halves[one, :, width:] = two_halves(table[...])
+
+    entry = lax.broadcasted_iota(jnp.int32, (idx_ref.shape[0], entries), 1)
+
+    def add(one, counts):
+        rows = mul(counts.astype(narrow), halves[one])
+        out_ref[...] += rows[:, :width] + rows[:, width:]
+
+    out_ref[...] = total_ref[...]
+    for one in range(len(tables)):
+        first = idx_ref[:, 2 * one : 2 * one + 1]
+        second = idx_ref[:, 2 * one + 1 : 2 * one + 2]
+
+        @pl.when(twice_ref[one] == 1)
+        def _():
+            add(one, hits(entry, first) + hits(entry, second))
+
+        @pl.when(twice_ref[one] == 0)
+        def _():
+            add(one, hits(entry, first))
+
+
+def add_rows(twice, indices, tables, total, part, parts):
     tokens = total.shape[0]
-    entries, width = table.shape
+    entries, width = tables[0].shape
+    block = PAGE
+    steps = tokens // block // parts
     return pl.pallas_call(
         lookup_kernel,
-        grid=(tokens // PAGE,),
-        in_specs=[
-            pl.BlockSpec((PAGE, 2), lambda step: (step, 0)),
-            whole(entries, width),
-            pl.BlockSpec((PAGE, width), lambda step: (step, 0)),
-        ],
-        out_specs=pl.BlockSpec((PAGE, width), lambda step: (step, 0)),
-        out_shape=shape((tokens, width)),
-        scratch_shapes=[pltpu.VMEM((entries, 2 * width), narrow)],
-        input_output_aliases={2: 0},
+        grid_spec=pltpu.PrefetchScalarGridSpec(
+            num_scalar_prefetch=1,
+            grid=(steps,),
+            in_specs=[
+                pl.BlockSpec((block, indices.shape[1]), lambda step, *_: (steps * part + step, 0))
+            ]
+            + [whole(entries, width)] * len(tables)
+            + [pl.BlockSpec((block, width), lambda step, *_: (steps * part + step, 0))],
+            out_specs=pl.BlockSpec((block, width), lambda step, *_: (step, 0)),
+            scratch_shapes=[pltpu.VMEM((len(tables), entries, 2 * width), narrow)],
+        ),
+        out_shape=shape((tokens // parts, width)),
         compiler_params=ROOM,
         cost_estimate=LITTLE,
         name="look_up",
-    )(indices, table, total)
+    )(twice, indices, *tables, total)
 
 
 def spread_kernel(idx_ref, rows_ref, out_ref):
@@ -192,15 +224,16 @@
     )(indices, rows)
 
 
-def project_kernel(
-    parts, text, gain, bias, weight, weight_bias, packed, normed, inverse, low
-):
-    group, _, width = parts.shape
+def project_kernel(*refs):
+    parts, (text, gain, bias, weight, weight_bias) = refs[:-9], refs[-9:-4]
+    packed, normed, inverse, low = refs[-4:]
+    group, rows, width = parts[0].shape
 
     @pl.when(pl.program_id(0) == 0)
     def _():
-        for one in range(group):
-            normed[:, one * width : (one + 1) * width] = parts[one]
+        for at, part in enumerate(parts):
+            for one in range(group):
+                normed[at * rows : (at + 1) * rows, one * width : (one + 1) * width] = part[one]
         normed[...], inverse[...] = normalize(normed[...] + text[...].astype(wide))
         low[...] = (normed[...] * gain[...] + bias[...]).astype(narrow)
 
@@ -214,8 +247,8 @@
     return pl.pallas_call(
         project_kernel,
         grid=(steps,),
-        in_specs=[
-            whole(*parts.shape),
+        in_specs=[whole(*part.shape) for part in parts]
+        + [
             whole(tokens, width),
             whole(1, width),
             whole(1, width),
@@ -237,7 +270,7 @@
         compiler_params=ROOM,
         cost_estimate=LITTLE,
         name="embed_and_project",
-    )(parts, text, gain, bias, weight, weight_bias)
+    )(*parts, text, gain, bias, weight, weight_bias)
 
 
 def one_head(rows, head):
@@ -253,29 +286,24 @@
 
 def attend_kernel(
     queries, keys, values, weight, weight_bias, normed_emb, emb_gain, emb_bias, gain, bias,
-    context, normed, inverse, low, total,
+    context, normed, inverse, low,
 ):
     pair = pl.program_id(0)
-    summed = None
+    lane = lax.broadcasted_iota(jnp.int32, values.shape, 1)
+    parts = []
     for head in range(2):
-        probs = head_probs(queries[...], keys[...], head).astype(narrow)
-        part = mul(probs, one_head(values[...], head))
-        summed = part if summed is None else summed + part
-    context[...] = summed.astype(narrow)
-    share = mul(context[...], weight[...])
-
-    @pl.when(pair == 0)
-    def _():
-        total[...] = share
-
-    @pl.when(pair > 0)
-    def _():
-        total[...] += share
+        scores = mul_rows(one_head(queries[...], head), keys[...]) * HEAD ** (-0.5)
+        exponent = jnp.exp(scores - jnp.max(scores, -1, keepdims=True))
+        probs = exponent * (1.0 / jnp.sum(exponent, -1, keepdims=True))
+        parts.append(mul(probs.astype(narrow), values[...]))
+    place = pl.multiple_of(pair * PAIR, PAIR)
+    context[:, pl.ds(place, PAIR)] = jnp.where(lane < HEAD, parts[0], parts[1]).astype(narrow)
 
     @pl.when(pair == pl.num_programs(0) - 1)
     def _():
         hidden = normed_emb[...] * emb_gain[...] + emb_bias[...]
-        normed[...], inverse[...] = normalize(hidden + (total[...] + weight_bias[...]))
+        attended = mul(context[...], weight[...]) + weight_bias[...]
+        normed[...], inverse[...] = normalize(hidden + attended)
         low[...] = (normed[...] * gain[...] + bias[...]).astype(narrow)
 
 
@@ -290,7 +318,7 @@
             pl.BlockSpec((tokens, PAIR), lambda pair: (0, pair)),
             pl.BlockSpec((tokens, PAIR), lambda pair: (0, pairs + pair)),
             pl.BlockSpec((tokens, PAIR), lambda pair: (0, 2 * pairs + pair)),
-            pl.BlockSpec((PAIR, width), lambda pair: (pair, 0)),
+            whole(*weight.shape),
             vector,
             whole(tokens, width),
             vector,
@@ -299,7 +327,7 @@
             vector,
         ],
         out_specs=[
-            pl.BlockSpec((tokens, PAIR), lambda pair: (0, pair)),
+            whole(tokens, width),
             whole(tokens, width),
             whole(tokens, 1),
             whole(tokens, width),
@@ -310,7 +338,6 @@
             shape((tokens, 1)),
             shape((tokens, width), narrow),
         ],
-        scratch_shapes=[pltpu.VMEM((tokens, width), wide)],
         compiler_params=ROOM,
         cost_estimate=LITTLE,
         name="attend",
@@ -464,7 +491,7 @@
             shape((1, width)),
         ],
         scratch_shapes=[pltpu.VMEM((tokens, width), wide)],
-        compiler_params=ROOM,
+        compiler_params=MOST,
         cost_estimate=LITTLE,
         name="feed_back",
     )(d_returned, w_back, pre_act, w_in, d_r2, normed, inverse, gain)
@@ -512,7 +539,7 @@
             pl.BlockSpec((1, PAIR), lambda pair: (0, pair)),
         ],
         out_shape=[shape((3, tokens, width), narrow), shape((1, width)), shape((1, width))],
-        compiler_params=ROOM,
+        compiler_params=MOST,
         cost_estimate=LITTLE,
         name="attend_back",
     )(packed, packed, packed, d_attended, weight)
@@ -570,7 +597,7 @@
             shape((1, width)),
             shape((group, tokens, columns)),
         ],
-        compiler_params=ROOM,
+        compiler_params=MOST,
         cost_estimate=LITTLE,
         name="embed_back",
     )(d_packed, weight, d_r1, normed, inverse, gain)
@@ -590,7 +617,7 @@
         in_specs=[pl.BlockSpec((tokens, block), lambda row: (0, row)), whole(tokens, width)],
         out_specs=pl.BlockSpec((block, width), lambda row: (row, 0)),
         out_shape=shape((rows, width)),
-        compiler_params=ROOM,
+        compiler_params=MOST,
         cost_estimate=LITTLE,
         name="outer",
     )(left, right)
@@ -661,7 +688,7 @@
                 out_specs=self.block(count, 0),
             ),
             out_shape=shape((count, half * self.rows, self.width)),
-            compiler_params=ROOM,
+            compiler_params=MOST,
             cost_estimate=LITTLE,
             name="halving_first",
         )(table, *[one[0] for one in self.streams], *[one[1] for one in self.streams])
@@ -689,7 +716,7 @@
                 shape((part, quarter * self.rows, self.width))
                 for part in (count, count // 2, count // 2)
             ],
-            compiler_params=ROOM,
+            compiler_params=MOST,
             cost_estimate=LITTLE,
             name="halving_next",
         )(table, *lefts, *lefts, *[one[1] for one in self.streams], arrived, arrived)
@@ -824,11 +851,27 @@
     own_columns = lax.dynamic_slice_in_dim(layout_tables[0], inner * columns, columns, 1)
     table_columns = [own_columns] + [around(own_columns, offset) for offset in range(1, planes)]
     group_boxes = lax.all_gather(boxes, "pages", axis=1, tiled=True, axis_index_groups=groups)
-    looked_up = jnp.zeros((group * token_rows, columns), wide)
-    for offset in [0, 1, planes - 1] + list(range(2, planes - 1)):
-        uses = jnp.stack(table_indices(group_boxes, (plane + offset) % planes))
-        looked_up = add_rows(uses.T, table_columns[offset], looked_up)
-    parts = exchange(looked_up.reshape(group, token_rows, columns))
+    tables = [(plane + offset) % planes for offset in range(planes)]
+    twice = jnp.stack([jnp.where(table < 2, 1, 0) for table in tables]).astype(jnp.int32)
+    split_boxes = group_boxes.reshape(4, group, PARTS, token_rows // PARTS).swapaxes(1, 2)
+    split_boxes = split_boxes.reshape(4, group * token_rows)
+    uses = jnp.stack([one for table in tables for one in table_indices(split_boxes, table)]).T
+    looked_up = add_rows(
+        twice[:1],
+        uses[:, :2],
+        table_columns[:1],
+        jnp.zeros((group * token_rows, columns), wide),
+        0,
+        1,
+    )
+    parts = [
+        exchange(
+            add_rows(twice[1:], uses[:, 2:], table_columns[1:], looked_up, part, PARTS).reshape(
+                group, token_rows // PARTS, columns
+            )
+        )
+        for part in range(PARTS)
+    ]
 
     bias_qkv = jnp.concatenate([b_query, jnp.zeros_like(b_query), b_value])
     packed, normed_emb, inverse_emb, emb_low = embed_and_project(
@@ -905,17 +948,14 @@
             d_packed, g_query_bias, g_value_bias = attend_back(packed, token(d_attended), w_out)
             d_packed = token.after(d_packed)
             emb_rows = emb_low.T
-            context_rows = context_low.T
-            quarter = model_width // 4
-            for name, width, column in (("q1", 3 * quarter, 0), ("q2", quarter, 3)):
-                halvings[name] = Halving(
-                    me,
-                    masks_one,
-                    masks_two,
-                    [(emb_rows, d_packed, one, column) for one in range(3)]
-                    + [(context_rows, d_attended, 0, column)],
-                    width,
-                )
+            halvings["q"] = Halving(
+                me,
+                masks_one,
+                masks_two,
+                [(emb_rows, d_packed, one, 0) for one in range(3)]
+                + [(context_low.T, d_attended, 0, 0)],
+                model_width,
+            )
         elif kind == "first":
             halvings[name].start(token)
         elif kind == "next":
@@ -923,8 +963,15 @@
         elif kind == "fold":
             halvings[name].third(token)
         elif kind == "finish":
-            shares[name] = halvings[name].shares(token) if name in halvings else flight[name]
-            shares[name] = token.after(shares[name])
+            share = halvings[name].shares(token) if name in halvings else token(flight[name])
+            pieces = SPLIT.get(name, (name,))
+            size = share.shape[0] // len(pieces)
+            share = token.after(
+                *[share[at * size : (at + 1) * size] for at in range(len(pieces))]
+            )
+            shares.update(zip(pieces, share))
+        elif kind == "send":
+            shares[name] = token(shares[name])
             flight[name] = inward(shares[name])
         elif kind == "exchange":
             shares[name] = token.after(shares[name] + token(flight[name]))
@@ -949,14 +996,13 @@
         elif kind == "spread":
             if name == "0":
                 embed_columns = token(flight["h"]).reshape(group * token_rows, columns)
-            uses = jnp.stack(table_indices(group_boxes, int(name)))
-            flight["t" + name] = token.after(spread_rows(token(uses), embed_columns, entries))
-            if int(name) == planes - 1:
-                table_shares = jnp.concatenate([flight["t" + str(one)] for one in range(planes)], 0)
-                flight["t"] = lax.all_to_all(table_shares, "emb", 0, 0, tiled=True)
+            offset = SPREAD[int(name)]
+            uses = jnp.stack(table_indices(group_boxes, (plane + offset) % planes))
+            part = token.after(spread_rows(token(uses), embed_columns, entries))
+            flight["t" + name] = around(part, planes - offset) if offset else part
         elif step == "tables 0":
-            owned = token(flight["t"]).reshape(planes, entries, columns)
-            table_total = token.after(functools.reduce(jnp.add, list(owned)))
+            owned = token(*[flight["t" + str(at)] for at in range(planes)])
+            table_total = token.after(functools.reduce(jnp.add, owned))
             row_masks = [mask for mask in masks_one if mask >= group]
             if row_masks:
                 table_total = halve(
@@ -1003,11 +1049,12 @@
         elif step == "vector 4":
             middle = jnp.logical_or(plane == 1, plane == 2)
             vector_share = jnp.where(middle, vector_share, token(flight["v4"]))[0]
+    for name, pieces in SPLIT.items():
+        shares[name] = jnp.concatenate([shares[one] for one in pieces], 0)
     g_back = shares["back"]
     g_in = jnp.concatenate(list(shares["in"]), 1)
-    g_four = jnp.concatenate([shares["q1"], shares["q2"]], 2)
-    g_qkv = jnp.concatenate(list(g_four[:3]), 1)
-    g_out = g_four[3]
+    g_qkv = jnp.concatenate(list(shares["q"][:3]), 1)
+    g_out = shares["q"][3]
 
     totals = []
     first = 0

time: 657 us -> 644 us (0.980)
  waiting for transfers between devices: 176 us -> 227 us
  Pallas kernels: 206 us -> 165 us
  starting transfers between devices: 125 us -> 108 us
  other arithmetic: 37.4 us -> 27.3 us
    ppermute x15 -> x10, waiting for transfers between devices: 63.5 us -> 11.4 us  [swap(): lax.ppermute(array, 'pages', [(one, one ^ mask) for one in range(lax.axis...]
    all_to_all x3, waiting for transfers between devices: 30.8 us -> 70.4 us  [exchange(): lax.all_to_all(blocks, 'pages', 0, 0, tiled=True, axis_index_groups=groups)]
    ppermute x3 -> x6, starting transfers between devices: 6.11 us -> 34.2 us  [around(): lax.ppermute(array, 'emb', [((one + offset) % planes, one) for one in ran...]
    ppermute x4 -> x6, starting transfers between devices: 51.8 us -> 32.7 us  [inward(): return lax.ppermute(share, 'emb', [(0, 1), (3, 2)])]
    ppermute x1, starting transfers between devices: 20.2 us -> 1.29 us  [on_device(): flight['v2'] = lax.ppermute(vector_share, 'emb', [(0, 1), (3, 2)])]
    ppermute x1, waiting for transfers between devices: 1.34 us -> 19.8 us  [on_device(): flight['v2'] = lax.ppermute(vector_share, 'emb', [(0, 1), (3, 2)])]
    ppermute x1, waiting for transfers between devices: 0.01 us -> 18.5 us  [on_device(): flight['v4'] = lax.ppermute(vector_share, 'emb', [(1, 0), (2, 3)])]
    ppermute x4 -> x6, waiting for transfers between devices: 22.1 us -> 39.8 us  [inward(): return lax.ppermute(share, 'emb', [(0, 1), (3, 2)])]
  transfers between devices with their start and end apart: 38 -> 41, of which waited for: 16 -> 15; matrix products, arithmetic and copies ran while one was open for 11% -> 7% of each run, Pallas kernels for 21% -> 16%
where the time goes in v5:
time: 644 us; the launch traced here: 636 us
  waiting for transfers between devices  227 us (35%)
  Pallas kernels  165 us (26%)
  starting transfers between devices  108 us (17%)
  local copies, waits for them, and re-layouts  75.1 us (12%)
  other arithmetic  27.3 us (4%)
  between operations  17.7 us (3%)
  blocking collectives  16.7 us (3%)
    all_to_all x3, waiting for transfers between devices, exchange(): lax.all_to_all(blocks, 'pages', 0, 0, tiled=True, axis_index_groups=groups)  70.4 us
    unnamed x159, local copies, waits for them, and re-layouts  54.4 us
    ppermute x6, waiting for transfers between devices, outward(): return lax.ppermute(share, 'emb', [(1, 0), (2, 3)])  50.7 us
    ppermute x6, waiting for transfers between devices, inward(): return lax.ppermute(share, 'emb', [(0, 1), (3, 2)])  39.8 us
    ppermute x6, starting transfers between devices, around(): lax.ppermute(array, 'emb', [((one + offset) % planes, one) for one in ran...  34.2 us
    ppermute x6, starting transfers between devices, inward(): return lax.ppermute(share, 'emb', [(0, 1), (3, 2)])  32.7 us
    pallas_call x2, Pallas kernels, add_rows(): pl.pallas_call(lookup_kernel, grid_spec=pltpu.PrefetchScalarGridSpec(num_...  24.2 us
    pallas_call x1, Pallas kernels, attend_back(): pl.pallas_call(attend_back_kernel, grid=(pairs,), in_specs=[pl.BlockSpec(...  22.8 us
  transfers between devices with their start and end apart: 41, of which 15 were waited for; matrix products, arithmetic and copies ran while one was open for 7% of the time, Pallas kernels for 16%

profile of v5, /device:TPU:0, one launch (start us, length us, event | category | flops | bytes accessed | tf_op | source)
XLA Modules:
  0.0 635.9 jit_solution(5028647134152937604)
XLA Ops:
  8.3 3.1 collective-permute-start.2
  15.3 9.4 %all_gather.3 = s32[4,4096]{1,0:T(4,128)S(1)} all-gather(s32[4,512]{1,0:T(4,128)} %param.24), channel_id=1, replica_groups={{0,4,8,12,16,20,24,28},{1,5,9,13,17,21,25,29},{2,6,10,14,18,22,26,30},{..., dimensions={1}, use_global_device_ids=true | all-gather | bytes 73728 | tf_op jit(solution)/shard_map/all_gather | solution.py:853
  26.0 6.1 look_up.2.refs_3_
  35.4 12.6 %collective-permute-done.1.refs_1_ = f32[1024,128]{1,0:T(8,128)} collective-permute-done((f32[1024,128]{1,0:T(8,128)S(1)}, f32[1024,128]{1,0:T(8,128)}, u32[]{:S(2)}, u32[]{:S(2)}) %collective-permute-start.1) | collective-permute-done | bytes 524320 | tf_op jit(solution)/shard_map/ppermute | solution.py:844
  49.6 18.1 %look_up.3 = f32[4096,128]{1,0:T(8,128)S(1)} custom-call(s32[3]{0:T(128)S(1)} %pad_add_fusion.5.twice_ref, s32[4096,6]{1,0:T(8,128)S(1)} %copy-done.21, f32[1024,128]{1,0:T(8,128)} %collective-permute-done.refs_0_, f32[1024,128]{1,0:T(8,128)} %collective-permute-done.1.refs_1_, f32[1024,128]{1,0:T(8,128)S(1)} %collective-permute-done.2.refs_2_, ...), custom_call_target="tpu_custom_call" | custom-call | flops 1024 | bytes 1024 | tf_op jit(solution)/shard_map/look_up/pallas_call | solution.py:173
  69.1 3.9 all-to-all-start
  73.1 26.6 %all-to-all-done.refs_0_ = f32[8,512,128]{2,1,0:T(8,128)S(1)} async-done(((f32[8,512,128]{2,1,0:T(8,128)}), f32[8,512,128]{2,1,0:T(8,128)S(1)}, u32[]{:S(2)}, u32[]{:S(2)}) %all-to-all-start) | async-done | bytes 2097184 | tf_op jit(solution)/shard_map/all_to_all | solution.py:849
  102.4 6.2 embed_and_project.1
  109.7 13.6 %attend.1 = (bf16[512,1024]{1,0:T(8,128)(2,1)S(1)}, f32[512,1024]{1,0:T(8,128)S(1)}, f32[512,1]{1,0:T(8,128)S(1)}, bf16[512,1024]{1,0:T(8,128)(2,1)S(1)}) custom-call(bf16[512,3072]{1,0:T(8,128)(2,1)S(1)} %get-tuple-element.253.queries.keys.values, bf16[512,3072]{1,0:T(8,128)(2,1)S(1)} %get-tuple-element.253.queries.keys.values, ...), custom_call_target="tpu_custom_call" | custom-call | flops 1024 | bytes 1024 | tf_op jit(solution)/shard_map/attend/pallas_call | solution.py:314
  123.4 18.9 %feed.1 = (f32[512,4096]{1,0:T(8,128)S(1)}, bf16[512,4096]{1,0:T(8,128)(2,1)S(1)}, bf16[512,1024]{1,0:T(8,128)(2,1)}, f32[512,1024]{1,0:T(8,128)S(1)}, bf16[512,...) custom-call(bf16[512,1024]{1,0:T(8,128)(2,1)S(1)} %get-tuple-element.256.low, ...), custom_call_target="tpu_custom_call" | custom-call | flops 1024 | bytes 1024 | tf_op jit(solution)/shard_map/feed/pallas_call | solution.py:386
  142.3 3.4 copy-done.23
  147.0 6.3 outer.1
  153.3 5.8 copy-done.8
  160.8 3.4 copy-done.9
  167.0 17.9 %feed_back.1 = (bf16[512,4096]{1,0:T(8,128)(2,1)S(1)}, f32[1,4096]{1,0:T(1,128)S(1)}, f32[512,1024]{1,0:T(8,128)S(1)}, bf16[512,1024]{1,0:T(8,128)(2,1)S(1)}, f3...) custom-call(bf16[512,1024]{1,0:T(8,128)(2,1)S(1)} %copy-done.30, ...), custom_call_target="tpu_custom_call" | custom-call | flops 1024 | bytes 1024 | tf_op jit(solution)/shard_map/feed_back/pallas_call | solution.py:462
  193.5 5.9 halving_first.2
  199.4 22.8 %attend_back.1 = (bf16[3,512,1024]{2,1,0:T(8,128)(2,1)S(1)}, f32[1,1024]{1,0:T(1,128)S(1)}, f32[1,1024]{1,0:T(1,128)S(1)}) custom-call(bf16[512,3072]{1,0:T(8,128)(2,1)S(1)} %copy-done.7, bf16[512,3072]{1,0:T(8,128)(2,1)S(1)} %copy-done.7, bf16[512,3072]{1,0:T(8,128)(2,1)S(1)} %copy-done.7, ...), custom_call_target="tpu_custom_call" | custom-call | flops 1024 | bytes 1024 | tf_op jit(solution)/shard_map/attend_back/pallas_call | solution.py:526
  222.3 4.0 copy-done.11
  226.3 9.2 %embed_back.1 = (f32[512,1024]{1,0:T(8,128)}, f32[1,1024]{1,0:T(1,128)S(1)}, f32[1,1024]{1,0:T(1,128)S(1)}, f32[1,1024]{1,0:T(1,128)S(1)}, f32[8,512,128]{2,1,0:T(8,128)S(1)}) custom-call(bf16[3,512,1024]{2,1,0:T(8,128)(2,1)S(1)} %get-tuple-element.280.d_packed.refs_4_.refs_5_.refs_6_.refs_8_.refs_9_.refs_10_, bf16[1024,3072]{1,0:T(8,128)(2,1)S(1)} %copy-done.11, ...), custom_call_target="tpu_custom_call" | custom-call | flops 1024 | bytes 1024 | tf_op jit(solution)/shard_map/embed_back/pallas_call | solution.py:580
  242.2 5.4 halving_first.3
  248.2 4.6 all-to-all-start.1
  252.8 43.9 %all-to-all-done.1 = f32[8,512,128]{2,1,0:T(8,128)} async-done(((f32[8,512,128]{2,1,0:T(8,128)}), f32[8,512,128]{2,1,0:T(8,128)}, u32[]{:S(2)}, u32[]{:S(2)}) %all-to-all-start.1) | async-done | bytes 2097184 | tf_op jit(solution)/shard_map/all_to_all | solution.py:849
  296.7 5.6 spread.4
  304.5 6.0 halving_next.2
  311.9 12.9 %collective-permute-start.4 = (f32[1024,128]{1,0:T(8,128)S(1)}, f32[1024,128]{1,0:T(8,128)S(1)}, u32[]{:S(2)}, u32[]{:S(2)}) collective-permute-start(f32[1024,128]{1,0:T(8,128)S(1)} %spread.4), channel_id=1, source_target_pairs={{2,0},{3,1},{0,2},{1,3},{6,4},{7,5},{4,6},{5,7},{10,8},{11,9},{8,1... | collective-permute-start | bytes 1572872 | tf_op jit(solution)/shard_map/ppermute | solution.py:844
  324.8 5.6 spread.5
  330.5 5.6 spread.6
  336.1 5.6 spread.7
  343.2 11.4 %collective-permute-done.8 = f32[2,256,1024]{2,1,0:T(8,128)S(1)} collective-permute-done((f32[2,256,1024]{2,1,0:T(8,128)S(1)}, f32[2,256,1024]{2,1,0:T(8,128)S(1)}, u32[]{:S(2)}, u32[]{:S(2)}) %collective-permute-start.8) | collective-permute-done | bytes 2097184 | tf_op jit(solution)/shard_map/ppermute | solution.py:772
  354.6 12.8 %collective-permute-start.6 = (f32[1024,128]{1,0:T(8,128)S(1)}, f32[1024,128]{1,0:T(8,128)S(1)}, u32[]{:S(2)}, u32[]{:S(2)}) collective-permute-start(f32[1024,128]{1,0:T(8,128)S(1)} %spread.5), channel_id=1, source_target_pairs={{3,0},{0,1},{1,2},{2,3},{7,4},{4,5},{5,6},{6,7},{11,8},{8,9},{9,10... | collective-permute-start | bytes 1572872 | tf_op jit(solution)/shard_map/ppermute | solution.py:844
  374.4 3.5 collective-permute-done.6
  378.8 6.0 halving_next.3
  389.4 5.0 all-to-all-start.2
  402.7 3.0 fusion.1
  409.8 15.5 %collective-permute-done.12 = f32[256,1024]{1,0:T(8,128)} collective-permute-done((f32[256,1024]{1,0:T(8,128)S(1)}, f32[256,1024]{1,0:T(8,128)}, u32[]{:S(2)}, u32[]{:S(2)}) %collective-permute-start.12) | collective-permute-done | bytes 1048608 | tf_op jit(solution)/shard_map/ppermute | solution.py:911
  430.8 7.5 %collective-permute-start.19 = (f32[2,128,1024]{2,1,0:T(8,128)}, f32[2,128,1024]{2,1,0:T(8,128)}, u32[]{:S(2)}, u32[]{:S(2)}) collective-permute-start(f32[2,128,1024]{2,1,0:T(8,128)} %get-tuple-element.392), channel_id=1, source_target_pairs={{0,1},{3,2},{4,5},{7,6},{8,9},{11,10},{12,13},{15,14},{16,17},{19,... | collective-permute-start | bytes 3145736 | tf_op jit(solution)/shard_map/ppermute | solution.py:911
  438.4 9.4 %collective-permute-done.16 = f32[256,1024]{1,0:T(8,128)} collective-permute-done((f32[256,1024]{1,0:T(8,128)S(1)}, f32[256,1024]{1,0:T(8,128)}, u32[]{:S(2)}, u32[]{:S(2)}) %collective-permute-start.16) | collective-permute-done | bytes 1048608 | tf_op jit(solution)/shard_map/ppermute | solution.py:911
  462.1 16.0 %collective-permute-done.21 = f32[256,1024]{1,0:T(8,128)S(1)} collective-permute-done((f32[256,1024]{1,0:T(8,128)S(1)}, f32[256,1024]{1,0:T(8,128)S(1)}, u32[]{:S(2)}, u32[]{:S(2)}) %collective-permute-start.21) | collective-permute-done | bytes 1048608 | tf_op jit(solution)/shard_map/ppermute | solution.py:917
  485.4 7.4 %all_to_all.27 = f32[8,1,1793]{2,1,0:T(1,128)S(1)} all-to-all(f32[8,1,1793]{2,1,0:T(1,128)S(1)} %all_to_all.20), channel_id=1, replica_groups=mesh['pages'=8,'emb'=4] {'pages'}, dimensions={0} | all-to-all | bytes 114752 | tf_op jit(solution)/shard_map/all_to_all | solution.py:1039
  492.8 6.4 %collective-permute-start.24 = (f32[2,128,1024]{2,1,0:T(8,128)S(1)}, f32[2,128,1024]{2,1,0:T(8,128)S(1)}, u32[]{:S(2)}, u32[]{:S(2)}) collective-permute-start(f32[2,128,1024]{2,1,0:T(8,128)S(1)} %copy-done.56), channel_id=1, source_target_pairs={{0,1},{3,2},{4,5},{7,6},{8,9},{11,10},{12,13},{15,14},{16,17},{19,... | collective-permute-start | bytes 3145736 | tf_op jit(solution)/shard_map/ppermute | solution.py:911
  499.2 3.7 fusion
  508.2 13.1 %collective-permute-done.24 = f32[2,128,1024]{2,1,0:T(8,128)S(1)} collective-permute-done((f32[2,128,1024]{2,1,0:T(8,128)S(1)}, f32[2,128,1024]{2,1,0:T(8,128)S(1)}, u32[]{:S(2)}, u32[]{:S(2)}) %collective-permute-start.24) | collective-permute-done | bytes 1048608 | tf_op jit(solution)/shard_map/ppermute | solution.py:911
  522.2 7.1 %collective-permute-start.23 = (f32[2,128,1024]{2,1,0:T(8,128)S(1)}, f32[2,128,1024]{2,1,0:T(8,128)S(1)}, u32[]{:S(2)}, u32[]{:S(2)}) collective-permute-start(f32[2,128,1024]{2,1,0:T(8,128)S(1)} %get-tuple-element.418), channel_id=1, source_target_pairs={{0,1},{3,2},{4,5},{7,6},{8,9},{11,10},{12,13},{15,14},{16,17},{19,... | collective-permute-start | bytes 3145736 | tf_op jit(solution)/shard_map/ppermute | solution.py:911
  530.6 19.8 %collective-permute-done.29 = f32[1,1793]{1,0:T(1,128)S(1)} collective-permute-done((f32[1,1793]{1,0:T(1,128)S(1)}, f32[1,1793]{1,0:T(1,128)S(1)}, u32[]{:S(2)}, u32[]{:S(2)}) %collective-permute-start.29) | collective-permute-done | bytes 7204 | tf_op jit(solution)/shard_map/ppermute | solution.py:1042
  553.1 6.4 %collective-permute-start.22 = (f32[2,128,1024]{2,1,0:T(8,128)S(1)}, f32[2,128,1024]{2,1,0:T(8,128)S(1)}, u32[]{:S(2)}, u32[]{:S(2)}) collective-permute-start(f32[2,128,1024]{2,1,0:T(8,128)S(1)} %get-tuple-element.417), channel_id=1, source_target_pairs={{0,1},{3,2},{4,5},{7,6},{8,9},{11,10},{12,13},{15,14},{16,17},{19,... | collective-permute-start | bytes 3145736 | tf_op jit(solution)/shard_map/ppermute | solution.py:911
  560.2 15.3 %collective-permute-done.31 = f32[2,128,1024]{2,1,0:T(8,128)S(1)} collective-permute-done((f32[2,128,1024]{2,1,0:T(8,128)S(1)}, f32[2,128,1024]{2,1,0:T(8,128)S(1)}, u32[]{:S(2)}, u32[]{:S(2)}) %collective-permute-start.31) | collective-permute-done | bytes 1048608 | tf_op jit(solution)/shard_map/ppermute | solution.py:917
  582.9 18.5 %collective-permute-done.35 = f32[1,1793]{1,0:T(1,128)S(1)} collective-permute-done((f32[1,1793]{1,0:T(1,128)S(1)}, f32[1,1793]{1,0:T(1,128)S(1)}, u32[]{:S(2)}, u32[]{:S(2)}) %collective-permute-start.35) | collective-permute-done | bytes 7204 | tf_op jit(solution)/shard_map/ppermute | solution.py:1048
  607.0 18.3 %collective-permute-done.36 = f32[2,128,1024]{2,1,0:T(8,128)S(1)} collective-permute-done((f32[2,128,1024]{2,1,0:T(8,128)S(1)}, f32[2,128,1024]{2,1,0:T(8,128)S(1)}, u32[]{:S(2)}, u32[]{:S(2)}) %collective-permute-start.36) | collective-permute-done | bytes 1048608 | tf_op jit(solution)/shard_map/ppermute | solution.py:917
  (285 shorter events, 119.9 us)
Async XLA Ops:
  8.3 27.1 %collective-permute-start.2 = (f32[1024,128]{1,0:T(8,128)S(1)}, f32[1024,128]{1,0:T(8,128)S(1)}, u32[]{:S(2)}, u32[]{:S(2)}) collective-permute-start(f32[1024,128]{1,0:T(8,128)S(1)} %dynamic-slice_bitcast_fusion.refs_0_), channel_id=1, source_target_pairs={{3,0},{0,1},{1,2},{2,3},{7,4},{4,5},{5,6},{6,7},{11,8},{8,9},{9,10... | collective-permute-start | bytes 1572872 | tf_op jit(solution)/shard_map/ppermute | solution.py:844
  11.4 36.7 %collective-permute-start.1 = (f32[1024,128]{1,0:T(8,128)S(1)}, f32[1024,128]{1,0:T(8,128)}, u32[]{:S(2)}, u32[]{:S(2)}) collective-permute-start(f32[1024,128]{1,0:T(8,128)S(1)} %dynamic-slice_bitcast_fusion.refs_0_), channel_id=1, source_target_pairs={{2,0},{3,1},{0,2},{1,3},{6,4},{7,5},{4,6},{5,7},{10,8},{11,9},{8,1... | collective-permute-start | bytes 1572872 | tf_op jit(solution)/shard_map/ppermute | solution.py:844
  14.0 34.1 %collective-permute-start = (f32[1024,128]{1,0:T(8,128)S(1)}, f32[1024,128]{1,0:T(8,128)}, u32[]{:S(2)}, u32[]{:S(2)}) collective-permute-start(f32[1024,128]{1,0:T(8,128)S(1)} %dynamic-slice_bitcast_fusion.refs_0_), channel_id=1, source_target_pairs={{1,0},{2,1},{3,2},{0,3},{5,4},{6,5},{7,6},{4,7},{9,8},{10,9},{11,1... | collective-permute-start | bytes 1572872 | tf_op jit(solution)/shard_map/ppermute | solution.py:844
  69.1 30.5 %copy-start.36 = (bf16[512,1024]{1,0:T(8,128)(2,1)S(1)}, bf16[512,1024]{1,0:T(8,128)(2,1)}, u32[]{:S(2)}) copy-start(bf16[512,1024]{1,0:T(8,128)(2,1)} %refs_1_.1) | copy-start | bytes 3145732
  69.1 30.5 %copy-start.43 = (f32[1024]{0:T(1024)S(1)}, f32[1024]{0:T(1024)}, u32[]{:S(2)}) copy-start(f32[1024]{0:T(1024)} %param.26) | copy-start | bytes 12292
  69.1 30.5 %copy-start.45 = (f32[1024]{0:T(1024)S(1)}, f32[1024]{0:T(1024)}, u32[]{:S(2)}) copy-start(f32[1024]{0:T(1024)} %param.27) | copy-start | bytes 12292
  69.1 30.5 %all-to-all-start = ((f32[8,512,128]{2,1,0:T(8,128)}), f32[8,512,128]{2,1,0:T(8,128)S(1)}, u32[]{:S(2)}, u32[]{:S(2)}) async-start(f32[8,512,128]{2,1,0:T(8,128)} %bitcast.115), calls=%async_computation | async-start | bytes 4194304 | tf_op jit(solution)/shard_map/all_to_all | solution.py:849
  73.0 325.0 %reduce-scatter.2.cloned.1.call-start = ((), (), s32[]{:S(2)}) async-start(), calls=%async_computation.5 | async-start | bytes 18874368 | tf_op jit(solution)/shard_map/reduce_scatter | solution.py:908
  199.4 22.9 %copy-start.16 = (f32[512,1024]{1,0:T(8,128)S(1)}, f32[512,1024]{1,0:T(8,128)}, u32[]{:S(2)}) copy-start(f32[512,1024]{1,0:T(8,128)} %copy-done.15) | copy-start | bytes 6291460
  199.4 22.9 %copy-start.34 = (f32[512,1024]{1,0:T(8,128)S(1)}, f32[512,1024]{1,0:T(8,128)}, u32[]{:S(2)}) copy-start(f32[512,1024]{1,0:T(8,128)} %copy-done.33) | copy-start | bytes 6291460
  199.4 22.9 %copy-start.42 = (f32[512,1]{1,0:T(8,128)S(1)}, f32[512,1]{1,0:T(8,128)}, u32[]{:S(2)}) copy-start(f32[512,1]{1,0:T(8,128)} %copy-done.41) | copy-start | bytes 6148
  199.4 103.0 %collective-permute-start.5 = (f32[4,512,1024]{2,1,0:T(8,128)}, f32[4,512,1024]{2,1,0:T(8,128)}, u32[]{:S(2)}, u32[]{:S(2)}) collective-permute-start(f32[4,512,1024]{2,1,0:T(8,128)} %halving_first.2), channel_id=1, source_target_pairs={{0,4},{4,0},{8,12},{12,8},{16,20},{20,16},{24,28},{28,24},{1,5},{5... | collective-permute-start | bytes 25165832 | tf_op jit(solution)/shard_map/ppermute | solution.py:772
  247.7 131.1 %collective-permute-start.3 = (f32[4,512,1024]{2,1,0:T(8,128)}, f32[4,512,1024]{2,1,0:T(8,128)}, u32[]{:S(2)}, u32[]{:S(2)}) collective-permute-start(f32[4,512,1024]{2,1,0:T(8,128)} %halving_first.3), channel_id=1, source_target_pairs={{0,4},{4,0},{8,12},{12,8},{16,20},{20,16},{24,28},{28,24},{1,5},{5... | collective-permute-start | bytes 25165832 | tf_op jit(solution)/shard_map/ppermute | solution.py:772
  248.2 48.5 %all-to-all-start.1 = ((f32[8,512,128]{2,1,0:T(8,128)}), f32[8,512,128]{2,1,0:T(8,128)}, u32[]{:S(2)}, u32[]{:S(2)}) async-start(f32[8,512,128]{2,1,0:T(8,128)} %copy-done.35), calls=%async_computation.1 | async-start | bytes 4194304 | tf_op jit(solution)/shard_map/all_to_all | solution.py:849
  310.5 57.4 %copy-start.27 = (f32[4,256,1024]{2,1,0:T(8,128)}, f32[4,256,1024]{2,1,0:T(8,128)S(1)}, u32[]{:S(2)}) copy-start(f32[4,256,1024]{2,1,0:T(8,128)S(1)} %get-tuple-element.318) | copy-start | bytes 12582916
  310.5 44.0 %collective-permute-start.8 = (f32[2,256,1024]{2,1,0:T(8,128)S(1)}, f32[2,256,1024]{2,1,0:T(8,128)S(1)}, u32[]{:S(2)}, u32[]{:S(2)}) collective-permute-start(f32[2,256,1024]{2,1,0:T(8,128)S(1)} %get-tuple-element.319), channel_id=1, source_target_pairs={{0,8},{4,12},{8,0},{12,4},{16,24},{20,28},{24,16},{28,20},{1,9},{5... | collective-permute-start | bytes 6291464 | tf_op jit(solution)/shard_map/ppermute | solution.py:772
  310.6 56.8 %collective-permute-start.9 = (f32[2,256,1024]{2,1,0:T(8,128)S(1)}, f32[2,256,1024]{2,1,0:T(8,128)S(1)}, u32[]{:S(2)}, u32[]{:S(2)}) collective-permute-start(f32[2,256,1024]{2,1,0:T(8,128)S(1)} %get-tuple-element.320), channel_id=1, source_target_pairs={{0,16},{4,20},{8,24},{12,28},{16,0},{20,4},{24,8},{28,12},{1,17},{... | collective-permute-start | bytes 6291464 | tf_op jit(solution)/shard_map/ppermute | solution.py:772
  311.9 61.0 %collective-permute-start.4 = (f32[1024,128]{1,0:T(8,128)S(1)}, f32[1024,128]{1,0:T(8,128)S(1)}, u32[]{:S(2)}, u32[]{:S(2)}) collective-permute-start(f32[1024,128]{1,0:T(8,128)S(1)} %spread.4), channel_id=1, source_target_pairs={{2,0},{3,1},{0,2},{1,3},{6,4},{7,5},{4,6},{5,7},{10,8},{11,9},{8,1... | collective-permute-start | bytes 1572872 | tf_op jit(solution)/shard_map/ppermute | solution.py:844
  341.7 32.7 %collective-permute-start.7 = (f32[1024,128]{1,0:T(8,128)S(1)}, f32[1024,128]{1,0:T(8,128)S(1)}, u32[]{:S(2)}, u32[]{:S(2)}) collective-permute-start(f32[1024,128]{1,0:T(8,128)S(1)} %spread.6), channel_id=1, source_target_pairs={{1,0},{2,1},{3,2},{0,3},{5,4},{6,5},{7,6},{4,7},{9,8},{10,9},{11,1... | collective-permute-start | bytes 1572872 | tf_op jit(solution)/shard_map/ppermute | solution.py:844
  354.6 23.3 %collective-permute-start.6 = (f32[1024,128]{1,0:T(8,128)S(1)}, f32[1024,128]{1,0:T(8,128)S(1)}, u32[]{:S(2)}, u32[]{:S(2)}) collective-permute-start(f32[1024,128]{1,0:T(8,128)S(1)} %spread.5), channel_id=1, source_target_pairs={{3,0},{0,1},{1,2},{2,3},{7,4},{4,5},{5,6},{6,7},{11,8},{8,9},{9,10... | collective-permute-start | bytes 1572872 | tf_op jit(solution)/shard_map/ppermute | solution.py:844
  371.5 31.2 %collective-permute-start.13 = (f32[2,128,1024]{2,1,0:T(8,128)}, f32[2,128,1024]{2,1,0:T(8,128)}, u32[]{:S(2)}, u32[]{:S(2)}) collective-permute-start(f32[2,128,1024]{2,1,0:T(8,128)} %get-tuple-element.349), channel_id=1, source_target_pairs={{0,16},{4,20},{8,24},{12,28},{16,0},{20,4},{24,8},{28,12},{1,17},{... | collective-permute-start | bytes 3145736 | tf_op jit(solution)/shard_map/ppermute | solution.py:772
  372.9 29.8 %collective-permute-start.14 = (f32[2,128,1024]{2,1,0:T(8,128)}, f32[2,128,1024]{2,1,0:T(8,128)}, u32[]{:S(2)}, u32[]{:S(2)}) collective-permute-start(f32[2,128,1024]{2,1,0:T(8,128)} %get-tuple-element.350), channel_id=1, source_target_pairs={{0,8},{4,12},{8,0},{12,4},{16,24},{20,28},{24,16},{28,20},{1,9},{5... | collective-permute-start | bytes 3145736 | tf_op jit(solution)/shard_map/ppermute | solution.py:772
  389.4 17.9 %all-to-all-start.2 = ((f32[8,128,128]{2,1,0:T(8,128)}), f32[8,128,128]{2,1,0:T(8,128)S(1)}, u32[]{:S(2)}, u32[]{:S(2)}) async-start(f32[8,128,128]{2,1,0:T(8,128)} %bitcast.142), calls=%async_computation.3 | async-start | bytes 1048576 | tf_op jit(solution)/shard_map/all_to_all | solution.py:849
  394.4 59.0 %collective-permute-start.10 = (f32[2,256,1024]{2,1,0:T(8,128)}, f32[2,256,1024]{2,1,0:T(8,128)}, u32[]{:S(2)}, u32[]{:S(2)}) collective-permute-start(f32[2,256,1024]{2,1,0:T(8,128)} %copy-done.53), channel_id=1, source_target_pairs={{0,8},{4,12},{8,0},{12,4},{16,24},{20,28},{24,16},{28,20},{1,9},{5... | collective-permute-start | bytes 6291464 | tf_op jit(solution)/shard_map/ppermute | solution.py:772
  396.5 57.0 %collective-permute-start.11 = (f32[2,256,1024]{2,1,0:T(8,128)}, f32[2,256,1024]{2,1,0:T(8,128)}, u32[]{:S(2)}, u32[]{:S(2)}) collective-permute-start(f32[2,256,1024]{2,1,0:T(8,128)} %copy-done.52), channel_id=1, source_target_pairs={{0,16},{4,20},{8,24},{12,28},{16,0},{20,4},{24,8},{28,12},{1,17},{... | collective-permute-start | bytes 6291464 | tf_op jit(solution)/shard_map/ppermute | solution.py:772
  399.8 25.5 %collective-permute-start.12 = (f32[256,1024]{1,0:T(8,128)S(1)}, f32[256,1024]{1,0:T(8,128)}, u32[]{:S(2)}, u32[]{:S(2)}) collective-permute-start(f32[256,1024]{1,0:T(8,128)S(1)} %get-tuple-element.346), channel_id=1, source_target_pairs={{0,1},{3,2},{4,5},{7,6},{8,9},{11,10},{12,13},{15,14},{16,17},{19,... | collective-permute-start | bytes 3145736 | tf_op jit(solution)/shard_map/ppermute | solution.py:911
  407.5 40.3 %collective-permute-start.16 = (f32[256,1024]{1,0:T(8,128)S(1)}, f32[256,1024]{1,0:T(8,128)}, u32[]{:S(2)}, u32[]{:S(2)}) collective-permute-start(f32[256,1024]{1,0:T(8,128)S(1)} %get-tuple-element.363), channel_id=1, source_target_pairs={{0,1},{3,2},{4,5},{7,6},{8,9},{11,10},{12,13},{15,14},{16,17},{19,... | collective-permute-start | bytes 3145736 | tf_op jit(solution)/shard_map/ppermute | solution.py:911
  426.7 24.1 %collective-permute-start.15 = (f32[256,1024]{1,0:T(8,128)S(1)}, f32[256,1024]{1,0:T(8,128)}, u32[]{:S(2)}, u32[]{:S(2)}) collective-permute-start(f32[256,1024]{1,0:T(8,128)S(1)} %add.121), channel_id=1, source_target_pairs={{1,2},{2,1},{5,6},{6,5},{9,10},{10,9},{13,14},{14,13},{17,18},{18,... | collective-permute-start | bytes 3145736 | tf_op jit(solution)/shard_map/ppermute | solution.py:914
  430.8 51.1 %collective-permute-start.19 = (f32[2,128,1024]{2,1,0:T(8,128)}, f32[2,128,1024]{2,1,0:T(8,128)}, u32[]{:S(2)}, u32[]{:S(2)}) collective-permute-start(f32[2,128,1024]{2,1,0:T(8,128)} %get-tuple-element.392), channel_id=1, source_target_pairs={{0,1},{3,2},{4,5},{7,6},{8,9},{11,10},{12,13},{15,14},{16,17},{19,... | collective-permute-start | bytes 3145736 | tf_op jit(solution)/shard_map/ppermute | solution.py:911
  449.1 30.0 %collective-permute-start.20 = (f32[256,1024]{1,0:T(8,128)S(1)}, f32[256,1024]{1,0:T(8,128)}, u32[]{:S(2)}, u32[]{:S(2)}) collective-permute-start(f32[256,1024]{1,0:T(8,128)S(1)} %add.122), channel_id=1, source_target_pairs={{1,2},{2,1},{5,6},{6,5},{9,10},{10,9},{13,14},{14,13},{17,18},{18,... | collective-permute-start | bytes 3145736 | tf_op jit(solution)/shard_map/ppermute | solution.py:914
  452.1 25.9 %collective-permute-start.21 = (f32[256,1024]{1,0:T(8,128)S(1)}, f32[256,1024]{1,0:T(8,128)S(1)}, u32[]{:S(2)}, u32[]{:S(2)}) collective-permute-start(f32[256,1024]{1,0:T(8,128)S(1)} %add.123), channel_id=1, source_target_pairs={{1,0},{2,3},{5,4},{6,7},{9,8},{10,11},{13,12},{14,15},{17,16},{18,... | collective-permute-start | bytes 3145736 | tf_op jit(solution)/shard_map/ppermute | solution.py:917
  461.5 37.7 %collective-permute-start.17 = (f32[2,128,1024]{2,1,0:T(8,128)}, f32[2,128,1024]{2,1,0:T(8,128)}, u32[]{:S(2)}, u32[]{:S(2)}) collective-permute-start(f32[2,128,1024]{2,1,0:T(8,128)} %get-tuple-element.389), channel_id=1, source_target_pairs={{0,16},{4,20},{8,24},{12,28},{16,0},{20,4},{24,8},{28,12},{1,17},{... | collective-permute-start | bytes 3145736 | tf_op jit(solution)/shard_map/ppermute | solution.py:772
  462.1 37.2 %collective-permute-start.18 = (f32[2,128,1024]{2,1,0:T(8,128)}, f32[2,128,1024]{2,1,0:T(8,128)}, u32[]{:S(2)}, u32[]{:S(2)}) collective-permute-start(f32[2,128,1024]{2,1,0:T(8,128)} %get-tuple-element.390), channel_id=1, source_target_pairs={{0,8},{4,12},{8,0},{12,4},{16,24},{20,28},{24,16},{28,20},{1,9},{5... | collective-permute-start | bytes 3145736 | tf_op jit(solution)/shard_map/ppermute | solution.py:772
  480.5 23.6 %collective-permute-start.26 = (f32[256,1024]{1,0:T(8,128)S(1)}, f32[256,1024]{1,0:T(8,128)}, u32[]{:S(2)}, u32[]{:S(2)}) collective-permute-start(f32[256,1024]{1,0:T(8,128)S(1)} %add.126), channel_id=1, source_target_pairs={{1,0},{2,3},{5,4},{6,7},{9,8},{10,11},{13,12},{14,15},{17,16},{18,... | collective-permute-start | bytes 3145736 | tf_op jit(solution)/shard_map/ppermute | solution.py:917
  483.7 21.9 %collective-permute-start.25 = (f32[2,128,1024]{2,1,0:T(8,128)S(1)}, f32[2,128,1024]{2,1,0:T(8,128)}, u32[]{:S(2)}, u32[]{:S(2)}) collective-permute-start(f32[2,128,1024]{2,1,0:T(8,128)S(1)} %add.127), channel_id=1, source_target_pairs={{1,2},{2,1},{5,6},{6,5},{9,10},{10,9},{13,14},{14,13},{17,18},{18,... | collective-permute-start | bytes 3145736 | tf_op jit(solution)/shard_map/ppermute | solution.py:914
  492.8 28.6 %collective-permute-start.24 = (f32[2,128,1024]{2,1,0:T(8,128)S(1)}, f32[2,128,1024]{2,1,0:T(8,128)S(1)}, u32[]{:S(2)}, u32[]{:S(2)}) collective-permute-start(f32[2,128,1024]{2,1,0:T(8,128)S(1)} %copy-done.56), channel_id=1, source_target_pairs={{0,1},{3,2},{4,5},{7,6},{8,9},{11,10},{12,13},{15,14},{16,17},{19,... | collective-permute-start | bytes 3145736 | tf_op jit(solution)/shard_map/ppermute | solution.py:911
  506.9 43.6 %collective-permute-start.28 = (f32[2,128,1024]{2,1,0:T(8,128)S(1)}, f32[2,128,1024]{2,1,0:T(8,128)S(1)}, u32[]{:S(2)}, u32[]{:S(2)}) collective-permute-start(f32[2,128,1024]{2,1,0:T(8,128)S(1)} %add.129), channel_id=1, source_target_pairs={{1,0},{2,3},{5,4},{6,7},{9,8},{10,11},{13,12},{14,15},{17,16},{18,... | collective-permute-start | bytes 3145736 | tf_op jit(solution)/shard_map/ppermute | solution.py:917
  521.5 29.2 %collective-permute-start.27 = (f32[2,128,1024]{2,1,0:T(8,128)S(1)}, f32[2,128,1024]{2,1,0:T(8,128)S(1)}, u32[]{:S(2)}, u32[]{:S(2)}) collective-permute-start(f32[2,128,1024]{2,1,0:T(8,128)S(1)} %add.130), channel_id=1, source_target_pairs={{1,2},{2,1},{5,6},{6,5},{9,10},{10,9},{13,14},{14,13},{17,18},{18,... | collective-permute-start | bytes 3145736 | tf_op jit(solution)/shard_map/ppermute | solution.py:914
  522.2 29.9 %collective-permute-start.23 = (f32[2,128,1024]{2,1,0:T(8,128)S(1)}, f32[2,128,1024]{2,1,0:T(8,128)S(1)}, u32[]{:S(2)}, u32[]{:S(2)}) collective-permute-start(f32[2,128,1024]{2,1,0:T(8,128)S(1)} %get-tuple-element.418), channel_id=1, source_target_pairs={{0,1},{3,2},{4,5},{7,6},{8,9},{11,10},{12,13},{15,14},{16,17},{19,... | collective-permute-start | bytes 3145736 | tf_op jit(solution)/shard_map/ppermute | solution.py:911
  529.3 21.1 %collective-permute-start.29 = (f32[1,1793]{1,0:T(1,128)S(1)}, f32[1,1793]{1,0:T(1,128)S(1)}, u32[]{:S(2)}, u32[]{:S(2)}) collective-permute-start(f32[1,1793]{1,0:T(1,128)S(1)} %broadcast_in_dim.27), channel_id=1, source_target_pairs={{0,1},{3,2},{4,5},{7,6},{8,9},{11,10},{12,13},{15,14},{16,17},{19,... | collective-permute-start | bytes 21524 | tf_op jit(solution)/shard_map/ppermute | solution.py:1042
  550.9 24.6 %collective-permute-start.31 = (f32[2,128,1024]{2,1,0:T(8,128)S(1)}, f32[2,128,1024]{2,1,0:T(8,128)S(1)}, u32[]{:S(2)}, u32[]{:S(2)}) collective-permute-start(f32[2,128,1024]{2,1,0:T(8,128)S(1)} %add.132), channel_id=1, source_target_pairs={{1,0},{2,3},{5,4},{6,7},{9,8},{10,11},{13,12},{14,15},{17,16},{18,... | collective-permute-start | bytes 3145736 | tf_op jit(solution)/shard_map/ppermute | solution.py:917
  552.4 23.3 %collective-permute-start.30 = (f32[2,128,1024]{2,1,0:T(8,128)S(1)}, f32[2,128,1024]{2,1,0:T(8,128)S(1)}, u32[]{:S(2)}, u32[]{:S(2)}) collective-permute-start(f32[2,128,1024]{2,1,0:T(8,128)S(1)} %add.133), channel_id=1, source_target_pairs={{1,2},{2,1},{5,6},{6,5},{9,10},{10,9},{13,14},{14,13},{17,18},{18,... | collective-permute-start | bytes 3145736 | tf_op jit(solution)/shard_map/ppermute | solution.py:914
  553.1 26.0 %collective-permute-start.22 = (f32[2,128,1024]{2,1,0:T(8,128)S(1)}, f32[2,128,1024]{2,1,0:T(8,128)S(1)}, u32[]{:S(2)}, u32[]{:S(2)}) collective-permute-start(f32[2,128,1024]{2,1,0:T(8,128)S(1)} %get-tuple-element.417), channel_id=1, source_target_pairs={{0,1},{3,2},{4,5},{7,6},{8,9},{11,10},{12,13},{15,14},{16,17},{19,... | collective-permute-start | bytes 3145736 | tf_op jit(solution)/shard_map/ppermute | solution.py:911
  559.5 0.7 collective-permute-start.32
  575.9 25.5 %collective-permute-start.34 = (f32[2,128,1024]{2,1,0:T(8,128)S(1)}, f32[2,128,1024]{2,1,0:T(8,128)S(1)}, u32[]{:S(2)}, u32[]{:S(2)}) collective-permute-start(f32[2,128,1024]{2,1,0:T(8,128)S(1)} %add.135), channel_id=1, source_target_pairs={{1,0},{2,3},{5,4},{6,7},{9,8},{10,11},{13,12},{14,15},{17,16},{18,... | collective-permute-start | bytes 3145736 | tf_op jit(solution)/shard_map/ppermute | solution.py:917
  579.3 22.2 %collective-permute-start.33 = (f32[2,128,1024]{2,1,0:T(8,128)S(1)}, f32[2,128,1024]{2,1,0:T(8,128)S(1)}, u32[]{:S(2)}, u32[]{:S(2)}) collective-permute-start(f32[2,128,1024]{2,1,0:T(8,128)S(1)} %add.136), channel_id=1, source_target_pairs={{1,2},{2,1},{5,6},{6,5},{9,10},{10,9},{13,14},{14,13},{17,18},{18,... | collective-permute-start | bytes 3145736 | tf_op jit(solution)/shard_map/ppermute | solution.py:914
  581.5 19.8 %collective-permute-start.35 = (f32[1,1793]{1,0:T(1,128)S(1)}, f32[1,1793]{1,0:T(1,128)S(1)}, u32[]{:S(2)}, u32[]{:S(2)}) collective-permute-start(f32[1,1793]{1,0:T(1,128)S(1)} %add.134), channel_id=1, source_target_pairs={{1,0},{2,3},{5,4},{6,7},{9,8},{10,11},{13,12},{14,15},{17,16},{18,... | collective-permute-start | bytes 21524 | tf_op jit(solution)/shard_map/ppermute | solution.py:1048
  601.7 23.5 %collective-permute-start.36 = (f32[2,128,1024]{2,1,0:T(8,128)S(1)}, f32[2,128,1024]{2,1,0:T(8,128)S(1)}, u32[]{:S(2)}, u32[]{:S(2)}) collective-permute-start(f32[2,128,1024]{2,1,0:T(8,128)S(1)} %add.137), channel_id=1, source_target_pairs={{1,0},{2,3},{5,4},{6,7},{9,8},{10,11},{13,12},{14,15},{17,16},{18,... | collective-permute-start | bytes 3145736 | tf_op jit(solution)/shard_map/ppermute | solution.py:917
  (62 other events, 361.8 us)
Sparse Core Ops, SparseCore 0:
  160.2 142.0 reduce-scatter.1

commit v6 on v5

--- a/solution.py
+++ b/solution.py
@@ -19,7 +19,6 @@
 
 wide = jnp.float32
 narrow = jnp.bfloat16
-ATTEND_PARTS = 4
 SPREAD = (2, 1, 3, 0)
 SPLIT = {"back": ("backa", "backb"), "in": ("ina", "inb"), "q": ("qa", "qb")}
 ORDER = (
@@ -627,11 +626,15 @@
     return ref[...].reshape(ref.shape[-2:])
 
 
+def product(left, right):
+    return mul_down(left, right) if left.shape[0] == right.shape[0] else mul(left, right)
+
+
 def first_kernel(plan, table, *refs):
     count = len(plan)
     lefts, rights, out = refs[:count], refs[count : 2 * count], refs[-1]
     for one in range(count):
-        out[one] = mul(lefts[one][...], flat(rights[one]))
+        out[one] = product(lefts[one][...], flat(rights[one]))
 
 
 def next_kernel(plan, table, *refs):
@@ -640,18 +643,21 @@
     arrived_keep, arrived_send, kept, sent_one, sent_two = refs[3 * count :]
     for one in range(count):
         right = flat(rights[one])
-        kept[one] = mul(keeps[one][...], right) + arrived_keep[one]
+        kept[one] = product(keeps[one][...], right) + arrived_keep[one]
         sent = sent_one if one < count // 2 else sent_two
-        sent[one % (count // 2)] = mul(sends[one][...], right) + arrived_send[one]
+        sent[one % (count // 2)] = product(sends[one][...], right) + arrived_send[one]
 
 
 class Halving:
     def __init__(self, me, masks_one, masks_two, streams, width):
         self.masks = (masks_one, masks_two)
-        self.streams = streams
         self.devices = lax.axis_size("pages")
         self.width = width
-        self.rows = streams[0][0].shape[0] // self.devices
+        self.rows = streams[0][0].shape[1] // self.devices
+        self.across = self.rows % 128 == 0
+        self.streams = [
+            (left if self.across else left.T, *rest) for left, *rest in streams
+        ]
         self.table = jnp.concatenate(
             [
                 jnp.bitwise_xor(me, jnp.array(flips_of(masks), jnp.int32))
@@ -661,9 +667,13 @@
 
     def left(self, one, start):
         place = (one >= len(self.streams) // 2) * self.devices + start
+        left = self.streams[one][0]
+        if self.across:
+            return pl.BlockSpec(
+                (left.shape[0], self.rows), lambda row, table: (0, table[place + row])
+            )
         return pl.BlockSpec(
-            (self.rows, self.streams[one][0].shape[1]),
-            lambda row, table: (table[place + row], 0),
+            (self.rows, left.shape[1]), lambda row, table: (table[place + row], 0)
         )
 
     def right(self, one):
@@ -856,19 +866,23 @@
     split_boxes = group_boxes.reshape(4, group, PARTS, token_rows // PARTS).swapaxes(1, 2)
     split_boxes = split_boxes.reshape(4, group * token_rows)
     uses = jnp.stack([one for table in tables for one in table_indices(split_boxes, table)]).T
-    looked_up = add_rows(
-        twice[:1],
-        uses[:, :2],
-        table_columns[:1],
-        jnp.zeros((group * token_rows, columns), wide),
-        0,
-        1,
-    )
+    def look_up(chosen, total, part, parts):
+        return add_rows(
+            jnp.stack([twice[one] for one in chosen]),
+            jnp.concatenate([uses[:, 2 * one : 2 * one + 2] for one in chosen], 1),
+            [table_columns[one] for one in chosen],
+            total,
+            part,
+            parts,
+        )
+
+    looked_up = jnp.zeros((group * token_rows, columns), wide)
+    near = sorted({1, planes - 1})
+    for chosen in ([0], near):
+        looked_up = look_up(chosen, looked_up, 0, 1)
     parts = [
         exchange(
-            add_rows(twice[1:], uses[:, 2:], table_columns[1:], looked_up, part, PARTS).reshape(
-                group, token_rows // PARTS, columns
-            )
+            look_up(list(range(2, planes - 1)), looked_up, part, PARTS).reshape(group, token_rows // PARTS, columns)
         )
         for part in range(PARTS)
     ]
@@ -936,24 +950,22 @@
                 token(row(attn_gain)),
             )
             d_pre, d_attended = token.after(d_pre, d_attended)
-            attn_rows = attn_low.T
             halvings["in"] = Halving(
                 me,
                 masks_one,
                 masks_two,
-                [(attn_rows, d_pre, 0, one) for one in range(4)],
+                [(attn_low, d_pre, 0, one) for one in range(4)],
                 model_width,
             )
         elif step == "attend all":
             d_packed, g_query_bias, g_value_bias = attend_back(packed, token(d_attended), w_out)
             d_packed = token.after(d_packed)
-            emb_rows = emb_low.T
             halvings["q"] = Halving(
                 me,
                 masks_one,
                 masks_two,
-                [(emb_rows, d_packed, one, 0) for one in range(3)]
-                + [(context_low.T, d_attended, 0, 0)],
+                [(emb_low, d_packed, one, 0) for one in range(3)]
+                + [(context_low, d_attended, 0, 0)],
                 model_width,
             )
         elif kind == "first":

time: 644 us -> 617 us (0.958)
  starting transfers between devices: 108 us -> 82.7 us
  local copies, waits for them, and re-layouts: 75.1 us -> 61.3 us
  waiting for transfers between devices: 227 us -> 236 us
    ppermute x10, waiting for transfers between devices: 11.4 us -> 34.3 us  [swap(): lax.ppermute(array, 'pages', [(one, one ^ mask) for one in range(lax.axis...]
    ppermute x6, starting transfers between devices: 34.2 us -> 11.6 us  [around(): lax.ppermute(array, 'emb', [((one + offset) % planes, one) for one in ran...]
    all_to_all x3, waiting for transfers between devices: 70.4 us -> 58.2 us  [exchange(): lax.all_to_all(blocks, 'pages', 0, 0, tiled=True, axis_index_groups=groups)]
    unnamed x159 -> x151, local copies, waits for them, and re-layouts: 54.4 us -> 43.9 us
    pallas_call x2 -> x3, Pallas kernels: 24.2 us -> 24.4 us  [add_rows(): pl.pallas_call(lookup_kernel, grid_spec=pltpu.PrefetchScalarGridSpec(num_...]
  transfers between devices with their start and end apart: 41 -> 41, of which waited for: 15 -> 16; matrix products, arithmetic and copies ran while one was open for 7% -> 7% of each run, Pallas kernels for 16% -> 19%
where the time goes in v6:
time: 617 us; the launch traced here: 609 us
  waiting for transfers between devices  236 us (38%)
  Pallas kernels  167 us (27%)
  starting transfers between devices  82.7 us (13%)
  local copies, waits for them, and re-layouts  61.3 us (10%)
  other arithmetic  27.4 us (4%)
  between operations  17.6 us (3%)
  blocking collectives  16.7 us (3%)
    all_to_all x3, waiting for transfers between devices, exchange(): lax.all_to_all(blocks, 'pages', 0, 0, tiled=True, axis_index_groups=groups)  58.2 us
    ppermute x6, waiting for transfers between devices, outward(): return lax.ppermute(share, 'emb', [(1, 0), (2, 3)])  50.2 us
    unnamed x151, local copies, waits for them, and re-layouts  43.9 us
    ppermute x6, waiting for transfers between devices, inward(): return lax.ppermute(share, 'emb', [(0, 1), (3, 2)])  40 us
    ppermute x10, waiting for transfers between devices, swap(): lax.ppermute(array, 'pages', [(one, one ^ mask) for one in range(lax.axis...  34.3 us
    ppermute x6, starting transfers between devices, inward(): return lax.ppermute(share, 'emb', [(0, 1), (3, 2)])  32.5 us
    pallas_call x3, Pallas kernels, add_rows(): pl.pallas_call(lookup_kernel, grid_spec=pltpu.PrefetchScalarGridSpec(num_...  24.4 us
    pallas_call x1, Pallas kernels, attend_back(): pl.pallas_call(attend_back_kernel, grid=(pairs,), in_specs=[pl.BlockSpec(...  22.8 us
  transfers between devices with their start and end apart: 41, of which 16 were waited for; matrix products, arithmetic and copies ran while one was open for 7% of the time, Pallas kernels for 19%

profile of v6, /device:TPU:0, one launch (start us, length us, event | category | flops | bytes accessed | tf_op | source)
XLA Modules:
  0.0 609.1 jit_solution(14681727276526142401)
XLA Ops:
  8.3 3.1 collective-permute-start.2
  14.4 9.4 %all_gather.3 = s32[4,4096]{1,0:T(4,128)S(1)} all-gather(s32[4,512]{1,0:T(4,128)} %param.24), channel_id=1, replica_groups={{0,4,8,12,16,20,24,28},{1,5,9,13,17,21,25,29},{2,6,10,14,18,22,26,30},{..., dimensions={1}, use_global_device_ids=true | all-gather | bytes 73728 | tf_op jit(solution)/shard_map/all_gather | solution.py:863
  25.1 6.1 look_up.3.refs_2_
  39.3 12.9 %look_up.4.refs_1_ = f32[4096,128]{1,0:T(8,128)S(1)} custom-call(s32[2]{0:T(128)S(1)} %pad_add_fusion.6.twice_ref, s32[4096,4]{1,0:T(8,128)S(1)} %copy-done.20, f32[1024,128]{1,0:T(8,128)} %collective-permute-done.1.refs_0_, f32[1024,128]{1,0:T(8,128)} %collective-permute-done.2.refs_1_, f32[4096,128]{1,0:T(8,128)S(1)} %copy-done.19), custom_call_target="tpu_custom_call" | custom-call | flops 1024 | bytes 1024 | tf_op jit(solution)/shard_map/look_up/pallas_call | solution.py:172
  52.2 6.8 %collective-permute-done.refs_0_ = f32[1024,128]{1,0:T(8,128)S(1)} collective-permute-done((f32[1024,128]{1,0:T(8,128)S(1)}, f32[1024,128]{1,0:T(8,128)S(1)}, u32[]{:S(2)}, u32[]{:S(2)}) %collective-permute-start) | collective-permute-done | bytes 524320 | tf_op jit(solution)/shard_map/ppermute | solution.py:854
  59.0 5.4 look_up.5
  65.7 3.9 all-to-all-start
  70.2 26.1 %all-to-all-done.refs_0_ = f32[8,512,128]{2,1,0:T(8,128)S(1)} async-done(((f32[8,512,128]{2,1,0:T(8,128)}), f32[8,512,128]{2,1,0:T(8,128)S(1)}, u32[]{:S(2)}, u32[]{:S(2)}) %all-to-all-start) | async-done | bytes 2097184 | tf_op jit(solution)/shard_map/all_to_all | solution.py:859
  100.3 5.7 embed_and_project.1
  106.2 13.5 %attend.1 = (bf16[512,1024]{1,0:T(8,128)(2,1)S(1)}, f32[512,1024]{1,0:T(8,128)S(1)}, f32[512,1]{1,0:T(8,128)S(1)}, bf16[512,1024]{1,0:T(8,128)(2,1)S(1)}) custom-call(bf16[512,3072]{1,0:T(8,128)(2,1)S(1)} %get-tuple-element.253.queries.keys.values, bf16[512,3072]{1,0:T(8,128)(2,1)S(1)} %get-tuple-element.253.queries.keys.values, ...), custom_call_target="tpu_custom_call" | custom-call | flops 1024 | bytes 1024 | tf_op jit(solution)/shard_map/attend/pallas_call | solution.py:313
  119.8 18.9 %feed.1 = (f32[512,4096]{1,0:T(8,128)S(1)}, bf16[512,4096]{1,0:T(8,128)(2,1)S(1)}, bf16[512,1024]{1,0:T(8,128)(2,1)}, f32[512,1024]{1,0:T(8,128)S(1)}, bf16[512,...) custom-call(bf16[512,1024]{1,0:T(8,128)(2,1)S(1)} %get-tuple-element.256.low.refs_0, ...), custom_call_target="tpu_custom_call" | custom-call | flops 1024 | bytes 1024 | tf_op jit(solution)/shard_map/feed/pallas_call | solution.py:385
  138.7 3.4 copy-done.21
  143.4 6.3 %outer.1 = f32[4096,1024]{1,0:T(8,128)S(1)} custom-call(bf16[512,4096]{1,0:T(8,128)(2,1)S(1)} %get-tuple-element.262.left, bf16[512,1024]{1,0:T(8,128)(2,1)S(1)} %get-tuple-element.264.right.d_returned), custom_call_target="tpu_custom_call" | custom-call | flops 1024 | bytes 1024 | tf_op jit(solution)/shard_map/outer/pallas_call | solution.py:613
  149.7 5.8 copy-done.6
  157.2 3.4 copy-done.7
  165.0 18.2 %feed_back.1 = (bf16[512,4096]{1,0:T(8,128)(2,1)S(1)}, f32[1,4096]{1,0:T(1,128)S(1)}, f32[512,1024]{1,0:T(8,128)S(1)}, bf16[512,1024]{1,0:T(8,128)(2,1)S(1)}, f3...) custom-call(bf16[512,1024]{1,0:T(8,128)(2,1)S(1)} %copy-done.27, ...), custom_call_target="tpu_custom_call" | custom-call | flops 1024 | bytes 1024 | tf_op jit(solution)/shard_map/feed_back/pallas_call | solution.py:461
  184.6 6.5 %halving_first.2 = f32[4,512,1024]{2,1,0:T(8,128)} custom-call(s32[16]{0:T(128)S(1)} %pad_add_fusion.5.table, bf16[512,1024]{1,0:T(8,128)(2,1)S(1)} %get-tuple-element.256.low.refs_0_.refs_1_.refs_2_.refs_3_.refs_4_.refs_5_.refs_6_.refs_7_, bf16[512,1024]{1,0:T(8,128)(2,1)S(1)} %get-tuple-element.256.low.refs_0_.refs_1_.refs_2_.refs_3_.refs_4_.refs_5_.refs_6_.refs_7_, ...), custom_call_target="tpu_custom_call" | custom-call | flops 1024 | bytes 1024 | tf_op jit(solution)/shard_map/halving_first/pallas_call | solution.py:691
  191.3 22.8 %attend_back.1 = (bf16[3,512,1024]{2,1,0:T(8,128)(2,1)S(1)}, f32[1,1024]{1,0:T(1,128)S(1)}, f32[1,1024]{1,0:T(1,128)S(1)}) custom-call(bf16[512,3072]{1,0:T(8,128)(2,1)S(1)} %copy-done.5, bf16[512,3072]{1,0:T(8,128)(2,1)S(1)} %copy-done.5, bf16[512,3072]{1,0:T(8,128)(2,1)S(1)} %copy-done.5, ...), custom_call_target="tpu_custom_call" | custom-call | flops 1024 | bytes 1024 | tf_op jit(solution)/shard_map/attend_back/pallas_call | solution.py:525
  214.2 9.2 %embed_back.1 = (f32[512,1024]{1,0:T(8,128)}, f32[1,1024]{1,0:T(1,128)S(1)}, f32[1,1024]{1,0:T(1,128)S(1)}, f32[1,1024]{1,0:T(1,128)S(1)}, f32[8,512,128]{2,1,0:T(8,128)S(1)}) custom-call(bf16[3,512,1024]{2,1,0:T(8,128)(2,1)S(1)} %get-tuple-element.280.d_packed.refs_4_.refs_5_.refs_6_.refs_8_.refs_9_.refs_10_, bf16[1024,3072]{1,0:T(8,128)(2,1)S(1)} %bitcast.89, ...), custom_call_target="tpu_custom_call" | custom-call | flops 1024 | bytes 1024 | tf_op jit(solution)/shard_map/embed_back/pallas_call | solution.py:579
  223.4 6.1 halving_first.3
  229.9 4.6 all-to-all-start.1
  234.6 32.2 %all-to-all-done.1 = f32[8,512,128]{2,1,0:T(8,128)} async-done(((f32[8,512,128]{2,1,0:T(8,128)}), f32[8,512,128]{2,1,0:T(8,128)}, u32[]{:S(2)}, u32[]{:S(2)}) %all-to-all-start.1) | async-done | bytes 2097184 | tf_op jit(solution)/shard_map/all_to_all | solution.py:859
  266.7 5.6 spread.4
  274.5 6.5 %halving_next.2 = (f32[4,256,1024]{2,1,0:T(8,128)S(1)}, f32[2,256,1024]{2,1,0:T(8,128)S(1)}, f32[2,256,1024]{2,1,0:T(8,128)S(1)}) custom-call(s32[16]{0:T(128)S(1)} %pad_add_fusion.5.table, bf16[512,1024]{1,0:T(8,128)(2,1)S(1)} %get-tuple-element.256.low.refs_0_.refs_1_.refs_2_.refs_3_.refs_4_.refs_5_.refs_6_.refs_7_, ...), custom_call_target="tpu_custom_call" | custom-call | flops 1024 | bytes 1024 | tf_op jit(solution)/shard_map/halving_next/pallas_call | solution.py:710
  282.3 3.0 collective-permute-start.4
  285.4 5.6 spread.5
  291.0 5.6 spread.6
  296.6 5.6 spread.7
  303.2 34.3 %collective-permute-done.8 = f32[2,256,1024]{2,1,0:T(8,128)S(1)} collective-permute-done((f32[2,256,1024]{2,1,0:T(8,128)S(1)}, f32[2,256,1024]{2,1,0:T(8,128)S(1)}, u32[]{:S(2)}, u32[]{:S(2)}) %collective-permute-start.8) | collective-permute-done | bytes 2097184 | tf_op jit(solution)/shard_map/ppermute | solution.py:782
  345.1 7.4 %collective-permute-done.6 = f32[1024,128]{1,0:T(8,128)S(1)} collective-permute-done((f32[1024,128]{1,0:T(8,128)S(1)}, f32[1024,128]{1,0:T(8,128)S(1)}, u32[]{:S(2)}, u32[]{:S(2)}) %collective-permute-start.6) | collective-permute-done | bytes 524320 | tf_op jit(solution)/shard_map/ppermute | solution.py:854
  353.4 6.5 %halving_next.3 = (f32[4,256,1024]{2,1,0:T(8,128)S(1)}, f32[2,256,1024]{2,1,0:T(8,128)S(1)}, f32[2,256,1024]{2,1,0:T(8,128)S(1)}) custom-call(s32[16]{0:T(128)S(1)} %pad_add_fusion.5.table, bf16[512,1024]{1,0:T(8,128)(2,1)S(1)} %get-tuple-element.252.refs_0_.refs_1_.refs_2_.refs_4_.refs_5_.refs_6_, ...), custom_call_target="tpu_custom_call" | custom-call | flops 1024 | bytes 1024 | tf_op jit(solution)/shard_map/halving_next/pallas_call | solution.py:710
  364.5 3.5 all-to-all-start.2
  373.3 2.9 collective-permute-start.12
  376.3 3.0 fusion.1
  383.3 15.3 %collective-permute-done.12 = f32[256,1024]{1,0:T(8,128)} collective-permute-done((f32[256,1024]{1,0:T(8,128)S(1)}, f32[256,1024]{1,0:T(8,128)}, u32[]{:S(2)}, u32[]{:S(2)}) %collective-permute-start.12) | collective-permute-done | bytes 1048608 | tf_op jit(solution)/shard_map/ppermute | solution.py:925
  404.2 7.2 %collective-permute-start.19 = (f32[2,128,1024]{2,1,0:T(8,128)}, f32[2,128,1024]{2,1,0:T(8,128)}, u32[]{:S(2)}, u32[]{:S(2)}) collective-permute-start(f32[2,128,1024]{2,1,0:T(8,128)} %get-tuple-element.392), channel_id=1, source_target_pairs={{0,1},{3,2},{4,5},{7,6},{8,9},{11,10},{12,13},{15,14},{16,17},{19,... | collective-permute-start | bytes 3145736 | tf_op jit(solution)/shard_map/ppermute | solution.py:925
  411.4 9.7 %collective-permute-done.16 = f32[256,1024]{1,0:T(8,128)} collective-permute-done((f32[256,1024]{1,0:T(8,128)S(1)}, f32[256,1024]{1,0:T(8,128)}, u32[]{:S(2)}, u32[]{:S(2)}) %collective-permute-start.16) | collective-permute-done | bytes 1048608 | tf_op jit(solution)/shard_map/ppermute | solution.py:925
  435.5 15.8 %collective-permute-done.21 = f32[256,1024]{1,0:T(8,128)S(1)} collective-permute-done((f32[256,1024]{1,0:T(8,128)S(1)}, f32[256,1024]{1,0:T(8,128)S(1)}, u32[]{:S(2)}, u32[]{:S(2)}) %collective-permute-start.21) | collective-permute-done | bytes 1048608 | tf_op jit(solution)/shard_map/ppermute | solution.py:931
  458.6 7.4 %all_to_all.27 = f32[8,1,1793]{2,1,0:T(1,128)S(1)} all-to-all(f32[8,1,1793]{2,1,0:T(1,128)S(1)} %all_to_all.20), channel_id=1, replica_groups=mesh['pages'=8,'emb'=4] {'pages'}, dimensions={0} | all-to-all | bytes 114752 | tf_op jit(solution)/shard_map/all_to_all | solution.py:1051
  466.0 6.5 %collective-permute-start.24 = (f32[2,128,1024]{2,1,0:T(8,128)S(1)}, f32[2,128,1024]{2,1,0:T(8,128)S(1)}, u32[]{:S(2)}, u32[]{:S(2)}) collective-permute-start(f32[2,128,1024]{2,1,0:T(8,128)S(1)} %copy-done.50), channel_id=1, source_target_pairs={{0,1},{3,2},{4,5},{7,6},{8,9},{11,10},{12,13},{15,14},{16,17},{19,... | collective-permute-start | bytes 3145736 | tf_op jit(solution)/shard_map/ppermute | solution.py:925
  472.5 3.7 fusion
  481.5 13.2 %collective-permute-done.24 = f32[2,128,1024]{2,1,0:T(8,128)S(1)} collective-permute-done((f32[2,128,1024]{2,1,0:T(8,128)S(1)}, f32[2,128,1024]{2,1,0:T(8,128)S(1)}, u32[]{:S(2)}, u32[]{:S(2)}) %collective-permute-start.24) | collective-permute-done | bytes 1048608 | tf_op jit(solution)/shard_map/ppermute | solution.py:925
  495.5 7.0 %collective-permute-start.23 = (f32[2,128,1024]{2,1,0:T(8,128)S(1)}, f32[2,128,1024]{2,1,0:T(8,128)S(1)}, u32[]{:S(2)}, u32[]{:S(2)}) collective-permute-start(f32[2,128,1024]{2,1,0:T(8,128)S(1)} %get-tuple-element.418), channel_id=1, source_target_pairs={{0,1},{3,2},{4,5},{7,6},{8,9},{11,10},{12,13},{15,14},{16,17},{19,... | collective-permute-start | bytes 3145736 | tf_op jit(solution)/shard_map/ppermute | solution.py:925
  503.9 19.8 %collective-permute-done.29 = f32[1,1793]{1,0:T(1,128)S(1)} collective-permute-done((f32[1,1793]{1,0:T(1,128)S(1)}, f32[1,1793]{1,0:T(1,128)S(1)}, u32[]{:S(2)}, u32[]{:S(2)}) %collective-permute-start.29) | collective-permute-done | bytes 7204 | tf_op jit(solution)/shard_map/ppermute | solution.py:1054
  526.3 6.5 %collective-permute-start.22 = (f32[2,128,1024]{2,1,0:T(8,128)S(1)}, f32[2,128,1024]{2,1,0:T(8,128)S(1)}, u32[]{:S(2)}, u32[]{:S(2)}) collective-permute-start(f32[2,128,1024]{2,1,0:T(8,128)S(1)} %get-tuple-element.417), channel_id=1, source_target_pairs={{0,1},{3,2},{4,5},{7,6},{8,9},{11,10},{12,13},{15,14},{16,17},{19,... | collective-permute-start | bytes 3145736 | tf_op jit(solution)/shard_map/ppermute | solution.py:925
  533.5 15.2 %collective-permute-done.31 = f32[2,128,1024]{2,1,0:T(8,128)S(1)} collective-permute-done((f32[2,128,1024]{2,1,0:T(8,128)S(1)}, f32[2,128,1024]{2,1,0:T(8,128)S(1)}, u32[]{:S(2)}, u32[]{:S(2)}) %collective-permute-start.31) | collective-permute-done | bytes 1048608 | tf_op jit(solution)/shard_map/ppermute | solution.py:931
  556.2 18.4 %collective-permute-done.35 = f32[1,1793]{1,0:T(1,128)S(1)} collective-permute-done((f32[1,1793]{1,0:T(1,128)S(1)}, f32[1,1793]{1,0:T(1,128)S(1)}, u32[]{:S(2)}, u32[]{:S(2)}) %collective-permute-start.35) | collective-permute-done | bytes 7204 | tf_op jit(solution)/shard_map/ppermute | solution.py:1060
  580.2 18.2 %collective-permute-done.36 = f32[2,128,1024]{2,1,0:T(8,128)S(1)} collective-permute-done((f32[2,128,1024]{2,1,0:T(8,128)S(1)}, f32[2,128,1024]{2,1,0:T(8,128)S(1)}, u32[]{:S(2)}, u32[]{:S(2)}) %collective-permute-start.36) | collective-permute-done | bytes 1048608 | tf_op jit(solution)/shard_map/ppermute | solution.py:931
  (277 shorter events, 107.6 us)
Async XLA Ops:
  8.3 26.9 %collective-permute-start.2 = (f32[1024,128]{1,0:T(8,128)S(1)}, f32[1024,128]{1,0:T(8,128)}, u32[]{:S(2)}, u32[]{:S(2)}) collective-permute-start(f32[1024,128]{1,0:T(8,128)S(1)} %dynamic-slice_bitcast_fusion.refs_0_), channel_id=1, source_target_pairs={{3,0},{0,1},{1,2},{2,3},{7,4},{4,5},{5,6},{6,7},{11,8},{8,9},{9,10... | collective-permute-start | bytes 1572872 | tf_op jit(solution)/shard_map/ppermute | solution.py:854
  11.4 24.7 %collective-permute-start.1 = (f32[1024,128]{1,0:T(8,128)S(1)}, f32[1024,128]{1,0:T(8,128)}, u32[]{:S(2)}, u32[]{:S(2)}) collective-permute-start(f32[1024,128]{1,0:T(8,128)S(1)} %dynamic-slice_bitcast_fusion.refs_0_), channel_id=1, source_target_pairs={{1,0},{2,1},{3,2},{0,3},{5,4},{6,5},{7,6},{4,7},{9,8},{10,9},{11,1... | collective-permute-start | bytes 1572872 | tf_op jit(solution)/shard_map/ppermute | solution.py:854
  13.5 45.6 %collective-permute-start = (f32[1024,128]{1,0:T(8,128)S(1)}, f32[1024,128]{1,0:T(8,128)S(1)}, u32[]{:S(2)}, u32[]{:S(2)}) collective-permute-start(f32[1024,128]{1,0:T(8,128)S(1)} %dynamic-slice_bitcast_fusion.refs_0_), channel_id=1, source_target_pairs={{2,0},{3,1},{0,2},{1,3},{6,4},{7,5},{4,6},{5,7},{10,8},{11,9},{8,1... | collective-permute-start | bytes 1572872 | tf_op jit(solution)/shard_map/ppermute | solution.py:854
  65.7 30.5 %copy-start.37 = (f32[1024]{0:T(1024)S(1)}, f32[1024]{0:T(1024)}, u32[]{:S(2)}) copy-start(f32[1024]{0:T(1024)} %param.26) | copy-start | bytes 12292
  65.7 30.5 %copy-start.39 = (f32[1024]{0:T(1024)S(1)}, f32[1024]{0:T(1024)}, u32[]{:S(2)}) copy-start(f32[1024]{0:T(1024)} %param.27) | copy-start | bytes 12292
  65.7 30.5 %all-to-all-start = ((f32[8,512,128]{2,1,0:T(8,128)}), f32[8,512,128]{2,1,0:T(8,128)S(1)}, u32[]{:S(2)}, u32[]{:S(2)}) async-start(f32[8,512,128]{2,1,0:T(8,128)} %bitcast.90), calls=%async_computation | async-start | bytes 4194304 | tf_op jit(solution)/shard_map/all_to_all | solution.py:859
  69.6 301.9 %reduce-scatter.2.cloned.1.call-start = ((), (), s32[]{:S(2)}) async-start(), calls=%async_computation.5 | async-start | bytes 18874368 | tf_op jit(solution)/shard_map/reduce_scatter | solution.py:922
  165.0 49.1 %slice-start = ((s8[6291456]{0:T(1024)(128)(4,1)}), s8[2097152]{0:T(1024)(128)(4,1)S(1)}, s32[]{:S(2)}) async-start(s8[6291456]{0:T(1024)(128)(4,1)} %bitcast.88), calls=%async_computation.6 | async-start | bytes 4194304
  184.6 38.8 %copy-start.9 = (bf16[512,1024]{1,0:T(8,128)(2,1)}, bf16[512,1024]{1,0:T(8,128)(2,1)S(1)}, u32[]{:S(2)}) copy-start(bf16[512,1024]{1,0:T(8,128)(2,1)S(1)} %get-tuple-element.277.d_attended.refs_7_.refs_11_) | copy-start | bytes 3145732
  184.6 29.5 %slice-start.1 = ((s8[6291456]{0:T(1024)(128)(4,1)}), s8[4194304]{0:T(1024)(128)(4,1)S(1)}, s32[]{:S(2)}) async-start(s8[6291456]{0:T(1024)(128)(4,1)} %bitcast.88), calls=%async_computation.7 | async-start | bytes 8388608
  191.2 23.0 %copy-start.36 = (f32[512,1]{1,0:T(8,128)S(1)}, f32[512,1]{1,0:T(8,128)}, u32[]{:S(2)}) copy-start(f32[512,1]{1,0:T(8,128)} %copy-done.35) | copy-start | bytes 6148
  191.2 81.2 %collective-permute-start.5 = (f32[4,512,1024]{2,1,0:T(8,128)}, f32[4,512,1024]{2,1,0:T(8,128)}, u32[]{:S(2)}, u32[]{:S(2)}) collective-permute-start(f32[4,512,1024]{2,1,0:T(8,128)} %halving_first.2), channel_id=1, source_target_pairs={{0,4},{4,0},{8,12},{12,8},{16,20},{20,16},{24,28},{28,24},{1,5},{5... | collective-permute-start | bytes 25165832 | tf_op jit(solution)/shard_map/ppermute | solution.py:782
  229.5 124.0 %collective-permute-start.3 = (f32[4,512,1024]{2,1,0:T(8,128)}, f32[4,512,1024]{2,1,0:T(8,128)}, u32[]{:S(2)}, u32[]{:S(2)}) collective-permute-start(f32[4,512,1024]{2,1,0:T(8,128)} %halving_first.3), channel_id=1, source_target_pairs={{0,4},{4,0},{8,12},{12,8},{16,20},{20,16},{24,28},{28,24},{1,5},{5... | collective-permute-start | bytes 25165832 | tf_op jit(solution)/shard_map/ppermute | solution.py:782
  229.9 36.8 %all-to-all-start.1 = ((f32[8,512,128]{2,1,0:T(8,128)}), f32[8,512,128]{2,1,0:T(8,128)}, u32[]{:S(2)}, u32[]{:S(2)}) async-start(f32[8,512,128]{2,1,0:T(8,128)} %copy-done.32), calls=%async_computation.1 | async-start | bytes 4194304 | tf_op jit(solution)/shard_map/all_to_all | solution.py:859
  281.1 58.4 %copy-start.24 = (f32[4,256,1024]{2,1,0:T(8,128)}, f32[4,256,1024]{2,1,0:T(8,128)S(1)}, u32[]{:S(2)}) copy-start(f32[4,256,1024]{2,1,0:T(8,128)S(1)} %get-tuple-element.318) | copy-start | bytes 12582916
  281.1 56.4 %collective-permute-start.8 = (f32[2,256,1024]{2,1,0:T(8,128)S(1)}, f32[2,256,1024]{2,1,0:T(8,128)S(1)}, u32[]{:S(2)}, u32[]{:S(2)}) collective-permute-start(f32[2,256,1024]{2,1,0:T(8,128)S(1)} %get-tuple-element.319), channel_id=1, source_target_pairs={{0,8},{4,12},{8,0},{12,4},{16,24},{20,28},{24,16},{28,20},{1,9},{5... | collective-permute-start | bytes 6291464 | tf_op jit(solution)/shard_map/ppermute | solution.py:782
  281.7 57.3 %collective-permute-start.9 = (f32[2,256,1024]{2,1,0:T(8,128)S(1)}, f32[2,256,1024]{2,1,0:T(8,128)S(1)}, u32[]{:S(2)}, u32[]{:S(2)}) collective-permute-start(f32[2,256,1024]{2,1,0:T(8,128)S(1)} %get-tuple-element.320), channel_id=1, source_target_pairs={{0,16},{4,20},{8,24},{12,28},{16,0},{20,4},{24,8},{28,12},{1,17},{... | collective-permute-start | bytes 6291464 | tf_op jit(solution)/shard_map/ppermute | solution.py:782
  282.3 62.2 %collective-permute-start.4 = (f32[1024,128]{1,0:T(8,128)S(1)}, f32[1024,128]{1,0:T(8,128)S(1)}, u32[]{:S(2)}, u32[]{:S(2)}) collective-permute-start(f32[1024,128]{1,0:T(8,128)S(1)} %spread.4), channel_id=1, source_target_pairs={{2,0},{3,1},{0,2},{1,3},{6,4},{7,5},{4,6},{5,7},{10,8},{11,9},{8,1... | collective-permute-start | bytes 1572872 | tf_op jit(solution)/shard_map/ppermute | solution.py:854
  302.2 42.9 %collective-permute-start.7 = (f32[1024,128]{1,0:T(8,128)S(1)}, f32[1024,128]{1,0:T(8,128)S(1)}, u32[]{:S(2)}, u32[]{:S(2)}) collective-permute-start(f32[1024,128]{1,0:T(8,128)S(1)} %spread.6), channel_id=1, source_target_pairs={{1,0},{2,1},{3,2},{0,3},{5,4},{6,5},{7,6},{4,7},{9,8},{10,9},{11,1... | collective-permute-start | bytes 1572872 | tf_op jit(solution)/shard_map/ppermute | solution.py:854
  337.5 15.0 %collective-permute-start.6 = (f32[1024,128]{1,0:T(8,128)S(1)}, f32[1024,128]{1,0:T(8,128)S(1)}, u32[]{:S(2)}, u32[]{:S(2)}) collective-permute-start(f32[1024,128]{1,0:T(8,128)S(1)} %spread.5), channel_id=1, source_target_pairs={{3,0},{0,1},{1,2},{2,3},{7,4},{4,5},{5,6},{6,7},{11,8},{8,9},{9,10... | collective-permute-start | bytes 1572872 | tf_op jit(solution)/shard_map/ppermute | solution.py:854
  343.1 33.2 %collective-permute-start.13 = (f32[2,128,1024]{2,1,0:T(8,128)}, f32[2,128,1024]{2,1,0:T(8,128)}, u32[]{:S(2)}, u32[]{:S(2)}) collective-permute-start(f32[2,128,1024]{2,1,0:T(8,128)} %get-tuple-element.349), channel_id=1, source_target_pairs={{0,16},{4,20},{8,24},{12,28},{16,0},{20,4},{24,8},{28,12},{1,17},{... | collective-permute-start | bytes 3145736 | tf_op jit(solution)/shard_map/ppermute | solution.py:782
  344.6 31.7 %collective-permute-start.14 = (f32[2,128,1024]{2,1,0:T(8,128)}, f32[2,128,1024]{2,1,0:T(8,128)}, u32[]{:S(2)}, u32[]{:S(2)}) collective-permute-start(f32[2,128,1024]{2,1,0:T(8,128)} %get-tuple-element.350), channel_id=1, source_target_pairs={{0,8},{4,12},{8,0},{12,4},{16,24},{20,28},{24,16},{28,20},{1,9},{5... | collective-permute-start | bytes 3145736 | tf_op jit(solution)/shard_map/ppermute | solution.py:782
  364.5 16.4 %all-to-all-start.2 = ((f32[8,128,128]{2,1,0:T(8,128)}), f32[8,128,128]{2,1,0:T(8,128)S(1)}, u32[]{:S(2)}, u32[]{:S(2)}) async-start(f32[8,128,128]{2,1,0:T(8,128)} %bitcast.117), calls=%async_computation.3 | async-start | bytes 1048576 | tf_op jit(solution)/shard_map/all_to_all | solution.py:859
  368.0 58.7 %collective-permute-start.10 = (f32[2,256,1024]{2,1,0:T(8,128)}, f32[2,256,1024]{2,1,0:T(8,128)}, u32[]{:S(2)}, u32[]{:S(2)}) collective-permute-start(f32[2,256,1024]{2,1,0:T(8,128)} %copy-done.47), channel_id=1, source_target_pairs={{0,8},{4,12},{8,0},{12,4},{16,24},{20,28},{24,16},{28,20},{1,9},{5... | collective-permute-start | bytes 6291464 | tf_op jit(solution)/shard_map/ppermute | solution.py:782
  370.0 56.8 %collective-permute-start.11 = (f32[2,256,1024]{2,1,0:T(8,128)}, f32[2,256,1024]{2,1,0:T(8,128)}, u32[]{:S(2)}, u32[]{:S(2)}) collective-permute-start(f32[2,256,1024]{2,1,0:T(8,128)} %copy-done.46), channel_id=1, source_target_pairs={{0,16},{4,20},{8,24},{12,28},{16,0},{20,4},{24,8},{28,12},{1,17},{... | collective-permute-start | bytes 6291464 | tf_op jit(solution)/shard_map/ppermute | solution.py:782
  373.3 25.3 %collective-permute-start.12 = (f32[256,1024]{1,0:T(8,128)S(1)}, f32[256,1024]{1,0:T(8,128)}, u32[]{:S(2)}, u32[]{:S(2)}) collective-permute-start(f32[256,1024]{1,0:T(8,128)S(1)} %get-tuple-element.346), channel_id=1, source_target_pairs={{0,1},{3,2},{4,5},{7,6},{8,9},{11,10},{12,13},{15,14},{16,17},{19,... | collective-permute-start | bytes 3145736 | tf_op jit(solution)/shard_map/ppermute | solution.py:925
  381.1 40.0 %collective-permute-start.16 = (f32[256,1024]{1,0:T(8,128)S(1)}, f32[256,1024]{1,0:T(8,128)}, u32[]{:S(2)}, u32[]{:S(2)}) collective-permute-start(f32[256,1024]{1,0:T(8,128)S(1)} %get-tuple-element.363), channel_id=1, source_target_pairs={{0,1},{3,2},{4,5},{7,6},{8,9},{11,10},{12,13},{15,14},{16,17},{19,... | collective-permute-start | bytes 3145736 | tf_op jit(solution)/shard_map/ppermute | solution.py:925
  400.0 24.1 %collective-permute-start.15 = (f32[256,1024]{1,0:T(8,128)S(1)}, f32[256,1024]{1,0:T(8,128)}, u32[]{:S(2)}, u32[]{:S(2)}) collective-permute-start(f32[256,1024]{1,0:T(8,128)S(1)} %add.121), channel_id=1, source_target_pairs={{1,2},{2,1},{5,6},{6,5},{9,10},{10,9},{13,14},{14,13},{17,18},{18,... | collective-permute-start | bytes 3145736 | tf_op jit(solution)/shard_map/ppermute | solution.py:928
  404.2 51.1 %collective-permute-start.19 = (f32[2,128,1024]{2,1,0:T(8,128)}, f32[2,128,1024]{2,1,0:T(8,128)}, u32[]{:S(2)}, u32[]{:S(2)}) collective-permute-start(f32[2,128,1024]{2,1,0:T(8,128)} %get-tuple-element.392), channel_id=1, source_target_pairs={{0,1},{3,2},{4,5},{7,6},{8,9},{11,10},{12,13},{15,14},{16,17},{19,... | collective-permute-start | bytes 3145736 | tf_op jit(solution)/shard_map/ppermute | solution.py:925
  422.4 30.0 %collective-permute-start.20 = (f32[256,1024]{1,0:T(8,128)S(1)}, f32[256,1024]{1,0:T(8,128)}, u32[]{:S(2)}, u32[]{:S(2)}) collective-permute-start(f32[256,1024]{1,0:T(8,128)S(1)} %add.122), channel_id=1, source_target_pairs={{1,2},{2,1},{5,6},{6,5},{9,10},{10,9},{13,14},{14,13},{17,18},{18,... | collective-permute-start | bytes 3145736 | tf_op jit(solution)/shard_map/ppermute | solution.py:928
  425.5 25.8 %collective-permute-start.21 = (f32[256,1024]{1,0:T(8,128)S(1)}, f32[256,1024]{1,0:T(8,128)S(1)}, u32[]{:S(2)}, u32[]{:S(2)}) collective-permute-start(f32[256,1024]{1,0:T(8,128)S(1)} %add.123), channel_id=1, source_target_pairs={{1,0},{2,3},{5,4},{6,7},{9,8},{10,11},{13,12},{14,15},{17,16},{18,... | collective-permute-start | bytes 3145736 | tf_op jit(solution)/shard_map/ppermute | solution.py:931
  434.8 37.7 %collective-permute-start.17 = (f32[2,128,1024]{2,1,0:T(8,128)}, f32[2,128,1024]{2,1,0:T(8,128)}, u32[]{:S(2)}, u32[]{:S(2)}) collective-permute-start(f32[2,128,1024]{2,1,0:T(8,128)} %get-tuple-element.389), channel_id=1, source_target_pairs={{0,16},{4,20},{8,24},{12,28},{16,0},{20,4},{24,8},{28,12},{1,17},{... | collective-permute-start | bytes 3145736 | tf_op jit(solution)/shard_map/ppermute | solution.py:782
  435.3 37.2 %collective-permute-start.18 = (f32[2,128,1024]{2,1,0:T(8,128)}, f32[2,128,1024]{2,1,0:T(8,128)}, u32[]{:S(2)}, u32[]{:S(2)}) collective-permute-start(f32[2,128,1024]{2,1,0:T(8,128)} %get-tuple-element.390), channel_id=1, source_target_pairs={{0,8},{4,12},{8,0},{12,4},{16,24},{20,28},{24,16},{28,20},{1,9},{5... | collective-permute-start | bytes 3145736 | tf_op jit(solution)/shard_map/ppermute | solution.py:782
  453.8 23.6 %collective-permute-start.26 = (f32[256,1024]{1,0:T(8,128)S(1)}, f32[256,1024]{1,0:T(8,128)}, u32[]{:S(2)}, u32[]{:S(2)}) collective-permute-start(f32[256,1024]{1,0:T(8,128)S(1)} %add.126), channel_id=1, source_target_pairs={{1,0},{2,3},{5,4},{6,7},{9,8},{10,11},{13,12},{14,15},{17,16},{18,... | collective-permute-start | bytes 3145736 | tf_op jit(solution)/shard_map/ppermute | solution.py:931
  456.9 21.9 %collective-permute-start.25 = (f32[2,128,1024]{2,1,0:T(8,128)S(1)}, f32[2,128,1024]{2,1,0:T(8,128)}, u32[]{:S(2)}, u32[]{:S(2)}) collective-permute-start(f32[2,128,1024]{2,1,0:T(8,128)S(1)} %add.127), channel_id=1, source_target_pairs={{1,2},{2,1},{5,6},{6,5},{9,10},{10,9},{13,14},{14,13},{17,18},{18,... | collective-permute-start | bytes 3145736 | tf_op jit(solution)/shard_map/ppermute | solution.py:928
  466.0 28.6 %collective-permute-start.24 = (f32[2,128,1024]{2,1,0:T(8,128)S(1)}, f32[2,128,1024]{2,1,0:T(8,128)S(1)}, u32[]{:S(2)}, u32[]{:S(2)}) collective-permute-start(f32[2,128,1024]{2,1,0:T(8,128)S(1)} %copy-done.50), channel_id=1, source_target_pairs={{0,1},{3,2},{4,5},{7,6},{8,9},{11,10},{12,13},{15,14},{16,17},{19,... | collective-permute-start | bytes 3145736 | tf_op jit(solution)/shard_map/ppermute | solution.py:925
  480.2 43.6 %collective-permute-start.28 = (f32[2,128,1024]{2,1,0:T(8,128)S(1)}, f32[2,128,1024]{2,1,0:T(8,128)S(1)}, u32[]{:S(2)}, u32[]{:S(2)}) collective-permute-start(f32[2,128,1024]{2,1,0:T(8,128)S(1)} %add.129), channel_id=1, source_target_pairs={{1,0},{2,3},{5,4},{6,7},{9,8},{10,11},{13,12},{14,15},{17,16},{18,... | collective-permute-start | bytes 3145736 | tf_op jit(solution)/shard_map/ppermute | solution.py:931
  494.8 29.1 %collective-permute-start.27 = (f32[2,128,1024]{2,1,0:T(8,128)S(1)}, f32[2,128,1024]{2,1,0:T(8,128)S(1)}, u32[]{:S(2)}, u32[]{:S(2)}) collective-permute-start(f32[2,128,1024]{2,1,0:T(8,128)S(1)} %add.130), channel_id=1, source_target_pairs={{1,2},{2,1},{5,6},{6,5},{9,10},{10,9},{13,14},{14,13},{17,18},{18,... | collective-permute-start | bytes 3145736 | tf_op jit(solution)/shard_map/ppermute | solution.py:928
  495.5 29.9 %collective-permute-start.23 = (f32[2,128,1024]{2,1,0:T(8,128)S(1)}, f32[2,128,1024]{2,1,0:T(8,128)S(1)}, u32[]{:S(2)}, u32[]{:S(2)}) collective-permute-start(f32[2,128,1024]{2,1,0:T(8,128)S(1)} %get-tuple-element.418), channel_id=1, source_target_pairs={{0,1},{3,2},{4,5},{7,6},{8,9},{11,10},{12,13},{15,14},{16,17},{19,... | collective-permute-start | bytes 3145736 | tf_op jit(solution)/shard_map/ppermute | solution.py:925
  502.6 21.1 %collective-permute-start.29 = (f32[1,1793]{1,0:T(1,128)S(1)}, f32[1,1793]{1,0:T(1,128)S(1)}, u32[]{:S(2)}, u32[]{:S(2)}) collective-permute-start(f32[1,1793]{1,0:T(1,128)S(1)} %broadcast_in_dim.27), channel_id=1, source_target_pairs={{0,1},{3,2},{4,5},{7,6},{8,9},{11,10},{12,13},{15,14},{16,17},{19,... | collective-permute-start | bytes 21524 | tf_op jit(solution)/shard_map/ppermute | solution.py:1054
  524.1 24.6 %collective-permute-start.31 = (f32[2,128,1024]{2,1,0:T(8,128)S(1)}, f32[2,128,1024]{2,1,0:T(8,128)S(1)}, u32[]{:S(2)}, u32[]{:S(2)}) collective-permute-start(f32[2,128,1024]{2,1,0:T(8,128)S(1)} %add.132), channel_id=1, source_target_pairs={{1,0},{2,3},{5,4},{6,7},{9,8},{10,11},{13,12},{14,15},{17,16},{18,... | collective-permute-start | bytes 3145736 | tf_op jit(solution)/shard_map/ppermute | solution.py:931
  525.6 23.3 %collective-permute-start.30 = (f32[2,128,1024]{2,1,0:T(8,128)S(1)}, f32[2,128,1024]{2,1,0:T(8,128)S(1)}, u32[]{:S(2)}, u32[]{:S(2)}) collective-permute-start(f32[2,128,1024]{2,1,0:T(8,128)S(1)} %add.133), channel_id=1, source_target_pairs={{1,2},{2,1},{5,6},{6,5},{9,10},{10,9},{13,14},{14,13},{17,18},{18,... | collective-permute-start | bytes 3145736 | tf_op jit(solution)/shard_map/ppermute | solution.py:928
  526.3 26.1 %collective-permute-start.22 = (f32[2,128,1024]{2,1,0:T(8,128)S(1)}, f32[2,128,1024]{2,1,0:T(8,128)S(1)}, u32[]{:S(2)}, u32[]{:S(2)}) collective-permute-start(f32[2,128,1024]{2,1,0:T(8,128)S(1)} %get-tuple-element.417), channel_id=1, source_target_pairs={{0,1},{3,2},{4,5},{7,6},{8,9},{11,10},{12,13},{15,14},{16,17},{19,... | collective-permute-start | bytes 3145736 | tf_op jit(solution)/shard_map/ppermute | solution.py:925
  532.8 0.7 collective-permute-start.32
  549.1 25.5 %collective-permute-start.34 = (f32[2,128,1024]{2,1,0:T(8,128)S(1)}, f32[2,128,1024]{2,1,0:T(8,128)S(1)}, u32[]{:S(2)}, u32[]{:S(2)}) collective-permute-start(f32[2,128,1024]{2,1,0:T(8,128)S(1)} %add.135), channel_id=1, source_target_pairs={{1,0},{2,3},{5,4},{6,7},{9,8},{10,11},{13,12},{14,15},{17,16},{18,... | collective-permute-start | bytes 3145736 | tf_op jit(solution)/shard_map/ppermute | solution.py:931
  552.6 22.1 %collective-permute-start.33 = (f32[2,128,1024]{2,1,0:T(8,128)S(1)}, f32[2,128,1024]{2,1,0:T(8,128)S(1)}, u32[]{:S(2)}, u32[]{:S(2)}) collective-permute-start(f32[2,128,1024]{2,1,0:T(8,128)S(1)} %add.136), channel_id=1, source_target_pairs={{1,2},{2,1},{5,6},{6,5},{9,10},{10,9},{13,14},{14,13},{17,18},{18,... | collective-permute-start | bytes 3145736 | tf_op jit(solution)/shard_map/ppermute | solution.py:928
  554.8 19.7 %collective-permute-start.35 = (f32[1,1793]{1,0:T(1,128)S(1)}, f32[1,1793]{1,0:T(1,128)S(1)}, u32[]{:S(2)}, u32[]{:S(2)}) collective-permute-start(f32[1,1793]{1,0:T(1,128)S(1)} %add.134), channel_id=1, source_target_pairs={{1,0},{2,3},{5,4},{6,7},{9,8},{10,11},{13,12},{14,15},{17,16},{18,... | collective-permute-start | bytes 21524 | tf_op jit(solution)/shard_map/ppermute | solution.py:1060
  574.9 23.5 %collective-permute-start.36 = (f32[2,128,1024]{2,1,0:T(8,128)S(1)}, f32[2,128,1024]{2,1,0:T(8,128)S(1)}, u32[]{:S(2)}, u32[]{:S(2)}) collective-permute-start(f32[2,128,1024]{2,1,0:T(8,128)S(1)} %add.137), channel_id=1, source_target_pairs={{1,0},{2,3},{5,4},{6,7},{9,8},{10,11},{13,12},{14,15},{17,16},{18,... | collective-permute-start | bytes 3145736 | tf_op jit(solution)/shard_map/ppermute | solution.py:931
  (58 other events, 353.6 us)
Sparse Core Ops, SparseCore 0:
  156.6 146.8 reduce-scatter.1

commit v7 on v6

--- a/solution.py
+++ b/solution.py
@@ -35,9 +35,9 @@
     "spread 3",
     "fold in",
     "tables 0",
-    "next q",
     "finish back",
     "send backa",
+    "next q",
     "finish in",
     "send backb",
     "tables 1",

time: 617 us -> 621 us (level)
  local copies, waits for them, and re-layouts: 61.3 us -> 69.6 us
    ppermute x10, waiting for transfers between devices: 34.3 us -> 44.7 us  [swap(): lax.ppermute(array, 'pages', [(one, one ^ mask) for one in range(lax.axis...]
    ppermute x6, waiting for transfers between devices: 40 us -> 30.5 us  [inward(): return lax.ppermute(share, 'emb', [(0, 1), (3, 2)])]
    unnamed x151 -> x167, local copies, waits for them, and re-layouts: 43.9 us -> 49.9 us
  transfers between devices with their start and end apart: 41 -> 41, of which waited for: 16 -> 18; matrix products, arithmetic and copies ran while one was open for 7% -> 8% of each run, Pallas kernels for 19% -> 19%
where the time goes in v7:
time: 621 us; the launch traced here: 613 us
  waiting for transfers between devices  233 us (38%)
  Pallas kernels  164 us (26%)
  starting transfers between devices  83 us (13%)
  local copies, waits for them, and re-layouts  69.6 us (11%)
  other arithmetic  27.3 us (4%)
  blocking collectives  17.8 us (3%)
  between operations  17.6 us (3%)
    all_to_all x3, waiting for transfers between devices, exchange(): lax.all_to_all(blocks, 'pages', 0, 0, tiled=True, axis_index_groups=groups)  58.9 us
    unnamed x167, local copies, waits for them, and re-layouts  49.9 us
    ppermute x6, waiting for transfers between devices, outward(): return lax.ppermute(share, 'emb', [(1, 0), (2, 3)])  45.8 us
    ppermute x10, waiting for transfers between devices, swap(): lax.ppermute(array, 'pages', [(one, one ^ mask) for one in range(lax.axis...  44.7 us
    ppermute x6, starting transfers between devices, inward(): return lax.ppermute(share, 'emb', [(0, 1), (3, 2)])  31.6 us
    ppermute x6, waiting for transfers between devices, inward(): return lax.ppermute(share, 'emb', [(0, 1), (3, 2)])  30.5 us
    pallas_call x3, Pallas kernels, add_rows(): pl.pallas_call(lookup_kernel, grid_spec=pltpu.PrefetchScalarGridSpec(num_...  24.4 us
    pallas_call x1, Pallas kernels, attend_back(): pl.pallas_call(attend_back_kernel, grid=(pairs,), in_specs=[pl.BlockSpec(...  22.8 us
  transfers between devices with their start and end apart: 41, of which 18 were waited for; matrix products, arithmetic and copies ran while one was open for 8% of the time, Pallas kernels for 19%

profile of v7, /device:TPU:0, one launch (start us, length us, event | category | flops | bytes accessed | tf_op | source)
XLA Modules:
  0.0 613.0 jit_solution(8527016362967166272)
XLA Ops:
  8.3 3.1 collective-permute-start.2
  14.4 9.4 %all_gather.3 = s32[4,4096]{1,0:T(4,128)S(1)} all-gather(s32[4,512]{1,0:T(4,128)} %param.24), channel_id=1, replica_groups={{0,4,8,12,16,20,24,28},{1,5,9,13,17,21,25,29},{2,6,10,14,18,22,26,30},{..., dimensions={1}, use_global_device_ids=true | all-gather | bytes 73728 | tf_op jit(solution)/shard_map/all_gather | solution.py:863
  25.1 6.1 look_up.3.refs_2_
  39.3 12.9 %look_up.4.refs_1_ = f32[4096,128]{1,0:T(8,128)S(1)} custom-call(s32[2]{0:T(128)S(1)} %pad_add_fusion.6.twice_ref, s32[4096,4]{1,0:T(8,128)S(1)} %copy-done.26, f32[1024,128]{1,0:T(8,128)} %collective-permute-done.1.refs_0_, f32[1024,128]{1,0:T(8,128)} %collective-permute-done.2.refs_1_, f32[4096,128]{1,0:T(8,128)S(1)} %copy-done.23), custom_call_target="tpu_custom_call" | custom-call | flops 1024 | bytes 1024 | tf_op jit(solution)/shard_map/look_up/pallas_call | solution.py:172
  52.2 6.8 %collective-permute-done.refs_0_ = f32[1024,128]{1,0:T(8,128)S(1)} collective-permute-done((f32[1024,128]{1,0:T(8,128)S(1)}, f32[1024,128]{1,0:T(8,128)S(1)}, u32[]{:S(2)}, u32[]{:S(2)}) %collective-permute-start) | collective-permute-done | bytes 524320 | tf_op jit(solution)/shard_map/ppermute | solution.py:854
  59.0 5.4 look_up.5
  65.8 3.9 all-to-all-start
  70.2 26.1 %all-to-all-done.refs_0_ = f32[8,512,128]{2,1,0:T(8,128)S(1)} async-done(((f32[8,512,128]{2,1,0:T(8,128)}), f32[8,512,128]{2,1,0:T(8,128)S(1)}, u32[]{:S(2)}, u32[]{:S(2)}) %all-to-all-start) | async-done | bytes 2097184 | tf_op jit(solution)/shard_map/all_to_all | solution.py:859
  102.0 5.7 embed_and_project.1
  108.5 13.5 %attend.1 = (bf16[512,1024]{1,0:T(8,128)(2,1)S(1)}, f32[512,1024]{1,0:T(8,128)S(1)}, f32[512,1]{1,0:T(8,128)S(1)}, bf16[512,1024]{1,0:T(8,128)(2,1)S(1)}) custom-call(bf16[512,3072]{1,0:T(8,128)(2,1)S(1)} %get-tuple-element.253.queries.keys.values, bf16[512,3072]{1,0:T(8,128)(2,1)S(1)} %get-tuple-element.253.queries.keys.values, ...), custom_call_target="tpu_custom_call" | custom-call | flops 1024 | bytes 1024 | tf_op jit(solution)/shard_map/attend/pallas_call | solution.py:313
  122.2 19.3 %feed.1 = (f32[512,4096]{1,0:T(8,128)S(1)}, bf16[512,4096]{1,0:T(8,128)(2,1)S(1)}, bf16[512,1024]{1,0:T(8,128)(2,1)}, f32[512,1024]{1,0:T(8,128)S(1)}, bf16[512,...) custom-call(bf16[512,1024]{1,0:T(8,128)(2,1)S(1)} %get-tuple-element.256.low.refs_0, ...), custom_call_target="tpu_custom_call" | custom-call | flops 1024 | bytes 1024 | tf_op jit(solution)/shard_map/feed/pallas_call | solution.py:385
  141.4 3.3 copy-done.27
  146.1 6.3 %outer.1 = f32[4096,1024]{1,0:T(8,128)S(1)} custom-call(bf16[512,4096]{1,0:T(8,128)(2,1)S(1)} %get-tuple-element.262.left, bf16[512,1024]{1,0:T(8,128)(2,1)S(1)} %get-tuple-element.264.right.d_returned), custom_call_target="tpu_custom_call" | custom-call | flops 1024 | bytes 1024 | tf_op jit(solution)/shard_map/outer/pallas_call | solution.py:613
  152.4 5.8 copy-done.8
  160.0 3.4 copy-done.9
  167.8 18.2 %feed_back.1 = (bf16[512,4096]{1,0:T(8,128)(2,1)S(1)}, f32[1,4096]{1,0:T(1,128)S(1)}, f32[512,1024]{1,0:T(8,128)S(1)}, bf16[512,1024]{1,0:T(8,128)(2,1)S(1)}, f3...) custom-call(bf16[512,1024]{1,0:T(8,128)(2,1)S(1)} %copy-done.33, ...), custom_call_target="tpu_custom_call" | custom-call | flops 1024 | bytes 1024 | tf_op jit(solution)/shard_map/feed_back/pallas_call | solution.py:461
  187.3 6.5 %halving_first.2 = f32[4,512,1024]{2,1,0:T(8,128)} custom-call(s32[16]{0:T(128)S(1)} %pad_add_fusion.5.table, bf16[512,1024]{1,0:T(8,128)(2,1)S(1)} %get-tuple-element.256.low.refs_0_.refs_1_.refs_2_.refs_3_.refs_4_.refs_5_.refs_6_.refs_7_, bf16[512,1024]{1,0:T(8,128)(2,1)S(1)} %get-tuple-element.256.low.refs_0_.refs_1_.refs_2_.refs_3_.refs_4_.refs_5_.refs_6_.refs_7_, ...), custom_call_target="tpu_custom_call" | custom-call | flops 1024 | bytes 1024 | tf_op jit(solution)/shard_map/halving_first/pallas_call | solution.py:691
  193.9 22.8 %attend_back.1 = (bf16[3,512,1024]{2,1,0:T(8,128)(2,1)S(1)}, f32[1,1024]{1,0:T(1,128)S(1)}, f32[1,1024]{1,0:T(1,128)S(1)}) custom-call(bf16[512,3072]{1,0:T(8,128)(2,1)S(1)} %copy-done.5, bf16[512,3072]{1,0:T(8,128)(2,1)S(1)} %copy-done.5, bf16[512,3072]{1,0:T(8,128)(2,1)S(1)} %copy-done.5, ...), custom_call_target="tpu_custom_call" | custom-call | flops 1024 | bytes 1024 | tf_op jit(solution)/shard_map/attend_back/pallas_call | solution.py:525
  216.8 9.2 %embed_back.1 = (f32[512,1024]{1,0:T(8,128)}, f32[1,1024]{1,0:T(1,128)S(1)}, f32[1,1024]{1,0:T(1,128)S(1)}, f32[1,1024]{1,0:T(1,128)S(1)}, f32[8,512,128]{2,1,0:T(8,128)S(1)}) custom-call(bf16[3,512,1024]{2,1,0:T(8,128)(2,1)S(1)} %get-tuple-element.280.d_packed.refs_4_.refs_5_.refs_6_.refs_8_.refs_9_.refs_10_, bf16[1024,3072]{1,0:T(8,128)(2,1)S(1)} %bitcast.93, ...), custom_call_target="tpu_custom_call" | custom-call | flops 1024 | bytes 1024 | tf_op jit(solution)/shard_map/embed_back/pallas_call | solution.py:579
  226.1 6.1 halving_first.3
  232.6 3.8 all-to-all-start.1
  236.5 32.8 %all-to-all-done.1 = f32[8,512,128]{2,1,0:T(8,128)S(1)} async-done(((f32[8,512,128]{2,1,0:T(8,128)}), f32[8,512,128]{2,1,0:T(8,128)S(1)}, u32[]{:S(2)}, u32[]{:S(2)}) %all-to-all-start.1) | async-done | bytes 2097184 | tf_op jit(solution)/shard_map/all_to_all | solution.py:859
  269.3 4.6 spread.4
  276.1 6.8 %halving_next.2 = (f32[4,256,1024]{2,1,0:T(8,128)S(1)}, f32[2,256,1024]{2,1,0:T(8,128)S(1)}, f32[2,256,1024]{2,1,0:T(8,128)S(1)}) custom-call(s32[16]{0:T(128)S(1)} %pad_add_fusion.5.table, bf16[512,1024]{1,0:T(8,128)(2,1)S(1)} %get-tuple-element.256.low.refs_0_.refs_1_.refs_2_.refs_3_.refs_4_.refs_5_.refs_6_.refs_7_, ...), custom_call_target="tpu_custom_call" | custom-call | flops 1024 | bytes 1024 | tf_op jit(solution)/shard_map/halving_next/pallas_call | solution.py:710
  286.5 4.5 spread.5
  291.0 4.6 spread.6
  295.6 4.6 spread.7
  301.6 39.3 %collective-permute-done.8 = f32[2,256,1024]{2,1,0:T(8,128)S(1)} collective-permute-done((f32[2,256,1024]{2,1,0:T(8,128)S(1)}, f32[2,256,1024]{2,1,0:T(8,128)S(1)}, u32[]{:S(2)}, u32[]{:S(2)}) %collective-permute-start.8) | collective-permute-done | bytes 2097184 | tf_op jit(solution)/shard_map/ppermute | solution.py:782
  348.6 7.4 %collective-permute-done.6 = f32[1024,128]{1,0:T(8,128)S(1)} collective-permute-done((f32[1024,128]{1,0:T(8,128)S(1)}, f32[1024,128]{1,0:T(8,128)S(1)}, u32[]{:S(2)}, u32[]{:S(2)}) %collective-permute-start.6) | collective-permute-done | bytes 524320 | tf_op jit(solution)/shard_map/ppermute | solution.py:854
  356.9 4.1 all-to-all-start.2
  361.1 3.3 fusion.5
  366.8 7.5 %halving_next.3 = (f32[4,256,1024]{2,1,0:T(8,128)S(1)}, f32[2,256,1024]{2,1,0:T(8,128)S(1)}, f32[2,256,1024]{2,1,0:T(8,128)S(1)}) custom-call(s32[16]{0:T(128)S(1)} %pad_add_fusion.5.table, bf16[512,1024]{1,0:T(8,128)(2,1)S(1)} %copy-done.7, bf16[512,1024]{1,0:T(8,128)(2,1)S(1)} %copy-done.7, bf16[512,1024]{1,0:T(8,128)(2,1)S(1)} %copy-done.7, ...), custom_call_target="tpu_custom_call" | custom-call | flops 1024 | bytes 1024 | tf_op jit(solution)/shard_map/halving_next/pallas_call | solution.py:710
  376.3 3.0 fusion.1
  393.7 6.0 collective-permute-done.12
  405.3 7.0 %collective-permute-start.19 = (f32[2,128,1024]{2,1,0:T(8,128)}, f32[2,128,1024]{2,1,0:T(8,128)}, u32[]{:S(2)}, u32[]{:S(2)}) collective-permute-start(f32[2,128,1024]{2,1,0:T(8,128)} %get-tuple-element.392), channel_id=1, source_target_pairs={{0,1},{3,2},{4,5},{7,6},{8,9},{11,10},{12,13},{15,14},{16,17},{19,... | collective-permute-start | bytes 3145736 | tf_op jit(solution)/shard_map/ppermute | solution.py:925
  412.4 9.8 %collective-permute-done.16 = f32[256,1024]{1,0:T(8,128)} collective-permute-done((f32[256,1024]{1,0:T(8,128)S(1)}, f32[256,1024]{1,0:T(8,128)}, u32[]{:S(2)}, u32[]{:S(2)}) %collective-permute-start.16) | collective-permute-done | bytes 1048608 | tf_op jit(solution)/shard_map/ppermute | solution.py:925
  427.8 3.9 collective-permute-done.10
  443.2 10.9 %collective-permute-done.21 = f32[256,1024]{1,0:T(8,128)S(1)} collective-permute-done((f32[256,1024]{1,0:T(8,128)S(1)}, f32[256,1024]{1,0:T(8,128)S(1)}, u32[]{:S(2)}, u32[]{:S(2)}) %collective-permute-start.21) | collective-permute-done | bytes 1048608 | tf_op jit(solution)/shard_map/ppermute | solution.py:931
  461.5 8.4 %all_to_all.27 = f32[8,1,1793]{2,1,0:T(1,128)S(1)} all-to-all(f32[8,1,1793]{2,1,0:T(1,128)S(1)} %all_to_all.20), channel_id=1, replica_groups=mesh['pages'=8,'emb'=4] {'pages'}, dimensions={0} | all-to-all | bytes 114752 | tf_op jit(solution)/shard_map/all_to_all | solution.py:1051
  470.0 6.5 %collective-permute-start.24 = (f32[2,128,1024]{2,1,0:T(8,128)S(1)}, f32[2,128,1024]{2,1,0:T(8,128)S(1)}, u32[]{:S(2)}, u32[]{:S(2)}) collective-permute-start(f32[2,128,1024]{2,1,0:T(8,128)S(1)} %copy-done.57), channel_id=1, source_target_pairs={{0,1},{3,2},{4,5},{7,6},{8,9},{11,10},{12,13},{15,14},{16,17},{19,... | collective-permute-start | bytes 3145736 | tf_op jit(solution)/shard_map/ppermute | solution.py:925
  476.5 3.7 fusion
  485.9 12.7 %collective-permute-done.24 = f32[2,128,1024]{2,1,0:T(8,128)S(1)} collective-permute-done((f32[2,128,1024]{2,1,0:T(8,128)S(1)}, f32[2,128,1024]{2,1,0:T(8,128)S(1)}, u32[]{:S(2)}, u32[]{:S(2)}) %collective-permute-start.24) | collective-permute-done | bytes 1048608 | tf_op jit(solution)/shard_map/ppermute | solution.py:925
  499.5 7.0 %collective-permute-start.23 = (f32[2,128,1024]{2,1,0:T(8,128)S(1)}, f32[2,128,1024]{2,1,0:T(8,128)S(1)}, u32[]{:S(2)}, u32[]{:S(2)}) collective-permute-start(f32[2,128,1024]{2,1,0:T(8,128)S(1)} %get-tuple-element.418), channel_id=1, source_target_pairs={{0,1},{3,2},{4,5},{7,6},{8,9},{11,10},{12,13},{15,14},{16,17},{19,... | collective-permute-start | bytes 3145736 | tf_op jit(solution)/shard_map/ppermute | solution.py:925
  507.8 19.8 %collective-permute-done.29 = f32[1,1793]{1,0:T(1,128)S(1)} collective-permute-done((f32[1,1793]{1,0:T(1,128)S(1)}, f32[1,1793]{1,0:T(1,128)S(1)}, u32[]{:S(2)}, u32[]{:S(2)}) %collective-permute-start.29) | collective-permute-done | bytes 7204 | tf_op jit(solution)/shard_map/ppermute | solution.py:1054
  530.2 6.5 %collective-permute-start.22 = (f32[2,128,1024]{2,1,0:T(8,128)S(1)}, f32[2,128,1024]{2,1,0:T(8,128)S(1)}, u32[]{:S(2)}, u32[]{:S(2)}) collective-permute-start(f32[2,128,1024]{2,1,0:T(8,128)S(1)} %get-tuple-element.417), channel_id=1, source_target_pairs={{0,1},{3,2},{4,5},{7,6},{8,9},{11,10},{12,13},{15,14},{16,17},{19,... | collective-permute-start | bytes 3145736 | tf_op jit(solution)/shard_map/ppermute | solution.py:925
  537.4 15.2 %collective-permute-done.31 = f32[2,128,1024]{2,1,0:T(8,128)S(1)} collective-permute-done((f32[2,128,1024]{2,1,0:T(8,128)S(1)}, f32[2,128,1024]{2,1,0:T(8,128)S(1)}, u32[]{:S(2)}, u32[]{:S(2)}) %collective-permute-start.31) | collective-permute-done | bytes 1048608 | tf_op jit(solution)/shard_map/ppermute | solution.py:931
  560.1 18.4 %collective-permute-done.35 = f32[1,1793]{1,0:T(1,128)S(1)} collective-permute-done((f32[1,1793]{1,0:T(1,128)S(1)}, f32[1,1793]{1,0:T(1,128)S(1)}, u32[]{:S(2)}, u32[]{:S(2)}) %collective-permute-start.35) | collective-permute-done | bytes 7204 | tf_op jit(solution)/shard_map/ppermute | solution.py:1060
  584.1 18.2 %collective-permute-done.36 = f32[2,128,1024]{2,1,0:T(8,128)S(1)} collective-permute-done((f32[2,128,1024]{2,1,0:T(8,128)S(1)}, f32[2,128,1024]{2,1,0:T(8,128)S(1)}, u32[]{:S(2)}, u32[]{:S(2)}) %collective-permute-start.36) | collective-permute-done | bytes 1048608 | tf_op jit(solution)/shard_map/ppermute | solution.py:931
  (293 shorter events, 121.1 us)
Async XLA Ops:
  8.3 26.9 %collective-permute-start.2 = (f32[1024,128]{1,0:T(8,128)S(1)}, f32[1024,128]{1,0:T(8,128)}, u32[]{:S(2)}, u32[]{:S(2)}) collective-permute-start(f32[1024,128]{1,0:T(8,128)S(1)} %dynamic-slice_bitcast_fusion.refs_0_), channel_id=1, source_target_pairs={{3,0},{0,1},{1,2},{2,3},{7,4},{4,5},{5,6},{6,7},{11,8},{8,9},{9,10... | collective-permute-start | bytes 1572872 | tf_op jit(solution)/shard_map/ppermute | solution.py:854
  11.4 24.7 %collective-permute-start.1 = (f32[1024,128]{1,0:T(8,128)S(1)}, f32[1024,128]{1,0:T(8,128)}, u32[]{:S(2)}, u32[]{:S(2)}) collective-permute-start(f32[1024,128]{1,0:T(8,128)S(1)} %dynamic-slice_bitcast_fusion.refs_0_), channel_id=1, source_target_pairs={{1,0},{2,1},{3,2},{0,3},{5,4},{6,5},{7,6},{4,7},{9,8},{10,9},{11,1... | collective-permute-start | bytes 1572872 | tf_op jit(solution)/shard_map/ppermute | solution.py:854
  13.5 45.6 %collective-permute-start = (f32[1024,128]{1,0:T(8,128)S(1)}, f32[1024,128]{1,0:T(8,128)S(1)}, u32[]{:S(2)}, u32[]{:S(2)}) collective-permute-start(f32[1024,128]{1,0:T(8,128)S(1)} %dynamic-slice_bitcast_fusion.refs_0_), channel_id=1, source_target_pairs={{2,0},{3,1},{0,2},{1,3},{6,4},{7,5},{4,6},{5,7},{10,8},{11,9},{8,1... | collective-permute-start | bytes 1572872 | tf_op jit(solution)/shard_map/ppermute | solution.py:854
  65.7 31.9 %copy-start.39 = (bf16[512,1024]{1,0:T(8,128)(2,1)S(1)}, bf16[512,1024]{1,0:T(8,128)(2,1)}, u32[]{:S(2)}) copy-start(bf16[512,1024]{1,0:T(8,128)(2,1)} %refs_1_.1) | copy-start | bytes 3145732
  65.7 31.9 %copy-start.43 = (f32[1024]{0:T(1024)S(1)}, f32[1024]{0:T(1024)}, u32[]{:S(2)}) copy-start(f32[1024]{0:T(1024)} %param.26) | copy-start | bytes 12292
  65.8 30.5 %all-to-all-start = ((f32[8,512,128]{2,1,0:T(8,128)}), f32[8,512,128]{2,1,0:T(8,128)S(1)}, u32[]{:S(2)}, u32[]{:S(2)}) async-start(f32[8,512,128]{2,1,0:T(8,128)} %bitcast.94), calls=%async_computation | async-start | bytes 4194304 | tf_op jit(solution)/shard_map/all_to_all | solution.py:859
  69.6 291.5 %reduce-scatter.2.cloned.1.call-start = ((), (), s32[]{:S(2)}) async-start(), calls=%async_computation.5 | async-start | bytes 18874368 | tf_op jit(solution)/shard_map/reduce_scatter | solution.py:922
  108.4 117.6 %copy-start.6 = (bf16[512,1024]{1,0:T(8,128)(2,1)}, bf16[512,1024]{1,0:T(8,128)(2,1)S(1)}, u32[]{:S(2)}) copy-start(bf16[512,1024]{1,0:T(8,128)(2,1)S(1)} %get-tuple-element.252.refs_0_.refs_1_.refs_2_.refs_4_.refs_5_.refs_6_) | copy-start | bytes 3145732
  122.1 103.9 %copy-start.11 = (bf16[512,1024]{1,0:T(8,128)(2,1)}, bf16[512,1024]{1,0:T(8,128)(2,1)S(1)}, u32[]{:S(2)}) copy-start(bf16[512,1024]{1,0:T(8,128)(2,1)S(1)} %get-tuple-element.255.refs_3_.refs_7_) | copy-start | bytes 3145732
  167.8 49.0 %slice-start = ((s8[6291456]{0:T(1024)(128)(4,1)}), s8[2097152]{0:T(1024)(128)(4,1)S(1)}, s32[]{:S(2)}) async-start(s8[6291456]{0:T(1024)(128)(4,1)} %bitcast.92), calls=%async_computation.6 | async-start | bytes 4194304
  187.3 38.7 %copy-start.13 = (bf16[512,1024]{1,0:T(8,128)(2,1)}, bf16[512,1024]{1,0:T(8,128)(2,1)S(1)}, u32[]{:S(2)}) copy-start(bf16[512,1024]{1,0:T(8,128)(2,1)S(1)} %get-tuple-element.277.d_attended.refs_7_.refs_11_) | copy-start | bytes 3145732
  193.8 80.0 %collective-permute-start.5 = (f32[4,512,1024]{2,1,0:T(8,128)}, f32[4,512,1024]{2,1,0:T(8,128)}, u32[]{:S(2)}, u32[]{:S(2)}) collective-permute-start(f32[4,512,1024]{2,1,0:T(8,128)} %halving_first.2), channel_id=1, source_target_pairs={{0,4},{4,0},{8,12},{12,8},{16,20},{20,16},{24,28},{28,24},{1,5},{5... | collective-permute-start | bytes 25165832 | tf_op jit(solution)/shard_map/ppermute | solution.py:782
  232.1 132.2 %collective-permute-start.3 = (f32[4,512,1024]{2,1,0:T(8,128)}, f32[4,512,1024]{2,1,0:T(8,128)}, u32[]{:S(2)}, u32[]{:S(2)}) collective-permute-start(f32[4,512,1024]{2,1,0:T(8,128)} %halving_first.3), channel_id=1, source_target_pairs={{0,4},{4,0},{8,12},{12,8},{16,20},{20,16},{24,28},{28,24},{1,5},{5... | collective-permute-start | bytes 25165832 | tf_op jit(solution)/shard_map/ppermute | solution.py:782
  232.6 36.7 %all-to-all-start.1 = ((f32[8,512,128]{2,1,0:T(8,128)}), f32[8,512,128]{2,1,0:T(8,128)S(1)}, u32[]{:S(2)}, u32[]{:S(2)}) async-start(f32[8,512,128]{2,1,0:T(8,128)} %copy-done.38), calls=%async_computation.2 | async-start | bytes 4194304 | tf_op jit(solution)/shard_map/all_to_all | solution.py:859
  282.8 60.2 %copy-start.30 = (f32[4,256,1024]{2,1,0:T(8,128)}, f32[4,256,1024]{2,1,0:T(8,128)S(1)}, u32[]{:S(2)}) copy-start(f32[4,256,1024]{2,1,0:T(8,128)S(1)} %get-tuple-element.319) | copy-start | bytes 12582916
  282.8 58.2 %collective-permute-start.8 = (f32[2,256,1024]{2,1,0:T(8,128)S(1)}, f32[2,256,1024]{2,1,0:T(8,128)S(1)}, u32[]{:S(2)}, u32[]{:S(2)}) collective-permute-start(f32[2,256,1024]{2,1,0:T(8,128)S(1)} %get-tuple-element.320), channel_id=1, source_target_pairs={{0,8},{4,12},{8,0},{12,4},{16,24},{20,28},{24,16},{28,20},{1,9},{5... | collective-permute-start | bytes 6291464 | tf_op jit(solution)/shard_map/ppermute | solution.py:782
  283.3 59.2 %collective-permute-start.9 = (f32[2,256,1024]{2,1,0:T(8,128)S(1)}, f32[2,256,1024]{2,1,0:T(8,128)S(1)}, u32[]{:S(2)}, u32[]{:S(2)}) collective-permute-start(f32[2,256,1024]{2,1,0:T(8,128)S(1)} %get-tuple-element.321), channel_id=1, source_target_pairs={{0,16},{4,20},{8,24},{12,28},{16,0},{20,4},{24,8},{28,12},{1,17},{... | collective-permute-start | bytes 6291464 | tf_op jit(solution)/shard_map/ppermute | solution.py:782
  284.0 64.0 %collective-permute-start.4 = (f32[1024,128]{1,0:T(8,128)S(1)}, f32[1024,128]{1,0:T(8,128)S(1)}, u32[]{:S(2)}, u32[]{:S(2)}) collective-permute-start(f32[1024,128]{1,0:T(8,128)S(1)} %spread.4), channel_id=1, source_target_pairs={{2,0},{3,1},{0,2},{1,3},{6,4},{7,5},{4,6},{5,7},{10,8},{11,9},{8,1... | collective-permute-start | bytes 1572872 | tf_op jit(solution)/shard_map/ppermute | solution.py:854
  300.2 48.4 %collective-permute-start.7 = (f32[1024,128]{1,0:T(8,128)S(1)}, f32[1024,128]{1,0:T(8,128)S(1)}, u32[]{:S(2)}, u32[]{:S(2)}) collective-permute-start(f32[1024,128]{1,0:T(8,128)S(1)} %spread.6), channel_id=1, source_target_pairs={{1,0},{2,1},{3,2},{0,3},{5,4},{6,5},{7,6},{4,7},{9,8},{10,9},{11,1... | collective-permute-start | bytes 1572872 | tf_op jit(solution)/shard_map/ppermute | solution.py:854
  341.0 15.0 %collective-permute-start.6 = (f32[1024,128]{1,0:T(8,128)S(1)}, f32[1024,128]{1,0:T(8,128)S(1)}, u32[]{:S(2)}, u32[]{:S(2)}) collective-permute-start(f32[1024,128]{1,0:T(8,128)S(1)} %spread.5), channel_id=1, source_target_pairs={{3,0},{0,1},{1,2},{2,3},{7,4},{4,5},{5,6},{6,7},{11,8},{8,9},{9,10... | collective-permute-start | bytes 1572872 | tf_op jit(solution)/shard_map/ppermute | solution.py:854
  346.5 29.7 %collective-permute-start.13 = (f32[2,128,1024]{2,1,0:T(8,128)}, f32[2,128,1024]{2,1,0:T(8,128)}, u32[]{:S(2)}, u32[]{:S(2)}) collective-permute-start(f32[2,128,1024]{2,1,0:T(8,128)} %get-tuple-element.349), channel_id=1, source_target_pairs={{0,16},{4,20},{8,24},{12,28},{16,0},{20,4},{24,8},{28,12},{1,17},{... | collective-permute-start | bytes 3145736 | tf_op jit(solution)/shard_map/ppermute | solution.py:782
  348.0 28.3 %collective-permute-start.14 = (f32[2,128,1024]{2,1,0:T(8,128)}, f32[2,128,1024]{2,1,0:T(8,128)}, u32[]{:S(2)}, u32[]{:S(2)}) collective-permute-start(f32[2,128,1024]{2,1,0:T(8,128)} %get-tuple-element.350), channel_id=1, source_target_pairs={{0,8},{4,12},{8,0},{12,4},{16,24},{20,28},{24,16},{28,20},{1,9},{5... | collective-permute-start | bytes 3145736 | tf_op jit(solution)/shard_map/ppermute | solution.py:782
  356.9 24.1 %all-to-all-start.2 = ((f32[8,128,128]{2,1,0:T(8,128)}), f32[8,128,128]{2,1,0:T(8,128)}, u32[]{:S(2)}, u32[]{:S(2)}) async-start(f32[8,128,128]{2,1,0:T(8,128)} %bitcast.18), calls=%async_computation.3 | async-start | bytes 1048576 | tf_op jit(solution)/shard_map/all_to_all | solution.py:859
  374.4 25.4 %collective-permute-start.12 = (f32[256,1024]{1,0:T(8,128)}, f32[256,1024]{1,0:T(8,128)S(1)}, u32[]{:S(2)}, u32[]{:S(2)}) collective-permute-start(f32[256,1024]{1,0:T(8,128)} %get-tuple-element.346), channel_id=1, source_target_pairs={{0,1},{3,2},{4,5},{7,6},{8,9},{11,10},{12,13},{15,14},{16,17},{19,... | collective-permute-start | bytes 3145736 | tf_op jit(solution)/shard_map/ppermute | solution.py:925
  383.5 48.2 %collective-permute-start.10 = (f32[2,256,1024]{2,1,0:T(8,128)}, f32[2,256,1024]{2,1,0:T(8,128)}, u32[]{:S(2)}, u32[]{:S(2)}) collective-permute-start(f32[2,256,1024]{2,1,0:T(8,128)} %copy-done.53), channel_id=1, source_target_pairs={{0,8},{4,12},{8,0},{12,4},{16,24},{20,28},{24,16},{28,20},{1,9},{5... | collective-permute-start | bytes 6291464 | tf_op jit(solution)/shard_map/ppermute | solution.py:782
  385.4 47.7 %collective-permute-start.11 = (f32[2,256,1024]{2,1,0:T(8,128)}, f32[2,256,1024]{2,1,0:T(8,128)}, u32[]{:S(2)}, u32[]{:S(2)}) collective-permute-start(f32[2,256,1024]{2,1,0:T(8,128)} %copy-done.52), channel_id=1, source_target_pairs={{0,16},{4,20},{8,24},{12,28},{16,0},{20,4},{24,8},{28,12},{1,17},{... | collective-permute-start | bytes 6291464 | tf_op jit(solution)/shard_map/ppermute | solution.py:782
  391.1 31.0 %collective-permute-start.16 = (f32[256,1024]{1,0:T(8,128)S(1)}, f32[256,1024]{1,0:T(8,128)}, u32[]{:S(2)}, u32[]{:S(2)}) collective-permute-start(f32[256,1024]{1,0:T(8,128)S(1)} %copy-done.58), channel_id=1, source_target_pairs={{0,1},{3,2},{4,5},{7,6},{8,9},{11,10},{12,13},{15,14},{16,17},{19,... | collective-permute-start | bytes 3145736 | tf_op jit(solution)/shard_map/ppermute | solution.py:925
  401.1 24.0 %collective-permute-start.15 = (f32[256,1024]{1,0:T(8,128)S(1)}, f32[256,1024]{1,0:T(8,128)}, u32[]{:S(2)}, u32[]{:S(2)}) collective-permute-start(f32[256,1024]{1,0:T(8,128)S(1)} %add.121), channel_id=1, source_target_pairs={{1,2},{2,1},{5,6},{6,5},{9,10},{10,9},{13,14},{14,13},{17,18},{18,... | collective-permute-start | bytes 3145736 | tf_op jit(solution)/shard_map/ppermute | solution.py:928
  405.3 52.7 %collective-permute-start.19 = (f32[2,128,1024]{2,1,0:T(8,128)}, f32[2,128,1024]{2,1,0:T(8,128)}, u32[]{:S(2)}, u32[]{:S(2)}) collective-permute-start(f32[2,128,1024]{2,1,0:T(8,128)} %get-tuple-element.392), channel_id=1, source_target_pairs={{0,1},{3,2},{4,5},{7,6},{8,9},{11,10},{12,13},{15,14},{16,17},{19,... | collective-permute-start | bytes 3145736 | tf_op jit(solution)/shard_map/ppermute | solution.py:925
  423.5 31.8 %collective-permute-start.20 = (f32[256,1024]{1,0:T(8,128)S(1)}, f32[256,1024]{1,0:T(8,128)}, u32[]{:S(2)}, u32[]{:S(2)}) collective-permute-start(f32[256,1024]{1,0:T(8,128)S(1)} %add.122), channel_id=1, source_target_pairs={{1,2},{2,1},{5,6},{6,5},{9,10},{10,9},{13,14},{14,13},{17,18},{18,... | collective-permute-start | bytes 3145736 | tf_op jit(solution)/shard_map/ppermute | solution.py:928
  426.5 27.6 %collective-permute-start.21 = (f32[256,1024]{1,0:T(8,128)S(1)}, f32[256,1024]{1,0:T(8,128)S(1)}, u32[]{:S(2)}, u32[]{:S(2)}) collective-permute-start(f32[256,1024]{1,0:T(8,128)S(1)} %add.123), channel_id=1, source_target_pairs={{1,0},{2,3},{5,4},{6,7},{9,8},{10,11},{13,12},{14,15},{17,16},{18,... | collective-permute-start | bytes 3145736 | tf_op jit(solution)/shard_map/ppermute | solution.py:931
  441.1 35.3 %collective-permute-start.17 = (f32[2,128,1024]{2,1,0:T(8,128)}, f32[2,128,1024]{2,1,0:T(8,128)}, u32[]{:S(2)}, u32[]{:S(2)}) collective-permute-start(f32[2,128,1024]{2,1,0:T(8,128)} %get-tuple-element.389), channel_id=1, source_target_pairs={{0,16},{4,20},{8,24},{12,28},{16,0},{20,4},{24,8},{28,12},{1,17},{... | collective-permute-start | bytes 3145736 | tf_op jit(solution)/shard_map/ppermute | solution.py:782
  442.6 33.8 %collective-permute-start.18 = (f32[2,128,1024]{2,1,0:T(8,128)}, f32[2,128,1024]{2,1,0:T(8,128)}, u32[]{:S(2)}, u32[]{:S(2)}) collective-permute-start(f32[2,128,1024]{2,1,0:T(8,128)} %get-tuple-element.390), channel_id=1, source_target_pairs={{0,8},{4,12},{8,0},{12,4},{16,24},{20,28},{24,16},{28,20},{1,9},{5... | collective-permute-start | bytes 3145736 | tf_op jit(solution)/shard_map/ppermute | solution.py:782
  456.6 25.2 %collective-permute-start.26 = (f32[256,1024]{1,0:T(8,128)S(1)}, f32[256,1024]{1,0:T(8,128)}, u32[]{:S(2)}, u32[]{:S(2)}) collective-permute-start(f32[256,1024]{1,0:T(8,128)S(1)} %add.126), channel_id=1, source_target_pairs={{1,0},{2,3},{5,4},{6,7},{9,8},{10,11},{13,12},{14,15},{17,16},{18,... | collective-permute-start | bytes 3145736 | tf_op jit(solution)/shard_map/ppermute | solution.py:931
  459.7 23.4 %collective-permute-start.25 = (f32[2,128,1024]{2,1,0:T(8,128)S(1)}, f32[2,128,1024]{2,1,0:T(8,128)}, u32[]{:S(2)}, u32[]{:S(2)}) collective-permute-start(f32[2,128,1024]{2,1,0:T(8,128)S(1)} %add.127), channel_id=1, source_target_pairs={{1,2},{2,1},{5,6},{6,5},{9,10},{10,9},{13,14},{14,13},{17,18},{18,... | collective-permute-start | bytes 3145736 | tf_op jit(solution)/shard_map/ppermute | solution.py:928
  470.0 28.6 %collective-permute-start.24 = (f32[2,128,1024]{2,1,0:T(8,128)S(1)}, f32[2,128,1024]{2,1,0:T(8,128)S(1)}, u32[]{:S(2)}, u32[]{:S(2)}) collective-permute-start(f32[2,128,1024]{2,1,0:T(8,128)S(1)} %copy-done.57), channel_id=1, source_target_pairs={{0,1},{3,2},{4,5},{7,6},{8,9},{11,10},{12,13},{15,14},{16,17},{19,... | collective-permute-start | bytes 3145736 | tf_op jit(solution)/shard_map/ppermute | solution.py:925
  484.6 43.1 %collective-permute-start.28 = (f32[2,128,1024]{2,1,0:T(8,128)S(1)}, f32[2,128,1024]{2,1,0:T(8,128)S(1)}, u32[]{:S(2)}, u32[]{:S(2)}) collective-permute-start(f32[2,128,1024]{2,1,0:T(8,128)S(1)} %add.129), channel_id=1, source_target_pairs={{1,0},{2,3},{5,4},{6,7},{9,8},{10,11},{13,12},{14,15},{17,16},{18,... | collective-permute-start | bytes 3145736 | tf_op jit(solution)/shard_map/ppermute | solution.py:931
  498.7 29.1 %collective-permute-start.27 = (f32[2,128,1024]{2,1,0:T(8,128)S(1)}, f32[2,128,1024]{2,1,0:T(8,128)S(1)}, u32[]{:S(2)}, u32[]{:S(2)}) collective-permute-start(f32[2,128,1024]{2,1,0:T(8,128)S(1)} %add.130), channel_id=1, source_target_pairs={{1,2},{2,1},{5,6},{6,5},{9,10},{10,9},{13,14},{14,13},{17,18},{18,... | collective-permute-start | bytes 3145736 | tf_op jit(solution)/shard_map/ppermute | solution.py:928
  499.5 29.8 %collective-permute-start.23 = (f32[2,128,1024]{2,1,0:T(8,128)S(1)}, f32[2,128,1024]{2,1,0:T(8,128)S(1)}, u32[]{:S(2)}, u32[]{:S(2)}) collective-permute-start(f32[2,128,1024]{2,1,0:T(8,128)S(1)} %get-tuple-element.418), channel_id=1, source_target_pairs={{0,1},{3,2},{4,5},{7,6},{8,9},{11,10},{12,13},{15,14},{16,17},{19,... | collective-permute-start | bytes 3145736 | tf_op jit(solution)/shard_map/ppermute | solution.py:925
  506.5 21.1 %collective-permute-start.29 = (f32[1,1793]{1,0:T(1,128)S(1)}, f32[1,1793]{1,0:T(1,128)S(1)}, u32[]{:S(2)}, u32[]{:S(2)}) collective-permute-start(f32[1,1793]{1,0:T(1,128)S(1)} %broadcast_in_dim.27), channel_id=1, source_target_pairs={{0,1},{3,2},{4,5},{7,6},{8,9},{11,10},{12,13},{15,14},{16,17},{19,... | collective-permute-start | bytes 21524 | tf_op jit(solution)/shard_map/ppermute | solution.py:1054
  528.0 24.6 %collective-permute-start.31 = (f32[2,128,1024]{2,1,0:T(8,128)S(1)}, f32[2,128,1024]{2,1,0:T(8,128)S(1)}, u32[]{:S(2)}, u32[]{:S(2)}) collective-permute-start(f32[2,128,1024]{2,1,0:T(8,128)S(1)} %add.132), channel_id=1, source_target_pairs={{1,0},{2,3},{5,4},{6,7},{9,8},{10,11},{13,12},{14,15},{17,16},{18,... | collective-permute-start | bytes 3145736 | tf_op jit(solution)/shard_map/ppermute | solution.py:931
  529.5 23.3 %collective-permute-start.30 = (f32[2,128,1024]{2,1,0:T(8,128)S(1)}, f32[2,128,1024]{2,1,0:T(8,128)S(1)}, u32[]{:S(2)}, u32[]{:S(2)}) collective-permute-start(f32[2,128,1024]{2,1,0:T(8,128)S(1)} %add.133), channel_id=1, source_target_pairs={{1,2},{2,1},{5,6},{6,5},{9,10},{10,9},{13,14},{14,13},{17,18},{18,... | collective-permute-start | bytes 3145736 | tf_op jit(solution)/shard_map/ppermute | solution.py:928
  530.2 26.1 %collective-permute-start.22 = (f32[2,128,1024]{2,1,0:T(8,128)S(1)}, f32[2,128,1024]{2,1,0:T(8,128)S(1)}, u32[]{:S(2)}, u32[]{:S(2)}) collective-permute-start(f32[2,128,1024]{2,1,0:T(8,128)S(1)} %get-tuple-element.417), channel_id=1, source_target_pairs={{0,1},{3,2},{4,5},{7,6},{8,9},{11,10},{12,13},{15,14},{16,17},{19,... | collective-permute-start | bytes 3145736 | tf_op jit(solution)/shard_map/ppermute | solution.py:925
  536.7 0.7 collective-permute-start.32
  553.0 25.5 %collective-permute-start.34 = (f32[2,128,1024]{2,1,0:T(8,128)S(1)}, f32[2,128,1024]{2,1,0:T(8,128)S(1)}, u32[]{:S(2)}, u32[]{:S(2)}) collective-permute-start(f32[2,128,1024]{2,1,0:T(8,128)S(1)} %add.135), channel_id=1, source_target_pairs={{1,0},{2,3},{5,4},{6,7},{9,8},{10,11},{13,12},{14,15},{17,16},{18,... | collective-permute-start | bytes 3145736 | tf_op jit(solution)/shard_map/ppermute | solution.py:931
  556.5 22.1 %collective-permute-start.33 = (f32[2,128,1024]{2,1,0:T(8,128)S(1)}, f32[2,128,1024]{2,1,0:T(8,128)S(1)}, u32[]{:S(2)}, u32[]{:S(2)}) collective-permute-start(f32[2,128,1024]{2,1,0:T(8,128)S(1)} %add.136), channel_id=1, source_target_pairs={{1,2},{2,1},{5,6},{6,5},{9,10},{10,9},{13,14},{14,13},{17,18},{18,... | collective-permute-start | bytes 3145736 | tf_op jit(solution)/shard_map/ppermute | solution.py:928
  558.7 19.7 %collective-permute-start.35 = (f32[1,1793]{1,0:T(1,128)S(1)}, f32[1,1793]{1,0:T(1,128)S(1)}, u32[]{:S(2)}, u32[]{:S(2)}) collective-permute-start(f32[1,1793]{1,0:T(1,128)S(1)} %add.134), channel_id=1, source_target_pairs={{1,0},{2,3},{5,4},{6,7},{9,8},{10,11},{13,12},{14,15},{17,16},{18,... | collective-permute-start | bytes 21524 | tf_op jit(solution)/shard_map/ppermute | solution.py:1060
  578.8 23.4 %collective-permute-start.36 = (f32[2,128,1024]{2,1,0:T(8,128)S(1)}, f32[2,128,1024]{2,1,0:T(8,128)S(1)}, u32[]{:S(2)}, u32[]{:S(2)}) collective-permute-start(f32[2,128,1024]{2,1,0:T(8,128)S(1)} %add.137), channel_id=1, source_target_pairs={{1,0},{2,3},{5,4},{6,7},{9,8},{10,11},{13,12},{14,15},{17,16},{18,... | collective-permute-start | bytes 3145736 | tf_op jit(solution)/shard_map/ppermute | solution.py:931
  (66 other events, 454.4 us)
Sparse Core Ops, SparseCore 0:
  159.4 149.3 reduce-scatter.1
